TPU v7x, 512 devices: a whole 4x8x8 slice. The times are simulated.
512 devices in a mesh: gx: 16 (over z, y_lo), gy: 32 (over x, y_hi, core).
Axes of the slice: x: 4, y: 8 (y_hi: 4, y_lo: 2; y = y_hi * 2 + y_lo), z: 8, core: 2. Of those that a mesh axis runs over, the one named last changes fastest.
Arguments:
- forcing_late: bfloat16 [4, 137, 512, 512], P(None, None, 'gx', 'gy'), may hold values from -6 to 6
- forcing_early: bfloat16 [4, 137, 512, 512], P(None, None, 'gx', 'gy'), may hold values from -6 to 6
- stencil_coef: float32 [4, 512, 512], P(None, 'gx', 'gy'), may hold values from 0.05 to 0.25
- jacobian: bfloat16 [16, 512, 4, 137, 137], P('gx', 'gy'), may hold values from -0.5 to 0.5
- cloudy_cols: int32 [16, 32, 48], P('gx', 'gy'), may hold values from 0 to 511, as said below
- cloudy_count: int32 [16, 32], P('gx', 'gy'), may hold values from 0 to 48, as said below
- owner_rank: int32 [16, 32, 48], P('gx', 'gy'), may hold values from 0 to 31, as said below
- owner_slot: int32 [16, 32, 48], P('gx', 'gy'), may hold values from 0 to 15, as said below
Outputs:
- adjoint_state: float32 [4, 137, 512, 512], P(None, None, 'gx', 'gy')
Inputs may be any that keep to these rules, and one draw needn't show every extreme that they name: `cloudy_count`: entries beyond a domain's count are to be ignored; the cloudy_cols of a domain are all distinct. Over one longitude row of domains the counts sum to 16 * 32, and one domain has exactly 48. `cloudy_cols`: distinct within a domain. `owner_rank`: within one longitude row of domains each owner receives exactly 16 live cloudy columns; one domain sends at most 2 of them to one owner, and some domain sends exactly 2 to some owner in every row. `owner_slot`: within one longitude row of domains the live columns that go to one owner take its slots 0 to 15, each once.
All inputs are finite; a program needn't handle non-finite values.
Results may differ from a plain program's by a relative error of at most 0.0008.
Values may be sent and summed in bfloat16 or wider, within the bound.
No kernel may reach another device: no remote copies, remote signals or barrier semaphores. Data moves between devices by JAX's collectives and lax.ppermute only.
A program may use at most 64 MiB of HBM per device.

v0:
```python
import jax
import jax.numpy as jnp
from jax import lax
from jax.sharding import PartitionSpec as P


def with_halo(block, sides, width, periodic):
    for axis, dim in sides:
        count = lax.axis_size(axis)
        forward = [(i, i + 1) for i in range(count - 1)]
        if periodic:
            forward.append((count - 1, 0))
        backward = [(target, source) for source, target in forward]
        low = lax.ppermute(
            lax.slice_in_dim(block, block.shape[dim] - width, None, axis=dim), axis, forward
        )
        high = lax.ppermute(lax.slice_in_dim(block, 0, width, axis=dim), axis, backward)
        block = jnp.concatenate([low, block, high], axis=dim)
    return block


def apply_stencil(field, lon_ext, lat_ext, stencil_coef):
    return (
        field
        + stencil_coef[0] * lon_ext[:, :, :-2, :]
        + stencil_coef[1] * lon_ext[:, :, 2:, :]
        + stencil_coef[2] * lat_ext[:, :, :, :-2]
        + stencil_coef[3] * lat_ext[:, :, :, 2:]
    )


def on_device(
    forcing_late,
    forcing_early,
    stencil_coef,
    jacobian,
    cloudy_cols,
    cloudy_count,
    owner_rank,
    owner_slot,
):
    fields, levels, span_lon, span_lat = forcing_late.shape
    column_depth = fields * levels
    columns_all = span_lon * span_lat
    groups = lax.axis_size("gy")
    own_slots = jacobian.shape[1]
    capacity = cloudy_cols.shape[2]
    pair_cap = (capacity + groups - 1) // groups
    columns = cloudy_cols[0, 0]
    entries = jnp.arange(capacity, dtype=jnp.int32)
    usable = entries < cloudy_count[0, 0]
    owners = owner_rank[0, 0]
    earlier = (
        (owners[:, None] == owners[None, :])
        & usable[None, :]
        & (entries[None, :] < entries[:, None])
    )
    order_rank = jnp.sum(earlier.astype(jnp.int32), axis=1)
    target = jnp.where(usable, owners * pair_cap + order_rank, groups * pair_cap)
    send_slot = (
        jnp.full((groups * pair_cap,), -1, jnp.int32).at[target].set(owner_slot[0, 0], mode="drop")
    )
    recv_slot = lax.all_to_all(
        send_slot.reshape(groups, pair_cap), "gy", split_axis=0, concat_axis=0, tiled=True
    ).reshape(-1)
    live = recv_slot >= 0
    recv_index = jnp.where(live, recv_slot, own_slots)
    fetch_index = jnp.minimum(recv_index, own_slots - 1)
    target_fetch = jnp.minimum(target, groups * pair_cap - 1)
    weight_mask = usable.astype(jnp.float32)[:, None]
    matrices = jacobian[0]

    def increment(adjoint):
        flattened = adjoint.reshape(column_depth, columns_all)
        picked = jnp.take(flattened, columns, axis=1).T.astype(jnp.bfloat16)
        outbox = (
            jnp.zeros((groups * pair_cap, column_depth), jnp.bfloat16)
            .at[target]
            .set(picked, mode="drop")
        )
        received = lax.all_to_all(
            outbox.reshape(groups, pair_cap, column_depth),
            "gy",
            split_axis=0,
            concat_axis=0,
            tiled=True,
        )
        received = received.reshape(groups * pair_cap, column_depth)
        placed = (
            jnp.zeros((own_slots, column_depth), jnp.bfloat16)
            .at[recv_index]
            .set(received, mode="drop")
        )
        result = jnp.einsum(
            "sfij,sfi->sfj",
            matrices,
            placed.reshape(own_slots, fields, levels),
            preferred_element_type=jnp.float32,
        ).reshape(own_slots, column_depth)
        answer = jnp.where(live[:, None], jnp.take(result, fetch_index, axis=0), 0.0)
        returned = lax.all_to_all(
            answer.reshape(groups, pair_cap, column_depth),
            "gy",
            split_axis=0,
            concat_axis=0,
            tiled=True,
        )
        returned_rows = (
            jnp.take(returned.reshape(groups * pair_cap, column_depth), target_fetch, axis=0)
            * weight_mask
        )
        increment_field = (
            jnp.zeros((column_depth, columns_all), jnp.float32).at[:, columns].add(returned_rows.T)
        )
        return increment_field.reshape(adjoint.shape)

    def main_sweep(field):
        lon_ext = with_halo(field, (("gx", 2),), 1, True)
        lat_ext = with_halo(field, (("gy", 3),), 1, False)
        return apply_stencil(field, lon_ext, lat_ext, stencil_coef)

    def advance(adjoint):
        return main_sweep(adjoint + increment(adjoint))

    adjoint = advance(forcing_late.astype(jnp.float32))
    adjoint = adjoint + forcing_early.astype(jnp.float32)
    return advance(adjoint)


def solution(mesh):
    return jax.shard_map(
        on_device,
        mesh=mesh,
        in_specs=(
            P(None, None, "gx", "gy"),
            P(None, None, "gx", "gy"),
            P(None, "gx", "gy"),
            P("gx", "gy", None, None, None),
            P("gx", "gy", None),
            P("gx", "gy"),
            P("gx", "gy", None),
            P("gx", "gy", None),
        ),
        out_specs=P(None, None, "gx", "gy"),
        check_vma=False,
    )
```

profile of v0, /device:TPU:1, one launch (start us, length us, event | category | flops | bytes accessed | tf_op | source)
XLA Modules:
  0.0 172.1 jit_solution(11128534165830638718)
XLA Ops:
  3.8 11.2 %all-to-all-start = ((s32[32,1,2]{2,1,0:T(1,128)}), s32[32,1,2]{2,1,0:T(1,128)S(1)}, u32[]{:S(2)}, u32[]{:S(2)}) async-start(s32[32,1,2]{2,1,0:T(1,128)} %bitcast.8), calls=%async_computation | async-start | bytes 32768 | tf_op jit(solution)/shard_map/all_to_all | solution.py:63
  17.1 2.0 %copy_convert_fusion = f32[4,137,32,16]{1,0,3,2:T(4,128)S(1)} fusion(bf16[4,137,32,16]{1,3,2,0:T(8,128)(2,1)} %param.14), kind=kLoop, calls=%fused_computation.42 | loop fusion | flops 280576 | bytes 1683456 | tf_op jit(solution)/shard_map/convert_element_type | solution.py:125
  22.3 2.1 %all-to-all-done = s32[32,1,2]{2,1,0:T(1,128)S(1)} async-done(((s32[32,1,2]{2,1,0:T(1,128)}), s32[32,1,2]{2,1,0:T(1,128)S(1)}, u32[]{:S(2)}, u32[]{:S(2)}) %all-to-all-start) | async-done | bytes 288 | tf_op jit(solution)/shard_map/all_to_all | solution.py:63
  24.4 7.7 %all-to-all-start.1 = ((bf16[32,2,548]{2,1,0:T(2,128)(2,1)}), bf16[32,2,548]{2,1,0:T(2,128)(2,1)S(1)}, u32[]{:S(2)}, u32[]{:S(2)}) async-start(bf16[32,2,548]{2,1,0:T(2,128)(2,1)} %reshape.188), calls=%async_computation.1 | async-start | bytes 163840 | tf_op jit(solution)/shard_map/all_to_all | solution.py:81
  33.5 8.5 %all-to-all-done.1 = bf16[32,2,548]{2,1,0:T(2,128)(2,1)S(1)} async-done(((bf16[32,2,548]{2,1,0:T(2,128)(2,1)}), bf16[32,2,548]{2,1,0:T(2,128)(2,1)S(1)}, u32[]{:S(2)}, u32[]{:S(2)}) %all-to-all-start.1) | async-done | bytes 70176 | tf_op jit(solution)/shard_map/all_to_all | solution.py:81
  43.0 3.0 %fusion.2 = f32[16,4,1,137]{3,2,1,0:T(1,128)S(1)} fusion(bf16[16,4,137,1]{2,3,1,0:T(2,128)(2,1)S(1)} %reshape.330, bf16[16,4,137,137]{3,1,2,0:T(4,128)(2,1)} %bitcast.79), kind=kOutput, calls=%fused_computation.15 | convolution fusion | flops 2402432 | bytes 2455040 | tf_op jit(solution)/shard_map/sfij,sfi->sfj/dot_general | solution.py:94
  47.7 3.9 %all-to-all-start.2 = ((f32[32,2,548]{2,1,0:T(2,128)}), f32[32,2,548]{2,1,0:T(2,128)S(1)}, u32[]{:S(2)}, u32[]{:S(2)}) async-start(f32[32,2,548]{2,1,0:T(2,128)} %reshape.192), calls=%async_computation.2 | async-start | bytes 327680 | tf_op jit(solution)/shard_map/all_to_all | solution.py:101
  51.7 11.5 %all-to-all-done.2 = f32[32,2,548]{2,1,0:T(2,128)S(1)} async-done(((f32[32,2,548]{2,1,0:T(2,128)}), f32[32,2,548]{2,1,0:T(2,128)S(1)}, u32[]{:S(2)}, u32[]{:S(2)}) %all-to-all-start.2) | async-done | bytes 140320 | tf_op jit(solution)/shard_map/all_to_all | solution.py:101
  66.2 2.4 %fusion.25 = f32[4,137,32,16]{1,0,3,2:T(4,128)S(1)} fusion(f32[4,137,32,16]{1,0,3,2:T(4,128)S(1)} %reshape.194, bf16[4,137,32,16]{1,3,2,0:T(8,128)(2,1)} %param.14), kind=kLoop, calls=%fused_computation.47 | loop fusion | flops 561152 | bytes 2805760 | tf_op jit(solution)/shard_map/add | solution.py:123
  70.0 2.8 %collective-permute-start = (f32[4,137,1,16]{1,0,3,2:T(4,128)S(1)}, f32[4,137,1,16]{1,0,3,2:T(4,128)S(1)}, u32[]{:S(2)}, u32[]{:S(2)}) collective-permute-start(f32[4,137,1,16]{1,0,3,2:T(4,128)S(1)} %get-tuple-element.16), channel_id=1, source_target_pairs={{0,32},{32,64},{64,96},{96,128},{128,160},{160,192},{192,224},{224... | collective-permute-start | bytes 105224 | tf_op jit(solution)/shard_map/ppermute | solution.py:14
  72.8 10.4 %collective-permute-start.1 = (f32[4,137,1,16]{1,0,3,2:T(4,128)S(1)}, f32[4,137,1,16]{1,0,3,2:T(4,128)S(1)}, u32[]{:S(2)}, u32[]{:S(2)}) collective-permute-start(f32[4,137,1,16]{1,0,3,2:T(4,128)S(1)} %get-tuple-element.17), channel_id=1, source_target_pairs={{32,0},{64,32},{96,64},{128,96},{160,128},{192,160},{224,192},{256... | collective-permute-start | bytes 105224 | tf_op jit(solution)/shard_map/ppermute | solution.py:17
  83.2 2.8 %collective-permute-start.2 = (f32[4,137,32,1]{1,0,3,2:T(4,128)S(1)}, f32[4,137,32,1]{1,0,3,2:T(4,128)S(1)}, u32[]{:S(2)}, u32[]{:S(2)}) collective-permute-start(f32[4,137,32,1]{1,0,3,2:T(4,128)S(1)} %get-tuple-element.18), channel_id=1, source_target_pairs={{0,1},{1,2},{2,3},{3,4},{4,5},{5,6},{6,7},{7,8},{8,9},{9,10},{10,1... | collective-permute-start | bytes 210440 | tf_op jit(solution)/shard_map/ppermute | solution.py:14
  86.0 2.1 %collective-permute-start.3 = (f32[4,137,32,1]{1,0,3,2:T(4,128)S(1)}, f32[4,137,32,1]{1,0,3,2:T(4,128)S(1)}, u32[]{:S(2)}, u32[]{:S(2)}) collective-permute-start(f32[4,137,32,1]{1,0,3,2:T(4,128)S(1)} %get-tuple-element.19), channel_id=1, source_target_pairs={{1,0},{2,1},{3,2},{4,3},{5,4},{6,5},{7,6},{8,7},{9,8},{10,9},{11,1... | collective-permute-start | bytes 210440 | tf_op jit(solution)/shard_map/ppermute | solution.py:17
  89.1 4.1 %collective-permute-done.3 = f32[4,137,32,1]{1,0,3,2:T(4,128)S(1)} collective-permute-done((f32[4,137,32,1]{1,0,3,2:T(4,128)S(1)}, f32[4,137,32,1]{1,0,3,2:T(4,128)S(1)}, u32[]{:S(2)}, u32[]{:S(2)}) %collective-permute-start.3) | collective-permute-done | bytes 70176 | tf_op jit(solution)/shard_map/ppermute | solution.py:17
  93.2 9.5 %fusion.14 = f32[4,137,32,16]{1,0,3,2:T(4,128)S(1)} fusion(f32[4,137,32,1]{1,0,3,2:T(4,128)S(1)} %collective-permute-done.3, f32[4,137,32,16]{1,0,3,2:T(4,128)} %copy-done, f32[4,137,32,1]{1,0,3,2:T(4,128)S(1)} %collective-permute-done.2, f32[4,137,1,16]{1,0,3,2:T(4,128)} %copy-done.2, f32[4,137,1,16]{1,0,3,2:T(4,128)S(1)} %collective-permute-done, ...), kind=kLoop, calls=%fused_computation.32 | loop fusion | flops 3928064 | bytes 3024384 | tf_op jit(solution)/shard_map/add | solution.py:126
  105.4 17.7 %all_to_all.29 = bf16[32,2,548]{2,1,0:T(2,128)(2,1)S(1)} all-to-all(bf16[32,2,548]{2,1,0:T(2,128)(2,1)S(1)} %reshape.196), channel_id=1, replica_groups=mesh['gx'=16,'gy'=32] {'gy'}, dimensions={0} | all-to-all | bytes 140288 | tf_op jit(solution)/shard_map/all_to_all | solution.py:81
  124.3 3.0 %fusion = f32[16,4,1,137]{3,2,1,0:T(1,128)S(1)} fusion(bf16[16,4,137,1]{2,3,1,0:T(2,128)(2,1)S(1)} %reshape.332, bf16[16,4,137,137]{3,1,2,0:T(4,128)(2,1)} %bitcast.80), kind=kOutput, calls=%fused_computation.13 | convolution fusion | flops 2402432 | bytes 2455040 | tf_op jit(solution)/shard_map/sfij,sfi->sfj/dot_general | solution.py:94
  128.4 14.3 %all_to_all.30 = f32[32,2,548]{2,1,0:T(2,128)S(1)} all-to-all(f32[32,2,548]{2,1,0:T(2,128)S(1)} %reshape.200), channel_id=1, replica_groups=mesh['gx'=16,'gy'=32] {'gy'}, dimensions={0} | all-to-all | bytes 280576 | tf_op jit(solution)/shard_map/all_to_all | solution.py:101
  143.5 3.4 %scatter_custom_fusion.6 = f32[548,512]{0,1:T(8,128)S(1)} fusion(s32[48]{0:T(128)} %copy-done.20, f32[]{:T(128)} %constant.3.clone.1, f32[]{:T(128)} %constant.15.clone.2, f32[48]{0:T(128)S(1)} %copy-done.16, pred[48]{0:T(512)(128)(4,1)S(1)} %copy-done.9, f32[64,548]{1,0:T(8,128)} %reshape.201, s32[1024]{0:T(1024)S(1)} %copy-done.4), kind=kCustom, calls=%fused_computation.43 | custom fusion | flops 78912 | bytes 1291504 | tf_op jit(solution)/shard_map/scatter-add | solution.py:113
  146.9 2.8 %reshape.202 = f32[4,137,32,16]{1,0,3,2:T(4,128)} reshape(f32[548,512]{0,1:T(8,128)S(1)} %scatter_custom_fusion.6) | data formatting | bytes 2244608 | tf_op jit(solution)/shard_map/reshape | solution.py:115
  149.7 2.1 %add.112 = f32[4,137,32,16]{1,0,3,2:T(4,128)S(1)} add(f32[4,137,32,16]{1,0,3,2:T(4,128)S(1)} %fusion.14, f32[4,137,32,16]{1,0,3,2:T(4,128)} %reshape.202) | non-fusion elementwise | flops 280576 | bytes 3366912 | tf_op jit(solution)/shard_map/add | solution.py:123
  153.8 2.4 %collective-permute-start.7 = (f32[4,137,32,1]{1,0,3,2:T(4,128)S(1)}, f32[4,137,32,1]{1,0,3,2:T(4,128)S(1)}, u32[]{:S(2)}, u32[]{:S(2)}) collective-permute-start(f32[4,137,32,1]{1,0,3,2:T(4,128)S(1)} %get-tuple-element.15), channel_id=1, source_target_pairs={{1,0},{2,1},{3,2},{4,3},{5,4},{6,5},{7,6},{8,7},{9,8},{10,9},{11,1... | collective-permute-start | bytes 210440 | tf_op jit(solution)/shard_map/ppermute | solution.py:17
  158.2 6.2 %collective-permute-start.5 = (f32[4,137,1,16]{1,0,3,2:T(4,128)S(1)}, f32[4,137,1,16]{1,0,3,2:T(4,128)S(1)}, u32[]{:S(2)}, u32[]{:S(2)}) collective-permute-start(f32[4,137,1,16]{1,0,3,2:T(4,128)S(1)} %get-tuple-element.13), channel_id=1, source_target_pairs={{32,0},{64,32},{96,64},{128,96},{160,128},{192,160},{224,192},{256... | collective-permute-start | bytes 105224 | tf_op jit(solution)/shard_map/ppermute | solution.py:17
  166.2 4.2 %fusion.5 = f32[4,137,32,16]{1,0,3,2:T(4,128)S(1)} fusion(f32[4,137,32,1]{1,0,3,2:T(4,128)S(1)} %collective-permute-done.7, f32[4,137,32,16]{1,0,3,2:T(4,128)S(1)} %add.112, f32[4,137,32,1]{1,0,3,2:T(4,128)S(1)} %collective-permute-done.6, f32[4,137,1,16]{1,0,3,2:T(4,128)S(1)} %collective-permute-done.5, f32[4,137,1,16]{1,0,3,2:T(4,128)S(1)} %collective-permute-done.4, ...), kind=kLoop, calls=%fused_computation.19 | loop fusion | flops 3366912 | bytes 2463232 | tf_op jit(solution)/shard_map/add | solution.py:24
  (106 shorter events, 30.7 us)
Async XLA Ops:
  2.2 18.4 %copy-start.17 = (s32[48]{0:T(128)}, s32[48]{0:T(128)S(1)}, u32[]{:S(2)}) copy-start(s32[48]{0:T(128)S(1)} %fusion.51) | copy-start | bytes 580
  3.8 20.6 %all-to-all-start = ((s32[32,1,2]{2,1,0:T(1,128)}), s32[32,1,2]{2,1,0:T(1,128)S(1)}, u32[]{:S(2)}, u32[]{:S(2)}) async-start(s32[32,1,2]{2,1,0:T(1,128)} %bitcast.8), calls=%async_computation | async-start | bytes 32768 | tf_op jit(solution)/shard_map/all_to_all | solution.py:63
  17.0 46.2 %copy-start.8 = (pred[48]{0:T(512)(128)(4,1)}, pred[48]{0:T(512)(128)(4,1)S(1)}, u32[]{:S(2)}) copy-start(pred[48]{0:T(512)(128)(4,1)S(1)} %get-tuple-element.10) | copy-start | bytes 148
  17.0 46.2 %copy-start.3 = (s32[1024]{0:T(1024)}, s32[1024]{0:T(1024)S(1)}, u32[]{:S(2)}) copy-start(s32[1024]{0:T(1024)S(1)} %pad_clamp_fusion) | copy-start | bytes 12292
  24.4 17.6 %all-to-all-start.1 = ((bf16[32,2,548]{2,1,0:T(2,128)(2,1)}), bf16[32,2,548]{2,1,0:T(2,128)(2,1)S(1)}, u32[]{:S(2)}, u32[]{:S(2)}) async-start(bf16[32,2,548]{2,1,0:T(2,128)(2,1)} %reshape.188), calls=%async_computation.1 | async-start | bytes 163840 | tf_op jit(solution)/shard_map/all_to_all | solution.py:81
  33.4 13.4 %copy-start.10 = (pred[64]{0:T(512)(128)(4,1)}, pred[64]{0:T(512)(128)(4,1)S(1)}, u32[]{:S(2)}) copy-start(pred[64]{0:T(512)(128)(4,1)S(1)} %get-tuple-element.6) | copy-start | bytes 196
  33.4 13.4 %copy-start.12 = (pred[64]{0:T(512)(128)(4,1)}, pred[64]{0:T(512)(128)(4,1)S(1)}, u32[]{:S(2)}) copy-start(pred[64]{0:T(512)(128)(4,1)S(1)} %get-tuple-element.24) | copy-start | bytes 196
  33.5 12.6 %copy-start.19 = (s32[64]{0:T(128)}, s32[64]{0:T(128)S(1)}, u32[]{:S(2)}) copy-start(s32[64]{0:T(128)S(1)} %fusion.50) | copy-start | bytes 772
  33.5 12.7 %copy-start.7 = (s32[1024]{0:T(1024)}, s32[1024]{0:T(1024)S(1)}, u32[]{:S(2)}) copy-start(s32[1024]{0:T(1024)S(1)} %pad_clamp_fusion.1) | copy-start | bytes 12292
  47.7 15.4 %all-to-all-start.2 = ((f32[32,2,548]{2,1,0:T(2,128)}), f32[32,2,548]{2,1,0:T(2,128)S(1)}, u32[]{:S(2)}, u32[]{:S(2)}) async-start(f32[32,2,548]{2,1,0:T(2,128)} %reshape.192), calls=%async_computation.2 | async-start | bytes 327680 | tf_op jit(solution)/shard_map/all_to_all | solution.py:101
  51.6 14.6 %copy-start.15 = (f32[48]{0:T(128)}, f32[48]{0:T(128)S(1)}, u32[]{:S(2)}) copy-start(f32[48]{0:T(128)S(1)} %fusion.58) | copy-start | bytes 580
  66.2 21.9 %copy-start.6 = (f32[4,32,16]{1,2,0:T(8,128)S(1)}, f32[4,32,16]{1,2,0:T(8,128)}, u32[]{:S(2)}) copy-start(f32[4,32,16]{1,2,0:T(8,128)} %param.16) | copy-start | bytes 24580
  66.2 27.0 %copy-start.1 = (bf16[4,137,32,16]{1,3,2,0:T(8,128)(2,1)S(1)}, bf16[4,137,32,16]{1,3,2,0:T(8,128)(2,1)}, u32[]{:S(2)}) copy-start(bf16[4,137,32,16]{1,3,2,0:T(8,128)(2,1)} %param.15) | copy-start | bytes 1683460
  70.0 18.5 %collective-permute-start = (f32[4,137,1,16]{1,0,3,2:T(4,128)S(1)}, f32[4,137,1,16]{1,0,3,2:T(4,128)S(1)}, u32[]{:S(2)}, u32[]{:S(2)}) collective-permute-start(f32[4,137,1,16]{1,0,3,2:T(4,128)S(1)} %get-tuple-element.16), channel_id=1, source_target_pairs={{0,32},{32,64},{64,96},{96,128},{128,160},{160,192},{192,224},{224... | collective-permute-start | bytes 105224 | tf_op jit(solution)/shard_map/ppermute | solution.py:14
  72.8 15.6 %collective-permute-start.1 = (f32[4,137,1,16]{1,0,3,2:T(4,128)S(1)}, f32[4,137,1,16]{1,0,3,2:T(4,128)S(1)}, u32[]{:S(2)}, u32[]{:S(2)}) collective-permute-start(f32[4,137,1,16]{1,0,3,2:T(4,128)S(1)} %get-tuple-element.17), channel_id=1, source_target_pairs={{32,0},{64,32},{96,64},{128,96},{160,128},{192,160},{224,192},{256... | collective-permute-start | bytes 105224 | tf_op jit(solution)/shard_map/ppermute | solution.py:17
  83.2 5.3 %collective-permute-start.2 = (f32[4,137,32,1]{1,0,3,2:T(4,128)S(1)}, f32[4,137,32,1]{1,0,3,2:T(4,128)S(1)}, u32[]{:S(2)}, u32[]{:S(2)}) collective-permute-start(f32[4,137,32,1]{1,0,3,2:T(4,128)S(1)} %get-tuple-element.18), channel_id=1, source_target_pairs={{0,1},{1,2},{2,3},{3,4},{4,5},{5,6},{6,7},{7,8},{8,9},{9,10},{10,1... | collective-permute-start | bytes 210440 | tf_op jit(solution)/shard_map/ppermute | solution.py:14
  86.0 7.2 %collective-permute-start.3 = (f32[4,137,32,1]{1,0,3,2:T(4,128)S(1)}, f32[4,137,32,1]{1,0,3,2:T(4,128)S(1)}, u32[]{:S(2)}, u32[]{:S(2)}) collective-permute-start(f32[4,137,32,1]{1,0,3,2:T(4,128)S(1)} %get-tuple-element.19), channel_id=1, source_target_pairs={{1,0},{2,1},{3,2},{4,3},{5,4},{6,5},{7,6},{8,7},{9,8},{10,9},{11,1... | collective-permute-start | bytes 210440 | tf_op jit(solution)/shard_map/ppermute | solution.py:17
  127.3 16.2 %copy-start.4 = (s32[1024]{0:T(1024)S(1)}, s32[1024]{0:T(1024)}, u32[]{:S(2)}) copy-start(s32[1024]{0:T(1024)} %copy-done.3) | copy-start | bytes 12292
  127.3 16.2 %copy-start.9 = (pred[48]{0:T(512)(128)(4,1)S(1)}, pred[48]{0:T(512)(128)(4,1)}, u32[]{:S(2)}) copy-start(pred[48]{0:T(512)(128)(4,1)} %copy-done.8) | copy-start | bytes 148
  127.3 16.2 %copy-start.16 = (f32[48]{0:T(128)S(1)}, f32[48]{0:T(128)}, u32[]{:S(2)}) copy-start(f32[48]{0:T(128)} %copy-done.15) | copy-start | bytes 580
  151.9 14.3 %collective-permute-start.6 = (f32[4,137,32,1]{1,0,3,2:T(4,128)S(1)}, f32[4,137,32,1]{1,0,3,2:T(4,128)S(1)}, u32[]{:S(2)}, u32[]{:S(2)}) collective-permute-start(f32[4,137,32,1]{1,0,3,2:T(4,128)S(1)} %get-tuple-element.14), channel_id=1, source_target_pairs={{0,1},{1,2},{2,3},{3,4},{4,5},{5,6},{6,7},{7,8},{8,9},{9,10},{10,1... | collective-permute-start | bytes 210440 | tf_op jit(solution)/shard_map/ppermute | solution.py:14
  153.8 12.4 %collective-permute-start.7 = (f32[4,137,32,1]{1,0,3,2:T(4,128)S(1)}, f32[4,137,32,1]{1,0,3,2:T(4,128)S(1)}, u32[]{:S(2)}, u32[]{:S(2)}) collective-permute-start(f32[4,137,32,1]{1,0,3,2:T(4,128)S(1)} %get-tuple-element.15), channel_id=1, source_target_pairs={{1,0},{2,1},{3,2},{4,3},{5,4},{6,5},{7,6},{8,7},{9,8},{10,9},{11,1... | collective-permute-start | bytes 210440 | tf_op jit(solution)/shard_map/ppermute | solution.py:17
  156.3 8.4 %collective-permute-start.4 = (f32[4,137,1,16]{1,0,3,2:T(4,128)S(1)}, f32[4,137,1,16]{1,0,3,2:T(4,128)S(1)}, u32[]{:S(2)}, u32[]{:S(2)}) collective-permute-start(f32[4,137,1,16]{1,0,3,2:T(4,128)S(1)} %get-tuple-element.12), channel_id=1, source_target_pairs={{0,32},{32,64},{64,96},{96,128},{128,160},{160,192},{192,224},{224... | collective-permute-start | bytes 105224 | tf_op jit(solution)/shard_map/ppermute | solution.py:14
  158.2 8.0 %collective-permute-start.5 = (f32[4,137,1,16]{1,0,3,2:T(4,128)S(1)}, f32[4,137,1,16]{1,0,3,2:T(4,128)S(1)}, u32[]{:S(2)}, u32[]{:S(2)}) collective-permute-start(f32[4,137,1,16]{1,0,3,2:T(4,128)S(1)} %get-tuple-element.13), channel_id=1, source_target_pairs={{32,0},{64,32},{96,64},{128,96},{160,128},{192,160},{224,192},{256... | collective-permute-start | bytes 105224 | tf_op jit(solution)/shard_map/ppermute | solution.py:17
  (8 other events, 34.5 us)
where the time goes:
time: 175 us; the launch traced here: 172 us
  starting transfers between devices  53.3 us (30%)
  blocking collectives  31.9 us (18%)
  other arithmetic  31.6 us (18%)
  waiting for transfers between devices  28.1 us (16%)
  local copies, waits for them, and re-layouts  20 us (11%)
  matrix products  6 us (3%)
    ppermute x4, starting transfers between devices, with_halo(): lax.ppermute(lax.slice_in_dim(block, 0, width, axis=dim), axis, backward)  21.1 us
    all_to_all x1, blocking collectives, increment(): lax.all_to_all(outbox.reshape(groups, pair_cap, column_depth), 'gy', spli...  17.7 us
    all_to_all x1, blocking collectives, increment(): lax.all_to_all(answer.reshape(groups, pair_cap, column_depth), 'gy', spli...  14.3 us
    all_to_all x1, waiting for transfers between devices, increment(): lax.all_to_all(answer.reshape(groups, pair_cap, column_depth), 'gy', spli...  11.5 us
    all_to_all x1, starting transfers between devices, on_device(): lax.all_to_all(send_slot.reshape(groups, pair_cap), 'gy', split_axis=0, c...  11.2 us
    add x1, other arithmetic, on_device(): adjoint = adjoint + forcing_early.astype(jnp.float32)  9.47 us
    ppermute x4, starting transfers between devices, with_halo(): lax.ppermute(lax.slice_in_dim(block, block.shape[dim] - width, None, axis...  9.46 us
    all_to_all x1, waiting for transfers between devices, increment(): lax.all_to_all(outbox.reshape(groups, pair_cap, column_depth), 'gy', spli...  8.52 us
  transfers between devices with their start and end apart: 11, of which 6 were waited for; matrix products, arithmetic and copies ran while one was open for 5% of the time, Pallas kernels for 0%

commit v1 on v0

v1 whole, which is shorter than its diff:
```python
import functools

import jax
import jax.numpy as jnp
from jax import lax
from jax.experimental import pallas as pl
from jax.experimental.pallas import tpu as pltpu
from jax.sharding import PartitionSpec as P

BF16 = jnp.bfloat16
F32 = jnp.float32
VMEM = pltpu.VMEM
SMEM = pltpu.SMEM
PAIR = 2


def call(kernel, out_shape, in_spaces, out_spaces, scratch=(), flops=1000, bytes_accessed=1000000):
    return pl.pallas_call(
        kernel,
        out_shape=out_shape,
        in_specs=[pl.BlockSpec(memory_space=space) for space in in_spaces],
        out_specs=[pl.BlockSpec(memory_space=space) for space in out_spaces],
        scratch_shapes=scratch,
        compiler_params=pltpu.CompilerParams(vmem_limit_bytes=40 * 1024 * 1024),
        cost_estimate=pl.CostEstimate(flops=flops, bytes_accessed=bytes_accessed, transcendentals=0),
    )


def entry_loop(count_ref, body):
    def step(e, carry):
        body(e)
        return carry

    lax.fori_loop(0, count_ref[0], step, 0)


def pack_first(cols, count, owner, slot, late, outbox, target, wide, rows, used):
    fields, span_lon, span_lat, levels = late.shape
    for f in range(fields):
        wide[f, :, :, :levels] = late[f].astype(F32)
    lane = lax.broadcasted_iota(jnp.int32, (1, levels + 1), 1)
    rows[...] = jnp.zeros(rows.shape, F32)
    for o in range(rows.shape[0] // (PAIR * fields)):
        used[o] = 0
    for e in range(target.shape[0]):
        target[e] = 0

    def body(e):
        o = owner[e]
        rank = used[o]
        used[o] = rank + 1
        t = o * PAIR + rank
        target[e] = t
        lon = cols[e] // span_lat
        lat = cols[e] % span_lat
        code = slot[e] * fields
        for f in range(fields):
            column = wide[f, lon, pl.ds(lat, 1), :]
            rows[pl.ds(t * fields + f, 1), :] = jnp.where(lane == levels, (code + f + 1).astype(F32), column)

    entry_loop(count, body)
    outbox[...] = rows[...].astype(BF16)


def place_kernel(received, placed, chosen_out):
    levels = placed.shape[1]
    values = received[...].astype(F32)
    codes = values[:, levels:]
    wanted = (lax.broadcasted_iota(jnp.int32, (values.shape[0], placed.shape[0]), 1) + 1).astype(F32)
    chosen = (codes == wanted).astype(BF16)
    chosen_out[...] = chosen
    placed[...] = lax.dot_general(
        chosen, values[:, :levels].astype(BF16), (((0,), (0,)), ((), ())), preferred_element_type=F32
    ).astype(BF16)


def place_again_kernel(received, chosen, placed):
    placed[...] = lax.dot_general(
        chosen[...], received[...], (((0,), (0,)), ((), ())), preferred_element_type=F32
    ).astype(BF16)


def split_dot(chosen, value):
    high = value.astype(BF16)
    rest = value - high.astype(F32)
    middle = rest.astype(BF16)
    low = (rest - middle.astype(F32)).astype(BF16)
    dot = functools.partial(jnp.dot, preferred_element_type=F32)
    return dot(chosen, high) + dot(chosen, middle) + dot(chosen, low)


def answer_kernel(result, chosen, answer):
    answer[...] = split_dot(chosen[...], result[...])


def add_increments(cols, count, target, returned, field):
    fields, span_lon, span_lat, levels = field.shape

    def body(e):
        t = target[e]
        lon = cols[e] // span_lat
        lat = cols[e] % span_lat
        for f in range(fields):
            here = (f, lon, pl.ds(lat, 1), slice(None))
            field[here] = field[here] + returned[pl.ds(t * fields + f, 1), :]

    entry_loop(count, body)


def store_edges(field, lon_low, lon_high, lat_low, lat_high):
    fields, span_lon, span_lat, levels = field.shape
    for f in range(fields):
        lon_low[f] = field[f, 0].astype(BF16)
        lon_high[f] = field[f, span_lon - 1].astype(BF16)
        lat_low[f] = jnp.concatenate([field[f, p, :1, :] for p in range(span_lon)], axis=0).astype(BF16)
        lat_high[f] = jnp.concatenate(
            [field[f, p, span_lat - 1 :, :] for p in range(span_lon)], axis=0
        ).astype(BF16)


def add_first(cols, count, target, late, returned, field, lon_low, lon_high, lat_low, lat_high):
    for f in range(field.shape[0]):
        field[f] = late[f].astype(F32)
    add_increments(cols, count, target, returned, field)
    store_edges(field, lon_low, lon_high, lat_low, lat_high)


def add_second(cols, count, target, base, returned, field, lon_low, lon_high, lat_low, lat_high):
    field[...] = base[...]
    add_increments(cols, count, target, returned, field)
    store_edges(field, lon_low, lon_high, lat_low, lat_high)


def stencil_into(field, coef, from_before, from_after, from_low, from_high, extra, out):
    fields, span_lon, span_lat, levels = field.shape
    row = lax.broadcasted_iota(jnp.int32, (span_lat, levels), 0)
    low_rows = [from_low[f].astype(F32) for f in range(fields)]
    high_rows = [from_high[f].astype(F32) for f in range(fields)]
    for p in range(span_lon):
        weight = [jnp.broadcast_to(coef[k, :, p : p + 1], (span_lat, levels)) for k in range(4)]
        for f in range(fields):
            here = field[f, p]
            before = field[f, p - 1] if p > 0 else from_before[f].astype(F32)
            after = field[f, p + 1] if p < span_lon - 1 else from_after[f].astype(F32)
            low = jnp.where(row == 0, low_rows[f][p : p + 1], pltpu.roll(here, 1, 0))
            high = jnp.where(row == span_lat - 1, high_rows[f][p : p + 1], pltpu.roll(here, span_lat - 1, 0))
            total = here + weight[0] * before + weight[1] * after + weight[2] * low + weight[3] * high
            if extra is not None:
                total = total + extra[f, p].astype(F32)
            out[f, p] = total


def step_first(cols, count, target, field, coef, from_before, from_after, from_low, from_high, early, out, outbox, rows):
    fields, span_lon, span_lat, levels = field.shape
    stencil_into(field, coef, from_before, from_after, from_low, from_high, early, out)
    rows[...] = jnp.zeros(rows.shape, F32)

    def body(e):
        t = target[e]
        lon = cols[e] // span_lat
        lat = cols[e] % span_lat
        for f in range(fields):
            rows[pl.ds(t * fields + f, 1), :] = out[f, lon, pl.ds(lat, 1), :]

    entry_loop(count, body)
    outbox[...] = rows[...].astype(BF16)


def step_second(field, coef, from_before, from_after, from_low, from_high, out):
    stencil_into(field, coef, from_before, from_after, from_low, from_high, None, out)


def exchange(rows, groups):
    width = rows.shape[1]
    moved = lax.all_to_all(
        rows.reshape(groups, rows.shape[0] // groups, width), "gy", split_axis=0, concat_axis=0, tiled=True
    )
    return moved.reshape(rows.shape)


def halos(lon_low, lon_high, lat_low, lat_high):
    lon = lax.axis_size("gx")
    lat = lax.axis_size("gy")
    up = [(i, (i + 1) % lon) for i in range(lon)]
    down = [(target, source) for source, target in up]
    north = [(i, i + 1) for i in range(lat - 1)]
    south = [(target, source) for source, target in north]
    from_before = lax.ppermute(lon_high, "gx", up)
    from_after = lax.ppermute(lon_low, "gx", down)
    from_low = lax.ppermute(lat_high, "gy", north)
    from_high = lax.ppermute(lat_low, "gy", south)
    return from_before, from_after, from_low, from_high


def on_device(late, early, stencil_coef, jacobian, cloudy_cols, cloudy_count, owner_rank, owner_slot):
    fields, levels, span_lon, span_lat = late.shape
    groups = lax.axis_size("gy")
    own_slots = jacobian.shape[1]
    capacity = cloudy_cols.shape[2]
    late = late.transpose(0, 2, 3, 1)
    early = early.transpose(0, 2, 3, 1)
    coef = stencil_coef.transpose(0, 2, 1)
    cols = cloudy_cols.reshape(capacity)
    count = cloudy_count.reshape(1)
    owner = owner_rank.reshape(capacity)
    slot = owner_slot.reshape(capacity)
    matrices = jacobian[0]
    shape = jax.ShapeDtypeStruct
    inbox_rows = groups * PAIR * fields
    grid = (fields, span_lon, span_lat, levels)

    outbox, target = call(
        pack_first,
        [shape((inbox_rows, levels + 1), BF16), shape((capacity,), jnp.int32)],
        [SMEM] * 4 + [VMEM],
        [VMEM, SMEM],
        [VMEM(grid[:3] + (levels + 1,), F32), VMEM((inbox_rows, levels + 1), F32), SMEM((groups,), jnp.int32)],
    )(cols, count, owner, slot, late)
    received = exchange(outbox, groups)
    placed, chosen = call(
        place_kernel,
        [shape((own_slots * fields, levels), BF16), shape((inbox_rows, own_slots * fields), BF16)],
        [VMEM],
        [VMEM] * 2,
    )(received)

    def apply(placed):
        result = jnp.einsum(
            "sfij,sfi->sfj",
            matrices,
            placed.reshape(own_slots, fields, levels),
            preferred_element_type=F32,
        ).reshape(own_slots * fields, levels)
        (answer,) = call(answer_kernel, [shape((inbox_rows, levels), F32)], [VMEM] * 2, [VMEM])(result, chosen)
        return exchange(answer, groups)

    edge_shapes = [shape((fields, span_lat, levels), BF16)] * 2 + [shape((fields, span_lon, levels), BF16)] * 2
    returned = apply(placed)
    field, *edges = call(add_first, [shape(grid, F32)] + edge_shapes, [SMEM] * 3 + [VMEM] * 2, [VMEM] * 5)(
        cols, count, target, late, returned
    )
    adjoint, outbox = call(
        step_first,
        [shape(grid, F32), shape((inbox_rows, levels), BF16)],
        [SMEM] * 3 + [VMEM] * 7,
        [VMEM] * 2,
        [VMEM((inbox_rows, levels), F32)],
    )(cols, count, target, field, coef, *halos(*edges), early)
    received = exchange(outbox, groups)
    (placed,) = call(place_again_kernel, [shape((own_slots * fields, levels), BF16)], [VMEM] * 2, [VMEM])(
        received, chosen
    )
    returned = apply(placed)
    field, *edges = call(add_second, [shape(grid, F32)] + edge_shapes, [SMEM] * 3 + [VMEM] * 2, [VMEM] * 5)(
        cols, count, target, adjoint, returned
    )
    (final,) = call(step_second, [shape(grid, F32)], [VMEM] * 6, [VMEM])(field, coef, *halos(*edges))
    return final.transpose(0, 3, 1, 2)


def solution(mesh):
    return jax.shard_map(
        on_device,
        mesh=mesh,
        in_specs=(
            P(None, None, "gx", "gy"),
            P(None, None, "gx", "gy"),
            P(None, "gx", "gy"),
            P("gx", "gy", None, None, None),
            P("gx", "gy", None),
            P("gx", "gy"),
            P("gx", "gy", None),
            P("gx", "gy", None),
        ),
        out_specs=P(None, None, "gx", "gy"),
        check_vma=False,
    )
```

time: 175 us -> 127 us (0.73)
  blocking collectives: 31.9 us -> 72.9 us
  other arithmetic: 31.6 us -> 0 us
  waiting for transfers between devices: 28.1 us -> 2.22 us
  starting transfers between devices: 53.3 us -> 30.6 us
  local copies, waits for them, and re-layouts: 20 us -> 3.32 us
  Pallas kernels: 0 us -> 9.02 us
    all_to_all x2 -> x4, blocking collectives: 31.9 us -> 72.9 us  [exchange(): lax.all_to_all(rows.reshape(groups, rows.shape[0] // groups, width), 'gy'...]
    all_to_all x3 -> x0, starting transfers between devices: 22.8 us -> none  [the longest x1 11.2 us: on_device(): lax.all_to_all(send_slot.reshape(groups, pair_cap), 'gy', split_axis=0, c...]
    all_to_all x3 -> x0, waiting for transfers between devices: 22.1 us -> none  [the longest x1 11.5 us: increment(): lax.all_to_all(answer.reshape(groups, pair_cap, column_depth), 'gy', spli...]
    add x4 -> x0, other arithmetic: 18.1 us -> none  [the longest x1 9.47 us: on_device(): adjoint = adjoint + forcing_early.astype(jnp.float32)]
    reshape x18 -> x4, local copies, waits for them, and re-layouts: 10.5 us -> 0.09 us  [the longest x2 0.05 us: apply(): result = jnp.einsum('sfij,sfi->sfj', matrices, placed.reshape(own_slots,...]
    pallas_call x0 -> x9, Pallas kernels: none -> 9.02 us  [the longest x1 2.49 us: on_device(): call(step_second, [shape(grid, F32)], [VMEM] * 6, [VMEM])]
    scatter-add x2 -> x0, other arithmetic: 4.79 us -> none  [increment(): jnp.zeros((column_depth, columns_all), jnp.float32).at[:, columns]]
    ppermute x8, waiting for transfers between devices: 5.95 us -> 2.22 us  [the longest x2 1.91 us: halos(): from_after = lax.ppermute(lon_low, 'gx', down)]
  transfers between devices with their start and end apart: 11 -> 8, of which waited for: 6 -> 4; matrix products, arithmetic and copies ran while one was open for 5% -> 0% of each run, Pallas kernels for 0% -> 0%
where the time goes in v1:
time: 127 us; the launch traced here: 125 us
  blocking collectives  72.9 us (57%)
  starting transfers between devices  30.6 us (24%)
  Pallas kernels  9.02 us (7%)
  matrix products  6 us (5%)
  local copies, waits for them, and re-layouts  3.32 us (3%)
  waiting for transfers between devices  2.22 us (2%)
    all_to_all x4, blocking collectives, exchange(): lax.all_to_all(rows.reshape(groups, rows.shape[0] // groups, width), 'gy'...  72.9 us
    ppermute x2, starting transfers between devices, halos(): from_after = lax.ppermute(lon_low, 'gx', down)  17.2 us
    dot_general x2, matrix products, apply(): jnp.einsum('sfij,sfi->sfj', matrices, placed.reshape(own_slots, fields, l...  6 us
    ppermute x2, starting transfers between devices, halos(): from_low = lax.ppermute(lat_high, 'gy', north)  5.25 us
    ppermute x2, starting transfers between devices, halos(): from_high = lax.ppermute(lat_low, 'gy', south)  4.29 us
    ppermute x2, starting transfers between devices, halos(): from_before = lax.ppermute(lon_high, 'gx', up)  3.84 us
    unnamed x16, local copies, waits for them, and re-layouts  3.2 us
  transfers between devices with their start and end apart: 8, of which 4 were waited for; matrix products, arithmetic and copies ran while one was open for 0% of the time, Pallas kernels for 0%

profile of v1, /device:TPU:1, one launch (start us, length us, event | category | flops | bytes accessed | tf_op | source)
XLA Modules:
  0.0 124.9 jit_solution(4959200577289226292)
XLA Ops:
  0.7 1.2 copy-done
  1.9 0.7 copy-done.4
  2.6 0.7 copy-done.6
  3.9 1.5 %shard_map.82 = (bf16[256,138]{1,0:T(8,128)(2,1)S(1)}, s32[48]{0:T(128)S(1)}) custom-call(s32[48]{0:T(128)S(1)} %bitcast.42, s32[1]{0:T(128)} %bitcast.25.count, s32[48]{0:T(128)S(1)} %bitcast.46, s32[48]{0:T(128)S(1)} %bitcast.47, bf16[4,32,16,137]{3,2,1,0:T(8,128)(2,1)S(1)} %bitcast.29), custom_call_target="tpu_custom_call" | custom-call | flops 1000 | bytes 1000000 | tf_op jit(solution)/shard_map/pallas_call | solution.py:212
  5.4 22.5 %all_to_all.20 = bf16[32,8,138]{2,1,0:T(8,128)(2,1)S(1)} all-to-all(bf16[32,8,138]{2,1,0:T(8,128)(2,1)S(1)} %bitcast.41), channel_id=1, replica_groups=mesh['gx'=16,'gy'=32] {'gy'}, dimensions={0} | all-to-all | bytes 141312 | tf_op jit(solution)/shard_map/all_to_all | solution.py:175
  28.2 3.0 %fusion.2 = f32[16,4,1,137]{3,2,1,0:T(1,128)S(1)} fusion(bf16[16,4,137,1]{2,3,1,0:T(2,128)(2,1)S(1)} %reshape.69, bf16[16,4,137,137]{3,1,2,0:T(4,128)(2,1)} %bitcast.48), kind=kOutput, calls=%fused_computation.2 | convolution fusion | flops 2402432 | bytes 2455040 | tf_op jit(solution)/shard_map/sfij,sfi->sfj/dot_general | solution.py:228
  31.5 16.5 %all_to_all.21 = f32[32,8,137]{2,1,0:T(8,128)S(1)} all-to-all(f32[32,8,137]{2,1,0:T(8,128)S(1)} %bitcast.33), channel_id=1, replica_groups=mesh['gx'=16,'gy'=32] {'gy'}, dimensions={0} | all-to-all | bytes 280576 | tf_op jit(solution)/shard_map/all_to_all | solution.py:175
  48.0 1.0 shard_map.85
  49.0 3.2 %collective-permute-start.2 = (bf16[4,32,137]{2,1,0:T(8,128)(2,1)S(1)}, bf16[4,32,137]{2,1,0:T(8,128)(2,1)S(1)}, u32[]{:S(2)}, u32[]{:S(2)}) collective-permute-start(bf16[4,32,137]{2,1,0:T(8,128)(2,1)S(1)} %get-tuple-element.28), channel_id=1, source_target_pairs={{0,1},{1,2},{2,3},{3,4},{4,5},{5,6},{6,7},{7,8},{8,9},{9,10},{10,1... | collective-permute-start | bytes 105224 | tf_op jit(solution)/shard_map/ppermute | solution.py:190
  52.2 1.9 %collective-permute-start.3 = (bf16[4,32,137]{2,1,0:T(8,128)(2,1)S(1)}, bf16[4,32,137]{2,1,0:T(8,128)(2,1)S(1)}, u32[]{:S(2)}, u32[]{:S(2)}) collective-permute-start(bf16[4,32,137]{2,1,0:T(8,128)(2,1)S(1)} %get-tuple-element.29), channel_id=1, source_target_pairs={{1,0},{2,1},{3,2},{4,3},{5,4},{6,5},{7,6},{8,7},{9,8},{10,9},{11,1... | collective-permute-start | bytes 105224 | tf_op jit(solution)/shard_map/ppermute | solution.py:191
  54.1 1.9 %collective-permute-start = (bf16[4,16,137]{2,1,0:T(8,128)(2,1)S(1)}, bf16[4,16,137]{2,1,0:T(8,128)(2,1)S(1)}, u32[]{:S(2)}, u32[]{:S(2)}) collective-permute-start(bf16[4,16,137]{2,1,0:T(8,128)(2,1)S(1)} %get-tuple-element.26), channel_id=1, source_target_pairs={{0,32},{32,64},{64,96},{96,128},{128,160},{160,192},{192,224},{224... | collective-permute-start | bytes 52616 | tf_op jit(solution)/shard_map/ppermute | solution.py:188
  56.0 10.4 %collective-permute-start.1 = (bf16[4,16,137]{2,1,0:T(8,128)(2,1)S(1)}, bf16[4,16,137]{2,1,0:T(8,128)(2,1)S(1)}, u32[]{:S(2)}, u32[]{:S(2)}) collective-permute-start(bf16[4,16,137]{2,1,0:T(8,128)(2,1)S(1)} %get-tuple-element.27), channel_id=1, source_target_pairs={{32,0},{64,32},{96,64},{128,96},{160,128},{192,160},{224,192},{256... | collective-permute-start | bytes 52616 | tf_op jit(solution)/shard_map/ppermute | solution.py:189
  66.6 0.9 collective-permute-done.1.from_after
  67.6 2.1 %shard_map.86 = (f32[4,32,16,137]{3,2,1,0:T(8,128)S(1)}, bf16[256,137]{1,0:T(8,128)(2,1)S(1)}) custom-call(s32[48]{0:T(128)S(1)} %bitcast.44, s32[1]{0:T(128)} %bitcast.27.count, s32[48]{0:T(128)S(1)} %get-tuple-element.21.target, f32[4,32,16,137]{3,2,1,0:T(8,128)S(1)} %get-tuple-element.25.field, f32[4,16,32]{2,1,0:T(8,128)S(1)} %bitcast.38, ...), custom_call_target="tpu_custom_call" | custom-call | flops 1000 | bytes 1000000 | tf_op jit(solution)/shard_map/pallas_call | solution.py:242
  69.7 18.0 %all_to_all.22 = bf16[32,8,137]{2,1,0:T(8,128)(2,1)S(1)} all-to-all(bf16[32,8,137]{2,1,0:T(8,128)(2,1)S(1)} %bitcast.40), channel_id=1, replica_groups=mesh['gx'=16,'gy'=32] {'gy'}, dimensions={0} | all-to-all | bytes 140288 | tf_op jit(solution)/shard_map/all_to_all | solution.py:175
  87.9 3.0 %fusion = f32[16,4,1,137]{3,2,1,0:T(1,128)S(1)} fusion(bf16[16,4,137,1]{2,3,1,0:T(2,128)(2,1)S(1)} %reshape.71, bf16[16,4,137,137]{3,1,2,0:T(4,128)(2,1)} %bitcast.49), kind=kOutput, calls=%fused_computation | convolution fusion | flops 2402432 | bytes 2455040 | tf_op jit(solution)/shard_map/sfij,sfi->sfj/dot_general | solution.py:228
  91.2 15.9 %all_to_all.23 = f32[32,8,137]{2,1,0:T(8,128)S(1)} all-to-all(f32[32,8,137]{2,1,0:T(8,128)S(1)} %bitcast.32), channel_id=1, replica_groups=mesh['gx'=16,'gy'=32] {'gy'}, dimensions={0} | all-to-all | bytes 280576 | tf_op jit(solution)/shard_map/all_to_all | solution.py:175
  107.1 1.0 shard_map.89
  108.1 2.1 %collective-permute-start.6 = (bf16[4,32,137]{2,1,0:T(8,128)(2,1)S(1)}, bf16[4,32,137]{2,1,0:T(8,128)(2,1)S(1)}, u32[]{:S(2)}, u32[]{:S(2)}) collective-permute-start(bf16[4,32,137]{2,1,0:T(8,128)(2,1)S(1)} %get-tuple-element.35), channel_id=1, source_target_pairs={{0,1},{1,2},{2,3},{3,4},{4,5},{5,6},{6,7},{7,8},{8,9},{9,10},{10,1... | collective-permute-start | bytes 105224 | tf_op jit(solution)/shard_map/ppermute | solution.py:190
  110.2 2.4 %collective-permute-start.7 = (bf16[4,32,137]{2,1,0:T(8,128)(2,1)S(1)}, bf16[4,32,137]{2,1,0:T(8,128)(2,1)S(1)}, u32[]{:S(2)}, u32[]{:S(2)}) collective-permute-start(bf16[4,32,137]{2,1,0:T(8,128)(2,1)S(1)} %get-tuple-element.36), channel_id=1, source_target_pairs={{1,0},{2,1},{3,2},{4,3},{5,4},{6,5},{7,6},{8,7},{9,8},{10,9},{11,1... | collective-permute-start | bytes 105224 | tf_op jit(solution)/shard_map/ppermute | solution.py:191
  112.6 1.9 %collective-permute-start.4 = (bf16[4,16,137]{2,1,0:T(8,128)(2,1)S(1)}, bf16[4,16,137]{2,1,0:T(8,128)(2,1)S(1)}, u32[]{:S(2)}, u32[]{:S(2)}) collective-permute-start(bf16[4,16,137]{2,1,0:T(8,128)(2,1)S(1)} %get-tuple-element.33), channel_id=1, source_target_pairs={{0,32},{32,64},{64,96},{96,128},{128,160},{160,192},{192,224},{224... | collective-permute-start | bytes 52616 | tf_op jit(solution)/shard_map/ppermute | solution.py:188
  114.5 6.8 %collective-permute-start.5 = (bf16[4,16,137]{2,1,0:T(8,128)(2,1)S(1)}, bf16[4,16,137]{2,1,0:T(8,128)(2,1)S(1)}, u32[]{:S(2)}, u32[]{:S(2)}) collective-permute-start(bf16[4,16,137]{2,1,0:T(8,128)(2,1)S(1)} %get-tuple-element.34), channel_id=1, source_target_pairs={{32,0},{64,32},{96,64},{128,96},{160,128},{192,160},{224,192},{256... | collective-permute-start | bytes 52616 | tf_op jit(solution)/shard_map/ppermute | solution.py:189
  121.4 1.0 collective-permute-done.5.from_after
  122.5 2.5 %shard_map.90 = f32[4,32,16,137]{3,2,1,0:T(8,128)} custom-call(f32[4,32,16,137]{3,2,1,0:T(8,128)S(1)} %get-tuple-element.32.field, f32[4,16,32]{2,1,0:T(8,128)S(1)} %bitcast.39, bf16[4,16,137]{2,1,0:T(8,128)(2,1)S(1)} %collective-permute-done.4.from_before, bf16[4,16,137]{2,1,0:T(8,128)(2,1)S(1)} %collective-permute-done.5.from_after, ...), custom_call_target="tpu_custom_call" | custom-call | flops 1000 | bytes 1000000 | tf_op jit(solution)/shard_map/pallas_call | solution.py:257
  (29 shorter events, 2.0 us)
Async XLA Ops:
  0.0 48.0 %copy-start.5 = (s32[1,1,48]{2,1,0:T(1,128)S(1)}, s32[1,1,48]{2,1,0:T(1,128)}, u32[]{:S(2)}) copy-start(s32[1,1,48]{2,1,0:T(1,128)} %param.12) | copy-start | bytes 580
  0.7 1.2 copy-start
  1.9 0.7 copy-start.4
  2.6 0.7 copy-start.6
  3.2 0.7 copy-start.7
  3.9 44.1 %copy-start.1 = (bf16[4,137,32,16]{1,3,2,0:T(8,128)(2,1)S(1)}, bf16[4,137,32,16]{1,3,2,0:T(8,128)(2,1)}, u32[]{:S(2)}) copy-start(bf16[4,137,32,16]{1,3,2,0:T(8,128)(2,1)} %param.8) | copy-start | bytes 1683460
  3.9 63.7 %copy-start.2 = (bf16[4,137,32,16]{1,3,2,0:T(8,128)(2,1)S(1)}, bf16[4,137,32,16]{1,3,2,0:T(8,128)(2,1)}, u32[]{:S(2)}) copy-start(bf16[4,137,32,16]{1,3,2,0:T(8,128)(2,1)} %param.9) | copy-start | bytes 1683460
  3.9 63.7 %copy-start.3 = (f32[4,32,16]{1,2,0:T(8,128)S(1)}, f32[4,32,16]{1,2,0:T(8,128)}, u32[]{:S(2)}) copy-start(f32[4,32,16]{1,2,0:T(8,128)} %param.10) | copy-start | bytes 24580
  49.0 18.6 %collective-permute-start.2 = (bf16[4,32,137]{2,1,0:T(8,128)(2,1)S(1)}, bf16[4,32,137]{2,1,0:T(8,128)(2,1)S(1)}, u32[]{:S(2)}, u32[]{:S(2)}) collective-permute-start(bf16[4,32,137]{2,1,0:T(8,128)(2,1)S(1)} %get-tuple-element.28), channel_id=1, source_target_pairs={{0,1},{1,2},{2,3},{3,4},{4,5},{5,6},{6,7},{7,8},{8,9},{9,10},{10,1... | collective-permute-start | bytes 105224 | tf_op jit(solution)/shard_map/ppermute | solution.py:190
  52.2 15.4 %collective-permute-start.3 = (bf16[4,32,137]{2,1,0:T(8,128)(2,1)S(1)}, bf16[4,32,137]{2,1,0:T(8,128)(2,1)S(1)}, u32[]{:S(2)}, u32[]{:S(2)}) collective-permute-start(bf16[4,32,137]{2,1,0:T(8,128)(2,1)S(1)} %get-tuple-element.29), channel_id=1, source_target_pairs={{1,0},{2,1},{3,2},{4,3},{5,4},{6,5},{7,6},{8,7},{9,8},{10,9},{11,1... | collective-permute-start | bytes 105224 | tf_op jit(solution)/shard_map/ppermute | solution.py:191
  54.1 12.6 %collective-permute-start = (bf16[4,16,137]{2,1,0:T(8,128)(2,1)S(1)}, bf16[4,16,137]{2,1,0:T(8,128)(2,1)S(1)}, u32[]{:S(2)}, u32[]{:S(2)}) collective-permute-start(bf16[4,16,137]{2,1,0:T(8,128)(2,1)S(1)} %get-tuple-element.26), channel_id=1, source_target_pairs={{0,32},{32,64},{64,96},{96,128},{128,160},{160,192},{192,224},{224... | collective-permute-start | bytes 52616 | tf_op jit(solution)/shard_map/ppermute | solution.py:188
  56.0 11.5 %collective-permute-start.1 = (bf16[4,16,137]{2,1,0:T(8,128)(2,1)S(1)}, bf16[4,16,137]{2,1,0:T(8,128)(2,1)S(1)}, u32[]{:S(2)}, u32[]{:S(2)}) collective-permute-start(bf16[4,16,137]{2,1,0:T(8,128)(2,1)S(1)} %get-tuple-element.27), channel_id=1, source_target_pairs={{32,0},{64,32},{96,64},{128,96},{160,128},{192,160},{224,192},{256... | collective-permute-start | bytes 52616 | tf_op jit(solution)/shard_map/ppermute | solution.py:189
  108.1 14.3 %collective-permute-start.6 = (bf16[4,32,137]{2,1,0:T(8,128)(2,1)S(1)}, bf16[4,32,137]{2,1,0:T(8,128)(2,1)S(1)}, u32[]{:S(2)}, u32[]{:S(2)}) collective-permute-start(bf16[4,32,137]{2,1,0:T(8,128)(2,1)S(1)} %get-tuple-element.35), channel_id=1, source_target_pairs={{0,1},{1,2},{2,3},{3,4},{4,5},{5,6},{6,7},{7,8},{8,9},{9,10},{10,1... | collective-permute-start | bytes 105224 | tf_op jit(solution)/shard_map/ppermute | solution.py:190
  110.2 12.2 %collective-permute-start.7 = (bf16[4,32,137]{2,1,0:T(8,128)(2,1)S(1)}, bf16[4,32,137]{2,1,0:T(8,128)(2,1)S(1)}, u32[]{:S(2)}, u32[]{:S(2)}) collective-permute-start(bf16[4,32,137]{2,1,0:T(8,128)(2,1)S(1)} %get-tuple-element.36), channel_id=1, source_target_pairs={{1,0},{2,1},{3,2},{4,3},{5,4},{6,5},{7,6},{8,7},{9,8},{10,9},{11,1... | collective-permute-start | bytes 105224 | tf_op jit(solution)/shard_map/ppermute | solution.py:191
  112.6 8.8 %collective-permute-start.4 = (bf16[4,16,137]{2,1,0:T(8,128)(2,1)S(1)}, bf16[4,16,137]{2,1,0:T(8,128)(2,1)S(1)}, u32[]{:S(2)}, u32[]{:S(2)}) collective-permute-start(bf16[4,16,137]{2,1,0:T(8,128)(2,1)S(1)} %get-tuple-element.33), channel_id=1, source_target_pairs={{0,32},{32,64},{64,96},{96,128},{128,160},{160,192},{192,224},{224... | collective-permute-start | bytes 52616 | tf_op jit(solution)/shard_map/ppermute | solution.py:188
  114.5 7.9 %collective-permute-start.5 = (bf16[4,16,137]{2,1,0:T(8,128)(2,1)S(1)}, bf16[4,16,137]{2,1,0:T(8,128)(2,1)S(1)}, u32[]{:S(2)}, u32[]{:S(2)}) collective-permute-start(bf16[4,16,137]{2,1,0:T(8,128)(2,1)S(1)} %get-tuple-element.34), channel_id=1, source_target_pairs={{32,0},{64,32},{96,64},{128,96},{160,128},{192,160},{224,192},{256... | collective-permute-start | bytes 52616 | tf_op jit(solution)/shard_map/ppermute | solution.py:189

commit v2 on v1

v2 whole, which is shorter than its diff:
```python
import functools

import jax
import jax.numpy as jnp
from jax import lax
from jax.experimental import pallas as pl
from jax.experimental.pallas import tpu as pltpu
from jax.sharding import PartitionSpec as P

BF16 = jnp.bfloat16
F32 = jnp.float32
VMEM = pltpu.VMEM
SMEM = pltpu.SMEM
HBM = pltpu.HBM
PAIR = 2
LANES = 128


def call(kernel, out_shape, in_spaces, out_spaces, scratch=(), aliases=None, flops=1000, touched=1000000, vmem=40):
    return pl.pallas_call(
        kernel,
        out_shape=out_shape,
        in_specs=[pl.BlockSpec(memory_space=space) for space in in_spaces],
        out_specs=[pl.BlockSpec(memory_space=space) for space in out_spaces],
        scratch_shapes=scratch,
        input_output_aliases=aliases or {},
        compiler_params=pltpu.CompilerParams(vmem_limit_bytes=vmem * 1024 * 1024),
        cost_estimate=pl.CostEstimate(flops=flops, bytes_accessed=touched, transcendentals=0),
    )


def entry_loop(count, body):
    def step(e, carry):
        body(e)
        return carry

    lax.fori_loop(0, count, step, 0)


def unpack_field(packed, field, f):
    field[f, 0] = packed[f, :, :LANES].astype(F32)
    field[f, 1, :, : packed.shape[2] - LANES] = packed[f, :, LANES:].astype(F32)


def pack_first(
    cols_hbm, count_hbm, owner_hbm, slot_hbm, late_hbm, outbox, plan, cols, count, owner, slot, late, field, rows, used, sems
):
    fields = field.shape[0]
    levels = late.shape[2]
    capacity = cols.shape[2]
    owners = used.shape[0]
    tail = levels - LANES
    end = lax.broadcasted_iota(jnp.int32, (1, LANES), 1)
    small = [(cols_hbm, cols), (count_hbm, count), (owner_hbm, owner), (slot_hbm, slot)]
    copies = [pltpu.make_async_copy(source, target, sems.at[i]) for i, (source, target) in enumerate(small)]
    copies += [pltpu.make_async_copy(late_hbm.at[f], late.at[f], sems.at[len(small) + f]) for f in range(fields)]
    for copy in copies:
        copy.start()
    rows[...] = jnp.zeros(rows.shape, F32)
    for o in range(owners):
        used[o] = 0
    for e in range(2 * capacity + 1):
        plan[e] = 0
    for f in range(fields):
        copies[len(small) + f].wait()
        unpack_field(late, field, f)
    for copy in copies[: len(small)]:
        copy.wait()
    live = count[0, 0]
    plan[0] = live

    def body(e):
        o = owner[0, 0, e]
        column = cols[0, 0, e]
        rank = used[o]
        used[o] = rank + 1
        plan[1 + e] = column
        plan[1 + capacity + e] = rank * (fields * owners) + o
        first = (o * PAIR + rank) * fields
        code = slot[0, 0, e] * fields
        for f in range(fields):
            mark = (code + (f + 1)).astype(F32)
            rows[0, pl.ds(first + f, 1), :] = field[f, 0, pl.ds(column, 1), :]
            rows[1, pl.ds(first + f, 1), :] = jnp.where(end == tail, mark, field[f, 1, pl.ds(column, 1), :])

    entry_loop(live, body)
    outbox[:, :LANES] = rows[0].astype(BF16)
    outbox[:, LANES:] = rows[1, :, : tail + 1].astype(BF16)


def place_first(received, placed, chosen_out, answering, wide):
    levels = placed.shape[1]
    values = received[...].astype(F32)
    codes = values[:, levels:]
    wanted = (lax.broadcasted_iota(jnp.int32, (values.shape[0], placed.shape[0]), 1) + 1).astype(F32)
    wide[...] = (codes == wanted).astype(F32)
    chosen = wide[...].astype(BF16)
    chosen_out[...] = chosen
    placed[...] = lax.dot_general(
        chosen, values[:, :levels].astype(BF16), (((0,), (0,)), ((), ())), preferred_element_type=F32
    ).astype(BF16)
    per_owner = 8
    owners = values.shape[0] // per_owner
    for r in range(per_owner):
        answering[r * owners : (r + 1) * owners, :] = wide[pl.ds(r, owners, stride=per_owner), :].astype(BF16)


def place_second(received, chosen, placed):
    placed[...] = lax.dot_general(
        chosen[...], received[...], (((0,), (0,)), ((), ())), preferred_element_type=F32
    ).astype(BF16)


def split_dot(chosen, value):
    high = value.astype(BF16)
    rest = value - high.astype(F32)
    middle = rest.astype(BF16)
    low = (rest - middle.astype(F32)).astype(BF16)
    dot = functools.partial(jnp.dot, preferred_element_type=F32)
    return dot(chosen, high) + dot(chosen, middle) + dot(chosen, low)


def answer_kernel(result, answering, answer, wide):
    owners = answer.shape[0]
    levels = result.shape[1]
    tail = levels - LANES
    per_owner = answering.shape[0] // owners
    wide[...] = jnp.zeros(wide.shape, F32)
    wide[:, :levels] = result[...]
    rows = split_dot(answering[...], wide[...])
    tails = jnp.zeros((owners, LANES), F32)
    for r in range(per_owner):
        block = rows[r * owners : (r + 1) * owners]
        answer[:, r * LANES : (r + 1) * LANES] = block[:, :LANES]
        end = block[:, LANES:]
        tails = tails + (pltpu.roll(end, tail * r, 1) if r else end)
    answer[:, per_owner * LANES :] = tails


def add_first(plan, returned, late, field, *rest, levels):
    for f in range(field.shape[0]):
        unpack_field(late, field, f)
    add_increments(plan, returned, field, field, *rest, levels=levels)


def add_increments(plan, returned, base, field, lon_low, lon_high, lat_low, lat_high, inbox, *, levels):
    fields, halves, columns_all, lanes = field.shape
    owners = returned.shape[0]
    per_owner = inbox.shape[1] // owners
    capacity = (plan.shape[0] - 1) // 2
    tail = levels - LANES
    tails = returned[:, per_owner * LANES :]
    for r in range(per_owner):
        inbox[0, r * owners : (r + 1) * owners] = returned[:, r * LANES : (r + 1) * LANES]
        inbox[1, r * owners : (r + 1) * owners] = pltpu.roll(tails, LANES - tail * r, 1) if r else tails

    def body(e):
        column = plan[1 + e]
        row = plan[1 + capacity + e]
        for f in range(fields):
            for h in range(halves):
                here = (f, h, pl.ds(column, 1), slice(None))
                field[here] = base[here] + inbox[h, pl.ds(row + f * owners, 1), :]

    entry_loop(plan[0], body)
    span_lat = lon_low.shape[2]
    span_lon = lat_low.shape[2]
    for f in range(fields):
        for h in range(halves):
            lon_low[f, h] = field[f, h, :span_lat].astype(BF16)
            lon_high[f, h] = field[f, h, columns_all - span_lat :].astype(BF16)
            lat_low[f, h] = field[f, h, pl.ds(0, span_lon, stride=span_lat), :].astype(BF16)
            lat_high[f, h] = field[f, h, pl.ds(span_lat - 1, span_lon, stride=span_lat), :].astype(BF16)


def inner_stencil(field, coef, extra, out):
    fields, halves, columns_all, lanes = field.shape
    span_lat, span_lon = coef.shape[1:]
    row = lax.broadcasted_iota(jnp.int32, (span_lat, 1), 0)
    for p in range(span_lon):
        weight = [coef[k, :, p : p + 1] for k in range(4)]
        weight[2] = jnp.where(row == 0, 0.0, weight[2])
        weight[3] = jnp.where(row == span_lat - 1, 0.0, weight[3])
        weight = [jnp.broadcast_to(w, (span_lat, lanes)) for w in weight]
        at = slice(p * span_lat, (p + 1) * span_lat)
        for f in range(fields):
            for h in range(halves):
                here = field[f, h, at]
                total = here + weight[2] * pltpu.roll(here, 1, 0) + weight[3] * pltpu.roll(here, span_lat - 1, 0)
                if p > 0:
                    total = total + weight[0] * field[f, h, (p - 1) * span_lat : p * span_lat]
                if p < span_lon - 1:
                    total = total + weight[1] * field[f, h, (p + 1) * span_lat : (p + 2) * span_lat]
                if extra is None:
                    out[f, h, at] = total
                elif h == 0:
                    out[f, h, at] = total + extra[f, at, :lanes].astype(F32)
                else:
                    tail = extra.shape[2] - lanes
                    out[f, h, at, :tail] = total[:, :tail] + extra[f, at, lanes:].astype(F32)


def inner_first(field, coef, early, out):
    inner_stencil(field, coef, early, out)


def inner_last(field, coef, out):
    inner_stencil(field, coef, None, out)


def edge_weights(coef):
    span_lat, span_lon = coef.shape[1:]
    same = lax.broadcasted_iota(jnp.int32, (span_lon, span_lon), 0) == lax.broadcasted_iota(
        jnp.int32, (span_lon, span_lon), 1
    )

    def upright(line):
        return jnp.sum(jnp.where(same, jnp.broadcast_to(line, (span_lon, span_lon)), 0.0), axis=1, keepdims=True)

    return (
        coef[0, :, :1],
        coef[1, :, span_lon - 1 :],
        upright(coef[2, :1, :]),
        upright(coef[3, span_lat - 1 :, :]),
    )


def add_edges(f, h, weights, from_before, from_after, from_low, from_high, out):
    columns_all = out.shape[2]
    span_lat = from_before.shape[2]
    span_lon = from_low.shape[2]
    first = (f, h, slice(0, span_lat))
    last = (f, h, slice(columns_all - span_lat, columns_all))
    low = (f, h, pl.ds(0, span_lon, stride=span_lat), slice(None))
    high = (f, h, pl.ds(span_lat - 1, span_lon, stride=span_lat), slice(None))
    for at, weight, edge in zip((first, last, low, high), weights, (from_before, from_after, from_low, from_high)):
        out[at] = out[at] + weight * edge[f, h].astype(F32)


def edges_first(plan, inner, coef, from_before, from_after, from_low, from_high, out, outbox, rows):
    fields, halves, columns_all, lanes = out.shape
    capacity = (plan.shape[0] - 1) // 2
    owners = rows.shape[1] // (PAIR * fields)
    tail = outbox.shape[1] - lanes
    weights = edge_weights(coef)
    rows[...] = jnp.zeros(rows.shape, F32)
    for f in range(fields):
        for h in range(halves):
            add_edges(f, h, weights, from_before, from_after, from_low, from_high, out)

    def body(e):
        column = plan[1 + e]
        row = plan[1 + capacity + e]
        rank = row // (fields * owners)
        first = ((row - rank * (fields * owners)) * PAIR + rank) * fields
        for f in range(fields):
            for h in range(halves):
                rows[h, pl.ds(first + f, 1), :] = out[f, h, pl.ds(column, 1), :]

    entry_loop(plan[0], body)
    outbox[:, :lanes] = rows[0].astype(BF16)
    outbox[:, lanes:] = rows[1, :, :tail].astype(BF16)


def edges_last(inner, coef, from_before, from_after, from_low, from_high, out_hbm, both, out, sems):
    fields, halves, columns_all, lanes = inner.shape
    tail = out.shape[2] - lanes
    weights = edge_weights(coef)
    copies = []
    for f in range(fields):
        for h in range(halves):
            both[f, h] = inner[f, h]
            add_edges(f, h, weights, from_before, from_after, from_low, from_high, both)
        out[f, :, :lanes] = both[f, 0]
        out[f, :, lanes:] = both[f, 1, :, :tail]
        copies.append(pltpu.make_async_copy(out.at[f], out_hbm.at[f], sems.at[f]))
        copies[f].start()
    for copy in copies:
        copy.wait()


def exchange(rows, groups):
    width = rows.shape[0] // groups
    moved = lax.all_to_all(
        rows.reshape(groups, width, rows.shape[1]), "gy", split_axis=0, concat_axis=0, tiled=True
    )
    return moved.reshape(rows.shape)


def halos(lon_low, lon_high, lat_low, lat_high):
    lon = lax.axis_size("gx")
    lat = lax.axis_size("gy")
    up = [(i, (i + 1) % lon) for i in range(lon)]
    down = [(target, source) for source, target in up]
    north = [(i, i + 1) for i in range(lat - 1)]
    south = [(target, source) for source, target in north]
    from_low = lax.ppermute(lat_high, "gy", north)
    from_high = lax.ppermute(lat_low, "gy", south)
    from_before = lax.ppermute(lon_high, "gx", up)
    from_after = lax.ppermute(lon_low, "gx", down)
    return from_before, from_after, from_low, from_high


def on_device(late, early, stencil_coef, jacobian, cloudy_cols, cloudy_count, owner_rank, owner_slot):
    fields, levels, span_lon, span_lat = late.shape
    groups = lax.axis_size("gy")
    own_slots = jacobian.shape[1]
    capacity = cloudy_cols.shape[2]
    columns_all = span_lon * span_lat
    late = late.transpose(0, 2, 3, 1).reshape(fields, columns_all, levels)
    early = early.transpose(0, 2, 3, 1).reshape(fields, columns_all, levels)
    coef = stencil_coef.transpose(0, 2, 1)
    matrices = jacobian[0]
    shape = jax.ShapeDtypeStruct
    per_owner = PAIR * fields
    inbox_rows = groups * per_owner
    grid = (fields, columns_all, levels)
    halves = (fields, 2, columns_all, LANES)
    plan_shape = shape((2 * capacity + 1,), jnp.int32)

    outbox, plan = call(
        pack_first,
        [shape((inbox_rows, levels + 1), BF16), plan_shape],
        [HBM] * 5,
        [VMEM, SMEM],
        [
            SMEM(cloudy_cols.shape, jnp.int32),
            SMEM(cloudy_count.shape, jnp.int32),
            SMEM(owner_rank.shape, jnp.int32),
            SMEM(owner_slot.shape, jnp.int32),
            VMEM(grid, BF16),
            VMEM(halves, F32),
            VMEM((2, inbox_rows, LANES), F32),
            SMEM((groups,), jnp.int32),
            pltpu.SemaphoreType.DMA((4 + fields,)),
        ],
        vmem=57,
    )(cloudy_cols, cloudy_count, owner_rank, owner_slot, late)
    received = exchange(outbox, groups)
    chosen_shape = shape((inbox_rows, own_slots * fields), BF16)
    placed_shape = shape((own_slots * fields, levels), BF16)
    placed, chosen, answering = call(
        place_first,
        [placed_shape, chosen_shape, chosen_shape],
        [VMEM],
        [VMEM] * 3,
        [VMEM(chosen_shape.shape, F32)],
    )(received)

    def apply(placed):
        result = jnp.einsum(
            "sfij,sfi->sfj",
            matrices,
            placed.reshape(own_slots, fields, levels),
            preferred_element_type=F32,
        ).reshape(own_slots * fields, levels)
        (answer,) = call(
            answer_kernel,
            [shape((groups, (per_owner + 1) * LANES), F32)],
            [VMEM] * 2,
            [VMEM],
            [VMEM((own_slots * fields, 2 * LANES), F32)],
        )(result, answering)
        return exchange(answer, groups)

    edge_shapes = [shape((fields, 2, span, LANES), BF16) for span in (span_lat, span_lat, span_lon, span_lon)]

    def add(kernel, returned, base, aliases):
        return call(
            functools.partial(kernel, levels=levels),
            [shape(halves, F32)] + edge_shapes,
            [SMEM] + [VMEM] * 2,
            [VMEM] * 5,
            [VMEM((2, inbox_rows, LANES), F32)],
            aliases,
        )(plan, returned, base)

    field, *edges = add(add_first, apply(placed), late, {})
    neighbours = halos(*edges)
    (inner,) = call(inner_first, [shape(halves, F32)], [VMEM] * 3, [VMEM], touched=6000000)(field, coef, early)
    adjoint, outbox = call(
        edges_first,
        [shape(halves, F32), shape((inbox_rows, levels), BF16)],
        [SMEM] + [VMEM] * 6,
        [VMEM] * 2,
        [VMEM((2, inbox_rows, LANES), F32)],
        {1: 0},
    )(plan, inner, coef, *neighbours)
    received = exchange(outbox, groups)
    (placed,) = call(place_second, [placed_shape], [VMEM] * 2, [VMEM])(received, chosen)
    field, *edges = add(add_increments, apply(placed), adjoint, {2: 0})
    neighbours = halos(*edges)
    (inner,) = call(inner_last, [shape(halves, F32)], [VMEM] * 2, [VMEM], touched=6000000)(field, coef)
    (final,) = call(
        edges_last,
        [shape(grid, F32)],
        [VMEM] * 6,
        [HBM],
        [VMEM(halves, F32), VMEM(grid, F32), pltpu.SemaphoreType.DMA((fields,))],
    )(inner, coef, *neighbours)
    return final.reshape(fields, span_lon, span_lat, levels).transpose(0, 3, 1, 2)


def solution(mesh):
    return jax.shard_map(
        on_device,
        mesh=mesh,
        in_specs=(
            P(None, None, "gx", "gy"),
            P(None, None, "gx", "gy"),
            P(None, "gx", "gy"),
            P("gx", "gy", None, None, None),
            P("gx", "gy", None),
            P("gx", "gy"),
            P("gx", "gy", None),
            P("gx", "gy", None),
        ),
        out_specs=P(None, None, "gx", "gy"),
        check_vma=False,
    )
```

time: 127 us -> 121 us (0.953)
  the two profiles are of different devices: /device:TPU:1 before, /device:TPU:2 now
where the time goes in v2:
time: 121 us; the launch traced here: 120 us
  blocking collectives  61.5 us (51%)
  starting transfers between devices  39.6 us (33%)
  Pallas kernels  10.7 us (9%)
  matrix products  6 us (5%)
    all_to_all x4, blocking collectives, exchange(): lax.all_to_all(rows.reshape(groups, width, rows.shape[1]), 'gy', split_ax...  61.5 us
    ppermute x2, starting transfers between devices, halos(): from_after = lax.ppermute(lon_low, 'gx', down)  17.6 us
    ppermute x2, starting transfers between devices, halos(): from_high = lax.ppermute(lat_low, 'gy', south)  11.6 us
    dot_general x2, matrix products, apply(): jnp.einsum('sfij,sfi->sfj', matrices, placed.reshape(own_slots, fields, l...  6 us
    ppermute x2, starting transfers between devices, halos(): from_low = lax.ppermute(lat_high, 'gy', north)  5.51 us
    ppermute x2, starting transfers between devices, halos(): from_before = lax.ppermute(lon_high, 'gx', up)  4.83 us
  transfers between devices with their start and end apart: 8, of which 2 were waited for; matrix products, arithmetic and copies ran while one was open for 0% of the time, Pallas kernels for 2%

profile of v2, /device:TPU:2, one launch (start us, length us, event | category | flops | bytes accessed | tf_op | source)
XLA Modules:
  0.0 120.1 jit_solution(16687334088408258247)
XLA Ops:
  0.8 2.4 %shard_map.82 = (bf16[256,138]{1,0:T(8,128)(2,1)}, s32[97]{0:T(128)}) custom-call(s32[1,1,48]{2,1,0:T(1,128)} %cols_hbm.1, s32[1,1]{1,0:T(1,128)S(6)} %copy.34.count_hbm, s32[1,1,48]{2,1,0:T(1,128)} %owner_hbm.1, s32[1,1,48]{2,1,0:T(1,128)} %slot_hbm.1, bf16[4,512,137]{2,1,0:T(8,128)(2,1)} %bitcast.31), custom_call_target="tpu_custom_call" | custom-call | flops 1000 | bytes 1000000 | tf_op jit(solution)/shard_map/pallas_call | solution.py:321
  3.1 19.4 %all_to_all.20 = bf16[32,8,138]{2,1,0:T(8,128)(2,1)S(1)} all-to-all(bf16[32,8,138]{2,1,0:T(8,128)(2,1)} %bitcast.49), channel_id=1, replica_groups=mesh['gx'=16,'gy'=32] {'gy'}, dimensions={0} | all-to-all | bytes 141312 | tf_op jit(solution)/shard_map/all_to_all | solution.py:284
  22.8 3.0 %fusion.2 = f32[16,4,1,137]{3,2,1,0:T(1,128)S(1)} fusion(bf16[16,4,137,1]{2,3,1,0:T(2,128)(2,1)S(1)} %reshape.65, bf16[16,4,137,137]{3,1,2,0:T(4,128)(2,1)} %bitcast.45), kind=kOutput, calls=%fused_computation.2 | convolution fusion | flops 2402432 | bytes 2455040 | tf_op jit(solution)/shard_map/sfij,sfi->sfj/dot_general | solution.py:351
  25.9 0.3 shard_map.84
  26.4 14.1 %all_to_all.21 = f32[32,1,1152]{2,1,0:T(1,128)S(1)} all-to-all(f32[32,1,1152]{2,1,0:T(1,128)S(1)} %copy.11), channel_id=1, replica_groups=mesh['gx'=16,'gy'=32] {'gy'}, dimensions={0} | all-to-all | bytes 294912 | tf_op jit(solution)/shard_map/all_to_all | solution.py:284
  40.5 1.1 shard_map.85
  41.6 2.9 %collective-permute-start.2 = (bf16[4,2,32,128]{3,2,1,0:T(8,128)(2,1)S(1)}, bf16[4,2,32,128]{3,2,1,0:T(8,128)(2,1)S(1)}, u32[]{:S(2)}, u32[]{:S(2)}) collective-permute-start(bf16[4,2,32,128]{3,2,1,0:T(8,128)(2,1)S(1)} %get-tuple-element.29), channel_id=1, source_target_pairs={{0,1},{1,2},{2,3},{3,4},{4,5},{5,6},{6,7},{7,8},{8,9},{9,10},{10,1... | collective-permute-start | bytes 196616 | tf_op jit(solution)/shard_map/ppermute | solution.py:297
  44.5 5.7 %collective-permute-start.3 = (bf16[4,2,32,128]{3,2,1,0:T(8,128)(2,1)S(1)}, bf16[4,2,32,128]{3,2,1,0:T(8,128)(2,1)S(1)}, u32[]{:S(2)}, u32[]{:S(2)}) collective-permute-start(bf16[4,2,32,128]{3,2,1,0:T(8,128)(2,1)S(1)} %get-tuple-element.30), channel_id=1, source_target_pairs={{1,0},{2,1},{3,2},{4,3},{5,4},{6,5},{7,6},{8,7},{9,8},{10,9},{11,1... | collective-permute-start | bytes 196616 | tf_op jit(solution)/shard_map/ppermute | solution.py:298
  50.2 2.9 %collective-permute-start = (bf16[4,2,16,128]{3,2,1,0:T(8,128)(2,1)S(1)}, bf16[4,2,16,128]{3,2,1,0:T(8,128)(2,1)S(1)}, u32[]{:S(2)}, u32[]{:S(2)}) collective-permute-start(bf16[4,2,16,128]{3,2,1,0:T(8,128)(2,1)S(1)} %get-tuple-element.27), channel_id=1, source_target_pairs={{0,32},{32,64},{64,96},{96,128},{128,160},{160,192},{192,224},{224... | collective-permute-start | bytes 98312 | tf_op jit(solution)/shard_map/ppermute | solution.py:299
  53.1 10.5 %collective-permute-start.1 = (bf16[4,2,16,128]{3,2,1,0:T(8,128)(2,1)S(1)}, bf16[4,2,16,128]{3,2,1,0:T(8,128)(2,1)S(1)}, u32[]{:S(2)}, u32[]{:S(2)}) collective-permute-start(bf16[4,2,16,128]{3,2,1,0:T(8,128)(2,1)S(1)} %get-tuple-element.28), channel_id=1, source_target_pairs={{32,0},{64,32},{96,64},{128,96},{160,128},{192,160},{224,192},{256... | collective-permute-start | bytes 98312 | tf_op jit(solution)/shard_map/ppermute | solution.py:300
  63.7 1.2 %shard_map.86.inner = f32[4,2,512,128]{3,2,1,0:T(8,128)S(1)} custom-call(f32[4,2,512,128]{3,2,1,0:T(8,128)S(1)} %get-tuple-element.26.field, f32[4,16,32]{2,1,0:T(8,128)S(1)} %bitcast.38, bf16[4,512,137]{2,1,0:T(8,128)(2,1)S(1)} %bitcast.33), custom_call_target="tpu_custom_call" | custom-call | flops 1000 | bytes 6000000 | tf_op jit(solution)/shard_map/pallas_call | solution.py:380
  65.2 1.1 shard_map.87
  66.4 14.0 %all_to_all.22 = bf16[32,8,137]{2,1,0:T(8,128)(2,1)S(1)} all-to-all(bf16[32,8,137]{2,1,0:T(8,128)(2,1)S(1)} %bitcast.44), channel_id=1, replica_groups=mesh['gx'=16,'gy'=32] {'gy'}, dimensions={0} | all-to-all | bytes 140288 | tf_op jit(solution)/shard_map/all_to_all | solution.py:284
  80.6 3.0 %fusion = f32[16,4,1,137]{3,2,1,0:T(1,128)S(1)} fusion(bf16[16,4,137,1]{2,3,1,0:T(2,128)(2,1)S(1)} %reshape.67, bf16[16,4,137,137]{3,1,2,0:T(4,128)(2,1)} %bitcast.46), kind=kOutput, calls=%fused_computation | convolution fusion | flops 2402432 | bytes 2455040 | tf_op jit(solution)/shard_map/sfij,sfi->sfj/dot_general | solution.py:351
  83.7 0.3 shard_map.89
  84.2 14.0 %all_to_all.23 = f32[32,1,1152]{2,1,0:T(1,128)S(1)} all-to-all(f32[32,1,1152]{2,1,0:T(1,128)S(1)} %copy.12), channel_id=1, replica_groups=mesh['gx'=16,'gy'=32] {'gy'}, dimensions={0} | all-to-all | bytes 294912 | tf_op jit(solution)/shard_map/all_to_all | solution.py:284
  98.2 1.2 shard_map.90
  99.3 2.6 %collective-permute-start.6 = (bf16[4,2,32,128]{3,2,1,0:T(8,128)(2,1)S(1)}, bf16[4,2,32,128]{3,2,1,0:T(8,128)(2,1)S(1)}, u32[]{:S(2)}, u32[]{:S(2)}) collective-permute-start(bf16[4,2,32,128]{3,2,1,0:T(8,128)(2,1)S(1)} %get-tuple-element.37), channel_id=1, source_target_pairs={{0,1},{1,2},{2,3},{3,4},{4,5},{5,6},{6,7},{7,8},{8,9},{9,10},{10,1... | collective-permute-start | bytes 196616 | tf_op jit(solution)/shard_map/ppermute | solution.py:297
  102.0 6.0 %collective-permute-start.7 = (bf16[4,2,32,128]{3,2,1,0:T(8,128)(2,1)S(1)}, bf16[4,2,32,128]{3,2,1,0:T(8,128)(2,1)S(1)}, u32[]{:S(2)}, u32[]{:S(2)}) collective-permute-start(bf16[4,2,32,128]{3,2,1,0:T(8,128)(2,1)S(1)} %get-tuple-element.38), channel_id=1, source_target_pairs={{1,0},{2,1},{3,2},{4,3},{5,4},{6,5},{7,6},{8,7},{9,8},{10,9},{11,1... | collective-permute-start | bytes 196616 | tf_op jit(solution)/shard_map/ppermute | solution.py:298
  107.9 1.9 %collective-permute-start.4 = (bf16[4,2,16,128]{3,2,1,0:T(8,128)(2,1)S(1)}, bf16[4,2,16,128]{3,2,1,0:T(8,128)(2,1)S(1)}, u32[]{:S(2)}, u32[]{:S(2)}) collective-permute-start(bf16[4,2,16,128]{3,2,1,0:T(8,128)(2,1)S(1)} %get-tuple-element.35), channel_id=1, source_target_pairs={{0,32},{32,64},{64,96},{96,128},{128,160},{160,192},{192,224},{224... | collective-permute-start | bytes 98312 | tf_op jit(solution)/shard_map/ppermute | solution.py:299
  109.8 7.1 %collective-permute-start.5 = (bf16[4,2,16,128]{3,2,1,0:T(8,128)(2,1)S(1)}, bf16[4,2,16,128]{3,2,1,0:T(8,128)(2,1)S(1)}, u32[]{:S(2)}, u32[]{:S(2)}) collective-permute-start(bf16[4,2,16,128]{3,2,1,0:T(8,128)(2,1)S(1)} %get-tuple-element.36), channel_id=1, source_target_pairs={{32,0},{64,32},{96,64},{128,96},{160,128},{192,160},{224,192},{256... | collective-permute-start | bytes 98312 | tf_op jit(solution)/shard_map/ppermute | solution.py:300
  116.9 1.1 shard_map.91.inner
  118.0 0.5 collective-permute-done.5.from_after
  118.5 1.6 %shard_map.92 = f32[4,512,137]{2,1,0:T(8,128)} custom-call(f32[4,2,512,128]{3,2,1,0:T(8,128)S(1)} %shard_map.91.inner, f32[4,16,32]{2,1,0:T(8,128)S(1)} %bitcast.41, bf16[4,2,16,128]{3,2,1,0:T(8,128)(2,1)S(1)} %collective-permute-done.4.from_before, bf16[4,2,16,128]{3,2,1,0:T(8,128)(2,1)S(1)} %collective-permute-done.5.from_after, ...), custom_call_target="tpu_custom_call" | custom-call | flops 1000 | bytes 1000000 | tf_op jit(solution)/shard_map/pallas_call | solution.py:394
  (27 shorter events, 1.2 us)
Async XLA Ops:
  0.0 40.5 %copy-start = (bf16[4,137,32,16]{1,3,2,0:T(8,128)(2,1)S(1)}, bf16[4,137,32,16]{1,3,2,0:T(8,128)(2,1)}, u32[]{:S(2)}) copy-start(bf16[4,137,32,16]{1,3,2,0:T(8,128)(2,1)} %param.8) | copy-start | bytes 1683460
  0.7 62.9 %copy-start.1 = (bf16[4,137,32,16]{1,3,2,0:T(8,128)(2,1)S(1)}, bf16[4,137,32,16]{1,3,2,0:T(8,128)(2,1)}, u32[]{:S(2)}) copy-start(bf16[4,137,32,16]{1,3,2,0:T(8,128)(2,1)} %param.9) | copy-start | bytes 1683460
  0.8 62.9 %copy-start.2 = (f32[4,32,16]{1,2,0:T(8,128)S(1)}, f32[4,32,16]{1,2,0:T(8,128)}, u32[]{:S(2)}) copy-start(f32[4,32,16]{1,2,0:T(8,128)} %param.10) | copy-start | bytes 24580
  3.1 37.4 %copy-start.3 = (s32[97]{0:T(128)S(1)}, s32[97]{0:T(128)}, u32[]{:S(2)}) copy-start(s32[97]{0:T(128)} %get-tuple-element.22.plan) | copy-start | bytes 1168
  41.6 23.6 %collective-permute-start.2 = (bf16[4,2,32,128]{3,2,1,0:T(8,128)(2,1)S(1)}, bf16[4,2,32,128]{3,2,1,0:T(8,128)(2,1)S(1)}, u32[]{:S(2)}, u32[]{:S(2)}) collective-permute-start(bf16[4,2,32,128]{3,2,1,0:T(8,128)(2,1)S(1)} %get-tuple-element.29), channel_id=1, source_target_pairs={{0,1},{1,2},{2,3},{3,4},{4,5},{5,6},{6,7},{7,8},{8,9},{9,10},{10,1... | collective-permute-start | bytes 196616 | tf_op jit(solution)/shard_map/ppermute | solution.py:297
  44.5 20.7 %collective-permute-start.3 = (bf16[4,2,32,128]{3,2,1,0:T(8,128)(2,1)S(1)}, bf16[4,2,32,128]{3,2,1,0:T(8,128)(2,1)S(1)}, u32[]{:S(2)}, u32[]{:S(2)}) collective-permute-start(bf16[4,2,32,128]{3,2,1,0:T(8,128)(2,1)S(1)} %get-tuple-element.30), channel_id=1, source_target_pairs={{1,0},{2,1},{3,2},{4,3},{5,4},{6,5},{7,6},{8,7},{9,8},{10,9},{11,1... | collective-permute-start | bytes 196616 | tf_op jit(solution)/shard_map/ppermute | solution.py:298
  50.2 14.7 %collective-permute-start = (bf16[4,2,16,128]{3,2,1,0:T(8,128)(2,1)S(1)}, bf16[4,2,16,128]{3,2,1,0:T(8,128)(2,1)S(1)}, u32[]{:S(2)}, u32[]{:S(2)}) collective-permute-start(bf16[4,2,16,128]{3,2,1,0:T(8,128)(2,1)S(1)} %get-tuple-element.27), channel_id=1, source_target_pairs={{0,32},{32,64},{64,96},{96,128},{128,160},{160,192},{192,224},{224... | collective-permute-start | bytes 98312 | tf_op jit(solution)/shard_map/ppermute | solution.py:299
  53.1 12.1 %collective-permute-start.1 = (bf16[4,2,16,128]{3,2,1,0:T(8,128)(2,1)S(1)}, bf16[4,2,16,128]{3,2,1,0:T(8,128)(2,1)S(1)}, u32[]{:S(2)}, u32[]{:S(2)}) collective-permute-start(bf16[4,2,16,128]{3,2,1,0:T(8,128)(2,1)S(1)} %get-tuple-element.28), channel_id=1, source_target_pairs={{32,0},{64,32},{96,64},{128,96},{160,128},{192,160},{224,192},{256... | collective-permute-start | bytes 98312 | tf_op jit(solution)/shard_map/ppermute | solution.py:300
  99.3 19.2 %collective-permute-start.6 = (bf16[4,2,32,128]{3,2,1,0:T(8,128)(2,1)S(1)}, bf16[4,2,32,128]{3,2,1,0:T(8,128)(2,1)S(1)}, u32[]{:S(2)}, u32[]{:S(2)}) collective-permute-start(bf16[4,2,32,128]{3,2,1,0:T(8,128)(2,1)S(1)} %get-tuple-element.37), channel_id=1, source_target_pairs={{0,1},{1,2},{2,3},{3,4},{4,5},{5,6},{6,7},{7,8},{8,9},{9,10},{10,1... | collective-permute-start | bytes 196616 | tf_op jit(solution)/shard_map/ppermute | solution.py:297
  102.0 16.5 %collective-permute-start.7 = (bf16[4,2,32,128]{3,2,1,0:T(8,128)(2,1)S(1)}, bf16[4,2,32,128]{3,2,1,0:T(8,128)(2,1)S(1)}, u32[]{:S(2)}, u32[]{:S(2)}) collective-permute-start(bf16[4,2,32,128]{3,2,1,0:T(8,128)(2,1)S(1)} %get-tuple-element.38), channel_id=1, source_target_pairs={{1,0},{2,1},{3,2},{4,3},{5,4},{6,5},{7,6},{8,7},{9,8},{10,9},{11,1... | collective-permute-start | bytes 196616 | tf_op jit(solution)/shard_map/ppermute | solution.py:298
  107.9 10.1 %collective-permute-start.4 = (bf16[4,2,16,128]{3,2,1,0:T(8,128)(2,1)S(1)}, bf16[4,2,16,128]{3,2,1,0:T(8,128)(2,1)S(1)}, u32[]{:S(2)}, u32[]{:S(2)}) collective-permute-start(bf16[4,2,16,128]{3,2,1,0:T(8,128)(2,1)S(1)} %get-tuple-element.35), channel_id=1, source_target_pairs={{0,32},{32,64},{64,96},{96,128},{128,160},{160,192},{192,224},{224... | collective-permute-start | bytes 98312 | tf_op jit(solution)/shard_map/ppermute | solution.py:299
  109.8 8.6 %collective-permute-start.5 = (bf16[4,2,16,128]{3,2,1,0:T(8,128)(2,1)S(1)}, bf16[4,2,16,128]{3,2,1,0:T(8,128)(2,1)S(1)}, u32[]{:S(2)}, u32[]{:S(2)}) collective-permute-start(bf16[4,2,16,128]{3,2,1,0:T(8,128)(2,1)S(1)} %get-tuple-element.36), channel_id=1, source_target_pairs={{32,0},{64,32},{96,64},{128,96},{160,128},{192,160},{224,192},{256... | collective-permute-start | bytes 98312 | tf_op jit(solution)/shard_map/ppermute | solution.py:300

commit v3 on v2

--- a/solution.py
+++ b/solution.py
@@ -14,6 +14,7 @@
 HBM = pltpu.HBM
 PAIR = 2
 LANES = 128
+GROUP = 4
 
 
 def call(kernel, out_shape, in_spaces, out_spaces, scratch=(), aliases=None, flops=1000, touched=1000000, vmem=40):
@@ -29,12 +30,15 @@
     )
 
 
-def entry_loop(count, body):
-    def step(e, carry):
-        body(e)
+def entry_groups(plan, body):
+    capacity = (plan.shape[0] - 1) // 2
+
+    def step(g, carry):
+        first = g * GROUP
+        body([(plan[1 + first + i], plan[1 + capacity + first + i]) for i in range(GROUP)])
         return carry
 
-    lax.fori_loop(0, count, step, 0)
+    lax.fori_loop(0, (plan[0] + (GROUP - 1)) // GROUP, step, 0)
 
 
 def unpack_field(packed, field, f):
@@ -56,59 +60,59 @@
     copies += [pltpu.make_async_copy(late_hbm.at[f], late.at[f], sems.at[len(small) + f]) for f in range(fields)]
     for copy in copies:
         copy.start()
-    rows[...] = jnp.zeros(rows.shape, F32)
     for o in range(owners):
         used[o] = 0
-    for e in range(2 * capacity + 1):
-        plan[e] = 0
-    for f in range(fields):
-        copies[len(small) + f].wait()
-        unpack_field(late, field, f)
     for copy in copies[: len(small)]:
         copy.wait()
     live = count[0, 0]
     plan[0] = live
 
-    def body(e):
+    def route(e, carry):
         o = owner[0, 0, e]
-        column = cols[0, 0, e]
         rank = used[o]
         used[o] = rank + 1
-        plan[1 + e] = column
+        plan[1 + e] = cols[0, 0, e]
         plan[1 + capacity + e] = rank * (fields * owners) + o
-        first = (o * PAIR + rank) * fields
-        code = slot[0, 0, e] * fields
-        for f in range(fields):
-            mark = (code + (f + 1)).astype(F32)
-            rows[0, pl.ds(first + f, 1), :] = field[f, 0, pl.ds(column, 1), :]
-            rows[1, pl.ds(first + f, 1), :] = jnp.where(end == tail, mark, field[f, 1, pl.ds(column, 1), :])
-
-    entry_loop(live, body)
+        return carry
+
+    lax.fori_loop(0, live, route, 0)
+    whole = (live // GROUP) * GROUP
+
+    def repeat(e, carry):
+        for part in (1, 1 + capacity):
+            plan[part + e] = plan[part + whole]
+        slot[0, 0, e] = slot[0, 0, whole]
+        return carry
+
+    lax.fori_loop(live, ((live + (GROUP - 1)) // GROUP) * GROUP, repeat, 0)
+    rows[...] = jnp.zeros(rows.shape, F32)
+    for f in range(fields):
+        copies[len(small) + f].wait()
+        unpack_field(late, field, f)
+
+    def gather(g, carry):
+        first = g * GROUP
+        found = []
+        for i in range(GROUP):
+            column = plan[1 + first + i]
+            row = outbox_row(plan[1 + capacity + first + i], owners, fields)
+            code = slot[0, 0, first + i] * fields
+            for f in range(fields):
+                mark = (code + (f + 1)).astype(F32)
+                found.append((0, row + f, field[f, 0, pl.ds(column, 1), :]))
+                found.append((1, row + f, jnp.where(end == tail, mark, field[f, 1, pl.ds(column, 1), :])))
+        for h, row, value in found:
+            rows[h, pl.ds(row, 1), :] = value
+        return carry
+
+    lax.fori_loop(0, (live + (GROUP - 1)) // GROUP, gather, 0)
     outbox[:, :LANES] = rows[0].astype(BF16)
     outbox[:, LANES:] = rows[1, :, : tail + 1].astype(BF16)
 
 
-def place_first(received, placed, chosen_out, answering, wide):
-    levels = placed.shape[1]
-    values = received[...].astype(F32)
-    codes = values[:, levels:]
-    wanted = (lax.broadcasted_iota(jnp.int32, (values.shape[0], placed.shape[0]), 1) + 1).astype(F32)
-    wide[...] = (codes == wanted).astype(F32)
-    chosen = wide[...].astype(BF16)
-    chosen_out[...] = chosen
-    placed[...] = lax.dot_general(
-        chosen, values[:, :levels].astype(BF16), (((0,), (0,)), ((), ())), preferred_element_type=F32
-    ).astype(BF16)
-    per_owner = 8
-    owners = values.shape[0] // per_owner
-    for r in range(per_owner):
-        answering[r * owners : (r + 1) * owners, :] = wide[pl.ds(r, owners, stride=per_owner), :].astype(BF16)
-
-
-def place_second(received, chosen, placed):
-    placed[...] = lax.dot_general(
-        chosen[...], received[...], (((0,), (0,)), ((), ())), preferred_element_type=F32
-    ).astype(BF16)
+def outbox_row(row, owners, fields):
+    rank = row // (fields * owners)
+    return ((row - rank * (fields * owners)) * PAIR + rank) * fields
 
 
 def split_dot(chosen, value):
@@ -120,14 +124,35 @@
     return dot(chosen, high) + dot(chosen, middle) + dot(chosen, low)
 
 
-def answer_kernel(result, answering, answer, wide):
+def fetch(matrices_hbm, matrices, sems):
+    copies = [
+        pltpu.make_async_copy(matrices_hbm.at[s], matrices.at[s], sems.at[s]) for s in range(matrices.shape[0])
+    ]
+    for copy in copies:
+        copy.start()
+    return copies
+
+
+def products(chosen, values, answering, matrices, copies, answer, spread, result):
+    own_slots, levels, fields, _ = matrices.shape
+    depth = levels * fields
+    placed = lax.dot_general(chosen, values, (((0,), (0,)), ((), ())), preferred_element_type=F32).astype(BF16)
+    iota = functools.partial(lax.broadcasted_iota, jnp.int32)
+    widen = (iota((levels, depth), 1) // fields == iota((levels, depth), 0)).astype(F32).astype(BF16)
+    wide = jnp.dot(placed, widen, preferred_element_type=F32)
+    own = iota(spread.shape, 1) % fields == iota(spread.shape, 0) % fields
+    spread[...] = jnp.where(own, wide, 0.0)
+    result[...] = jnp.zeros(result.shape, F32)
+    for s in range(own_slots):
+        at = slice(s * fields, (s + 1) * fields)
+        copies[s].wait()
+        result[at, :levels] = jnp.dot(
+            spread[at].astype(BF16), matrices[s].reshape(depth, levels), preferred_element_type=F32
+        )
     owners = answer.shape[0]
-    levels = result.shape[1]
     tail = levels - LANES
     per_owner = answering.shape[0] // owners
-    wide[...] = jnp.zeros(wide.shape, F32)
-    wide[:, :levels] = result[...]
-    rows = split_dot(answering[...], wide[...])
+    rows = split_dot(answering, result[...])
     tails = jnp.zeros((owners, LANES), F32)
     for r in range(per_owner):
         block = rows[r * owners : (r + 1) * owners]
@@ -137,6 +162,29 @@
     answer[:, per_owner * LANES :] = tails
 
 
+def physics_first(received, matrices_hbm, answer, chosen_out, answering_out, spread, result, matrices, sems, choice):
+    copies = fetch(matrices_hbm, matrices, sems)
+    levels = matrices.shape[1]
+    owners = answer.shape[0]
+    per_owner = received.shape[0] // owners
+    values = received[...].astype(F32)
+    codes = values[:, levels:]
+    wanted = (lax.broadcasted_iota(jnp.int32, choice.shape, 1) + 1).astype(F32)
+    choice[...] = (codes == wanted).astype(F32)
+    chosen = choice[...].astype(BF16)
+    answering = jnp.concatenate(
+        [choice[pl.ds(r, owners, stride=per_owner), :] for r in range(per_owner)], axis=0
+    ).astype(BF16)
+    chosen_out[...] = chosen
+    answering_out[...] = answering
+    products(chosen, values[:, :levels].astype(BF16), answering, matrices, copies, answer, spread, result)
+
+
+def physics_second(received, matrices_hbm, chosen, answering, answer, spread, result, matrices, sems):
+    copies = fetch(matrices_hbm, matrices, sems)
+    products(chosen[...], received[...], answering[...], matrices, copies, answer, spread, result)
+
+
 def add_first(plan, returned, late, field, *rest, levels):
     for f in range(field.shape[0]):
         unpack_field(late, field, f)
@@ -147,22 +195,23 @@
     fields, halves, columns_all, lanes = field.shape
     owners = returned.shape[0]
     per_owner = inbox.shape[1] // owners
-    capacity = (plan.shape[0] - 1) // 2
     tail = levels - LANES
     tails = returned[:, per_owner * LANES :]
     for r in range(per_owner):
         inbox[0, r * owners : (r + 1) * owners] = returned[:, r * LANES : (r + 1) * LANES]
         inbox[1, r * owners : (r + 1) * owners] = pltpu.roll(tails, LANES - tail * r, 1) if r else tails
 
-    def body(e):
-        column = plan[1 + e]
-        row = plan[1 + capacity + e]
-        for f in range(fields):
-            for h in range(halves):
-                here = (f, h, pl.ds(column, 1), slice(None))
-                field[here] = base[here] + inbox[h, pl.ds(row + f * owners, 1), :]
-
-    entry_loop(plan[0], body)
+    def body(entries):
+        found = []
+        for column, row in entries:
+            for f in range(fields):
+                for h in range(halves):
+                    here = (f, h, pl.ds(column, 1), slice(None))
+                    found.append((here, base[here] + inbox[h, pl.ds(row + f * owners, 1), :]))
+        for here, value in found:
+            field[here] = value
+
+    entry_groups(plan, body)
     span_lat = lon_low.shape[2]
     span_lon = lat_low.shape[2]
     for f in range(fields):
@@ -239,7 +288,6 @@
 
 def edges_first(plan, inner, coef, from_before, from_after, from_low, from_high, out, outbox, rows):
     fields, halves, columns_all, lanes = out.shape
-    capacity = (plan.shape[0] - 1) // 2
     owners = rows.shape[1] // (PAIR * fields)
     tail = outbox.shape[1] - lanes
     weights = edge_weights(coef)
@@ -248,16 +296,17 @@
         for h in range(halves):
             add_edges(f, h, weights, from_before, from_after, from_low, from_high, out)
 
-    def body(e):
-        column = plan[1 + e]
-        row = plan[1 + capacity + e]
-        rank = row // (fields * owners)
-        first = ((row - rank * (fields * owners)) * PAIR + rank) * fields
-        for f in range(fields):
-            for h in range(halves):
-                rows[h, pl.ds(first + f, 1), :] = out[f, h, pl.ds(column, 1), :]
-
-    entry_loop(plan[0], body)
+    def body(entries):
+        found = []
+        for column, row in entries:
+            first = outbox_row(row, owners, fields)
+            for f in range(fields):
+                for h in range(halves):
+                    found.append((h, first + f, out[f, h, pl.ds(column, 1), :]))
+        for h, row, value in found:
+            rows[h, pl.ds(row, 1), :] = value
+
+    entry_groups(plan, body)
     outbox[:, :lanes] = rows[0].astype(BF16)
     outbox[:, lanes:] = rows[1, :, :tail].astype(BF16)
 
@@ -310,7 +359,7 @@
     late = late.transpose(0, 2, 3, 1).reshape(fields, columns_all, levels)
     early = early.transpose(0, 2, 3, 1).reshape(fields, columns_all, levels)
     coef = stencil_coef.transpose(0, 2, 1)
-    matrices = jacobian[0]
+    matrices = jacobian[0].transpose(0, 2, 1, 3)
     shape = jax.ShapeDtypeStruct
     per_owner = PAIR * fields
     inbox_rows = groups * per_owner
@@ -338,30 +387,22 @@
     )(cloudy_cols, cloudy_count, owner_rank, owner_slot, late)
     received = exchange(outbox, groups)
     chosen_shape = shape((inbox_rows, own_slots * fields), BF16)
-    placed_shape = shape((own_slots * fields, levels), BF16)
-    placed, chosen, answering = call(
-        place_first,
-        [placed_shape, chosen_shape, chosen_shape],
-        [VMEM],
+    answer_shape = shape((groups, (per_owner + 1) * LANES), F32)
+    spaces = [
+        VMEM((own_slots * fields, levels * fields), F32),
+        VMEM((own_slots * fields, 2 * LANES), F32),
+        VMEM(matrices.shape, BF16),
+        pltpu.SemaphoreType.DMA((own_slots,)),
+    ]
+    answer, chosen, answering = call(
+        physics_first,
+        [answer_shape, chosen_shape, chosen_shape],
+        [VMEM, HBM],
         [VMEM] * 3,
-        [VMEM(chosen_shape.shape, F32)],
-    )(received)
-
-    def apply(placed):
-        result = jnp.einsum(
-            "sfij,sfi->sfj",
-            matrices,
-            placed.reshape(own_slots, fields, levels),
-            preferred_element_type=F32,
-        ).reshape(own_slots * fields, levels)
-        (answer,) = call(
-            answer_kernel,
-            [shape((groups, (per_owner + 1) * LANES), F32)],
-            [VMEM] * 2,
-            [VMEM],
-            [VMEM((own_slots * fields, 2 * LANES), F32)],
-        )(result, answering)
-        return exchange(answer, groups)
+        spaces + [VMEM(chosen_shape.shape, F32)],
+        vmem=50,
+    )(received, matrices)
+    returned = exchange(answer, groups)
 
     edge_shapes = [shape((fields, 2, span, LANES), BF16) for span in (span_lat, span_lat, span_lon, span_lon)]
 
@@ -375,7 +416,7 @@
             aliases,
         )(plan, returned, base)
 
-    field, *edges = add(add_first, apply(placed), late, {})
+    field, *edges = add(add_first, returned, late, {})
     neighbours = halos(*edges)
     (inner,) = call(inner_first, [shape(halves, F32)], [VMEM] * 3, [VMEM], touched=6000000)(field, coef, early)
     adjoint, outbox = call(
@@ -387,8 +428,11 @@
         {1: 0},
     )(plan, inner, coef, *neighbours)
     received = exchange(outbox, groups)
-    (placed,) = call(place_second, [placed_shape], [VMEM] * 2, [VMEM])(received, chosen)
-    field, *edges = add(add_increments, apply(placed), adjoint, {2: 0})
+    (answer,) = call(physics_second, [answer_shape], [VMEM, HBM] + [VMEM] * 2, [VMEM], spaces, vmem=50)(
+        received, matrices, chosen, answering
+    )
+    returned = exchange(answer, groups)
+    field, *edges = add(add_increments, returned, adjoint, {2: 0})
     neighbours = halos(*edges)
     (inner,) = call(inner_last, [shape(halves, F32)], [VMEM] * 2, [VMEM], touched=6000000)(field, coef)
     (final,) = call(

time: 121 us -> 121 us (level)
  Pallas kernels: 10.7 us -> 18 us
  matrix products: 6 us -> 0 us
    pallas_call x4 -> x2, Pallas kernels: 1.08 us -> 9.17 us  [the longest x1 4.67 us: on_device(): call(physics_first, [answer_shape, chosen_shape, chosen_shape], [VMEM, HB...]
    dot_general x2 -> x0, matrix products: 6 us -> none  [apply(): jnp.einsum('sfij,sfi->sfj', matrices, placed.reshape(own_slots, fields, l...]
where the time goes in v3:
time: 121 us
  blocking collectives  61.3 us (51%)
  starting transfers between devices  39.1 us (32%)
  Pallas kernels  18 us (15%)
    all_to_all x4, blocking collectives, exchange(): lax.all_to_all(rows.reshape(groups, width, rows.shape[1]), 'gy', split_ax...  61.3 us
    ppermute x2, starting transfers between devices, halos(): from_after = lax.ppermute(lon_low, 'gx', down)  16.7 us
    ppermute x2, starting transfers between devices, halos(): from_high = lax.ppermute(lat_low, 'gy', south)  11.4 us
    ppermute x2, starting transfers between devices, halos(): from_low = lax.ppermute(lat_high, 'gy', north)  5.74 us
    ppermute x2, starting transfers between devices, halos(): from_before = lax.ppermute(lon_high, 'gx', up)  5.27 us
    pallas_call x1, Pallas kernels, on_device(): call(physics_first, [answer_shape, chosen_shape, chosen_shape], [VMEM, HB...  4.67 us
    pallas_call x1, Pallas kernels, on_device(): call(physics_second, [answer_shape], [VMEM, HBM] + [VMEM] * 2, [VMEM], sp...  4.5 us
  transfers between devices with their start and end apart: 8, of which 2 were waited for; matrix products, arithmetic and copies ran while one was open for 0% of the time, Pallas kernels for 2%

profile of v3, /device:TPU:2, one launch (start us, length us, event | category | flops | bytes accessed | tf_op | source)
XLA Modules:
  0.0 120.5 jit_solution(12823887297411079529)
XLA Ops:
  0.7 2.2 %shard_map.82 = (bf16[256,138]{1,0:T(8,128)(2,1)}, s32[97]{0:T(128)}) custom-call(s32[1,1,48]{2,1,0:T(1,128)} %cols_hbm.1, s32[1,1]{1,0:T(1,128)S(6)} %copy.21.count_hbm, s32[1,1,48]{2,1,0:T(1,128)} %owner_hbm.1, s32[1,1,48]{2,1,0:T(1,128)} %slot_hbm.1, bf16[4,512,137]{2,1,0:T(8,128)(2,1)} %bitcast.25), custom_call_target="tpu_custom_call" | custom-call | flops 1000 | bytes 1000000 | tf_op jit(solution)/shard_map/pallas_call | solution.py:370
  2.8 19.5 %all_to_all.20 = bf16[32,8,138]{2,1,0:T(8,128)(2,1)S(1)} all-to-all(bf16[32,8,138]{2,1,0:T(8,128)(2,1)} %bitcast.41), channel_id=1, replica_groups=mesh['gx'=16,'gy'=32] {'gy'}, dimensions={0} | all-to-all | bytes 141312 | tf_op jit(solution)/shard_map/all_to_all | solution.py:333
  22.3 4.7 %shard_map.83 = (f32[32,1152]{1,0:T(8,128)S(1)}, bf16[256,64]{1,0:T(8,128)(2,1)S(1)}, bf16[256,64]{1,0:T(8,128)(2,1)S(1)}) custom-call(bf16[256,138]{1,0:T(8,128)(2,1)S(1)} %bitcast.35, bf16[16,137,4,137]{3,2,1,0:T(4,128)(2,1)} %bitcast.39), custom_call_target="tpu_custom_call" | custom-call | flops 1000 | bytes 1000000 | tf_op jit(solution)/shard_map/pallas_call | solution.py:397
  27.0 0.2 copy.11
  27.2 14.3 %all_to_all.21 = f32[32,1,1152]{2,1,0:T(1,128)S(1)} all-to-all(f32[32,1,1152]{2,1,0:T(1,128)S(1)} %copy.11), channel_id=1, replica_groups=mesh['gx'=16,'gy'=32] {'gy'}, dimensions={0} | all-to-all | bytes 294912 | tf_op jit(solution)/shard_map/all_to_all | solution.py:333
  41.5 1.0 shard_map.84
  42.5 3.0 %collective-permute-start.2 = (bf16[4,2,32,128]{3,2,1,0:T(8,128)(2,1)S(1)}, bf16[4,2,32,128]{3,2,1,0:T(8,128)(2,1)S(1)}, u32[]{:S(2)}, u32[]{:S(2)}) collective-permute-start(bf16[4,2,32,128]{3,2,1,0:T(8,128)(2,1)S(1)} %get-tuple-element.28), channel_id=1, source_target_pairs={{0,1},{1,2},{2,3},{3,4},{4,5},{5,6},{6,7},{7,8},{8,9},{9,10},{10,1... | collective-permute-start | bytes 196616 | tf_op jit(solution)/shard_map/ppermute | solution.py:346
  45.5 5.6 %collective-permute-start.3 = (bf16[4,2,32,128]{3,2,1,0:T(8,128)(2,1)S(1)}, bf16[4,2,32,128]{3,2,1,0:T(8,128)(2,1)S(1)}, u32[]{:S(2)}, u32[]{:S(2)}) collective-permute-start(bf16[4,2,32,128]{3,2,1,0:T(8,128)(2,1)S(1)} %get-tuple-element.29), channel_id=1, source_target_pairs={{1,0},{2,1},{3,2},{4,3},{5,4},{6,5},{7,6},{8,7},{9,8},{10,9},{11,1... | collective-permute-start | bytes 196616 | tf_op jit(solution)/shard_map/ppermute | solution.py:347
  51.1 3.4 %collective-permute-start = (bf16[4,2,16,128]{3,2,1,0:T(8,128)(2,1)S(1)}, bf16[4,2,16,128]{3,2,1,0:T(8,128)(2,1)S(1)}, u32[]{:S(2)}, u32[]{:S(2)}) collective-permute-start(bf16[4,2,16,128]{3,2,1,0:T(8,128)(2,1)S(1)} %get-tuple-element.26), channel_id=1, source_target_pairs={{0,32},{32,64},{64,96},{96,128},{128,160},{160,192},{192,224},{224... | collective-permute-start | bytes 98312 | tf_op jit(solution)/shard_map/ppermute | solution.py:348
  54.5 10.1 %collective-permute-start.1 = (bf16[4,2,16,128]{3,2,1,0:T(8,128)(2,1)S(1)}, bf16[4,2,16,128]{3,2,1,0:T(8,128)(2,1)S(1)}, u32[]{:S(2)}, u32[]{:S(2)}) collective-permute-start(bf16[4,2,16,128]{3,2,1,0:T(8,128)(2,1)S(1)} %get-tuple-element.27), channel_id=1, source_target_pairs={{32,0},{64,32},{96,64},{128,96},{160,128},{192,160},{224,192},{256... | collective-permute-start | bytes 98312 | tf_op jit(solution)/shard_map/ppermute | solution.py:349
  64.6 1.2 %shard_map.85.inner = f32[4,2,512,128]{3,2,1,0:T(8,128)S(1)} custom-call(f32[4,2,512,128]{3,2,1,0:T(8,128)S(1)} %get-tuple-element.25.field, f32[4,16,32]{2,1,0:T(8,128)S(1)} %bitcast.31, bf16[4,512,137]{2,1,0:T(8,128)(2,1)S(1)} %bitcast.27), custom_call_target="tpu_custom_call" | custom-call | flops 1000 | bytes 6000000 | tf_op jit(solution)/shard_map/pallas_call | solution.py:421
  65.8 0.3 collective-permute-done.1.from_after
  66.1 1.0 shard_map.86
  67.1 13.5 %all_to_all.22 = bf16[32,8,137]{2,1,0:T(8,128)(2,1)S(1)} all-to-all(bf16[32,8,137]{2,1,0:T(8,128)(2,1)S(1)} %bitcast.38), channel_id=1, replica_groups=mesh['gx'=16,'gy'=32] {'gy'}, dimensions={0} | all-to-all | bytes 140288 | tf_op jit(solution)/shard_map/all_to_all | solution.py:333
  80.7 4.5 %shard_map.87 = f32[32,1152]{1,0:T(8,128)S(1)} custom-call(bf16[256,137]{1,0:T(8,128)(2,1)S(1)} %bitcast.36, bf16[16,137,4,137]{3,2,1,0:T(4,128)(2,1)} %bitcast.40, bf16[256,64]{1,0:T(8,128)(2,1)S(1)} %get-tuple-element.31.chosen, bf16[256,64]{1,0:T(8,128)(2,1)S(1)} %get-tuple-element.32.answering), custom_call_target="tpu_custom_call" | custom-call | flops 1000 | bytes 1000000 | tf_op jit(solution)/shard_map/pallas_call | solution.py:431
  85.3 14.0 %all_to_all.23 = f32[32,1,1152]{2,1,0:T(1,128)S(1)} all-to-all(f32[32,1,1152]{2,1,0:T(1,128)S(1)} %copy.12), channel_id=1, replica_groups=mesh['gx'=16,'gy'=32] {'gy'}, dimensions={0} | all-to-all | bytes 294912 | tf_op jit(solution)/shard_map/all_to_all | solution.py:333
  99.3 0.9 shard_map.88
  100.2 2.7 %collective-permute-start.6 = (bf16[4,2,32,128]{3,2,1,0:T(8,128)(2,1)S(1)}, bf16[4,2,32,128]{3,2,1,0:T(8,128)(2,1)S(1)}, u32[]{:S(2)}, u32[]{:S(2)}) collective-permute-start(bf16[4,2,32,128]{3,2,1,0:T(8,128)(2,1)S(1)} %get-tuple-element.37), channel_id=1, source_target_pairs={{0,1},{1,2},{2,3},{3,4},{4,5},{5,6},{6,7},{7,8},{8,9},{9,10},{10,1... | collective-permute-start | bytes 196616 | tf_op jit(solution)/shard_map/ppermute | solution.py:346
  103.0 5.8 %collective-permute-start.7 = (bf16[4,2,32,128]{3,2,1,0:T(8,128)(2,1)S(1)}, bf16[4,2,32,128]{3,2,1,0:T(8,128)(2,1)S(1)}, u32[]{:S(2)}, u32[]{:S(2)}) collective-permute-start(bf16[4,2,32,128]{3,2,1,0:T(8,128)(2,1)S(1)} %get-tuple-element.38), channel_id=1, source_target_pairs={{1,0},{2,1},{3,2},{4,3},{5,4},{6,5},{7,6},{8,7},{9,8},{10,9},{11,1... | collective-permute-start | bytes 196616 | tf_op jit(solution)/shard_map/ppermute | solution.py:347
  108.8 1.9 %collective-permute-start.4 = (bf16[4,2,16,128]{3,2,1,0:T(8,128)(2,1)S(1)}, bf16[4,2,16,128]{3,2,1,0:T(8,128)(2,1)S(1)}, u32[]{:S(2)}, u32[]{:S(2)}) collective-permute-start(bf16[4,2,16,128]{3,2,1,0:T(8,128)(2,1)S(1)} %get-tuple-element.35), channel_id=1, source_target_pairs={{0,32},{32,64},{64,96},{96,128},{128,160},{160,192},{192,224},{224... | collective-permute-start | bytes 98312 | tf_op jit(solution)/shard_map/ppermute | solution.py:348
  110.7 6.6 %collective-permute-start.5 = (bf16[4,2,16,128]{3,2,1,0:T(8,128)(2,1)S(1)}, bf16[4,2,16,128]{3,2,1,0:T(8,128)(2,1)S(1)}, u32[]{:S(2)}, u32[]{:S(2)}) collective-permute-start(bf16[4,2,16,128]{3,2,1,0:T(8,128)(2,1)S(1)} %get-tuple-element.36), channel_id=1, source_target_pairs={{32,0},{64,32},{96,64},{128,96},{160,128},{192,160},{224,192},{256... | collective-permute-start | bytes 98312 | tf_op jit(solution)/shard_map/ppermute | solution.py:349
  117.4 1.0 shard_map.89.inner
  118.4 0.5 collective-permute-done.5.from_after
  118.9 1.6 %shard_map.90 = f32[4,512,137]{2,1,0:T(8,128)} custom-call(f32[4,2,512,128]{3,2,1,0:T(8,128)S(1)} %shard_map.89.inner, f32[4,16,32]{2,1,0:T(8,128)S(1)} %bitcast.34, bf16[4,2,16,128]{3,2,1,0:T(8,128)(2,1)S(1)} %collective-permute-done.4.from_before, bf16[4,2,16,128]{3,2,1,0:T(8,128)(2,1)S(1)} %collective-permute-done.5.from_after, ...), custom_call_target="tpu_custom_call" | custom-call | flops 1000 | bytes 1000000 | tf_op jit(solution)/shard_map/pallas_call | solution.py:438
  (17 shorter events, 0.2 us)
Async XLA Ops:
  22.3 19.2 %copy-start = (bf16[4,137,32,16]{1,3,2,0:T(8,128)(2,1)S(1)}, bf16[4,137,32,16]{1,3,2,0:T(8,128)(2,1)}, u32[]{:S(2)}) copy-start(bf16[4,137,32,16]{1,3,2,0:T(8,128)(2,1)} %param.8) | copy-start | bytes 1683460
  22.3 19.2 %copy-start.3 = (s32[97]{0:T(128)S(1)}, s32[97]{0:T(128)}, u32[]{:S(2)}) copy-start(s32[97]{0:T(128)} %get-tuple-element.22.plan) | copy-start | bytes 1168
  27.0 37.6 %copy-start.1 = (bf16[4,137,32,16]{1,3,2,0:T(8,128)(2,1)S(1)}, bf16[4,137,32,16]{1,3,2,0:T(8,128)(2,1)}, u32[]{:S(2)}) copy-start(bf16[4,137,32,16]{1,3,2,0:T(8,128)(2,1)} %param.9) | copy-start | bytes 1683460
  27.0 37.6 %copy-start.2 = (f32[4,32,16]{1,2,0:T(8,128)S(1)}, f32[4,32,16]{1,2,0:T(8,128)}, u32[]{:S(2)}) copy-start(f32[4,32,16]{1,2,0:T(8,128)} %param.10) | copy-start | bytes 24580
  42.5 23.6 %collective-permute-start.2 = (bf16[4,2,32,128]{3,2,1,0:T(8,128)(2,1)S(1)}, bf16[4,2,32,128]{3,2,1,0:T(8,128)(2,1)S(1)}, u32[]{:S(2)}, u32[]{:S(2)}) collective-permute-start(bf16[4,2,32,128]{3,2,1,0:T(8,128)(2,1)S(1)} %get-tuple-element.28), channel_id=1, source_target_pairs={{0,1},{1,2},{2,3},{3,4},{4,5},{5,6},{6,7},{7,8},{8,9},{9,10},{10,1... | collective-permute-start | bytes 196616 | tf_op jit(solution)/shard_map/ppermute | solution.py:346
  45.5 20.6 %collective-permute-start.3 = (bf16[4,2,32,128]{3,2,1,0:T(8,128)(2,1)S(1)}, bf16[4,2,32,128]{3,2,1,0:T(8,128)(2,1)S(1)}, u32[]{:S(2)}, u32[]{:S(2)}) collective-permute-start(bf16[4,2,32,128]{3,2,1,0:T(8,128)(2,1)S(1)} %get-tuple-element.29), channel_id=1, source_target_pairs={{1,0},{2,1},{3,2},{4,3},{5,4},{6,5},{7,6},{8,7},{9,8},{10,9},{11,1... | collective-permute-start | bytes 196616 | tf_op jit(solution)/shard_map/ppermute | solution.py:347
  51.1 14.7 %collective-permute-start = (bf16[4,2,16,128]{3,2,1,0:T(8,128)(2,1)S(1)}, bf16[4,2,16,128]{3,2,1,0:T(8,128)(2,1)S(1)}, u32[]{:S(2)}, u32[]{:S(2)}) collective-permute-start(bf16[4,2,16,128]{3,2,1,0:T(8,128)(2,1)S(1)} %get-tuple-element.26), channel_id=1, source_target_pairs={{0,32},{32,64},{64,96},{96,128},{128,160},{160,192},{192,224},{224... | collective-permute-start | bytes 98312 | tf_op jit(solution)/shard_map/ppermute | solution.py:348
  54.5 11.6 %collective-permute-start.1 = (bf16[4,2,16,128]{3,2,1,0:T(8,128)(2,1)S(1)}, bf16[4,2,16,128]{3,2,1,0:T(8,128)(2,1)S(1)}, u32[]{:S(2)}, u32[]{:S(2)}) collective-permute-start(bf16[4,2,16,128]{3,2,1,0:T(8,128)(2,1)S(1)} %get-tuple-element.27), channel_id=1, source_target_pairs={{32,0},{64,32},{96,64},{128,96},{160,128},{192,160},{224,192},{256... | collective-permute-start | bytes 98312 | tf_op jit(solution)/shard_map/ppermute | solution.py:349
  100.2 18.7 %collective-permute-start.6 = (bf16[4,2,32,128]{3,2,1,0:T(8,128)(2,1)S(1)}, bf16[4,2,32,128]{3,2,1,0:T(8,128)(2,1)S(1)}, u32[]{:S(2)}, u32[]{:S(2)}) collective-permute-start(bf16[4,2,32,128]{3,2,1,0:T(8,128)(2,1)S(1)} %get-tuple-element.37), channel_id=1, source_target_pairs={{0,1},{1,2},{2,3},{3,4},{4,5},{5,6},{6,7},{7,8},{8,9},{9,10},{10,1... | collective-permute-start | bytes 196616 | tf_op jit(solution)/shard_map/ppermute | solution.py:346
  103.0 16.0 %collective-permute-start.7 = (bf16[4,2,32,128]{3,2,1,0:T(8,128)(2,1)S(1)}, bf16[4,2,32,128]{3,2,1,0:T(8,128)(2,1)S(1)}, u32[]{:S(2)}, u32[]{:S(2)}) collective-permute-start(bf16[4,2,32,128]{3,2,1,0:T(8,128)(2,1)S(1)} %get-tuple-element.38), channel_id=1, source_target_pairs={{1,0},{2,1},{3,2},{4,3},{5,4},{6,5},{7,6},{8,7},{9,8},{10,9},{11,1... | collective-permute-start | bytes 196616 | tf_op jit(solution)/shard_map/ppermute | solution.py:347
  108.8 9.6 %collective-permute-start.4 = (bf16[4,2,16,128]{3,2,1,0:T(8,128)(2,1)S(1)}, bf16[4,2,16,128]{3,2,1,0:T(8,128)(2,1)S(1)}, u32[]{:S(2)}, u32[]{:S(2)}) collective-permute-start(bf16[4,2,16,128]{3,2,1,0:T(8,128)(2,1)S(1)} %get-tuple-element.35), channel_id=1, source_target_pairs={{0,32},{32,64},{64,96},{96,128},{128,160},{160,192},{192,224},{224... | collective-permute-start | bytes 98312 | tf_op jit(solution)/shard_map/ppermute | solution.py:348
  110.7 8.2 %collective-permute-start.5 = (bf16[4,2,16,128]{3,2,1,0:T(8,128)(2,1)S(1)}, bf16[4,2,16,128]{3,2,1,0:T(8,128)(2,1)S(1)}, u32[]{:S(2)}, u32[]{:S(2)}) collective-permute-start(bf16[4,2,16,128]{3,2,1,0:T(8,128)(2,1)S(1)} %get-tuple-element.36), channel_id=1, source_target_pairs={{32,0},{64,32},{96,64},{128,96},{160,128},{192,160},{224,192},{256... | collective-permute-start | bytes 98312 | tf_op jit(solution)/shard_map/ppermute | solution.py:349

commit v4 on v3

--- a/solution.py
+++ b/solution.py
@@ -15,6 +15,7 @@
 PAIR = 2
 LANES = 128
 GROUP = 4
+AHEAD = 4
 
 
 def call(kernel, out_shape, in_spaces, out_spaces, scratch=(), aliases=None, flops=1000, touched=1000000, vmem=40):
@@ -128,7 +129,7 @@
     copies = [
         pltpu.make_async_copy(matrices_hbm.at[s], matrices.at[s], sems.at[s]) for s in range(matrices.shape[0])
     ]
-    for copy in copies:
+    for copy in copies[:AHEAD]:
         copy.start()
     return copies
 
@@ -145,7 +146,10 @@
     result[...] = jnp.zeros(result.shape, F32)
     for s in range(own_slots):
         at = slice(s * fields, (s + 1) * fields)
-        copies[s].wait()
+        if copies:
+            copies[s].wait()
+            if s + AHEAD < own_slots:
+                copies[s + AHEAD].start()
         result[at, :levels] = jnp.dot(
             spread[at].astype(BF16), matrices[s].reshape(depth, levels), preferred_element_type=F32
         )
@@ -180,9 +184,8 @@
     products(chosen, values[:, :levels].astype(BF16), answering, matrices, copies, answer, spread, result)
 
 
-def physics_second(received, matrices_hbm, chosen, answering, answer, spread, result, matrices, sems):
-    copies = fetch(matrices_hbm, matrices, sems)
-    products(chosen[...], received[...], answering[...], matrices, copies, answer, spread, result)
+def physics_second(received, matrices, chosen, answering, answer, spread, result):
+    products(chosen[...], received[...], answering[...], matrices, [], answer, spread, result)
 
 
 def add_first(plan, returned, late, field, *rest, levels):
@@ -391,15 +394,18 @@
     spaces = [
         VMEM((own_slots * fields, levels * fields), F32),
         VMEM((own_slots * fields, 2 * LANES), F32),
-        VMEM(matrices.shape, BF16),
-        pltpu.SemaphoreType.DMA((own_slots,)),
     ]
     answer, chosen, answering = call(
         physics_first,
         [answer_shape, chosen_shape, chosen_shape],
         [VMEM, HBM],
         [VMEM] * 3,
-        spaces + [VMEM(chosen_shape.shape, F32)],
+        spaces
+        + [
+            VMEM(matrices.shape, BF16),
+            pltpu.SemaphoreType.DMA((own_slots,)),
+            VMEM(chosen_shape.shape, F32),
+        ],
         vmem=50,
     )(received, matrices)
     returned = exchange(answer, groups)
@@ -428,7 +434,7 @@
         {1: 0},
     )(plan, inner, coef, *neighbours)
     received = exchange(outbox, groups)
-    (answer,) = call(physics_second, [answer_shape], [VMEM, HBM] + [VMEM] * 2, [VMEM], spaces, vmem=50)(
+    (answer,) = call(physics_second, [answer_shape], [VMEM] * 4, [VMEM], spaces)(
         received, matrices, chosen, answering
     )
     returned = exchange(answer, groups)

time: 121 us -> 119 us (0.983)
  Pallas kernels: 18 us -> 16 us
    pallas_call x1, Pallas kernels: 4.5 us -> 1.35 us  [on_device(): call(physics_second, [answer_shape], [VMEM] * 4, [VMEM], spaces)]
where the time goes in v4:
time: 119 us; the launch traced here: 118 us
  blocking collectives  61.3 us (52%)
  starting transfers between devices  38.8 us (33%)
  Pallas kernels  16 us (13%)
    all_to_all x4, blocking collectives, exchange(): lax.all_to_all(rows.reshape(groups, width, rows.shape[1]), 'gy', split_ax...  61.3 us
    ppermute x2, starting transfers between devices, halos(): from_after = lax.ppermute(lon_low, 'gx', down)  16.8 us
    ppermute x2, starting transfers between devices, halos(): from_high = lax.ppermute(lat_low, 'gy', south)  11.7 us
    ppermute x2, starting transfers between devices, halos(): from_low = lax.ppermute(lat_high, 'gy', north)  5.58 us
    pallas_call x1, Pallas kernels, on_device(): call(physics_first, [answer_shape, chosen_shape, chosen_shape], [VMEM, HB...  5.43 us
    ppermute x2, starting transfers between devices, halos(): from_before = lax.ppermute(lon_high, 'gx', up)  4.76 us
  transfers between devices with their start and end apart: 8, of which 2 were waited for; matrix products, arithmetic and copies ran while one was open for 0% of the time, Pallas kernels for 2%

profile of v4, /device:TPU:2, one launch (start us, length us, event | category | flops | bytes accessed | tf_op | source)
XLA Modules:
  0.0 118.3 jit_solution(17595585826115487621)
XLA Ops:
  0.7 2.3 %shard_map.82 = (bf16[256,138]{1,0:T(8,128)(2,1)}, s32[97]{0:T(128)}) custom-call(s32[1,1,48]{2,1,0:T(1,128)} %cols_hbm.1, s32[1,1]{1,0:T(1,128)S(6)} %copy.21.count_hbm, s32[1,1,48]{2,1,0:T(1,128)} %owner_hbm.1, s32[1,1,48]{2,1,0:T(1,128)} %slot_hbm.1, bf16[4,512,137]{2,1,0:T(8,128)(2,1)} %bitcast.29), custom_call_target="tpu_custom_call" | custom-call | flops 1000 | bytes 1000000 | tf_op jit(solution)/shard_map/pallas_call | solution.py:373
  2.9 19.5 %all_to_all.20 = bf16[32,8,138]{2,1,0:T(8,128)(2,1)S(1)} all-to-all(bf16[32,8,138]{2,1,0:T(8,128)(2,1)} %bitcast.43), channel_id=1, replica_groups=mesh['gx'=16,'gy'=32] {'gy'}, dimensions={0} | all-to-all | bytes 141312 | tf_op jit(solution)/shard_map/all_to_all | solution.py:336
  22.4 5.4 %shard_map.83 = (f32[32,1152]{1,0:T(8,128)S(1)}, bf16[256,64]{1,0:T(8,128)(2,1)S(1)}, bf16[256,64]{1,0:T(8,128)(2,1)S(1)}) custom-call(bf16[256,138]{1,0:T(8,128)(2,1)S(1)} %bitcast.39, bf16[16,137,4,137]{3,2,1,0:T(4,128)(2,1)} %bitcast.25), custom_call_target="tpu_custom_call" | custom-call | flops 1000 | bytes 1000000 | tf_op jit(solution)/shard_map/pallas_call | solution.py:398
  27.8 0.2 copy.11
  28.0 14.2 %all_to_all.21 = f32[32,1,1152]{2,1,0:T(1,128)S(1)} all-to-all(f32[32,1,1152]{2,1,0:T(1,128)S(1)} %copy.11), channel_id=1, replica_groups=mesh['gx'=16,'gy'=32] {'gy'}, dimensions={0} | all-to-all | bytes 294912 | tf_op jit(solution)/shard_map/all_to_all | solution.py:336
  42.3 1.1 shard_map.84
  43.4 3.0 %collective-permute-start.2 = (bf16[4,2,32,128]{3,2,1,0:T(8,128)(2,1)S(1)}, bf16[4,2,32,128]{3,2,1,0:T(8,128)(2,1)S(1)}, u32[]{:S(2)}, u32[]{:S(2)}) collective-permute-start(bf16[4,2,32,128]{3,2,1,0:T(8,128)(2,1)S(1)} %get-tuple-element.28), channel_id=1, source_target_pairs={{0,1},{1,2},{2,3},{3,4},{4,5},{5,6},{6,7},{7,8},{8,9},{9,10},{10,1... | collective-permute-start | bytes 196616 | tf_op jit(solution)/shard_map/ppermute | solution.py:349
  46.4 5.7 %collective-permute-start.3 = (bf16[4,2,32,128]{3,2,1,0:T(8,128)(2,1)S(1)}, bf16[4,2,32,128]{3,2,1,0:T(8,128)(2,1)S(1)}, u32[]{:S(2)}, u32[]{:S(2)}) collective-permute-start(bf16[4,2,32,128]{3,2,1,0:T(8,128)(2,1)S(1)} %get-tuple-element.29), channel_id=1, source_target_pairs={{1,0},{2,1},{3,2},{4,3},{5,4},{6,5},{7,6},{8,7},{9,8},{10,9},{11,1... | collective-permute-start | bytes 196616 | tf_op jit(solution)/shard_map/ppermute | solution.py:350
  52.1 2.8 %collective-permute-start = (bf16[4,2,16,128]{3,2,1,0:T(8,128)(2,1)S(1)}, bf16[4,2,16,128]{3,2,1,0:T(8,128)(2,1)S(1)}, u32[]{:S(2)}, u32[]{:S(2)}) collective-permute-start(bf16[4,2,16,128]{3,2,1,0:T(8,128)(2,1)S(1)} %get-tuple-element.26), channel_id=1, source_target_pairs={{0,32},{32,64},{64,96},{96,128},{128,160},{160,192},{192,224},{224... | collective-permute-start | bytes 98312 | tf_op jit(solution)/shard_map/ppermute | solution.py:351
  55.0 10.4 %collective-permute-start.1 = (bf16[4,2,16,128]{3,2,1,0:T(8,128)(2,1)S(1)}, bf16[4,2,16,128]{3,2,1,0:T(8,128)(2,1)S(1)}, u32[]{:S(2)}, u32[]{:S(2)}) collective-permute-start(bf16[4,2,16,128]{3,2,1,0:T(8,128)(2,1)S(1)} %get-tuple-element.27), channel_id=1, source_target_pairs={{32,0},{64,32},{96,64},{128,96},{160,128},{192,160},{224,192},{256... | collective-permute-start | bytes 98312 | tf_op jit(solution)/shard_map/ppermute | solution.py:352
  65.4 1.2 %shard_map.85.inner = f32[4,2,512,128]{3,2,1,0:T(8,128)S(1)} custom-call(f32[4,2,512,128]{3,2,1,0:T(8,128)S(1)} %get-tuple-element.25.field, f32[4,16,32]{2,1,0:T(8,128)S(1)} %bitcast.35, bf16[4,512,137]{2,1,0:T(8,128)(2,1)S(1)} %bitcast.31), custom_call_target="tpu_custom_call" | custom-call | flops 1000 | bytes 6000000 | tf_op jit(solution)/shard_map/pallas_call | solution.py:427
  66.6 0.3 collective-permute-done.1.from_after
  66.9 1.1 shard_map.86
  68.0 13.6 %all_to_all.22 = bf16[32,8,137]{2,1,0:T(8,128)(2,1)S(1)} all-to-all(bf16[32,8,137]{2,1,0:T(8,128)(2,1)S(1)} %bitcast.42), channel_id=1, replica_groups=mesh['gx'=16,'gy'=32] {'gy'}, dimensions={0} | all-to-all | bytes 140288 | tf_op jit(solution)/shard_map/all_to_all | solution.py:336
  81.6 1.4 %shard_map.87 = f32[32,1152]{1,0:T(8,128)S(1)} custom-call(bf16[256,137]{1,0:T(8,128)(2,1)S(1)} %bitcast.40, bf16[16,137,4,137]{3,2,1,0:T(4,128)(2,1)S(1)} %bitcast.28, bf16[256,64]{1,0:T(8,128)(2,1)S(1)} %get-tuple-element.31.chosen, bf16[256,64]{1,0:T(8,128)(2,1)S(1)} %get-tuple-element.32.answering), custom_call_target="tpu_custom_call" | custom-call | flops 1000 | bytes 1000000 | tf_op jit(solution)/shard_map/pallas_call | solution.py:437
  83.2 14.0 %all_to_all.23 = f32[32,1,1152]{2,1,0:T(1,128)S(1)} all-to-all(f32[32,1,1152]{2,1,0:T(1,128)S(1)} %copy.12), channel_id=1, replica_groups=mesh['gx'=16,'gy'=32] {'gy'}, dimensions={0} | all-to-all | bytes 294912 | tf_op jit(solution)/shard_map/all_to_all | solution.py:336
  97.2 1.0 shard_map.88
  98.2 2.6 %collective-permute-start.6 = (bf16[4,2,32,128]{3,2,1,0:T(8,128)(2,1)S(1)}, bf16[4,2,32,128]{3,2,1,0:T(8,128)(2,1)S(1)}, u32[]{:S(2)}, u32[]{:S(2)}) collective-permute-start(bf16[4,2,32,128]{3,2,1,0:T(8,128)(2,1)S(1)} %get-tuple-element.37), channel_id=1, source_target_pairs={{0,1},{1,2},{2,3},{3,4},{4,5},{5,6},{6,7},{7,8},{8,9},{9,10},{10,1... | collective-permute-start | bytes 196616 | tf_op jit(solution)/shard_map/ppermute | solution.py:349
  100.8 6.0 %collective-permute-start.7 = (bf16[4,2,32,128]{3,2,1,0:T(8,128)(2,1)S(1)}, bf16[4,2,32,128]{3,2,1,0:T(8,128)(2,1)S(1)}, u32[]{:S(2)}, u32[]{:S(2)}) collective-permute-start(bf16[4,2,32,128]{3,2,1,0:T(8,128)(2,1)S(1)} %get-tuple-element.38), channel_id=1, source_target_pairs={{1,0},{2,1},{3,2},{4,3},{5,4},{6,5},{7,6},{8,7},{9,8},{10,9},{11,1... | collective-permute-start | bytes 196616 | tf_op jit(solution)/shard_map/ppermute | solution.py:350
  106.7 1.9 %collective-permute-start.4 = (bf16[4,2,16,128]{3,2,1,0:T(8,128)(2,1)S(1)}, bf16[4,2,16,128]{3,2,1,0:T(8,128)(2,1)S(1)}, u32[]{:S(2)}, u32[]{:S(2)}) collective-permute-start(bf16[4,2,16,128]{3,2,1,0:T(8,128)(2,1)S(1)} %get-tuple-element.35), channel_id=1, source_target_pairs={{0,32},{32,64},{64,96},{96,128},{128,160},{160,192},{192,224},{224... | collective-permute-start | bytes 98312 | tf_op jit(solution)/shard_map/ppermute | solution.py:351
  108.7 6.4 %collective-permute-start.5 = (bf16[4,2,16,128]{3,2,1,0:T(8,128)(2,1)S(1)}, bf16[4,2,16,128]{3,2,1,0:T(8,128)(2,1)S(1)}, u32[]{:S(2)}, u32[]{:S(2)}) collective-permute-start(bf16[4,2,16,128]{3,2,1,0:T(8,128)(2,1)S(1)} %get-tuple-element.36), channel_id=1, source_target_pairs={{32,0},{64,32},{96,64},{128,96},{160,128},{192,160},{224,192},{256... | collective-permute-start | bytes 98312 | tf_op jit(solution)/shard_map/ppermute | solution.py:352
  115.1 1.0 shard_map.89.inner
  116.2 0.5 collective-permute-done.5.from_after
  116.7 1.6 %shard_map.90 = f32[4,512,137]{2,1,0:T(8,128)} custom-call(f32[4,2,512,128]{3,2,1,0:T(8,128)S(1)} %shard_map.89.inner, f32[4,16,32]{2,1,0:T(8,128)S(1)} %bitcast.38, bf16[4,2,16,128]{3,2,1,0:T(8,128)(2,1)S(1)} %collective-permute-done.4.from_before, bf16[4,2,16,128]{3,2,1,0:T(8,128)(2,1)S(1)} %collective-permute-done.5.from_after, ...), custom_call_target="tpu_custom_call" | custom-call | flops 1000 | bytes 1000000 | tf_op jit(solution)/shard_map/pallas_call | solution.py:444
  (22 shorter events, 0.2 us)
Async XLA Ops:
  22.4 19.9 %copy-start = (bf16[4,137,32,16]{1,3,2,0:T(8,128)(2,1)S(1)}, bf16[4,137,32,16]{1,3,2,0:T(8,128)(2,1)}, u32[]{:S(2)}) copy-start(bf16[4,137,32,16]{1,3,2,0:T(8,128)(2,1)} %param.8) | copy-start | bytes 1683460
  22.4 19.9 %copy-start.3 = (s32[97]{0:T(128)S(1)}, s32[97]{0:T(128)}, u32[]{:S(2)}) copy-start(s32[97]{0:T(128)} %get-tuple-element.22.plan) | copy-start | bytes 1168
  27.8 37.6 %copy-start.1 = (bf16[4,137,32,16]{1,3,2,0:T(8,128)(2,1)S(1)}, bf16[4,137,32,16]{1,3,2,0:T(8,128)(2,1)}, u32[]{:S(2)}) copy-start(bf16[4,137,32,16]{1,3,2,0:T(8,128)(2,1)} %param.9) | copy-start | bytes 1683460
  27.8 37.6 %copy-start.2 = (f32[4,32,16]{1,2,0:T(8,128)S(1)}, f32[4,32,16]{1,2,0:T(8,128)}, u32[]{:S(2)}) copy-start(f32[4,32,16]{1,2,0:T(8,128)} %param.10) | copy-start | bytes 24580
  42.3 39.4 %slice-start = ((s8[4489216]{0:T(1024)(128)(4,1)}), s8[4194304]{0:T(1024)(128)(4,1)S(1)}, s32[]{:S(2)}) async-start(s8[4489216]{0:T(1024)(128)(4,1)} %bitcast.26), calls=%async_computation.4 | async-start | bytes 8388608
  43.4 23.6 %collective-permute-start.2 = (bf16[4,2,32,128]{3,2,1,0:T(8,128)(2,1)S(1)}, bf16[4,2,32,128]{3,2,1,0:T(8,128)(2,1)S(1)}, u32[]{:S(2)}, u32[]{:S(2)}) collective-permute-start(bf16[4,2,32,128]{3,2,1,0:T(8,128)(2,1)S(1)} %get-tuple-element.28), channel_id=1, source_target_pairs={{0,1},{1,2},{2,3},{3,4},{4,5},{5,6},{6,7},{7,8},{8,9},{9,10},{10,1... | collective-permute-start | bytes 196616 | tf_op jit(solution)/shard_map/ppermute | solution.py:349
  46.4 20.6 %collective-permute-start.3 = (bf16[4,2,32,128]{3,2,1,0:T(8,128)(2,1)S(1)}, bf16[4,2,32,128]{3,2,1,0:T(8,128)(2,1)S(1)}, u32[]{:S(2)}, u32[]{:S(2)}) collective-permute-start(bf16[4,2,32,128]{3,2,1,0:T(8,128)(2,1)S(1)} %get-tuple-element.29), channel_id=1, source_target_pairs={{1,0},{2,1},{3,2},{4,3},{5,4},{6,5},{7,6},{8,7},{9,8},{10,9},{11,1... | collective-permute-start | bytes 196616 | tf_op jit(solution)/shard_map/ppermute | solution.py:350
  52.1 14.5 %collective-permute-start = (bf16[4,2,16,128]{3,2,1,0:T(8,128)(2,1)S(1)}, bf16[4,2,16,128]{3,2,1,0:T(8,128)(2,1)S(1)}, u32[]{:S(2)}, u32[]{:S(2)}) collective-permute-start(bf16[4,2,16,128]{3,2,1,0:T(8,128)(2,1)S(1)} %get-tuple-element.26), channel_id=1, source_target_pairs={{0,32},{32,64},{64,96},{96,128},{128,160},{160,192},{192,224},{224... | collective-permute-start | bytes 98312 | tf_op jit(solution)/shard_map/ppermute | solution.py:351
  55.0 12.0 %collective-permute-start.1 = (bf16[4,2,16,128]{3,2,1,0:T(8,128)(2,1)S(1)}, bf16[4,2,16,128]{3,2,1,0:T(8,128)(2,1)S(1)}, u32[]{:S(2)}, u32[]{:S(2)}) collective-permute-start(bf16[4,2,16,128]{3,2,1,0:T(8,128)(2,1)S(1)} %get-tuple-element.27), channel_id=1, source_target_pairs={{32,0},{64,32},{96,64},{128,96},{160,128},{192,160},{224,192},{256... | collective-permute-start | bytes 98312 | tf_op jit(solution)/shard_map/ppermute | solution.py:352
  65.4 16.3 %slice-start.1 = ((s8[4489216]{0:T(1024)(128)(4,1)}), s8[294912]{0:T(1024)(128)(4,1)S(1)}, s32[]{:S(2)}) async-start(s8[4489216]{0:T(1024)(128)(4,1)} %bitcast.26), calls=%async_computation.5 | async-start | bytes 589824
  98.2 18.5 %collective-permute-start.6 = (bf16[4,2,32,128]{3,2,1,0:T(8,128)(2,1)S(1)}, bf16[4,2,32,128]{3,2,1,0:T(8,128)(2,1)S(1)}, u32[]{:S(2)}, u32[]{:S(2)}) collective-permute-start(bf16[4,2,32,128]{3,2,1,0:T(8,128)(2,1)S(1)} %get-tuple-element.37), channel_id=1, source_target_pairs={{0,1},{1,2},{2,3},{3,4},{4,5},{5,6},{6,7},{7,8},{8,9},{9,10},{10,1... | collective-permute-start | bytes 196616 | tf_op jit(solution)/shard_map/ppermute | solution.py:349
  100.8 15.9 %collective-permute-start.7 = (bf16[4,2,32,128]{3,2,1,0:T(8,128)(2,1)S(1)}, bf16[4,2,32,128]{3,2,1,0:T(8,128)(2,1)S(1)}, u32[]{:S(2)}, u32[]{:S(2)}) collective-permute-start(bf16[4,2,32,128]{3,2,1,0:T(8,128)(2,1)S(1)} %get-tuple-element.38), channel_id=1, source_target_pairs={{1,0},{2,1},{3,2},{4,3},{5,4},{6,5},{7,6},{8,7},{9,8},{10,9},{11,1... | collective-permute-start | bytes 196616 | tf_op jit(solution)/shard_map/ppermute | solution.py:350
  106.7 9.4 %collective-permute-start.4 = (bf16[4,2,16,128]{3,2,1,0:T(8,128)(2,1)S(1)}, bf16[4,2,16,128]{3,2,1,0:T(8,128)(2,1)S(1)}, u32[]{:S(2)}, u32[]{:S(2)}) collective-permute-start(bf16[4,2,16,128]{3,2,1,0:T(8,128)(2,1)S(1)} %get-tuple-element.35), channel_id=1, source_target_pairs={{0,32},{32,64},{64,96},{96,128},{128,160},{160,192},{192,224},{224... | collective-permute-start | bytes 98312 | tf_op jit(solution)/shard_map/ppermute | solution.py:351
  108.7 8.0 %collective-permute-start.5 = (bf16[4,2,16,128]{3,2,1,0:T(8,128)(2,1)S(1)}, bf16[4,2,16,128]{3,2,1,0:T(8,128)(2,1)S(1)}, u32[]{:S(2)}, u32[]{:S(2)}) collective-permute-start(bf16[4,2,16,128]{3,2,1,0:T(8,128)(2,1)S(1)} %get-tuple-element.36), channel_id=1, source_target_pairs={{32,0},{64,32},{96,64},{128,96},{160,128},{192,160},{224,192},{256... | collective-permute-start | bytes 98312 | tf_op jit(solution)/shard_map/ppermute | solution.py:352

commit v5 on v4

--- a/solution.py
+++ b/solution.py
@@ -15,7 +15,6 @@
 PAIR = 2
 LANES = 128
 GROUP = 4
-AHEAD = 4
 
 
 def call(kernel, out_shape, in_spaces, out_spaces, scratch=(), aliases=None, flops=1000, touched=1000000, vmem=40):
@@ -125,16 +124,7 @@
     return dot(chosen, high) + dot(chosen, middle) + dot(chosen, low)
 
 
-def fetch(matrices_hbm, matrices, sems):
-    copies = [
-        pltpu.make_async_copy(matrices_hbm.at[s], matrices.at[s], sems.at[s]) for s in range(matrices.shape[0])
-    ]
-    for copy in copies[:AHEAD]:
-        copy.start()
-    return copies
-
-
-def products(chosen, values, answering, matrices, copies, answer, spread, result):
+def products(chosen, values, answering, matrices, answer, spread, result):
     own_slots, levels, fields, _ = matrices.shape
     depth = levels * fields
     placed = lax.dot_general(chosen, values, (((0,), (0,)), ((), ())), preferred_element_type=F32).astype(BF16)
@@ -146,10 +136,6 @@
     result[...] = jnp.zeros(result.shape, F32)
     for s in range(own_slots):
         at = slice(s * fields, (s + 1) * fields)
-        if copies:
-            copies[s].wait()
-            if s + AHEAD < own_slots:
-                copies[s + AHEAD].start()
         result[at, :levels] = jnp.dot(
             spread[at].astype(BF16), matrices[s].reshape(depth, levels), preferred_element_type=F32
         )
@@ -166,8 +152,7 @@
     answer[:, per_owner * LANES :] = tails
 
 
-def physics_first(received, matrices_hbm, answer, chosen_out, answering_out, spread, result, matrices, sems, choice):
-    copies = fetch(matrices_hbm, matrices, sems)
+def physics_first(received, matrices, answer, chosen_out, answering_out, spread, result, choice):
     levels = matrices.shape[1]
     owners = answer.shape[0]
     per_owner = received.shape[0] // owners
@@ -181,20 +166,19 @@
     ).astype(BF16)
     chosen_out[...] = chosen
     answering_out[...] = answering
-    products(chosen, values[:, :levels].astype(BF16), answering, matrices, copies, answer, spread, result)
+    products(chosen, values[:, :levels].astype(BF16), answering, matrices, answer, spread, result)
 
 
 def physics_second(received, matrices, chosen, answering, answer, spread, result):
-    products(chosen[...], received[...], answering[...], matrices, [], answer, spread, result)
-
-
-def add_first(plan, returned, late, field, *rest, levels):
+    products(chosen[...], received[...], answering[...], matrices, answer, spread, result)
+
+
+def widen(late, field):
     for f in range(field.shape[0]):
         unpack_field(late, field, f)
-    add_increments(plan, returned, field, field, *rest, levels=levels)
-
-
-def add_increments(plan, returned, base, field, lon_low, lon_high, lat_low, lat_high, inbox, *, levels):
+
+
+def add_increments(plan, returned, base, field, lon_even, lon_odd, lat_even, lat_odd, inbox, *, levels):
     fields, halves, columns_all, lanes = field.shape
     owners = returned.shape[0]
     per_owner = inbox.shape[1] // owners
@@ -215,14 +199,23 @@
             field[here] = value
 
     entry_groups(plan, body)
-    span_lat = lon_low.shape[2]
-    span_lon = lat_low.shape[2]
+    span_lat = lon_even.shape[2]
+    span_lon = lat_even.shape[2]
+    lon_up, lat_up = upward()
     for f in range(fields):
         for h in range(halves):
-            lon_low[f, h] = field[f, h, :span_lat].astype(BF16)
-            lon_high[f, h] = field[f, h, columns_all - span_lat :].astype(BF16)
-            lat_low[f, h] = field[f, h, pl.ds(0, span_lon, stride=span_lat), :].astype(BF16)
-            lat_high[f, h] = field[f, h, pl.ds(span_lat - 1, span_lon, stride=span_lat), :].astype(BF16)
+            low = field[f, h, :span_lat].astype(BF16)
+            high = field[f, h, columns_all - span_lat :].astype(BF16)
+            lon_even[f, h] = jnp.where(lon_up, high, low)
+            lon_odd[f, h] = jnp.where(lon_up, low, high)
+            low = field[f, h, pl.ds(0, span_lon, stride=span_lat), :].astype(BF16)
+            high = field[f, h, pl.ds(span_lat - 1, span_lon, stride=span_lat), :].astype(BF16)
+            lat_even[f, h] = jnp.where(lat_up, high, low)
+            lat_odd[f, h] = jnp.where(lat_up, low, high)
+
+
+def upward():
+    return lax.axis_index("gx") % 2 == 0, lax.axis_index("gy") % 2 == 0
 
 
 def inner_stencil(field, coef, extra, out):
@@ -277,19 +270,27 @@
     )
 
 
-def add_edges(f, h, weights, from_before, from_after, from_low, from_high, out):
+def add_edges(f, h, weights, lon_even, lon_odd, lat_even, lat_odd, out):
     columns_all = out.shape[2]
-    span_lat = from_before.shape[2]
-    span_lon = from_low.shape[2]
-    first = (f, h, slice(0, span_lat))
-    last = (f, h, slice(columns_all - span_lat, columns_all))
-    low = (f, h, pl.ds(0, span_lon, stride=span_lat), slice(None))
-    high = (f, h, pl.ds(span_lat - 1, span_lon, stride=span_lat), slice(None))
-    for at, weight, edge in zip((first, last, low, high), weights, (from_before, from_after, from_low, from_high)):
-        out[at] = out[at] + weight * edge[f, h].astype(F32)
-
-
-def edges_first(plan, inner, coef, from_before, from_after, from_low, from_high, out, outbox, rows):
+    span_lat = lon_even.shape[2]
+    span_lon = lat_even.shape[2]
+    places = (
+        (slice(0, span_lat), slice(None)),
+        (slice(columns_all - span_lat, columns_all), slice(None)),
+        (pl.ds(0, span_lon, stride=span_lat), slice(None)),
+        (pl.ds(span_lat - 1, span_lon, stride=span_lat), slice(None)),
+    )
+    lon_up, lat_up = upward()
+    edges = []
+    for up, even, odd in ((lon_up, lon_even, lon_odd), (lat_up, lat_even, lat_odd)):
+        first, second = even[f, h].astype(F32), odd[f, h].astype(F32)
+        edges += [jnp.where(up, second, first), jnp.where(up, first, second)]
+    for place, weight, edge in zip(places, weights, edges):
+        at = (f, h) + place
+        out[at] = out[at] + weight * edge
+
+
+def edges_first(plan, inner, coef, lon_even, lon_odd, lat_even, lat_odd, out, outbox, rows):
     fields, halves, columns_all, lanes = out.shape
     owners = rows.shape[1] // (PAIR * fields)
     tail = outbox.shape[1] - lanes
@@ -297,7 +298,7 @@
     rows[...] = jnp.zeros(rows.shape, F32)
     for f in range(fields):
         for h in range(halves):
-            add_edges(f, h, weights, from_before, from_after, from_low, from_high, out)
+            add_edges(f, h, weights, lon_even, lon_odd, lat_even, lat_odd, out)
 
     def body(entries):
         found = []
@@ -314,7 +315,7 @@
     outbox[:, lanes:] = rows[1, :, :tail].astype(BF16)
 
 
-def edges_last(inner, coef, from_before, from_after, from_low, from_high, out_hbm, both, out, sems):
+def edges_last(inner, coef, lon_even, lon_odd, lat_even, lat_odd, out_hbm, both, out, sems):
     fields, halves, columns_all, lanes = inner.shape
     tail = out.shape[2] - lanes
     weights = edge_weights(coef)
@@ -322,7 +323,7 @@
     for f in range(fields):
         for h in range(halves):
             both[f, h] = inner[f, h]
-            add_edges(f, h, weights, from_before, from_after, from_low, from_high, both)
+            add_edges(f, h, weights, lon_even, lon_odd, lat_even, lat_odd, both)
         out[f, :, :lanes] = both[f, 0]
         out[f, :, lanes:] = both[f, 1, :, :tail]
         copies.append(pltpu.make_async_copy(out.at[f], out_hbm.at[f], sems.at[f]))
@@ -339,18 +340,21 @@
     return moved.reshape(rows.shape)
 
 
-def halos(lon_low, lon_high, lat_low, lat_high):
-    lon = lax.axis_size("gx")
-    lat = lax.axis_size("gy")
-    up = [(i, (i + 1) % lon) for i in range(lon)]
-    down = [(target, source) for source, target in up]
-    north = [(i, i + 1) for i in range(lat - 1)]
-    south = [(target, source) for source, target in north]
-    from_low = lax.ppermute(lat_high, "gy", north)
-    from_high = lax.ppermute(lat_low, "gy", south)
-    from_before = lax.ppermute(lon_high, "gx", up)
-    from_after = lax.ppermute(lon_low, "gx", down)
-    return from_before, from_after, from_low, from_high
+def swap(edge, axis, start, periodic):
+    count = lax.axis_size(axis)
+    pairs = [(i, i + 1) for i in range(start, count - 1, 2)]
+    if start and periodic:
+        pairs.append((count - 1, 0))
+    return lax.ppermute(edge, axis, pairs + [(high, low) for low, high in pairs])
+
+
+def halos(lon_even, lon_odd, lat_even, lat_odd):
+    return (
+        swap(lon_even, "gx", 0, True),
+        swap(lon_odd, "gx", 1, True),
+        swap(lat_even, "gy", 0, False),
+        swap(lat_odd, "gy", 1, False),
+    )
 
 
 def on_device(late, early, stencil_coef, jacobian, cloudy_cols, cloudy_count, owner_rank, owner_slot):
@@ -388,6 +392,7 @@
         ],
         vmem=57,
     )(cloudy_cols, cloudy_count, owner_rank, owner_slot, late)
+    (field,) = call(widen, [shape(halves, F32)], [VMEM], [VMEM], touched=12000000)(late)
     received = exchange(outbox, groups)
     chosen_shape = shape((inbox_rows, own_slots * fields), BF16)
     answer_shape = shape((groups, (per_owner + 1) * LANES), F32)
@@ -398,31 +403,28 @@
     answer, chosen, answering = call(
         physics_first,
         [answer_shape, chosen_shape, chosen_shape],
-        [VMEM, HBM],
+        [VMEM] * 2,
         [VMEM] * 3,
         spaces
         + [
-            VMEM(matrices.shape, BF16),
-            pltpu.SemaphoreType.DMA((own_slots,)),
             VMEM(chosen_shape.shape, F32),
         ],
-        vmem=50,
     )(received, matrices)
     returned = exchange(answer, groups)
 
     edge_shapes = [shape((fields, 2, span, LANES), BF16) for span in (span_lat, span_lat, span_lon, span_lon)]
 
-    def add(kernel, returned, base, aliases):
+    def add(returned, base):
         return call(
-            functools.partial(kernel, levels=levels),
+            functools.partial(add_increments, levels=levels),
             [shape(halves, F32)] + edge_shapes,
             [SMEM] + [VMEM] * 2,
             [VMEM] * 5,
             [VMEM((2, inbox_rows, LANES), F32)],
-            aliases,
+            {2: 0},
         )(plan, returned, base)
 
-    field, *edges = add(add_first, returned, late, {})
+    field, *edges = add(returned, field)
     neighbours = halos(*edges)
     (inner,) = call(inner_first, [shape(halves, F32)], [VMEM] * 3, [VMEM], touched=6000000)(field, coef, early)
     adjoint, outbox = call(
@@ -438,7 +440,7 @@
         received, matrices, chosen, answering
     )
     returned = exchange(answer, groups)
-    field, *edges = add(add_increments, returned, adjoint, {2: 0})
+    field, *edges = add(returned, adjoint)
     neighbours = halos(*edges)
     (inner,) = call(inner_last, [shape(halves, F32)], [VMEM] * 2, [VMEM], touched=6000000)(field, coef)
     (final,) = call(

time: 119 us -> 117 us (0.983)
  the two profiles are of different devices: /device:TPU:2 before, /device:TPU:1 now
where the time goes in v5:
time: 117 us; the launch traced here: 116 us
  blocking collectives  53.4 us (46%)
  starting transfers between devices  35 us (30%)
  Pallas kernels  11.9 us (10%)
  waiting for transfers between devices  11.6 us (10%)
  local copies, waits for them, and re-layouts  3.3 us (3%)
    all_to_all x3, blocking collectives, exchange(): lax.all_to_all(rows.reshape(groups, width, rows.shape[1]), 'gy', split_ax...  53.4 us
    ppermute x8, starting transfers between devices, swap(): lax.ppermute(edge, axis, pairs + [(high, low) for low, high in pairs])  31.3 us
    all_to_all x1, waiting for transfers between devices, exchange(): lax.all_to_all(rows.reshape(groups, width, rows.shape[1]), 'gy', split_ax...  11.3 us
    all_to_all x1, starting transfers between devices, exchange(): lax.all_to_all(rows.reshape(groups, width, rows.shape[1]), 'gy', split_ax...  3.68 us
  transfers between devices with their start and end apart: 9, of which 3 were waited for; matrix products, arithmetic and copies ran while one was open for 0% of the time, Pallas kernels for 2%

profile of v5, /device:TPU:1, one launch (start us, length us, event | category | flops | bytes accessed | tf_op | source)
XLA Modules:
  0.0 116.1 jit_solution(3876399977113996628)
XLA Ops:
  0.7 2.2 %shard_map.82 = (bf16[256,138]{1,0:T(8,128)(2,1)}, s32[97]{0:T(128)}) custom-call(s32[1,1,48]{2,1,0:T(1,128)} %cols_hbm.1, s32[1,1]{1,0:T(1,128)S(6)} %copy.23.count_hbm, s32[1,1,48]{2,1,0:T(1,128)} %owner_hbm.1, s32[1,1,48]{2,1,0:T(1,128)} %slot_hbm.1, bf16[4,512,137]{2,1,0:T(8,128)(2,1)} %bitcast.29), custom_call_target="tpu_custom_call" | custom-call | flops 1000 | bytes 1000000 | tf_op jit(solution)/shard_map/pallas_call | solution.py:377
  2.9 21.9 %all_to_all.20 = bf16[32,8,138]{2,1,0:T(8,128)(2,1)S(1)} all-to-all(bf16[32,8,138]{2,1,0:T(8,128)(2,1)} %bitcast.43), channel_id=1, replica_groups=mesh['gx'=16,'gy'=32] {'gy'}, dimensions={0} | all-to-all | bytes 141312 | tf_op jit(solution)/shard_map/all_to_all | solution.py:337
  24.8 2.3 %copy-done = bf16[1,16,4,137,137]{4,2,3,1,0:T(4,128)(2,1)S(1)} copy-done((bf16[1,16,4,137,137]{4,2,3,1,0:T(4,128)(2,1)S(1)}, bf16[1,16,4,137,137]{4,2,3,1,0:T(4,128)(2,1)}, u32[]{:S(2)}) %copy-start) | copy-done | bytes 2402456
  27.0 1.4 %shard_map.83 = (f32[32,1152]{1,0:T(8,128)S(1)}, bf16[256,64]{1,0:T(8,128)(2,1)S(1)}, bf16[256,64]{1,0:T(8,128)(2,1)S(1)}) custom-call(bf16[256,138]{1,0:T(8,128)(2,1)S(1)} %bitcast.39, bf16[16,137,4,137]{3,2,1,0:T(4,128)(2,1)S(1)} %bitcast.25), custom_call_target="tpu_custom_call" | custom-call | flops 1000 | bytes 1000000 | tf_op jit(solution)/shard_map/pallas_call | solution.py:403
  28.5 0.8 copy.12
  29.3 3.7 %all-to-all-start.1 = ((f32[32,1,1152]{2,1,0:T(1,128)}), f32[32,1,1152]{2,1,0:T(1,128)S(1)}, u32[]{:S(2)}, u32[]{:S(2)}) async-start(f32[32,1,1152]{2,1,0:T(1,128)} %copy.12), calls=%async_computation.1 | async-start | bytes 294912 | tf_op jit(solution)/shard_map/all_to_all | solution.py:337
  33.2 11.3 %all-to-all-done.1 = f32[32,1,1152]{2,1,0:T(1,128)S(1)} async-done(((f32[32,1,1152]{2,1,0:T(1,128)}), f32[32,1,1152]{2,1,0:T(1,128)S(1)}, u32[]{:S(2)}, u32[]{:S(2)}) %all-to-all-start.1) | async-done | bytes 147488 | tf_op jit(solution)/shard_map/all_to_all | solution.py:337
  44.5 1.0 shard_map.85
  45.5 2.2 %collective-permute-start.2 = (bf16[4,2,32,128]{3,2,1,0:T(8,128)(2,1)S(1)}, bf16[4,2,32,128]{3,2,1,0:T(8,128)(2,1)S(1)}, u32[]{:S(2)}, u32[]{:S(2)}) collective-permute-start(bf16[4,2,32,128]{3,2,1,0:T(8,128)(2,1)S(1)} %get-tuple-element.28), channel_id=1, source_target_pairs={{0,1},{2,3},{4,5},{6,7},{8,9},{10,11},{12,13},{14,15},{16,17},{18,... | collective-permute-start | bytes 196616 | tf_op jit(solution)/shard_map/ppermute | solution.py:348
  47.6 1.9 %collective-permute-start.3 = (bf16[4,2,32,128]{3,2,1,0:T(8,128)(2,1)S(1)}, bf16[4,2,32,128]{3,2,1,0:T(8,128)(2,1)S(1)}, u32[]{:S(2)}, u32[]{:S(2)}) collective-permute-start(bf16[4,2,32,128]{3,2,1,0:T(8,128)(2,1)S(1)} %get-tuple-element.29), channel_id=1, source_target_pairs={{1,2},{3,4},{5,6},{7,8},{9,10},{11,12},{13,14},{15,16},{17,18},{19... | collective-permute-start | bytes 196616 | tf_op jit(solution)/shard_map/ppermute | solution.py:348
  49.6 3.4 %collective-permute-start = (bf16[4,2,16,128]{3,2,1,0:T(8,128)(2,1)S(1)}, bf16[4,2,16,128]{3,2,1,0:T(8,128)(2,1)S(1)}, u32[]{:S(2)}, u32[]{:S(2)}) collective-permute-start(bf16[4,2,16,128]{3,2,1,0:T(8,128)(2,1)S(1)} %get-tuple-element.26), channel_id=1, source_target_pairs={{0,32},{64,96},{128,160},{192,224},{256,288},{320,352},{384,416},{... | collective-permute-start | bytes 98312 | tf_op jit(solution)/shard_map/ppermute | solution.py:348
  53.0 10.5 %collective-permute-start.1 = (bf16[4,2,16,128]{3,2,1,0:T(8,128)(2,1)S(1)}, bf16[4,2,16,128]{3,2,1,0:T(8,128)(2,1)S(1)}, u32[]{:S(2)}, u32[]{:S(2)}) collective-permute-start(bf16[4,2,16,128]{3,2,1,0:T(8,128)(2,1)S(1)} %get-tuple-element.27), channel_id=1, source_target_pairs={{32,64},{96,128},{160,192},{224,256},{288,320},{352,384},{416,448}... | collective-permute-start | bytes 98312 | tf_op jit(solution)/shard_map/ppermute | solution.py:348
  63.6 1.2 %shard_map.86.inner = f32[4,2,512,128]{3,2,1,0:T(8,128)S(1)} custom-call(f32[4,2,512,128]{3,2,1,0:T(8,128)S(1)} %get-tuple-element.25.field, f32[4,16,32]{2,1,0:T(8,128)S(1)} %bitcast.35, bf16[4,512,137]{2,1,0:T(8,128)(2,1)S(1)} %bitcast.31), custom_call_target="tpu_custom_call" | custom-call | flops 1000 | bytes 6000000 | tf_op jit(solution)/shard_map/pallas_call | solution.py:429
  64.8 1.1 shard_map.87
  65.9 17.4 %all_to_all.21 = bf16[32,8,137]{2,1,0:T(8,128)(2,1)S(1)} all-to-all(bf16[32,8,137]{2,1,0:T(8,128)(2,1)S(1)} %bitcast.42), channel_id=1, replica_groups=mesh['gx'=16,'gy'=32] {'gy'}, dimensions={0} | all-to-all | bytes 140288 | tf_op jit(solution)/shard_map/all_to_all | solution.py:337
  83.3 1.4 %shard_map.88 = f32[32,1152]{1,0:T(8,128)S(1)} custom-call(bf16[256,137]{1,0:T(8,128)(2,1)S(1)} %bitcast.40, bf16[16,137,4,137]{3,2,1,0:T(4,128)(2,1)S(1)} %bitcast.28, bf16[256,64]{1,0:T(8,128)(2,1)S(1)} %get-tuple-element.31.chosen, bf16[256,64]{1,0:T(8,128)(2,1)S(1)} %get-tuple-element.32.answering), custom_call_target="tpu_custom_call" | custom-call | flops 1000 | bytes 1000000 | tf_op jit(solution)/shard_map/pallas_call | solution.py:439
  84.8 14.1 %all_to_all.22 = f32[32,1,1152]{2,1,0:T(1,128)S(1)} all-to-all(f32[32,1,1152]{2,1,0:T(1,128)S(1)} %copy.13), channel_id=1, replica_groups=mesh['gx'=16,'gy'=32] {'gy'}, dimensions={0} | all-to-all | bytes 294912 | tf_op jit(solution)/shard_map/all_to_all | solution.py:337
  99.0 1.0 shard_map.89
  99.9 1.9 %collective-permute-start.6 = (bf16[4,2,32,128]{3,2,1,0:T(8,128)(2,1)S(1)}, bf16[4,2,32,128]{3,2,1,0:T(8,128)(2,1)S(1)}, u32[]{:S(2)}, u32[]{:S(2)}) collective-permute-start(bf16[4,2,32,128]{3,2,1,0:T(8,128)(2,1)S(1)} %get-tuple-element.37), channel_id=1, source_target_pairs={{0,1},{2,3},{4,5},{6,7},{8,9},{10,11},{12,13},{14,15},{16,17},{18,... | collective-permute-start | bytes 196616 | tf_op jit(solution)/shard_map/ppermute | solution.py:348
  101.9 1.9 %collective-permute-start.7 = (bf16[4,2,32,128]{3,2,1,0:T(8,128)(2,1)S(1)}, bf16[4,2,32,128]{3,2,1,0:T(8,128)(2,1)S(1)}, u32[]{:S(2)}, u32[]{:S(2)}) collective-permute-start(bf16[4,2,32,128]{3,2,1,0:T(8,128)(2,1)S(1)} %get-tuple-element.38), channel_id=1, source_target_pairs={{1,2},{3,4},{5,6},{7,8},{9,10},{11,12},{13,14},{15,16},{17,18},{19... | collective-permute-start | bytes 196616 | tf_op jit(solution)/shard_map/ppermute | solution.py:348
  103.8 1.9 %collective-permute-start.4 = (bf16[4,2,16,128]{3,2,1,0:T(8,128)(2,1)S(1)}, bf16[4,2,16,128]{3,2,1,0:T(8,128)(2,1)S(1)}, u32[]{:S(2)}, u32[]{:S(2)}) collective-permute-start(bf16[4,2,16,128]{3,2,1,0:T(8,128)(2,1)S(1)} %get-tuple-element.35), channel_id=1, source_target_pairs={{0,32},{64,96},{128,160},{192,224},{256,288},{320,352},{384,416},{... | collective-permute-start | bytes 98312 | tf_op jit(solution)/shard_map/ppermute | solution.py:348
  105.7 7.5 %collective-permute-start.5 = (bf16[4,2,16,128]{3,2,1,0:T(8,128)(2,1)S(1)}, bf16[4,2,16,128]{3,2,1,0:T(8,128)(2,1)S(1)}, u32[]{:S(2)}, u32[]{:S(2)}) collective-permute-start(bf16[4,2,16,128]{3,2,1,0:T(8,128)(2,1)S(1)} %get-tuple-element.36), channel_id=1, source_target_pairs={{32,64},{96,128},{160,192},{224,256},{288,320},{352,384},{416,448}... | collective-permute-start | bytes 98312 | tf_op jit(solution)/shard_map/ppermute | solution.py:348
  113.2 1.0 shard_map.90.inner
  114.5 1.6 %shard_map.91 = f32[4,512,137]{2,1,0:T(8,128)} custom-call(f32[4,2,512,128]{3,2,1,0:T(8,128)S(1)} %shard_map.90.inner, f32[4,16,32]{2,1,0:T(8,128)S(1)} %bitcast.38, bf16[4,2,16,128]{3,2,1,0:T(8,128)(2,1)S(1)} %collective-permute-done.4.lon_even, bf16[4,2,16,128]{3,2,1,0:T(8,128)(2,1)S(1)} %collective-permute-done.5.lon_odd, ...), custom_call_target="tpu_custom_call" | custom-call | flops 1000 | bytes 1000000 | tf_op jit(solution)/shard_map/pallas_call | solution.py:446
  (26 shorter events, 0.7 us)
Async XLA Ops:
  24.8 2.3 %copy-start = (bf16[1,16,4,137,137]{4,2,3,1,0:T(4,128)(2,1)S(1)}, bf16[1,16,4,137,137]{4,2,3,1,0:T(4,128)(2,1)}, u32[]{:S(2)}) copy-start(bf16[1,16,4,137,137]{4,2,3,1,0:T(4,128)(2,1)} %param.11) | copy-start | bytes 7207300
  27.0 6.0 %copy-start.1 = (bf16[4,137,32,16]{1,3,2,0:T(8,128)(2,1)S(1)}, bf16[4,137,32,16]{1,3,2,0:T(8,128)(2,1)}, u32[]{:S(2)}) copy-start(bf16[4,137,32,16]{1,3,2,0:T(8,128)(2,1)} %param.8) | copy-start | bytes 1683460
  28.5 16.0 %copy-start.4 = (s32[97]{0:T(128)S(1)}, s32[97]{0:T(128)}, u32[]{:S(2)}) copy-start(s32[97]{0:T(128)} %get-tuple-element.22.plan) | copy-start | bytes 1168
  29.3 15.1 %all-to-all-start.1 = ((f32[32,1,1152]{2,1,0:T(1,128)}), f32[32,1,1152]{2,1,0:T(1,128)S(1)}, u32[]{:S(2)}, u32[]{:S(2)}) async-start(f32[32,1,1152]{2,1,0:T(1,128)} %copy.12), calls=%async_computation.1 | async-start | bytes 294912 | tf_op jit(solution)/shard_map/all_to_all | solution.py:337
  33.0 30.5 %copy-start.3 = (f32[4,32,16]{1,2,0:T(8,128)S(1)}, f32[4,32,16]{1,2,0:T(8,128)}, u32[]{:S(2)}) copy-start(f32[4,32,16]{1,2,0:T(8,128)} %param.10) | copy-start | bytes 24580
  33.2 30.4 %copy-start.2 = (bf16[4,137,32,16]{1,3,2,0:T(8,128)(2,1)S(1)}, bf16[4,137,32,16]{1,3,2,0:T(8,128)(2,1)}, u32[]{:S(2)}) copy-start(bf16[4,137,32,16]{1,3,2,0:T(8,128)(2,1)} %param.9) | copy-start | bytes 1683460
  44.5 38.8 %slice-start = ((s8[4489216]{0:T(1024)(128)(4,1)}), s8[4194304]{0:T(1024)(128)(4,1)S(1)}, s32[]{:S(2)}) async-start(s8[4489216]{0:T(1024)(128)(4,1)} %bitcast.26), calls=%async_computation.4 | async-start | bytes 8388608
  45.5 19.4 %collective-permute-start.2 = (bf16[4,2,32,128]{3,2,1,0:T(8,128)(2,1)S(1)}, bf16[4,2,32,128]{3,2,1,0:T(8,128)(2,1)S(1)}, u32[]{:S(2)}, u32[]{:S(2)}) collective-permute-start(bf16[4,2,32,128]{3,2,1,0:T(8,128)(2,1)S(1)} %get-tuple-element.28), channel_id=1, source_target_pairs={{0,1},{2,3},{4,5},{6,7},{8,9},{10,11},{12,13},{14,15},{16,17},{18,... | collective-permute-start | bytes 196616 | tf_op jit(solution)/shard_map/ppermute | solution.py:348
  47.6 17.2 %collective-permute-start.3 = (bf16[4,2,32,128]{3,2,1,0:T(8,128)(2,1)S(1)}, bf16[4,2,32,128]{3,2,1,0:T(8,128)(2,1)S(1)}, u32[]{:S(2)}, u32[]{:S(2)}) collective-permute-start(bf16[4,2,32,128]{3,2,1,0:T(8,128)(2,1)S(1)} %get-tuple-element.29), channel_id=1, source_target_pairs={{1,2},{3,4},{5,6},{7,8},{9,10},{11,12},{13,14},{15,16},{17,18},{19... | collective-permute-start | bytes 196616 | tf_op jit(solution)/shard_map/ppermute | solution.py:348
  49.6 15.2 %collective-permute-start = (bf16[4,2,16,128]{3,2,1,0:T(8,128)(2,1)S(1)}, bf16[4,2,16,128]{3,2,1,0:T(8,128)(2,1)S(1)}, u32[]{:S(2)}, u32[]{:S(2)}) collective-permute-start(bf16[4,2,16,128]{3,2,1,0:T(8,128)(2,1)S(1)} %get-tuple-element.26), channel_id=1, source_target_pairs={{0,32},{64,96},{128,160},{192,224},{256,288},{320,352},{384,416},{... | collective-permute-start | bytes 98312 | tf_op jit(solution)/shard_map/ppermute | solution.py:348
  53.0 11.8 %collective-permute-start.1 = (bf16[4,2,16,128]{3,2,1,0:T(8,128)(2,1)S(1)}, bf16[4,2,16,128]{3,2,1,0:T(8,128)(2,1)S(1)}, u32[]{:S(2)}, u32[]{:S(2)}) collective-permute-start(bf16[4,2,16,128]{3,2,1,0:T(8,128)(2,1)S(1)} %get-tuple-element.27), channel_id=1, source_target_pairs={{32,64},{96,128},{160,192},{224,256},{288,320},{352,384},{416,448}... | collective-permute-start | bytes 98312 | tf_op jit(solution)/shard_map/ppermute | solution.py:348
  63.6 19.7 %slice-start.1 = ((s8[4489216]{0:T(1024)(128)(4,1)}), s8[294912]{0:T(1024)(128)(4,1)S(1)}, s32[]{:S(2)}) async-start(s8[4489216]{0:T(1024)(128)(4,1)} %bitcast.26), calls=%async_computation.5 | async-start | bytes 589824
  99.9 14.6 %collective-permute-start.6 = (bf16[4,2,32,128]{3,2,1,0:T(8,128)(2,1)S(1)}, bf16[4,2,32,128]{3,2,1,0:T(8,128)(2,1)S(1)}, u32[]{:S(2)}, u32[]{:S(2)}) collective-permute-start(bf16[4,2,32,128]{3,2,1,0:T(8,128)(2,1)S(1)} %get-tuple-element.37), channel_id=1, source_target_pairs={{0,1},{2,3},{4,5},{6,7},{8,9},{10,11},{12,13},{14,15},{16,17},{18,... | collective-permute-start | bytes 196616 | tf_op jit(solution)/shard_map/ppermute | solution.py:348
  101.9 12.7 %collective-permute-start.7 = (bf16[4,2,32,128]{3,2,1,0:T(8,128)(2,1)S(1)}, bf16[4,2,32,128]{3,2,1,0:T(8,128)(2,1)S(1)}, u32[]{:S(2)}, u32[]{:S(2)}) collective-permute-start(bf16[4,2,32,128]{3,2,1,0:T(8,128)(2,1)S(1)} %get-tuple-element.38), channel_id=1, source_target_pairs={{1,2},{3,4},{5,6},{7,8},{9,10},{11,12},{13,14},{15,16},{17,18},{19... | collective-permute-start | bytes 196616 | tf_op jit(solution)/shard_map/ppermute | solution.py:348
  103.8 10.5 %collective-permute-start.4 = (bf16[4,2,16,128]{3,2,1,0:T(8,128)(2,1)S(1)}, bf16[4,2,16,128]{3,2,1,0:T(8,128)(2,1)S(1)}, u32[]{:S(2)}, u32[]{:S(2)}) collective-permute-start(bf16[4,2,16,128]{3,2,1,0:T(8,128)(2,1)S(1)} %get-tuple-element.35), channel_id=1, source_target_pairs={{0,32},{64,96},{128,160},{192,224},{256,288},{320,352},{384,416},{... | collective-permute-start | bytes 98312 | tf_op jit(solution)/shard_map/ppermute | solution.py:348
  105.7 8.8 %collective-permute-start.5 = (bf16[4,2,16,128]{3,2,1,0:T(8,128)(2,1)S(1)}, bf16[4,2,16,128]{3,2,1,0:T(8,128)(2,1)S(1)}, u32[]{:S(2)}, u32[]{:S(2)}) collective-permute-start(bf16[4,2,16,128]{3,2,1,0:T(8,128)(2,1)S(1)} %get-tuple-element.36), channel_id=1, source_target_pairs={{32,64},{96,128},{160,192},{224,256},{288,320},{352,384},{416,448}... | collective-permute-start | bytes 98312 | tf_op jit(solution)/shard_map/ppermute | solution.py:348

commit v6 on v5

--- a/solution.py
+++ b/solution.py
@@ -46,15 +46,18 @@
     field[f, 1, :, : packed.shape[2] - LANES] = packed[f, :, LANES:].astype(F32)
 
 
+def tail_lanes(block, start):
+    end = block[:, LANES:]
+    return pltpu.roll(end, start, 1) if start else end
+
+
 def pack_first(
-    cols_hbm, count_hbm, owner_hbm, slot_hbm, late_hbm, outbox, plan, cols, count, owner, slot, late, field, rows, used, sems
+    cols_hbm, count_hbm, owner_hbm, slot_hbm, late_hbm, outbox, plan, cols, count, owner, slot, late, pick, codes, wide, used, sems
 ):
-    fields = field.shape[0]
-    levels = late.shape[2]
+    fields, _, levels = late.shape
     capacity = cols.shape[2]
     owners = used.shape[0]
     tail = levels - LANES
-    end = lax.broadcasted_iota(jnp.int32, (1, LANES), 1)
     small = [(cols_hbm, cols), (count_hbm, count), (owner_hbm, owner), (slot_hbm, slot)]
     copies = [pltpu.make_async_copy(source, target, sems.at[i]) for i, (source, target) in enumerate(small)]
     copies += [pltpu.make_async_copy(late_hbm.at[f], late.at[f], sems.at[len(small) + f]) for f in range(fields)]
@@ -62,17 +65,24 @@
         copy.start()
     for o in range(owners):
         used[o] = 0
+    pick[...] = jnp.zeros(pick.shape, F32)
+    codes[...] = jnp.zeros(codes.shape, F32)
+    wide[...] = jnp.zeros(wide.shape, F32)
     for copy in copies[: len(small)]:
         copy.wait()
     live = count[0, 0]
     plan[0] = live
+    places = lax.broadcasted_iota(jnp.int32, (1, pick.shape[1]), 1)
 
     def route(e, carry):
         o = owner[0, 0, e]
         rank = used[o]
         used[o] = rank + 1
-        plan[1 + e] = cols[0, 0, e]
+        column = cols[0, 0, e]
+        plan[1 + e] = column
         plan[1 + capacity + e] = rank * (fields * owners) + o
+        pick[pl.ds(o * PAIR + rank, 1), :] = (places == column).astype(F32)
+        codes[pl.ds(o * PAIR + rank, 1), :] = jnp.full((1, LANES), slot[0, 0, e] + 1, jnp.int32).astype(F32)
         return carry
 
     lax.fori_loop(0, live, route, 0)
@@ -81,38 +91,23 @@
     def repeat(e, carry):
         for part in (1, 1 + capacity):
             plan[part + e] = plan[part + whole]
-        slot[0, 0, e] = slot[0, 0, whole]
         return carry
 
     lax.fori_loop(live, ((live + (GROUP - 1)) // GROUP) * GROUP, repeat, 0)
-    rows[...] = jnp.zeros(rows.shape, F32)
+    chosen = pick[...].astype(BF16)
+    rows, lanes = [], lax.broadcasted_iota(jnp.int32, codes.shape, 1)
+    tails = jnp.where(lanes == tail * fields, codes[...], 0.0)
     for f in range(fields):
         copies[len(small) + f].wait()
-        unpack_field(late, field, f)
-
-    def gather(g, carry):
-        first = g * GROUP
-        found = []
-        for i in range(GROUP):
-            column = plan[1 + first + i]
-            row = outbox_row(plan[1 + capacity + first + i], owners, fields)
-            code = slot[0, 0, first + i] * fields
-            for f in range(fields):
-                mark = (code + (f + 1)).astype(F32)
-                found.append((0, row + f, field[f, 0, pl.ds(column, 1), :]))
-                found.append((1, row + f, jnp.where(end == tail, mark, field[f, 1, pl.ds(column, 1), :])))
-        for h, row, value in found:
-            rows[h, pl.ds(row, 1), :] = value
-        return carry
-
-    lax.fori_loop(0, (live + (GROUP - 1)) // GROUP, gather, 0)
-    outbox[:, :LANES] = rows[0].astype(BF16)
-    outbox[:, LANES:] = rows[1, :, : tail + 1].astype(BF16)
+        wide[:, :levels] = jnp.dot(chosen, late[f], preferred_element_type=F32)
+        rows.append(wide[:, :LANES])
+        tails = tails + tail_lanes(wide[...], tail * f)
+    outbox[...] = jnp.concatenate(rows + [tails], axis=1).astype(BF16).reshape(outbox.shape)
 
 
 def outbox_row(row, owners, fields):
     rank = row // (fields * owners)
-    return ((row - rank * (fields * owners)) * PAIR + rank) * fields
+    return (row - rank * (fields * owners)) * PAIR + rank
 
 
 def split_dot(chosen, value):
@@ -124,58 +119,64 @@
     return dot(chosen, high) + dot(chosen, middle) + dot(chosen, low)
 
 
-def products(chosen, values, answering, matrices, answer, spread, result):
+def products(chosen, received, matrices, answer, spread, result):
     own_slots, levels, fields, _ = matrices.shape
+    owners = received.shape[0]
     depth = levels * fields
-    placed = lax.dot_general(chosen, values, (((0,), (0,)), ((), ())), preferred_element_type=F32).astype(BF16)
+    tail = levels - LANES
     iota = functools.partial(lax.broadcasted_iota, jnp.int32)
-    widen = (iota((levels, depth), 1) // fields == iota((levels, depth), 0)).astype(F32).astype(BF16)
-    wide = jnp.dot(placed, widen, preferred_element_type=F32)
+    values = received[...].reshape(owners * PAIR, received.shape[2]).astype(F32)
+    choice = chosen[...].astype(BF16)
+    field_of_row = iota((own_slots * fields, levels), 0) % fields
+    placed = jnp.zeros((own_slots * fields, levels), F32)
+    tails = values[:, fields * LANES :]
+    for f in range(fields):
+        end = pltpu.roll(tails, LANES - tail * f, 1) if f else tails
+        full = jnp.concatenate([values[:, f * LANES : (f + 1) * LANES], end[:, :tail]], axis=1)
+        every = lax.dot_general(
+            choice, full.astype(BF16), (((0,), (0,)), ((), ())), preferred_element_type=F32
+        )
+        placed = jnp.where(field_of_row == f, every, placed)
+    spreader = (iota((levels, depth), 1) // fields == iota((levels, depth), 0)).astype(F32).astype(BF16)
     own = iota(spread.shape, 1) % fields == iota(spread.shape, 0) % fields
-    spread[...] = jnp.where(own, wide, 0.0)
+    spread[...] = jnp.where(own, jnp.dot(placed.astype(BF16), spreader, preferred_element_type=F32), 0.0)
     result[...] = jnp.zeros(result.shape, F32)
     for s in range(own_slots):
         at = slice(s * fields, (s + 1) * fields)
         result[at, :levels] = jnp.dot(
             spread[at].astype(BF16), matrices[s].reshape(depth, levels), preferred_element_type=F32
         )
-    owners = answer.shape[0]
-    tail = levels - LANES
-    per_owner = answering.shape[0] // owners
-    rows = split_dot(answering, result[...])
-    tails = jnp.zeros((owners, LANES), F32)
-    for r in range(per_owner):
-        block = rows[r * owners : (r + 1) * owners]
-        answer[:, r * LANES : (r + 1) * LANES] = block[:, :LANES]
-        end = block[:, LANES:]
-        tails = tails + (pltpu.roll(end, tail * r, 1) if r else end)
-    answer[:, per_owner * LANES :] = tails
-
-
-def physics_first(received, matrices, answer, chosen_out, answering_out, spread, result, choice):
-    levels = matrices.shape[1]
-    owners = answer.shape[0]
-    per_owner = received.shape[0] // owners
-    values = received[...].astype(F32)
-    codes = values[:, levels:]
-    wanted = (lax.broadcasted_iota(jnp.int32, choice.shape, 1) + 1).astype(F32)
-    choice[...] = (codes == wanted).astype(F32)
-    chosen = choice[...].astype(BF16)
-    answering = jnp.concatenate(
-        [choice[pl.ds(r, owners, stride=per_owner), :] for r in range(per_owner)], axis=0
-    ).astype(BF16)
-    chosen_out[...] = chosen
-    answering_out[...] = answering
-    products(chosen, values[:, :levels].astype(BF16), answering, matrices, answer, spread, result)
-
-
-def physics_second(received, matrices, chosen, answering, answer, spread, result):
-    products(chosen[...], received[...], answering[...], matrices, answer, spread, result)
-
-
-def widen(late, field):
+    backward = []
+    for k in range(PAIR):
+        rows = chosen[pl.ds(k, owners, stride=PAIR), :][:, : own_slots * fields]
+        field_of_lane = iota(rows.shape, 1) % fields
+        backward += [jnp.where(field_of_lane == f, rows, 0.0) for f in range(fields)]
+    rows = split_dot(jnp.concatenate(backward, axis=0).astype(BF16), result[...])
+    blocks = [rows[r * owners : (r + 1) * owners] for r in range(PAIR * fields)]
+    tails = tail_lanes(blocks[0], 0)
+    for r in range(1, PAIR * fields):
+        tails = tails + tail_lanes(blocks[r], tail * r)
+    answer[...] = jnp.concatenate([block[:, :LANES] for block in blocks] + [tails], axis=1).reshape(answer.shape)
+
+
+def physics_first(received, matrices, answer, chosen_out, spread, result):
+    own_slots, levels, fields, _ = matrices.shape
+    owners = received.shape[0]
+    code_lane = fields * levels
+    codes = received[...].reshape(owners * PAIR, received.shape[2]).astype(F32)[:, code_lane : code_lane + 1]
+    wanted = (lax.broadcasted_iota(jnp.int32, chosen_out.shape, 1) // fields + 1).astype(F32)
+    chosen_out[...] = (codes == wanted).astype(F32)
+    products(chosen_out, received, matrices, answer, spread, result)
+
+
+def physics_second(received, matrices, chosen, answer, spread, result):
+    products(chosen, received, matrices, answer, spread, result)
+
+
+def add_first(plan, returned, late, field, *rest, levels):
     for f in range(field.shape[0]):
         unpack_field(late, field, f)
+    add_increments(plan, returned, field, field, *rest, levels=levels)
 
 
 def add_increments(plan, returned, base, field, lon_even, lon_odd, lat_even, lat_odd, inbox, *, levels):
@@ -183,9 +184,10 @@
     owners = returned.shape[0]
     per_owner = inbox.shape[1] // owners
     tail = levels - LANES
-    tails = returned[:, per_owner * LANES :]
+    lines = returned[...].reshape(owners, returned.shape[2])
+    tails = lines[:, per_owner * LANES :]
     for r in range(per_owner):
-        inbox[0, r * owners : (r + 1) * owners] = returned[:, r * LANES : (r + 1) * LANES]
+        inbox[0, r * owners : (r + 1) * owners] = lines[:, r * LANES : (r + 1) * LANES]
         inbox[1, r * owners : (r + 1) * owners] = pltpu.roll(tails, LANES - tail * r, 1) if r else tails
 
     def body(entries):
@@ -290,10 +292,10 @@
         out[at] = out[at] + weight * edge
 
 
-def edges_first(plan, inner, coef, lon_even, lon_odd, lat_even, lat_odd, out, outbox, rows):
+def edges_first(plan, inner, coef, lon_even, lon_odd, lat_even, lat_odd, out, outbox, rows, *, levels):
     fields, halves, columns_all, lanes = out.shape
-    owners = rows.shape[1] // (PAIR * fields)
-    tail = outbox.shape[1] - lanes
+    owners = outbox.shape[0]
+    tail = levels - lanes
     weights = edge_weights(coef)
     rows[...] = jnp.zeros(rows.shape, F32)
     for f in range(fields):
@@ -303,16 +305,22 @@
     def body(entries):
         found = []
         for column, row in entries:
-            first = outbox_row(row, owners, fields)
+            at = outbox_row(row, owners, fields)
             for f in range(fields):
                 for h in range(halves):
-                    found.append((h, first + f, out[f, h, pl.ds(column, 1), :]))
+                    found.append((h, f * (PAIR * owners) + at, out[f, h, pl.ds(column, 1), :]))
         for h, row, value in found:
             rows[h, pl.ds(row, 1), :] = value
 
     entry_groups(plan, body)
-    outbox[:, :lanes] = rows[0].astype(BF16)
-    outbox[:, lanes:] = rows[1, :, :tail].astype(BF16)
+    blocks = [slice(f * PAIR * owners, (f + 1) * PAIR * owners) for f in range(fields)]
+    lane = lax.broadcasted_iota(jnp.int32, (PAIR * owners, lanes), 1)
+    tails = jnp.zeros((PAIR * owners, lanes), F32)
+    for f in range(fields):
+        end = jnp.where(lane < tail, rows[1, blocks[f]], 0.0)
+        tails = tails + (pltpu.roll(end, tail * f, 1) if f else end)
+    packed = jnp.concatenate([rows[0, block] for block in blocks] + [tails], axis=1)
+    outbox[...] = packed.astype(BF16).reshape(outbox.shape)
 
 
 def edges_last(inner, coef, lon_even, lon_odd, lat_even, lat_odd, out_hbm, both, out, sems):
@@ -332,12 +340,8 @@
         copy.wait()
 
 
-def exchange(rows, groups):
-    width = rows.shape[0] // groups
-    moved = lax.all_to_all(
-        rows.reshape(groups, width, rows.shape[1]), "gy", split_axis=0, concat_axis=0, tiled=True
-    )
-    return moved.reshape(rows.shape)
+def exchange(lines):
+    return lax.all_to_all(lines, "gy", split_axis=0, concat_axis=0, tiled=True)
 
 
 def swap(edge, axis, start, periodic):
@@ -374,9 +378,10 @@
     halves = (fields, 2, columns_all, LANES)
     plan_shape = shape((2 * capacity + 1,), jnp.int32)
 
+    outbox_shape = shape((groups, PAIR, (fields + 1) * LANES), BF16)
     outbox, plan = call(
         pack_first,
-        [shape((inbox_rows, levels + 1), BF16), plan_shape],
+        [outbox_shape, plan_shape],
         [HBM] * 5,
         [VMEM, SMEM],
         [
@@ -385,62 +390,52 @@
             SMEM(owner_rank.shape, jnp.int32),
             SMEM(owner_slot.shape, jnp.int32),
             VMEM(grid, BF16),
-            VMEM(halves, F32),
-            VMEM((2, inbox_rows, LANES), F32),
+            VMEM((groups * PAIR, columns_all), F32),
+            VMEM((groups * PAIR, LANES), F32),
+            VMEM((groups * PAIR, 2 * LANES), F32),
             SMEM((groups,), jnp.int32),
             pltpu.SemaphoreType.DMA((4 + fields,)),
         ],
         vmem=57,
     )(cloudy_cols, cloudy_count, owner_rank, owner_slot, late)
-    (field,) = call(widen, [shape(halves, F32)], [VMEM], [VMEM], touched=12000000)(late)
-    received = exchange(outbox, groups)
-    chosen_shape = shape((inbox_rows, own_slots * fields), BF16)
-    answer_shape = shape((groups, (per_owner + 1) * LANES), F32)
+    chosen_shape = shape((groups * PAIR, own_slots * fields), F32)
+    answer_shape = shape((groups, 1, (per_owner + 1) * LANES), F32)
     spaces = [
         VMEM((own_slots * fields, levels * fields), F32),
         VMEM((own_slots * fields, 2 * LANES), F32),
     ]
-    answer, chosen, answering = call(
-        physics_first,
-        [answer_shape, chosen_shape, chosen_shape],
-        [VMEM] * 2,
-        [VMEM] * 3,
-        spaces
-        + [
-            VMEM(chosen_shape.shape, F32),
-        ],
-    )(received, matrices)
-    returned = exchange(answer, groups)
+    answer, chosen = call(physics_first, [answer_shape, chosen_shape], [VMEM] * 2, [VMEM] * 2, spaces)(
+        exchange(outbox), matrices
+    )
+    returned = exchange(answer)
 
     edge_shapes = [shape((fields, 2, span, LANES), BF16) for span in (span_lat, span_lat, span_lon, span_lon)]
 
-    def add(returned, base):
+    def add(kernel, returned, base, aliases):
         return call(
-            functools.partial(add_increments, levels=levels),
+            functools.partial(kernel, levels=levels),
             [shape(halves, F32)] + edge_shapes,
             [SMEM] + [VMEM] * 2,
             [VMEM] * 5,
             [VMEM((2, inbox_rows, LANES), F32)],
-            {2: 0},
+            aliases,
         )(plan, returned, base)
 
-    field, *edges = add(returned, field)
+    field, *edges = add(add_first, returned, late, {})
     neighbours = halos(*edges)
     (inner,) = call(inner_first, [shape(halves, F32)], [VMEM] * 3, [VMEM], touched=6000000)(field, coef, early)
     adjoint, outbox = call(
-        edges_first,
-        [shape(halves, F32), shape((inbox_rows, levels), BF16)],
+        functools.partial(edges_first, levels=levels),
+        [shape(halves, F32), outbox_shape],
         [SMEM] + [VMEM] * 6,
         [VMEM] * 2,
         [VMEM((2, inbox_rows, LANES), F32)],
         {1: 0},
     )(plan, inner, coef, *neighbours)
-    received = exchange(outbox, groups)
-    (answer,) = call(physics_second, [answer_shape], [VMEM] * 4, [VMEM], spaces)(
-        received, matrices, chosen, answering
-    )
-    returned = exchange(answer, groups)
-    field, *edges = add(returned, adjoint)
+    (answer,) = call(physics_second, [answer_shape], [VMEM] * 3, [VMEM], spaces)(
+        exchange(outbox), matrices, chosen
+    )
+    field, *edges = add(add_increments, exchange(answer), adjoint, {2: 0})
     neighbours = halos(*edges)
     (inner,) = call(inner_last, [shape(halves, F32)], [VMEM] * 2, [VMEM], touched=6000000)(field, coef)
     (final,) = call(

time: 117 us -> 115 us (0.983)
  blocking collectives: 53.4 us -> 66.7 us
  waiting for transfers between devices: 11.6 us -> 0.31 us
  starting transfers between devices: 35 us -> 30.8 us
    all_to_all x3 -> x4, blocking collectives: 53.4 us -> 66.7 us  [exchange(): return lax.all_to_all(lines, 'gy', split_axis=0, concat_axis=0, tiled=True)]
    all_to_all x1 -> x0, waiting for transfers between devices: 11.3 us -> none  [exchange(): lax.all_to_all(rows.reshape(groups, width, rows.shape[1]), 'gy', split_ax...]
    all_to_all x1 -> x0, starting transfers between devices: 3.68 us -> none  [exchange(): lax.all_to_all(rows.reshape(groups, width, rows.shape[1]), 'gy', split_ax...]
    pallas_call x7 -> x6, Pallas kernels: 8.13 us -> 8.82 us  [the longest x1 2.72 us: on_device(): call(pack_first, [outbox_shape, plan_shape], [HBM] * 5, [VMEM, SMEM], [SM...]
  transfers between devices with their start and end apart: 9 -> 8, of which waited for: 3 -> 2; matrix products, arithmetic and copies ran while one was open for 0% -> 0% of each run, Pallas kernels for 2% -> 2%
where the time goes in v6:
time: 115 us; the launch traced here: 114 us
  blocking collectives  66.7 us (58%)
  starting transfers between devices  30.8 us (27%)
  Pallas kernels  12.6 us (11%)
  local copies, waits for them, and re-layouts  2.3 us (2%)
    all_to_all x4, blocking collectives, exchange(): return lax.all_to_all(lines, 'gy', split_axis=0, concat_axis=0, tiled=True)  66.7 us
    ppermute x8, starting transfers between devices, swap(): lax.ppermute(edge, axis, pairs + [(high, low) for low, high in pairs])  30.8 us
    pallas_call x1, Pallas kernels, on_device(): call(pack_first, [outbox_shape, plan_shape], [HBM] * 5, [VMEM, SMEM], [SM...  2.72 us
  transfers between devices with their start and end apart: 8, of which 2 were waited for; matrix products, arithmetic and copies ran while one was open for 0% of the time, Pallas kernels for 2%

profile of v6, /device:TPU:1, one launch (start us, length us, event | category | flops | bytes accessed | tf_op | source)
XLA Modules:
  0.0 113.5 jit_solution(9122347691931993674)
XLA Ops:
  0.7 2.7 %shard_map.82 = (bf16[32,2,640]{2,1,0:T(2,128)(2,1)}, s32[97]{0:T(128)}) custom-call(s32[1,1,48]{2,1,0:T(1,128)} %cols_hbm.1, s32[1,1]{1,0:T(1,128)S(6)} %copy.13.count_hbm, s32[1,1,48]{2,1,0:T(1,128)} %owner_hbm.1, s32[1,1,48]{2,1,0:T(1,128)} %slot_hbm.1, bf16[4,512,137]{2,1,0:T(8,128)(2,1)} %bitcast.17), custom_call_target="tpu_custom_call" | custom-call | flops 1000 | bytes 1000000 | tf_op jit(solution)/shard_map/pallas_call | solution.py:382
  3.4 21.2 %all_to_all.20.received = bf16[32,2,640]{2,1,0:T(2,128)(2,1)S(1)} all-to-all(bf16[32,2,640]{2,1,0:T(2,128)(2,1)} %get-tuple-element.22), channel_id=1, replica_groups=mesh['gx'=16,'gy'=32] {'gy'}, dimensions={0} | all-to-all | bytes 163840 | tf_op jit(solution)/shard_map/all_to_all | solution.py:344
  24.6 2.3 %copy-done = bf16[1,16,4,137,137]{4,2,3,1,0:T(4,128)(2,1)S(1)} copy-done((bf16[1,16,4,137,137]{4,2,3,1,0:T(4,128)(2,1)S(1)}, bf16[1,16,4,137,137]{4,2,3,1,0:T(4,128)(2,1)}, u32[]{:S(2)}) %copy-start) | copy-done | bytes 2402456
  26.8 1.5 %shard_map.83 = (f32[32,1,1152]{2,1,0:T(1,128)S(1)}, f32[64,64]{1,0:T(8,128)S(1)}) custom-call(bf16[32,2,640]{2,1,0:T(2,128)(2,1)S(1)} %all_to_all.20.received, bf16[16,137,4,137]{3,2,1,0:T(4,128)(2,1)S(1)} %bitcast.13), custom_call_target="tpu_custom_call" | custom-call | flops 1000 | bytes 1000000 | tf_op jit(solution)/shard_map/pallas_call | solution.py:407
  28.3 14.4 %all_to_all.21.returned = f32[32,1,1152]{2,1,0:T(1,128)S(1)} all-to-all(f32[32,1,1152]{2,1,0:T(1,128)S(1)} %get-tuple-element.23), channel_id=1, replica_groups=mesh['gx'=16,'gy'=32] {'gy'}, dimensions={0} | all-to-all | bytes 294912 | tf_op jit(solution)/shard_map/all_to_all | solution.py:344
  42.7 1.1 shard_map.84
  43.8 2.3 %collective-permute-start.2 = (bf16[4,2,32,128]{3,2,1,0:T(8,128)(2,1)S(1)}, bf16[4,2,32,128]{3,2,1,0:T(8,128)(2,1)S(1)}, u32[]{:S(2)}, u32[]{:S(2)}) collective-permute-start(bf16[4,2,32,128]{3,2,1,0:T(8,128)(2,1)S(1)} %get-tuple-element.27), channel_id=1, source_target_pairs={{0,1},{2,3},{4,5},{6,7},{8,9},{10,11},{12,13},{14,15},{16,17},{18,... | collective-permute-start | bytes 196616 | tf_op jit(solution)/shard_map/ppermute | solution.py:352
  46.1 2.1 %collective-permute-start.3 = (bf16[4,2,32,128]{3,2,1,0:T(8,128)(2,1)S(1)}, bf16[4,2,32,128]{3,2,1,0:T(8,128)(2,1)S(1)}, u32[]{:S(2)}, u32[]{:S(2)}) collective-permute-start(bf16[4,2,32,128]{3,2,1,0:T(8,128)(2,1)S(1)} %get-tuple-element.28), channel_id=1, source_target_pairs={{1,2},{3,4},{5,6},{7,8},{9,10},{11,12},{13,14},{15,16},{17,18},{19... | collective-permute-start | bytes 196616 | tf_op jit(solution)/shard_map/ppermute | solution.py:352
  48.2 3.2 %collective-permute-start = (bf16[4,2,16,128]{3,2,1,0:T(8,128)(2,1)S(1)}, bf16[4,2,16,128]{3,2,1,0:T(8,128)(2,1)S(1)}, u32[]{:S(2)}, u32[]{:S(2)}) collective-permute-start(bf16[4,2,16,128]{3,2,1,0:T(8,128)(2,1)S(1)} %get-tuple-element.25), channel_id=1, source_target_pairs={{0,32},{64,96},{128,160},{192,224},{256,288},{320,352},{384,416},{... | collective-permute-start | bytes 98312 | tf_op jit(solution)/shard_map/ppermute | solution.py:352
  51.4 10.7 %collective-permute-start.1 = (bf16[4,2,16,128]{3,2,1,0:T(8,128)(2,1)S(1)}, bf16[4,2,16,128]{3,2,1,0:T(8,128)(2,1)S(1)}, u32[]{:S(2)}, u32[]{:S(2)}) collective-permute-start(bf16[4,2,16,128]{3,2,1,0:T(8,128)(2,1)S(1)} %get-tuple-element.26), channel_id=1, source_target_pairs={{32,64},{96,128},{160,192},{224,256},{288,320},{352,384},{416,448}... | collective-permute-start | bytes 98312 | tf_op jit(solution)/shard_map/ppermute | solution.py:352
  62.1 1.2 %shard_map.85.inner = f32[4,2,512,128]{3,2,1,0:T(8,128)S(1)} custom-call(f32[4,2,512,128]{3,2,1,0:T(8,128)S(1)} %get-tuple-element.24.field, f32[4,16,32]{2,1,0:T(8,128)S(1)} %bitcast.20, bf16[4,512,137]{2,1,0:T(8,128)(2,1)S(1)} %bitcast.19), custom_call_target="tpu_custom_call" | custom-call | flops 1000 | bytes 6000000 | tf_op jit(solution)/shard_map/pallas_call | solution.py:426
  63.3 0.1 collective-permute-done.1.lon_odd
  63.4 1.1 shard_map.86
  64.5 17.1 %all_to_all.22.received = bf16[32,2,640]{2,1,0:T(2,128)(2,1)S(1)} all-to-all(bf16[32,2,640]{2,1,0:T(2,128)(2,1)S(1)} %get-tuple-element.29), channel_id=1, replica_groups=mesh['gx'=16,'gy'=32] {'gy'}, dimensions={0} | all-to-all | bytes 163840 | tf_op jit(solution)/shard_map/all_to_all | solution.py:344
  81.5 1.4 %shard_map.87 = f32[32,1,1152]{2,1,0:T(1,128)S(1)} custom-call(bf16[32,2,640]{2,1,0:T(2,128)(2,1)S(1)} %all_to_all.22.received, bf16[16,137,4,137]{3,2,1,0:T(4,128)(2,1)S(1)} %bitcast.16, f32[64,64]{1,0:T(8,128)S(1)} %get-tuple-element.30.chosen), custom_call_target="tpu_custom_call" | custom-call | flops 1000 | bytes 1000000 | tf_op jit(solution)/shard_map/pallas_call | solution.py:435
  83.0 14.1 %all_to_all.23.returned = f32[32,1,1152]{2,1,0:T(1,128)S(1)} all-to-all(f32[32,1,1152]{2,1,0:T(1,128)S(1)} %shard_map.87), channel_id=1, replica_groups=mesh['gx'=16,'gy'=32] {'gy'}, dimensions={0} | all-to-all | bytes 294912 | tf_op jit(solution)/shard_map/all_to_all | solution.py:344
  97.1 1.0 shard_map.88
  98.1 2.1 %collective-permute-start.6 = (bf16[4,2,32,128]{3,2,1,0:T(8,128)(2,1)S(1)}, bf16[4,2,32,128]{3,2,1,0:T(8,128)(2,1)S(1)}, u32[]{:S(2)}, u32[]{:S(2)}) collective-permute-start(bf16[4,2,32,128]{3,2,1,0:T(8,128)(2,1)S(1)} %get-tuple-element.35), channel_id=1, source_target_pairs={{0,1},{2,3},{4,5},{6,7},{8,9},{10,11},{12,13},{14,15},{16,17},{18,... | collective-permute-start | bytes 196616 | tf_op jit(solution)/shard_map/ppermute | solution.py:352
  100.2 1.9 %collective-permute-start.7 = (bf16[4,2,32,128]{3,2,1,0:T(8,128)(2,1)S(1)}, bf16[4,2,32,128]{3,2,1,0:T(8,128)(2,1)S(1)}, u32[]{:S(2)}, u32[]{:S(2)}) collective-permute-start(bf16[4,2,32,128]{3,2,1,0:T(8,128)(2,1)S(1)} %get-tuple-element.36), channel_id=1, source_target_pairs={{1,2},{3,4},{5,6},{7,8},{9,10},{11,12},{13,14},{15,16},{17,18},{19... | collective-permute-start | bytes 196616 | tf_op jit(solution)/shard_map/ppermute | solution.py:352
  102.1 1.9 %collective-permute-start.4 = (bf16[4,2,16,128]{3,2,1,0:T(8,128)(2,1)S(1)}, bf16[4,2,16,128]{3,2,1,0:T(8,128)(2,1)S(1)}, u32[]{:S(2)}, u32[]{:S(2)}) collective-permute-start(bf16[4,2,16,128]{3,2,1,0:T(8,128)(2,1)S(1)} %get-tuple-element.33), channel_id=1, source_target_pairs={{0,32},{64,96},{128,160},{192,224},{256,288},{320,352},{384,416},{... | collective-permute-start | bytes 98312 | tf_op jit(solution)/shard_map/ppermute | solution.py:352
  104.0 6.6 %collective-permute-start.5 = (bf16[4,2,16,128]{3,2,1,0:T(8,128)(2,1)S(1)}, bf16[4,2,16,128]{3,2,1,0:T(8,128)(2,1)S(1)}, u32[]{:S(2)}, u32[]{:S(2)}) collective-permute-start(bf16[4,2,16,128]{3,2,1,0:T(8,128)(2,1)S(1)} %get-tuple-element.34), channel_id=1, source_target_pairs={{32,64},{96,128},{160,192},{224,256},{288,320},{352,384},{416,448}... | collective-permute-start | bytes 98312 | tf_op jit(solution)/shard_map/ppermute | solution.py:352
  110.7 1.0 shard_map.89.inner
  111.7 0.2 collective-permute-done.5.lon_odd
  112.0 1.6 %shard_map.90 = f32[4,512,137]{2,1,0:T(8,128)} custom-call(f32[4,2,512,128]{3,2,1,0:T(8,128)S(1)} %shard_map.89.inner, f32[4,16,32]{2,1,0:T(8,128)S(1)} %bitcast.23, bf16[4,2,16,128]{3,2,1,0:T(8,128)(2,1)S(1)} %collective-permute-done.4.lon_even, bf16[4,2,16,128]{3,2,1,0:T(8,128)(2,1)S(1)} %collective-permute-done.5.lon_odd, ...), custom_call_target="tpu_custom_call" | custom-call | flops 1000 | bytes 1000000 | tf_op jit(solution)/shard_map/pallas_call | solution.py:441
  (20 shorter events, 0.0 us)
Async XLA Ops:
  24.6 2.3 %copy-start = (bf16[1,16,4,137,137]{4,2,3,1,0:T(4,128)(2,1)S(1)}, bf16[1,16,4,137,137]{4,2,3,1,0:T(4,128)(2,1)}, u32[]{:S(2)}) copy-start(bf16[1,16,4,137,137]{4,2,3,1,0:T(4,128)(2,1)} %param.11) | copy-start | bytes 7207300
  26.8 15.9 %copy-start.1 = (bf16[4,137,32,16]{1,3,2,0:T(8,128)(2,1)S(1)}, bf16[4,137,32,16]{1,3,2,0:T(8,128)(2,1)}, u32[]{:S(2)}) copy-start(bf16[4,137,32,16]{1,3,2,0:T(8,128)(2,1)} %param.8) | copy-start | bytes 1683460
  26.8 15.9 %copy-start.4 = (s32[97]{0:T(128)S(1)}, s32[97]{0:T(128)}, u32[]{:S(2)}) copy-start(s32[97]{0:T(128)} %get-tuple-element.21.plan) | copy-start | bytes 1168
  26.8 35.3 %copy-start.2 = (bf16[4,137,32,16]{1,3,2,0:T(8,128)(2,1)S(1)}, bf16[4,137,32,16]{1,3,2,0:T(8,128)(2,1)}, u32[]{:S(2)}) copy-start(bf16[4,137,32,16]{1,3,2,0:T(8,128)(2,1)} %param.9) | copy-start | bytes 1683460
  26.8 35.3 %copy-start.3 = (f32[4,32,16]{1,2,0:T(8,128)S(1)}, f32[4,32,16]{1,2,0:T(8,128)}, u32[]{:S(2)}) copy-start(f32[4,32,16]{1,2,0:T(8,128)} %param.10) | copy-start | bytes 24580
  42.7 38.8 %slice-start = ((s8[4489216]{0:T(1024)(128)(4,1)}), s8[4194304]{0:T(1024)(128)(4,1)S(1)}, s32[]{:S(2)}) async-start(s8[4489216]{0:T(1024)(128)(4,1)} %bitcast.14), calls=%async_computation.4 | async-start | bytes 8388608
  43.8 19.6 %collective-permute-start.2 = (bf16[4,2,32,128]{3,2,1,0:T(8,128)(2,1)S(1)}, bf16[4,2,32,128]{3,2,1,0:T(8,128)(2,1)S(1)}, u32[]{:S(2)}, u32[]{:S(2)}) collective-permute-start(bf16[4,2,32,128]{3,2,1,0:T(8,128)(2,1)S(1)} %get-tuple-element.27), channel_id=1, source_target_pairs={{0,1},{2,3},{4,5},{6,7},{8,9},{10,11},{12,13},{14,15},{16,17},{18,... | collective-permute-start | bytes 196616 | tf_op jit(solution)/shard_map/ppermute | solution.py:352
  46.1 17.3 %collective-permute-start.3 = (bf16[4,2,32,128]{3,2,1,0:T(8,128)(2,1)S(1)}, bf16[4,2,32,128]{3,2,1,0:T(8,128)(2,1)S(1)}, u32[]{:S(2)}, u32[]{:S(2)}) collective-permute-start(bf16[4,2,32,128]{3,2,1,0:T(8,128)(2,1)S(1)} %get-tuple-element.28), channel_id=1, source_target_pairs={{1,2},{3,4},{5,6},{7,8},{9,10},{11,12},{13,14},{15,16},{17,18},{19... | collective-permute-start | bytes 196616 | tf_op jit(solution)/shard_map/ppermute | solution.py:352
  48.2 15.1 %collective-permute-start = (bf16[4,2,16,128]{3,2,1,0:T(8,128)(2,1)S(1)}, bf16[4,2,16,128]{3,2,1,0:T(8,128)(2,1)S(1)}, u32[]{:S(2)}, u32[]{:S(2)}) collective-permute-start(bf16[4,2,16,128]{3,2,1,0:T(8,128)(2,1)S(1)} %get-tuple-element.25), channel_id=1, source_target_pairs={{0,32},{64,96},{128,160},{192,224},{256,288},{320,352},{384,416},{... | collective-permute-start | bytes 98312 | tf_op jit(solution)/shard_map/ppermute | solution.py:352
  51.4 12.0 %collective-permute-start.1 = (bf16[4,2,16,128]{3,2,1,0:T(8,128)(2,1)S(1)}, bf16[4,2,16,128]{3,2,1,0:T(8,128)(2,1)S(1)}, u32[]{:S(2)}, u32[]{:S(2)}) collective-permute-start(bf16[4,2,16,128]{3,2,1,0:T(8,128)(2,1)S(1)} %get-tuple-element.26), channel_id=1, source_target_pairs={{32,64},{96,128},{160,192},{224,256},{288,320},{352,384},{416,448}... | collective-permute-start | bytes 98312 | tf_op jit(solution)/shard_map/ppermute | solution.py:352
  62.1 19.4 %slice-start.1 = ((s8[4489216]{0:T(1024)(128)(4,1)}), s8[294912]{0:T(1024)(128)(4,1)S(1)}, s32[]{:S(2)}) async-start(s8[4489216]{0:T(1024)(128)(4,1)} %bitcast.14), calls=%async_computation.5 | async-start | bytes 589824
  98.1 13.9 %collective-permute-start.6 = (bf16[4,2,32,128]{3,2,1,0:T(8,128)(2,1)S(1)}, bf16[4,2,32,128]{3,2,1,0:T(8,128)(2,1)S(1)}, u32[]{:S(2)}, u32[]{:S(2)}) collective-permute-start(bf16[4,2,32,128]{3,2,1,0:T(8,128)(2,1)S(1)} %get-tuple-element.35), channel_id=1, source_target_pairs={{0,1},{2,3},{4,5},{6,7},{8,9},{10,11},{12,13},{14,15},{16,17},{18,... | collective-permute-start | bytes 196616 | tf_op jit(solution)/shard_map/ppermute | solution.py:352
  100.2 11.8 %collective-permute-start.7 = (bf16[4,2,32,128]{3,2,1,0:T(8,128)(2,1)S(1)}, bf16[4,2,32,128]{3,2,1,0:T(8,128)(2,1)S(1)}, u32[]{:S(2)}, u32[]{:S(2)}) collective-permute-start(bf16[4,2,32,128]{3,2,1,0:T(8,128)(2,1)S(1)} %get-tuple-element.36), channel_id=1, source_target_pairs={{1,2},{3,4},{5,6},{7,8},{9,10},{11,12},{13,14},{15,16},{17,18},{19... | collective-permute-start | bytes 196616 | tf_op jit(solution)/shard_map/ppermute | solution.py:352
  102.1 9.6 %collective-permute-start.4 = (bf16[4,2,16,128]{3,2,1,0:T(8,128)(2,1)S(1)}, bf16[4,2,16,128]{3,2,1,0:T(8,128)(2,1)S(1)}, u32[]{:S(2)}, u32[]{:S(2)}) collective-permute-start(bf16[4,2,16,128]{3,2,1,0:T(8,128)(2,1)S(1)} %get-tuple-element.33), channel_id=1, source_target_pairs={{0,32},{64,96},{128,160},{192,224},{256,288},{320,352},{384,416},{... | collective-permute-start | bytes 98312 | tf_op jit(solution)/shard_map/ppermute | solution.py:352
  104.0 7.9 %collective-permute-start.5 = (bf16[4,2,16,128]{3,2,1,0:T(8,128)(2,1)S(1)}, bf16[4,2,16,128]{3,2,1,0:T(8,128)(2,1)S(1)}, u32[]{:S(2)}, u32[]{:S(2)}) collective-permute-start(bf16[4,2,16,128]{3,2,1,0:T(8,128)(2,1)S(1)} %get-tuple-element.34), channel_id=1, source_target_pairs={{32,64},{96,128},{160,192},{224,256},{288,320},{352,384},{416,448}... | collective-permute-start | bytes 98312 | tf_op jit(solution)/shard_map/ppermute | solution.py:352

commit v7 on v6

--- a/solution.py
+++ b/solution.py
@@ -52,7 +52,7 @@
 
 
 def pack_first(
-    cols_hbm, count_hbm, owner_hbm, slot_hbm, late_hbm, outbox, plan, cols, count, owner, slot, late, pick, codes, wide, used, sems
+    cols_hbm, count_hbm, owner_hbm, slot_hbm, late_hbm, outbox, plan, cols, count, owner, slot, late, field, rows, codes, used, sems
 ):
     fields, _, levels = late.shape
     capacity = cols.shape[2]
@@ -65,23 +65,19 @@
         copy.start()
     for o in range(owners):
         used[o] = 0
-    pick[...] = jnp.zeros(pick.shape, F32)
+    rows[...] = jnp.zeros(rows.shape, F32)
     codes[...] = jnp.zeros(codes.shape, F32)
-    wide[...] = jnp.zeros(wide.shape, F32)
     for copy in copies[: len(small)]:
         copy.wait()
     live = count[0, 0]
     plan[0] = live
-    places = lax.broadcasted_iota(jnp.int32, (1, pick.shape[1]), 1)
 
     def route(e, carry):
         o = owner[0, 0, e]
         rank = used[o]
         used[o] = rank + 1
-        column = cols[0, 0, e]
-        plan[1 + e] = column
+        plan[1 + e] = cols[0, 0, e]
         plan[1 + capacity + e] = rank * (fields * owners) + o
-        pick[pl.ds(o * PAIR + rank, 1), :] = (places == column).astype(F32)
         codes[pl.ds(o * PAIR + rank, 1), :] = jnp.full((1, LANES), slot[0, 0, e] + 1, jnp.int32).astype(F32)
         return carry
 
@@ -94,15 +90,45 @@
         return carry
 
     lax.fori_loop(live, ((live + (GROUP - 1)) // GROUP) * GROUP, repeat, 0)
-    chosen = pick[...].astype(BF16)
-    rows, lanes = [], lax.broadcasted_iota(jnp.int32, codes.shape, 1)
-    tails = jnp.where(lanes == tail * fields, codes[...], 0.0)
     for f in range(fields):
         copies[len(small) + f].wait()
-        wide[:, :levels] = jnp.dot(chosen, late[f], preferred_element_type=F32)
-        rows.append(wide[:, :LANES])
-        tails = tails + tail_lanes(wide[...], tail * f)
-    outbox[...] = jnp.concatenate(rows + [tails], axis=1).astype(BF16).reshape(outbox.shape)
+        unpack_field(late, field, f)
+    gather_columns(plan, field, rows, owners)
+    lane = lax.broadcasted_iota(jnp.int32, codes.shape, 1)
+    pack_rows(rows, jnp.where(lane == tail * fields, codes[...], 0.0), tail, outbox)
+
+
+def gather_columns(plan, field, rows, owners):
+    fields, halves = field.shape[:2]
+
+    def body(entries):
+        found = []
+        for column, row in entries:
+            at = outbox_row(row, owners, fields)
+            for f in range(fields):
+                for h in range(halves):
+                    found.append((h, f * (PAIR * owners) + at, field[f, h, pl.ds(column, 1), :]))
+        for h, row, value in found:
+            rows[h, pl.ds(row, 1), :] = value
+
+    entry_groups(plan, body)
+
+
+def pack_rows(rows, tails, tail, outbox):
+    count = outbox.shape[0] * outbox.shape[1]
+    blocks = [slice(f * count, (f + 1) * count) for f in range(rows.shape[1] // count)]
+    tails = tails + side_by_side([rows[1, block] for block in blocks], tail)
+    packed = jnp.concatenate([rows[0, block] for block in blocks] + [tails], axis=1)
+    outbox[...] = packed.astype(BF16).reshape(outbox.shape)
+
+
+def side_by_side(ends, tail):
+    lane = lax.broadcasted_iota(jnp.int32, ends[0].shape, 1)
+    total = jnp.zeros(ends[0].shape, F32)
+    for f, end in enumerate(ends):
+        end = jnp.where(lane < tail, end, 0.0)
+        total = total + (pltpu.roll(end, tail * f, 1) if f else end)
+    return total
 
 
 def outbox_row(row, owners, fields):
@@ -201,19 +227,35 @@
             field[here] = value
 
     entry_groups(plan, body)
-    span_lat = lon_even.shape[2]
-    span_lon = lat_even.shape[2]
+    span_lon = lat_even.shape[1]
+    span_lat = columns_all // span_lon
     lon_up, lat_up = upward()
-    for f in range(fields):
-        for h in range(halves):
-            low = field[f, h, :span_lat].astype(BF16)
-            high = field[f, h, columns_all - span_lat :].astype(BF16)
-            lon_even[f, h] = jnp.where(lon_up, high, low)
-            lon_odd[f, h] = jnp.where(lon_up, low, high)
-            low = field[f, h, pl.ds(0, span_lon, stride=span_lat), :].astype(BF16)
-            high = field[f, h, pl.ds(span_lat - 1, span_lon, stride=span_lat), :].astype(BF16)
-            lat_even[f, h] = jnp.where(lat_up, high, low)
-            lat_odd[f, h] = jnp.where(lat_up, low, high)
+    places = edge_places(columns_all, span_lon)
+    lon_low, lon_high, lat_low, lat_high = [edge_blocks(field, place, tail) for place in places]
+    for up, even, odd, lows, highs in (
+        (lon_up, lon_even, lon_odd, lon_low, lon_high),
+        (lat_up, lat_even, lat_odd, lat_low, lat_high),
+    ):
+        for block, (low, high) in enumerate(zip(lows, highs)):
+            even[block, : low.shape[0]] = jnp.where(up, high, low).astype(BF16)
+            odd[block, : low.shape[0]] = jnp.where(up, low, high).astype(BF16)
+
+
+def edge_places(columns_all, span_lon):
+    span_lat = columns_all // span_lon
+    return (
+        slice(0, span_lat),
+        slice(columns_all - span_lat, columns_all),
+        pl.ds(0, span_lon, stride=span_lat),
+        pl.ds(span_lat - 1, span_lon, stride=span_lat),
+    )
+
+
+def edge_blocks(field, place, tail):
+    fields = field.shape[0]
+    return [field[f, 0, place, :] for f in range(fields)] + [
+        side_by_side([field[f, 1, place, :] for f in range(fields)], tail)
+    ]
 
 
 def upward():
@@ -272,66 +314,44 @@
     )
 
 
-def add_edges(f, h, weights, lon_even, lon_odd, lat_even, lat_odd, out):
-    columns_all = out.shape[2]
-    span_lat = lon_even.shape[2]
-    span_lon = lat_even.shape[2]
-    places = (
-        (slice(0, span_lat), slice(None)),
-        (slice(columns_all - span_lat, columns_all), slice(None)),
-        (pl.ds(0, span_lon, stride=span_lat), slice(None)),
-        (pl.ds(span_lat - 1, span_lon, stride=span_lat), slice(None)),
-    )
+def add_edges(f, weights, lon_even, lon_odd, lat_even, lat_odd, out, tail):
+    fields, _, columns_all, lanes = out.shape
+    span_lon = lat_even.shape[1]
+    span_lat = columns_all // span_lon
     lon_up, lat_up = upward()
-    edges = []
-    for up, even, odd in ((lon_up, lon_even, lon_odd), (lat_up, lat_even, lat_odd)):
-        first, second = even[f, h].astype(F32), odd[f, h].astype(F32)
-        edges += [jnp.where(up, second, first), jnp.where(up, first, second)]
-    for place, weight, edge in zip(places, weights, edges):
-        at = (f, h) + place
-        out[at] = out[at] + weight * edge
-
-
-def edges_first(plan, inner, coef, lon_even, lon_odd, lat_even, lat_odd, out, outbox, rows, *, levels):
+    for h, block in ((0, f), (1, fields)):
+        edges = []
+        for up, even, odd, count in ((lon_up, lon_even, lon_odd, span_lat), (lat_up, lat_even, lat_odd, span_lon)):
+            first, second = even[block, :count].astype(F32), odd[block, :count].astype(F32)
+            if h and f:
+                first, second = [pltpu.roll(edge, lanes - tail * f, 1) for edge in (first, second)]
+            edges += [jnp.where(up, second, first), jnp.where(up, first, second)]
+        for place, weight, edge in zip(edge_places(columns_all, span_lon), weights, edges):
+            at = (f, h, place, slice(None))
+            out[at] = out[at] + weight * edge
+
+
+def edges_first(plan, inner, coef, lon_odd, lon_even, lat_odd, lat_even, out, outbox, rows, *, levels):
     fields, halves, columns_all, lanes = out.shape
     owners = outbox.shape[0]
     tail = levels - lanes
     weights = edge_weights(coef)
     rows[...] = jnp.zeros(rows.shape, F32)
     for f in range(fields):
-        for h in range(halves):
-            add_edges(f, h, weights, lon_even, lon_odd, lat_even, lat_odd, out)
-
-    def body(entries):
-        found = []
-        for column, row in entries:
-            at = outbox_row(row, owners, fields)
-            for f in range(fields):
-                for h in range(halves):
-                    found.append((h, f * (PAIR * owners) + at, out[f, h, pl.ds(column, 1), :]))
-        for h, row, value in found:
-            rows[h, pl.ds(row, 1), :] = value
-
-    entry_groups(plan, body)
-    blocks = [slice(f * PAIR * owners, (f + 1) * PAIR * owners) for f in range(fields)]
-    lane = lax.broadcasted_iota(jnp.int32, (PAIR * owners, lanes), 1)
-    tails = jnp.zeros((PAIR * owners, lanes), F32)
-    for f in range(fields):
-        end = jnp.where(lane < tail, rows[1, blocks[f]], 0.0)
-        tails = tails + (pltpu.roll(end, tail * f, 1) if f else end)
-    packed = jnp.concatenate([rows[0, block] for block in blocks] + [tails], axis=1)
-    outbox[...] = packed.astype(BF16).reshape(outbox.shape)
-
-
-def edges_last(inner, coef, lon_even, lon_odd, lat_even, lat_odd, out_hbm, both, out, sems):
+        add_edges(f, weights, lon_even, lon_odd, lat_even, lat_odd, out, tail)
+
+    gather_columns(plan, out, rows, owners)
+    pack_rows(rows, 0.0, tail, outbox)
+
+
+def edges_last(inner, coef, lon_odd, lon_even, lat_odd, lat_even, out_hbm, both, out, sems):
     fields, halves, columns_all, lanes = inner.shape
     tail = out.shape[2] - lanes
     weights = edge_weights(coef)
     copies = []
     for f in range(fields):
-        for h in range(halves):
-            both[f, h] = inner[f, h]
-            add_edges(f, h, weights, lon_even, lon_odd, lat_even, lat_odd, both)
+        both[f] = inner[f]
+        add_edges(f, weights, lon_even, lon_odd, lat_even, lat_odd, both, tail)
         out[f, :, :lanes] = both[f, 0]
         out[f, :, lanes:] = both[f, 1, :, :tail]
         copies.append(pltpu.make_async_copy(out.at[f], out_hbm.at[f], sems.at[f]))
@@ -353,12 +373,11 @@
 
 
 def halos(lon_even, lon_odd, lat_even, lat_odd):
-    return (
-        swap(lon_even, "gx", 0, True),
-        swap(lon_odd, "gx", 1, True),
-        swap(lat_even, "gy", 0, False),
-        swap(lat_odd, "gy", 1, False),
-    )
+    lon_odd = swap(lon_odd, "gx", 1, True)
+    lon_even = swap(lon_even, "gx", 0, True)
+    lat_odd = swap(lat_odd, "gy", 1, False)
+    lat_even = swap(lat_even, "gy", 0, False)
+    return lon_odd, lon_even, lat_odd, lat_even
 
 
 def on_device(late, early, stencil_coef, jacobian, cloudy_cols, cloudy_count, owner_rank, owner_slot):
@@ -390,9 +409,9 @@
             SMEM(owner_rank.shape, jnp.int32),
             SMEM(owner_slot.shape, jnp.int32),
             VMEM(grid, BF16),
-            VMEM((groups * PAIR, columns_all), F32),
+            VMEM(halves, F32),
+            VMEM((2, inbox_rows, LANES), F32),
             VMEM((groups * PAIR, LANES), F32),
-            VMEM((groups * PAIR, 2 * LANES), F32),
             SMEM((groups,), jnp.int32),
             pltpu.SemaphoreType.DMA((4 + fields,)),
         ],
@@ -409,7 +428,7 @@
     )
     returned = exchange(answer)
 
-    edge_shapes = [shape((fields, 2, span, LANES), BF16) for span in (span_lat, span_lat, span_lon, span_lon)]
+    edge_shapes = [shape((fields + 1, span_lon, LANES), BF16)] * 4
 
     def add(kernel, returned, base, aliases):
         return call(

time: 115 us -> 111 us (0.965)
  starting transfers between devices: 30.8 us -> 26.9 us
    ppermute x8, starting transfers between devices: 30.8 us -> 26.9 us  [swap(): lax.ppermute(edge, axis, pairs + [(high, low) for low, high in pairs])]
where the time goes in v7:
time: 111 us; the launch traced here: 110 us
  blocking collectives  66.7 us (60%)
  starting transfers between devices  26.9 us (24%)
  Pallas kernels  12 us (11%)
  local copies, waits for them, and re-layouts  2.3 us (2%)
  waiting for transfers between devices  1.23 us (1%)
    all_to_all x4, blocking collectives, exchange(): return lax.all_to_all(lines, 'gy', split_axis=0, concat_axis=0, tiled=True)  66.7 us
    ppermute x8, starting transfers between devices, swap(): lax.ppermute(edge, axis, pairs + [(high, low) for low, high in pairs])  26.9 us
    unnamed x14, local copies, waits for them, and re-layouts  2.3 us
  transfers between devices with their start and end apart: 8, of which 2 were waited for; matrix products, arithmetic and copies ran while one was open for 0% of the time, Pallas kernels for 2%

profile of v7, /device:TPU:1, one launch (start us, length us, event | category | flops | bytes accessed | tf_op | source)
XLA Modules:
  0.0 110.0 jit_solution(6537442748249427689)
XLA Ops:
  0.7 2.2 %shard_map.82 = (bf16[32,2,640]{2,1,0:T(2,128)(2,1)}, s32[97]{0:T(128)}) custom-call(s32[1,1,48]{2,1,0:T(1,128)} %cols_hbm.1, s32[1,1]{1,0:T(1,128)S(6)} %copy.13.count_hbm, s32[1,1,48]{2,1,0:T(1,128)} %owner_hbm.1, s32[1,1,48]{2,1,0:T(1,128)} %slot_hbm.1, bf16[4,512,137]{2,1,0:T(8,128)(2,1)} %bitcast.17), custom_call_target="tpu_custom_call" | custom-call | flops 1000 | bytes 1000000 | tf_op jit(solution)/shard_map/pallas_call | solution.py:401
  2.8 21.3 %all_to_all.20.received = bf16[32,2,640]{2,1,0:T(2,128)(2,1)S(1)} all-to-all(bf16[32,2,640]{2,1,0:T(2,128)(2,1)} %get-tuple-element.22), channel_id=1, replica_groups=mesh['gx'=16,'gy'=32] {'gy'}, dimensions={0} | all-to-all | bytes 163840 | tf_op jit(solution)/shard_map/all_to_all | solution.py:364
  24.1 2.3 %copy-done = bf16[1,16,4,137,137]{4,2,3,1,0:T(4,128)(2,1)S(1)} copy-done((bf16[1,16,4,137,137]{4,2,3,1,0:T(4,128)(2,1)S(1)}, bf16[1,16,4,137,137]{4,2,3,1,0:T(4,128)(2,1)}, u32[]{:S(2)}) %copy-start) | copy-done | bytes 2402456
  26.4 1.5 %shard_map.83 = (f32[32,1,1152]{2,1,0:T(1,128)S(1)}, f32[64,64]{1,0:T(8,128)S(1)}) custom-call(bf16[32,2,640]{2,1,0:T(2,128)(2,1)S(1)} %all_to_all.20.received, bf16[16,137,4,137]{3,2,1,0:T(4,128)(2,1)S(1)} %bitcast.13), custom_call_target="tpu_custom_call" | custom-call | flops 1000 | bytes 1000000 | tf_op jit(solution)/shard_map/pallas_call | solution.py:426
  27.8 14.3 %all_to_all.21.returned = f32[32,1,1152]{2,1,0:T(1,128)S(1)} all-to-all(f32[32,1,1152]{2,1,0:T(1,128)S(1)} %get-tuple-element.23), channel_id=1, replica_groups=mesh['gx'=16,'gy'=32] {'gy'}, dimensions={0} | all-to-all | bytes 294912 | tf_op jit(solution)/shard_map/all_to_all | solution.py:364
  42.2 1.0 shard_map.84
  43.2 11.5 %collective-permute-start = (bf16[5,32,128]{2,1,0:T(8,128)(2,1)S(1)}, bf16[5,32,128]{2,1,0:T(8,128)(2,1)S(1)}, u32[]{:S(2)}, u32[]{:S(2)}) collective-permute-start(bf16[5,32,128]{2,1,0:T(8,128)(2,1)S(1)} %get-tuple-element.25), channel_id=1, source_target_pairs={{32,64},{96,128},{160,192},{224,256},{288,320},{352,384},{416,448}... | collective-permute-start | bytes 122888 | tf_op jit(solution)/shard_map/ppermute | solution.py:372
  54.7 1.9 %collective-permute-start.1 = (bf16[5,32,128]{2,1,0:T(8,128)(2,1)S(1)}, bf16[5,32,128]{2,1,0:T(8,128)(2,1)S(1)}, u32[]{:S(2)}, u32[]{:S(2)}) collective-permute-start(bf16[5,32,128]{2,1,0:T(8,128)(2,1)S(1)} %get-tuple-element.26), channel_id=1, source_target_pairs={{0,32},{64,96},{128,160},{192,224},{256,288},{320,352},{384,416},{... | collective-permute-start | bytes 122888 | tf_op jit(solution)/shard_map/ppermute | solution.py:372
  56.6 2.7 %collective-permute-start.2 = (bf16[5,32,128]{2,1,0:T(8,128)(2,1)S(1)}, bf16[5,32,128]{2,1,0:T(8,128)(2,1)S(1)}, u32[]{:S(2)}, u32[]{:S(2)}) collective-permute-start(bf16[5,32,128]{2,1,0:T(8,128)(2,1)S(1)} %get-tuple-element.27), channel_id=1, source_target_pairs={{1,2},{3,4},{5,6},{7,8},{9,10},{11,12},{13,14},{15,16},{17,18},{19... | collective-permute-start | bytes 122888 | tf_op jit(solution)/shard_map/ppermute | solution.py:372
  59.3 1.9 %collective-permute-start.3 = (bf16[5,32,128]{2,1,0:T(8,128)(2,1)S(1)}, bf16[5,32,128]{2,1,0:T(8,128)(2,1)S(1)}, u32[]{:S(2)}, u32[]{:S(2)}) collective-permute-start(bf16[5,32,128]{2,1,0:T(8,128)(2,1)S(1)} %get-tuple-element.28), channel_id=1, source_target_pairs={{0,1},{2,3},{4,5},{6,7},{8,9},{10,11},{12,13},{14,15},{16,17},{18,... | collective-permute-start | bytes 122888 | tf_op jit(solution)/shard_map/ppermute | solution.py:372
  61.3 1.2 %shard_map.85.inner = f32[4,2,512,128]{3,2,1,0:T(8,128)S(1)} custom-call(f32[4,2,512,128]{3,2,1,0:T(8,128)S(1)} %get-tuple-element.24.field, f32[4,16,32]{2,1,0:T(8,128)S(1)} %bitcast.20, bf16[4,512,137]{2,1,0:T(8,128)(2,1)S(1)} %bitcast.19), custom_call_target="tpu_custom_call" | custom-call | flops 1000 | bytes 6000000 | tf_op jit(solution)/shard_map/pallas_call | solution.py:445
  62.5 0.3 collective-permute-done.2.lat_odd
  62.8 1.0 shard_map.86
  63.9 16.3 %all_to_all.22.received = bf16[32,2,640]{2,1,0:T(2,128)(2,1)S(1)} all-to-all(bf16[32,2,640]{2,1,0:T(2,128)(2,1)S(1)} %get-tuple-element.29), channel_id=1, replica_groups=mesh['gx'=16,'gy'=32] {'gy'}, dimensions={0} | all-to-all | bytes 163840 | tf_op jit(solution)/shard_map/all_to_all | solution.py:364
  80.2 1.4 %shard_map.87 = f32[32,1,1152]{2,1,0:T(1,128)S(1)} custom-call(bf16[32,2,640]{2,1,0:T(2,128)(2,1)S(1)} %all_to_all.22.received, bf16[16,137,4,137]{3,2,1,0:T(4,128)(2,1)S(1)} %bitcast.16, f32[64,64]{1,0:T(8,128)S(1)} %get-tuple-element.30.chosen), custom_call_target="tpu_custom_call" | custom-call | flops 1000 | bytes 1000000 | tf_op jit(solution)/shard_map/pallas_call | solution.py:454
  81.6 14.8 %all_to_all.23.returned = f32[32,1,1152]{2,1,0:T(1,128)S(1)} all-to-all(f32[32,1,1152]{2,1,0:T(1,128)S(1)} %shard_map.87), channel_id=1, replica_groups=mesh['gx'=16,'gy'=32] {'gy'}, dimensions={0} | all-to-all | bytes 294912 | tf_op jit(solution)/shard_map/all_to_all | solution.py:364
  96.4 1.0 shard_map.88
  97.4 2.8 %collective-permute-start.4 = (bf16[5,32,128]{2,1,0:T(8,128)(2,1)S(1)}, bf16[5,32,128]{2,1,0:T(8,128)(2,1)S(1)}, u32[]{:S(2)}, u32[]{:S(2)}) collective-permute-start(bf16[5,32,128]{2,1,0:T(8,128)(2,1)S(1)} %get-tuple-element.33), channel_id=1, source_target_pairs={{32,64},{96,128},{160,192},{224,256},{288,320},{352,384},{416,448}... | collective-permute-start | bytes 122888 | tf_op jit(solution)/shard_map/ppermute | solution.py:372
  100.2 1.9 %collective-permute-start.5 = (bf16[5,32,128]{2,1,0:T(8,128)(2,1)S(1)}, bf16[5,32,128]{2,1,0:T(8,128)(2,1)S(1)}, u32[]{:S(2)}, u32[]{:S(2)}) collective-permute-start(bf16[5,32,128]{2,1,0:T(8,128)(2,1)S(1)} %get-tuple-element.34), channel_id=1, source_target_pairs={{0,32},{64,96},{128,160},{192,224},{256,288},{320,352},{384,416},{... | collective-permute-start | bytes 122888 | tf_op jit(solution)/shard_map/ppermute | solution.py:372
  102.1 2.3 %collective-permute-start.6 = (bf16[5,32,128]{2,1,0:T(8,128)(2,1)S(1)}, bf16[5,32,128]{2,1,0:T(8,128)(2,1)S(1)}, u32[]{:S(2)}, u32[]{:S(2)}) collective-permute-start(bf16[5,32,128]{2,1,0:T(8,128)(2,1)S(1)} %get-tuple-element.35), channel_id=1, source_target_pairs={{1,2},{3,4},{5,6},{7,8},{9,10},{11,12},{13,14},{15,16},{17,18},{19... | collective-permute-start | bytes 122888 | tf_op jit(solution)/shard_map/ppermute | solution.py:372
  104.4 1.9 %collective-permute-start.7 = (bf16[5,32,128]{2,1,0:T(8,128)(2,1)S(1)}, bf16[5,32,128]{2,1,0:T(8,128)(2,1)S(1)}, u32[]{:S(2)}, u32[]{:S(2)}) collective-permute-start(bf16[5,32,128]{2,1,0:T(8,128)(2,1)S(1)} %get-tuple-element.36), channel_id=1, source_target_pairs={{0,1},{2,3},{4,5},{6,7},{8,9},{10,11},{12,13},{14,15},{16,17},{18,... | collective-permute-start | bytes 122888 | tf_op jit(solution)/shard_map/ppermute | solution.py:372
  106.4 1.0 shard_map.89.inner
  107.4 0.9 collective-permute-done.6.lat_odd
  108.3 1.7 %shard_map.90 = f32[4,512,137]{2,1,0:T(8,128)} custom-call(f32[4,2,512,128]{3,2,1,0:T(8,128)S(1)} %shard_map.89.inner, f32[4,16,32]{2,1,0:T(8,128)S(1)} %bitcast.23, bf16[5,32,128]{2,1,0:T(8,128)(2,1)S(1)} %collective-permute-done.4.lon_odd, bf16[5,32,128]{2,1,0:T(8,128)(2,1)S(1)} %collective-permute-done.5.lon_even, ...), custom_call_target="tpu_custom_call" | custom-call | flops 1000 | bytes 1000000 | tf_op jit(solution)/shard_map/pallas_call | solution.py:460
  (20 shorter events, 0.0 us)
Async XLA Ops:
  24.1 2.3 %copy-start = (bf16[1,16,4,137,137]{4,2,3,1,0:T(4,128)(2,1)S(1)}, bf16[1,16,4,137,137]{4,2,3,1,0:T(4,128)(2,1)}, u32[]{:S(2)}) copy-start(bf16[1,16,4,137,137]{4,2,3,1,0:T(4,128)(2,1)} %param.11) | copy-start | bytes 7207300
  26.3 15.8 %copy-start.1 = (bf16[4,137,32,16]{1,3,2,0:T(8,128)(2,1)S(1)}, bf16[4,137,32,16]{1,3,2,0:T(8,128)(2,1)}, u32[]{:S(2)}) copy-start(bf16[4,137,32,16]{1,3,2,0:T(8,128)(2,1)} %param.8) | copy-start | bytes 1683460
  26.3 15.8 %copy-start.4 = (s32[97]{0:T(128)S(1)}, s32[97]{0:T(128)}, u32[]{:S(2)}) copy-start(s32[97]{0:T(128)} %get-tuple-element.21.plan) | copy-start | bytes 1168
  26.4 34.9 %copy-start.2 = (bf16[4,137,32,16]{1,3,2,0:T(8,128)(2,1)S(1)}, bf16[4,137,32,16]{1,3,2,0:T(8,128)(2,1)}, u32[]{:S(2)}) copy-start(bf16[4,137,32,16]{1,3,2,0:T(8,128)(2,1)} %param.9) | copy-start | bytes 1683460
  26.4 34.9 %copy-start.3 = (f32[4,32,16]{1,2,0:T(8,128)S(1)}, f32[4,32,16]{1,2,0:T(8,128)}, u32[]{:S(2)}) copy-start(f32[4,32,16]{1,2,0:T(8,128)} %param.10) | copy-start | bytes 24580
  42.2 38.0 %slice-start = ((s8[4489216]{0:T(1024)(128)(4,1)}), s8[4194304]{0:T(1024)(128)(4,1)S(1)}, s32[]{:S(2)}) async-start(s8[4489216]{0:T(1024)(128)(4,1)} %bitcast.14), calls=%async_computation.4 | async-start | bytes 8388608
  43.2 19.3 %collective-permute-start = (bf16[5,32,128]{2,1,0:T(8,128)(2,1)S(1)}, bf16[5,32,128]{2,1,0:T(8,128)(2,1)S(1)}, u32[]{:S(2)}, u32[]{:S(2)}) collective-permute-start(bf16[5,32,128]{2,1,0:T(8,128)(2,1)S(1)} %get-tuple-element.25), channel_id=1, source_target_pairs={{32,64},{96,128},{160,192},{224,256},{288,320},{352,384},{416,448}... | collective-permute-start | bytes 122888 | tf_op jit(solution)/shard_map/ppermute | solution.py:372
  54.7 7.8 %collective-permute-start.1 = (bf16[5,32,128]{2,1,0:T(8,128)(2,1)S(1)}, bf16[5,32,128]{2,1,0:T(8,128)(2,1)S(1)}, u32[]{:S(2)}, u32[]{:S(2)}) collective-permute-start(bf16[5,32,128]{2,1,0:T(8,128)(2,1)S(1)} %get-tuple-element.26), channel_id=1, source_target_pairs={{0,32},{64,96},{128,160},{192,224},{256,288},{320,352},{384,416},{... | collective-permute-start | bytes 122888 | tf_op jit(solution)/shard_map/ppermute | solution.py:372
  56.6 6.2 %collective-permute-start.2 = (bf16[5,32,128]{2,1,0:T(8,128)(2,1)S(1)}, bf16[5,32,128]{2,1,0:T(8,128)(2,1)S(1)}, u32[]{:S(2)}, u32[]{:S(2)}) collective-permute-start(bf16[5,32,128]{2,1,0:T(8,128)(2,1)S(1)} %get-tuple-element.27), channel_id=1, source_target_pairs={{1,2},{3,4},{5,6},{7,8},{9,10},{11,12},{13,14},{15,16},{17,18},{19... | collective-permute-start | bytes 122888 | tf_op jit(solution)/shard_map/ppermute | solution.py:372
  59.3 3.5 %collective-permute-start.3 = (bf16[5,32,128]{2,1,0:T(8,128)(2,1)S(1)}, bf16[5,32,128]{2,1,0:T(8,128)(2,1)S(1)}, u32[]{:S(2)}, u32[]{:S(2)}) collective-permute-start(bf16[5,32,128]{2,1,0:T(8,128)(2,1)S(1)} %get-tuple-element.28), channel_id=1, source_target_pairs={{0,1},{2,3},{4,5},{6,7},{8,9},{10,11},{12,13},{14,15},{16,17},{18,... | collective-permute-start | bytes 122888 | tf_op jit(solution)/shard_map/ppermute | solution.py:372
  61.3 18.9 %slice-start.1 = ((s8[4489216]{0:T(1024)(128)(4,1)}), s8[294912]{0:T(1024)(128)(4,1)S(1)}, s32[]{:S(2)}) async-start(s8[4489216]{0:T(1024)(128)(4,1)} %bitcast.14), calls=%async_computation.5 | async-start | bytes 589824
  97.4 10.0 %collective-permute-start.4 = (bf16[5,32,128]{2,1,0:T(8,128)(2,1)S(1)}, bf16[5,32,128]{2,1,0:T(8,128)(2,1)S(1)}, u32[]{:S(2)}, u32[]{:S(2)}) collective-permute-start(bf16[5,32,128]{2,1,0:T(8,128)(2,1)S(1)} %get-tuple-element.33), channel_id=1, source_target_pairs={{32,64},{96,128},{160,192},{224,256},{288,320},{352,384},{416,448}... | collective-permute-start | bytes 122888 | tf_op jit(solution)/shard_map/ppermute | solution.py:372
  100.2 7.3 %collective-permute-start.5 = (bf16[5,32,128]{2,1,0:T(8,128)(2,1)S(1)}, bf16[5,32,128]{2,1,0:T(8,128)(2,1)S(1)}, u32[]{:S(2)}, u32[]{:S(2)}) collective-permute-start(bf16[5,32,128]{2,1,0:T(8,128)(2,1)S(1)} %get-tuple-element.34), channel_id=1, source_target_pairs={{0,32},{64,96},{128,160},{192,224},{256,288},{320,352},{384,416},{... | collective-permute-start | bytes 122888 | tf_op jit(solution)/shard_map/ppermute | solution.py:372
  102.1 6.2 %collective-permute-start.6 = (bf16[5,32,128]{2,1,0:T(8,128)(2,1)S(1)}, bf16[5,32,128]{2,1,0:T(8,128)(2,1)S(1)}, u32[]{:S(2)}, u32[]{:S(2)}) collective-permute-start(bf16[5,32,128]{2,1,0:T(8,128)(2,1)S(1)} %get-tuple-element.35), channel_id=1, source_target_pairs={{1,2},{3,4},{5,6},{7,8},{9,10},{11,12},{13,14},{15,16},{17,18},{19... | collective-permute-start | bytes 122888 | tf_op jit(solution)/shard_map/ppermute | solution.py:372
  104.4 3.9 %collective-permute-start.7 = (bf16[5,32,128]{2,1,0:T(8,128)(2,1)S(1)}, bf16[5,32,128]{2,1,0:T(8,128)(2,1)S(1)}, u32[]{:S(2)}, u32[]{:S(2)}) collective-permute-start(bf16[5,32,128]{2,1,0:T(8,128)(2,1)S(1)} %get-tuple-element.36), channel_id=1, source_target_pairs={{0,1},{2,3},{4,5},{6,7},{8,9},{10,11},{12,13},{14,15},{16,17},{18,... | collective-permute-start | bytes 122888 | tf_op jit(solution)/shard_map/ppermute | solution.py:372

commit v8 on v7

--- a/solution.py
+++ b/solution.py
@@ -237,8 +237,8 @@
         (lat_up, lat_even, lat_odd, lat_low, lat_high),
     ):
         for block, (low, high) in enumerate(zip(lows, highs)):
-            even[block, : low.shape[0]] = jnp.where(up, high, low).astype(BF16)
-            odd[block, : low.shape[0]] = jnp.where(up, low, high).astype(BF16)
+            even[block, : low.shape[0]] = jnp.where(up, high, low).astype(even.dtype)
+            odd[block, : low.shape[0]] = jnp.where(up, low, high).astype(odd.dtype)
 
 
 def edge_places(columns_all, span_lon):
@@ -350,7 +350,6 @@
     weights = edge_weights(coef)
     copies = []
     for f in range(fields):
-        both[f] = inner[f]
         add_edges(f, weights, lon_even, lon_odd, lat_even, lat_odd, both, tail)
         out[f, :, :lanes] = both[f, 0]
         out[f, :, lanes:] = both[f, 1, :, :tail]
@@ -428,19 +427,17 @@
     )
     returned = exchange(answer)
 
-    edge_shapes = [shape((fields + 1, span_lon, LANES), BF16)] * 4
-
-    def add(kernel, returned, base, aliases):
+    def add(kernel, returned, base, aliases, edge_type):
         return call(
             functools.partial(kernel, levels=levels),
-            [shape(halves, F32)] + edge_shapes,
+            [shape(halves, F32)] + [shape((fields + 1, span_lon, LANES), edge_type)] * 4,
             [SMEM] + [VMEM] * 2,
             [VMEM] * 5,
             [VMEM((2, inbox_rows, LANES), F32)],
             aliases,
         )(plan, returned, base)
 
-    field, *edges = add(add_first, returned, late, {})
+    field, *edges = add(add_first, returned, late, {}, F32)
     neighbours = halos(*edges)
     (inner,) = call(inner_first, [shape(halves, F32)], [VMEM] * 3, [VMEM], touched=6000000)(field, coef, early)
     adjoint, outbox = call(
@@ -454,15 +451,16 @@
     (answer,) = call(physics_second, [answer_shape], [VMEM] * 3, [VMEM], spaces)(
         exchange(outbox), matrices, chosen
     )
-    field, *edges = add(add_increments, exchange(answer), adjoint, {2: 0})
+    field, *edges = add(add_increments, exchange(answer), adjoint, {2: 0}, BF16)
     neighbours = halos(*edges)
     (inner,) = call(inner_last, [shape(halves, F32)], [VMEM] * 2, [VMEM], touched=6000000)(field, coef)
-    (final,) = call(
+    final, _ = call(
         edges_last,
-        [shape(grid, F32)],
+        [shape(grid, F32), shape(halves, F32)],
         [VMEM] * 6,
-        [HBM],
-        [VMEM(halves, F32), VMEM(grid, F32), pltpu.SemaphoreType.DMA((fields,))],
+        [HBM, VMEM],
+        [VMEM(grid, F32), pltpu.SemaphoreType.DMA((fields,))],
+        {0: 1},
     )(inner, coef, *neighbours)
     return final.reshape(fields, span_lon, span_lat, levels).transpose(0, 3, 1, 2)
 

time: 111 us -> 111 us (level)
  no operation moved by 1% of the time
where the time goes in v8:
time: 111 us
  blocking collectives  66.7 us (60%)
  starting transfers between devices  27.2 us (25%)
  Pallas kernels  12 us (11%)
  local copies, waits for them, and re-layouts  2.3 us (2%)
  waiting for transfers between devices  1.73 us (2%)
    all_to_all x4, blocking collectives, exchange(): return lax.all_to_all(lines, 'gy', split_axis=0, concat_axis=0, tiled=True)  66.7 us
    ppermute x8, starting transfers between devices, swap(): lax.ppermute(edge, axis, pairs + [(high, low) for low, high in pairs])  27.2 us
    unnamed x14, local copies, waits for them, and re-layouts  2.3 us
  transfers between devices with their start and end apart: 8, of which 2 were waited for; matrix products, arithmetic and copies ran while one was open for 0% of the time, Pallas kernels for 2%

profile of v8, /device:TPU:1, one launch (start us, length us, event | category | flops | bytes accessed | tf_op | source)
XLA Modules:
  0.0 110.7 jit_solution(11349482803734139200)
XLA Ops:
  0.7 2.2 %shard_map.82 = (bf16[32,2,640]{2,1,0:T(2,128)(2,1)}, s32[97]{0:T(128)}) custom-call(s32[1,1,48]{2,1,0:T(1,128)} %cols_hbm.1, s32[1,1]{1,0:T(1,128)S(6)} %copy.15.count_hbm, s32[1,1,48]{2,1,0:T(1,128)} %owner_hbm.1, s32[1,1,48]{2,1,0:T(1,128)} %slot_hbm.1, bf16[4,512,137]{2,1,0:T(8,128)(2,1)} %bitcast.17), custom_call_target="tpu_custom_call" | custom-call | flops 1000 | bytes 1000000 | tf_op jit(solution)/shard_map/pallas_call | solution.py:400
  2.8 21.2 %all_to_all.20.received = bf16[32,2,640]{2,1,0:T(2,128)(2,1)S(1)} all-to-all(bf16[32,2,640]{2,1,0:T(2,128)(2,1)} %get-tuple-element.23), channel_id=1, replica_groups=mesh['gx'=16,'gy'=32] {'gy'}, dimensions={0} | all-to-all | bytes 163840 | tf_op jit(solution)/shard_map/all_to_all | solution.py:363
  24.1 2.3 %copy-done = bf16[1,16,4,137,137]{4,2,3,1,0:T(4,128)(2,1)S(1)} copy-done((bf16[1,16,4,137,137]{4,2,3,1,0:T(4,128)(2,1)S(1)}, bf16[1,16,4,137,137]{4,2,3,1,0:T(4,128)(2,1)}, u32[]{:S(2)}) %copy-start) | copy-done | bytes 2402456
  26.3 1.5 %shard_map.83 = (f32[32,1,1152]{2,1,0:T(1,128)S(1)}, f32[64,64]{1,0:T(8,128)S(1)}) custom-call(bf16[32,2,640]{2,1,0:T(2,128)(2,1)S(1)} %all_to_all.20.received, bf16[16,137,4,137]{3,2,1,0:T(4,128)(2,1)S(1)} %bitcast.13), custom_call_target="tpu_custom_call" | custom-call | flops 1000 | bytes 1000000 | tf_op jit(solution)/shard_map/pallas_call | solution.py:425
  27.8 14.4 %all_to_all.21.returned = f32[32,1,1152]{2,1,0:T(1,128)S(1)} all-to-all(f32[32,1,1152]{2,1,0:T(1,128)S(1)} %get-tuple-element.24), channel_id=1, replica_groups=mesh['gx'=16,'gy'=32] {'gy'}, dimensions={0} | all-to-all | bytes 294912 | tf_op jit(solution)/shard_map/all_to_all | solution.py:363
  42.2 1.0 shard_map.84
  43.3 11.8 %collective-permute-start = (f32[5,32,128]{2,1,0:T(8,128)S(1)}, f32[5,32,128]{2,1,0:T(8,128)S(1)}, u32[]{:S(2)}, u32[]{:S(2)}) collective-permute-start(f32[5,32,128]{2,1,0:T(8,128)S(1)} %get-tuple-element.26), channel_id=1, source_target_pairs={{32,64},{96,128},{160,192},{224,256},{288,320},{352,384},{416,448}... | collective-permute-start | bytes 245768 | tf_op jit(solution)/shard_map/ppermute | solution.py:371
  55.1 1.9 %collective-permute-start.1 = (f32[5,32,128]{2,1,0:T(8,128)S(1)}, f32[5,32,128]{2,1,0:T(8,128)S(1)}, u32[]{:S(2)}, u32[]{:S(2)}) collective-permute-start(f32[5,32,128]{2,1,0:T(8,128)S(1)} %get-tuple-element.27), channel_id=1, source_target_pairs={{0,32},{64,96},{128,160},{192,224},{256,288},{320,352},{384,416},{... | collective-permute-start | bytes 245768 | tf_op jit(solution)/shard_map/ppermute | solution.py:371
  57.0 2.7 %collective-permute-start.2 = (f32[5,32,128]{2,1,0:T(8,128)S(1)}, f32[5,32,128]{2,1,0:T(8,128)S(1)}, u32[]{:S(2)}, u32[]{:S(2)}) collective-permute-start(f32[5,32,128]{2,1,0:T(8,128)S(1)} %get-tuple-element.28), channel_id=1, source_target_pairs={{1,2},{3,4},{5,6},{7,8},{9,10},{11,12},{13,14},{15,16},{17,18},{19... | collective-permute-start | bytes 245768 | tf_op jit(solution)/shard_map/ppermute | solution.py:371
  59.7 1.9 %collective-permute-start.3 = (f32[5,32,128]{2,1,0:T(8,128)S(1)}, f32[5,32,128]{2,1,0:T(8,128)S(1)}, u32[]{:S(2)}, u32[]{:S(2)}) collective-permute-start(f32[5,32,128]{2,1,0:T(8,128)S(1)} %get-tuple-element.29), channel_id=1, source_target_pairs={{0,1},{2,3},{4,5},{6,7},{8,9},{10,11},{12,13},{14,15},{16,17},{18,... | collective-permute-start | bytes 245768 | tf_op jit(solution)/shard_map/ppermute | solution.py:371
  61.6 1.2 %shard_map.85.inner = f32[4,2,512,128]{3,2,1,0:T(8,128)S(1)} custom-call(f32[4,2,512,128]{3,2,1,0:T(8,128)S(1)} %get-tuple-element.25.field, f32[4,16,32]{2,1,0:T(8,128)S(1)} %bitcast.20, bf16[4,512,137]{2,1,0:T(8,128)(2,1)S(1)} %bitcast.19), custom_call_target="tpu_custom_call" | custom-call | flops 1000 | bytes 6000000 | tf_op jit(solution)/shard_map/pallas_call | solution.py:442
  62.8 0.8 collective-permute-done.2.lat_odd
  63.6 1.0 shard_map.86
  64.7 16.2 %all_to_all.22.received = bf16[32,2,640]{2,1,0:T(2,128)(2,1)S(1)} all-to-all(bf16[32,2,640]{2,1,0:T(2,128)(2,1)S(1)} %get-tuple-element.30), channel_id=1, replica_groups=mesh['gx'=16,'gy'=32] {'gy'}, dimensions={0} | all-to-all | bytes 163840 | tf_op jit(solution)/shard_map/all_to_all | solution.py:363
  80.9 1.4 %shard_map.87 = f32[32,1,1152]{2,1,0:T(1,128)S(1)} custom-call(bf16[32,2,640]{2,1,0:T(2,128)(2,1)S(1)} %all_to_all.22.received, bf16[16,137,4,137]{3,2,1,0:T(4,128)(2,1)S(1)} %bitcast.16, f32[64,64]{1,0:T(8,128)S(1)} %get-tuple-element.31.chosen), custom_call_target="tpu_custom_call" | custom-call | flops 1000 | bytes 1000000 | tf_op jit(solution)/shard_map/pallas_call | solution.py:451
  82.3 14.8 %all_to_all.23.returned = f32[32,1,1152]{2,1,0:T(1,128)S(1)} all-to-all(f32[32,1,1152]{2,1,0:T(1,128)S(1)} %shard_map.87), channel_id=1, replica_groups=mesh['gx'=16,'gy'=32] {'gy'}, dimensions={0} | all-to-all | bytes 294912 | tf_op jit(solution)/shard_map/all_to_all | solution.py:363
  97.2 1.0 shard_map.88
  98.1 2.4 %collective-permute-start.4 = (bf16[5,32,128]{2,1,0:T(8,128)(2,1)S(1)}, bf16[5,32,128]{2,1,0:T(8,128)(2,1)S(1)}, u32[]{:S(2)}, u32[]{:S(2)}) collective-permute-start(bf16[5,32,128]{2,1,0:T(8,128)(2,1)S(1)} %get-tuple-element.34), channel_id=1, source_target_pairs={{32,64},{96,128},{160,192},{224,256},{288,320},{352,384},{416,448}... | collective-permute-start | bytes 122888 | tf_op jit(solution)/shard_map/ppermute | solution.py:371
  100.6 2.2 %collective-permute-start.5 = (bf16[5,32,128]{2,1,0:T(8,128)(2,1)S(1)}, bf16[5,32,128]{2,1,0:T(8,128)(2,1)S(1)}, u32[]{:S(2)}, u32[]{:S(2)}) collective-permute-start(bf16[5,32,128]{2,1,0:T(8,128)(2,1)S(1)} %get-tuple-element.35), channel_id=1, source_target_pairs={{0,32},{64,96},{128,160},{192,224},{256,288},{320,352},{384,416},{... | collective-permute-start | bytes 122888 | tf_op jit(solution)/shard_map/ppermute | solution.py:371
  102.8 2.3 %collective-permute-start.6 = (bf16[5,32,128]{2,1,0:T(8,128)(2,1)S(1)}, bf16[5,32,128]{2,1,0:T(8,128)(2,1)S(1)}, u32[]{:S(2)}, u32[]{:S(2)}) collective-permute-start(bf16[5,32,128]{2,1,0:T(8,128)(2,1)S(1)} %get-tuple-element.36), channel_id=1, source_target_pairs={{1,2},{3,4},{5,6},{7,8},{9,10},{11,12},{13,14},{15,16},{17,18},{19... | collective-permute-start | bytes 122888 | tf_op jit(solution)/shard_map/ppermute | solution.py:371
  105.1 1.9 %collective-permute-start.7 = (bf16[5,32,128]{2,1,0:T(8,128)(2,1)S(1)}, bf16[5,32,128]{2,1,0:T(8,128)(2,1)S(1)}, u32[]{:S(2)}, u32[]{:S(2)}) collective-permute-start(bf16[5,32,128]{2,1,0:T(8,128)(2,1)S(1)} %get-tuple-element.37), channel_id=1, source_target_pairs={{0,1},{2,3},{4,5},{6,7},{8,9},{10,11},{12,13},{14,15},{16,17},{18,... | collective-permute-start | bytes 122888 | tf_op jit(solution)/shard_map/ppermute | solution.py:371
  107.1 1.0 shard_map.89.inner
  108.1 0.9 collective-permute-done.6.lat_odd
  109.0 1.6 %shard_map.90 = (f32[4,512,137]{2,1,0:T(8,128)}, f32[4,2,512,128]{3,2,1,0:T(8,128)S(1)}) custom-call(f32[4,2,512,128]{3,2,1,0:T(8,128)S(1)} %shard_map.89.inner, f32[4,16,32]{2,1,0:T(8,128)S(1)} %bitcast.23, bf16[5,32,128]{2,1,0:T(8,128)(2,1)S(1)} %collective-permute-done.4.lon_odd, ...), custom_call_target="tpu_custom_call", output_to_operand_aliasing={{1}: (0, {})} | custom-call | flops 1000 | bytes 1000000 | tf_op jit(solution)/shard_map/pallas_call | solution.py:457
  (20 shorter events, 0.0 us)
Async XLA Ops:
  24.1 2.3 %copy-start = (bf16[1,16,4,137,137]{4,2,3,1,0:T(4,128)(2,1)S(1)}, bf16[1,16,4,137,137]{4,2,3,1,0:T(4,128)(2,1)}, u32[]{:S(2)}) copy-start(bf16[1,16,4,137,137]{4,2,3,1,0:T(4,128)(2,1)} %param.11) | copy-start | bytes 7207300
  26.3 15.9 %copy-start.1 = (bf16[4,137,32,16]{1,3,2,0:T(8,128)(2,1)S(1)}, bf16[4,137,32,16]{1,3,2,0:T(8,128)(2,1)}, u32[]{:S(2)}) copy-start(bf16[4,137,32,16]{1,3,2,0:T(8,128)(2,1)} %param.8) | copy-start | bytes 1683460
  26.3 15.9 %copy-start.4 = (s32[97]{0:T(128)S(1)}, s32[97]{0:T(128)}, u32[]{:S(2)}) copy-start(s32[97]{0:T(128)} %get-tuple-element.22.plan) | copy-start | bytes 1168
  26.3 35.3 %copy-start.2 = (bf16[4,137,32,16]{1,3,2,0:T(8,128)(2,1)S(1)}, bf16[4,137,32,16]{1,3,2,0:T(8,128)(2,1)}, u32[]{:S(2)}) copy-start(bf16[4,137,32,16]{1,3,2,0:T(8,128)(2,1)} %param.9) | copy-start | bytes 1683460
  26.3 35.3 %copy-start.3 = (f32[4,32,16]{1,2,0:T(8,128)S(1)}, f32[4,32,16]{1,2,0:T(8,128)}, u32[]{:S(2)}) copy-start(f32[4,32,16]{1,2,0:T(8,128)} %param.10) | copy-start | bytes 24580
  42.2 38.7 %slice-start = ((s8[4489216]{0:T(1024)(128)(4,1)}), s8[4194304]{0:T(1024)(128)(4,1)S(1)}, s32[]{:S(2)}) async-start(s8[4489216]{0:T(1024)(128)(4,1)} %bitcast.14), calls=%async_computation.4 | async-start | bytes 8388608
  43.3 19.5 %collective-permute-start = (f32[5,32,128]{2,1,0:T(8,128)S(1)}, f32[5,32,128]{2,1,0:T(8,128)S(1)}, u32[]{:S(2)}, u32[]{:S(2)}) collective-permute-start(f32[5,32,128]{2,1,0:T(8,128)S(1)} %get-tuple-element.26), channel_id=1, source_target_pairs={{32,64},{96,128},{160,192},{224,256},{288,320},{352,384},{416,448}... | collective-permute-start | bytes 245768 | tf_op jit(solution)/shard_map/ppermute | solution.py:371
  55.1 7.8 %collective-permute-start.1 = (f32[5,32,128]{2,1,0:T(8,128)S(1)}, f32[5,32,128]{2,1,0:T(8,128)S(1)}, u32[]{:S(2)}, u32[]{:S(2)}) collective-permute-start(f32[5,32,128]{2,1,0:T(8,128)S(1)} %get-tuple-element.27), channel_id=1, source_target_pairs={{0,32},{64,96},{128,160},{192,224},{256,288},{320,352},{384,416},{... | collective-permute-start | bytes 245768 | tf_op jit(solution)/shard_map/ppermute | solution.py:371
  57.0 6.7 %collective-permute-start.2 = (f32[5,32,128]{2,1,0:T(8,128)S(1)}, f32[5,32,128]{2,1,0:T(8,128)S(1)}, u32[]{:S(2)}, u32[]{:S(2)}) collective-permute-start(f32[5,32,128]{2,1,0:T(8,128)S(1)} %get-tuple-element.28), channel_id=1, source_target_pairs={{1,2},{3,4},{5,6},{7,8},{9,10},{11,12},{13,14},{15,16},{17,18},{19... | collective-permute-start | bytes 245768 | tf_op jit(solution)/shard_map/ppermute | solution.py:371
  59.7 4.0 %collective-permute-start.3 = (f32[5,32,128]{2,1,0:T(8,128)S(1)}, f32[5,32,128]{2,1,0:T(8,128)S(1)}, u32[]{:S(2)}, u32[]{:S(2)}) collective-permute-start(f32[5,32,128]{2,1,0:T(8,128)S(1)} %get-tuple-element.29), channel_id=1, source_target_pairs={{0,1},{2,3},{4,5},{6,7},{8,9},{10,11},{12,13},{14,15},{16,17},{18,... | collective-permute-start | bytes 245768 | tf_op jit(solution)/shard_map/ppermute | solution.py:371
  61.6 19.3 %slice-start.1 = ((s8[4489216]{0:T(1024)(128)(4,1)}), s8[294912]{0:T(1024)(128)(4,1)S(1)}, s32[]{:S(2)}) async-start(s8[4489216]{0:T(1024)(128)(4,1)} %bitcast.14), calls=%async_computation.5 | async-start | bytes 589824
  98.1 10.0 %collective-permute-start.4 = (bf16[5,32,128]{2,1,0:T(8,128)(2,1)S(1)}, bf16[5,32,128]{2,1,0:T(8,128)(2,1)S(1)}, u32[]{:S(2)}, u32[]{:S(2)}) collective-permute-start(bf16[5,32,128]{2,1,0:T(8,128)(2,1)S(1)} %get-tuple-element.34), channel_id=1, source_target_pairs={{32,64},{96,128},{160,192},{224,256},{288,320},{352,384},{416,448}... | collective-permute-start | bytes 122888 | tf_op jit(solution)/shard_map/ppermute | solution.py:371
  100.6 7.6 %collective-permute-start.5 = (bf16[5,32,128]{2,1,0:T(8,128)(2,1)S(1)}, bf16[5,32,128]{2,1,0:T(8,128)(2,1)S(1)}, u32[]{:S(2)}, u32[]{:S(2)}) collective-permute-start(bf16[5,32,128]{2,1,0:T(8,128)(2,1)S(1)} %get-tuple-element.35), channel_id=1, source_target_pairs={{0,32},{64,96},{128,160},{192,224},{256,288},{320,352},{384,416},{... | collective-permute-start | bytes 122888 | tf_op jit(solution)/shard_map/ppermute | solution.py:371
  102.8 6.2 %collective-permute-start.6 = (bf16[5,32,128]{2,1,0:T(8,128)(2,1)S(1)}, bf16[5,32,128]{2,1,0:T(8,128)(2,1)S(1)}, u32[]{:S(2)}, u32[]{:S(2)}) collective-permute-start(bf16[5,32,128]{2,1,0:T(8,128)(2,1)S(1)} %get-tuple-element.36), channel_id=1, source_target_pairs={{1,2},{3,4},{5,6},{7,8},{9,10},{11,12},{13,14},{15,16},{17,18},{19... | collective-permute-start | bytes 122888 | tf_op jit(solution)/shard_map/ppermute | solution.py:371
  105.1 3.9 %collective-permute-start.7 = (bf16[5,32,128]{2,1,0:T(8,128)(2,1)S(1)}, bf16[5,32,128]{2,1,0:T(8,128)(2,1)S(1)}, u32[]{:S(2)}, u32[]{:S(2)}) collective-permute-start(bf16[5,32,128]{2,1,0:T(8,128)(2,1)S(1)} %get-tuple-element.37), channel_id=1, source_target_pairs={{0,1},{2,3},{4,5},{6,7},{8,9},{10,11},{12,13},{14,15},{16,17},{18,... | collective-permute-start | bytes 122888 | tf_op jit(solution)/shard_map/ppermute | solution.py:371

commit v9 on v8

--- a/solution.py
+++ b/solution.py
@@ -331,7 +331,7 @@
             out[at] = out[at] + weight * edge
 
 
-def edges_first(plan, inner, coef, lon_odd, lon_even, lat_odd, lat_even, out, outbox, rows, *, levels):
+def edges_first(plan, inner, coef, lon_odd, lat_odd, lon_even, lat_even, out, outbox, rows, *, levels):
     fields, halves, columns_all, lanes = out.shape
     owners = outbox.shape[0]
     tail = levels - lanes
@@ -344,7 +344,7 @@
     pack_rows(rows, 0.0, tail, outbox)
 
 
-def edges_last(inner, coef, lon_odd, lon_even, lat_odd, lat_even, out_hbm, both, out, sems):
+def edges_last(inner, coef, lon_odd, lat_odd, lon_even, lat_even, out_hbm, both, out, sems):
     fields, halves, columns_all, lanes = inner.shape
     tail = out.shape[2] - lanes
     weights = edge_weights(coef)
@@ -373,10 +373,10 @@
 
 def halos(lon_even, lon_odd, lat_even, lat_odd):
     lon_odd = swap(lon_odd, "gx", 1, True)
+    lat_odd = swap(lat_odd, "gy", 1, False)
     lon_even = swap(lon_even, "gx", 0, True)
-    lat_odd = swap(lat_odd, "gy", 1, False)
     lat_even = swap(lat_even, "gy", 0, False)
-    return lon_odd, lon_even, lat_odd, lat_even
+    return lon_odd, lat_odd, lon_even, lat_even
 
 
 def on_device(late, early, stencil_coef, jacobian, cloudy_cols, cloudy_count, owner_rank, owner_slot):

time: 111 us -> 110 us (level)
  no operation moved by 1% of the time
where the time goes in v9:
time: 110 us
  blocking collectives  66.5 us (60%)
  starting transfers between devices  27.3 us (25%)
  Pallas kernels  12 us (11%)
  local copies, waits for them, and re-layouts  2.3 us (2%)
    all_to_all x4, blocking collectives, exchange(): return lax.all_to_all(lines, 'gy', split_axis=0, concat_axis=0, tiled=True)  66.5 us
    ppermute x8, starting transfers between devices, swap(): lax.ppermute(edge, axis, pairs + [(high, low) for low, high in pairs])  27.3 us
    unnamed x14, local copies, waits for them, and re-layouts  2.3 us
  transfers between devices with their start and end apart: 8, of which 2 were waited for; matrix products, arithmetic and copies ran while one was open for 0% of the time, Pallas kernels for 2%

profile of v9, /device:TPU:1, one launch (start us, length us, event | category | flops | bytes accessed | tf_op | source)
XLA Modules:
  0.0 109.6 jit_solution(8581376956959767790)
XLA Ops:
  0.7 2.2 %shard_map.82 = (bf16[32,2,640]{2,1,0:T(2,128)(2,1)}, s32[97]{0:T(128)}) custom-call(s32[1,1,48]{2,1,0:T(1,128)} %cols_hbm.1, s32[1,1]{1,0:T(1,128)S(6)} %copy.15.count_hbm, s32[1,1,48]{2,1,0:T(1,128)} %owner_hbm.1, s32[1,1,48]{2,1,0:T(1,128)} %slot_hbm.1, bf16[4,512,137]{2,1,0:T(8,128)(2,1)} %bitcast.17), custom_call_target="tpu_custom_call" | custom-call | flops 1000 | bytes 1000000 | tf_op jit(solution)/shard_map/pallas_call | solution.py:400
  2.8 21.3 %all_to_all.20.received = bf16[32,2,640]{2,1,0:T(2,128)(2,1)S(1)} all-to-all(bf16[32,2,640]{2,1,0:T(2,128)(2,1)} %get-tuple-element.23), channel_id=1, replica_groups=mesh['gx'=16,'gy'=32] {'gy'}, dimensions={0} | all-to-all | bytes 163840 | tf_op jit(solution)/shard_map/all_to_all | solution.py:363
  24.1 2.3 %copy-done = bf16[1,16,4,137,137]{4,2,3,1,0:T(4,128)(2,1)S(1)} copy-done((bf16[1,16,4,137,137]{4,2,3,1,0:T(4,128)(2,1)S(1)}, bf16[1,16,4,137,137]{4,2,3,1,0:T(4,128)(2,1)}, u32[]{:S(2)}) %copy-start) | copy-done | bytes 2402456
  26.4 1.5 %shard_map.83 = (f32[32,1,1152]{2,1,0:T(1,128)S(1)}, f32[64,64]{1,0:T(8,128)S(1)}) custom-call(bf16[32,2,640]{2,1,0:T(2,128)(2,1)S(1)} %all_to_all.20.received, bf16[16,137,4,137]{3,2,1,0:T(4,128)(2,1)S(1)} %bitcast.13), custom_call_target="tpu_custom_call" | custom-call | flops 1000 | bytes 1000000 | tf_op jit(solution)/shard_map/pallas_call | solution.py:425
  27.9 14.4 %all_to_all.21.returned = f32[32,1,1152]{2,1,0:T(1,128)S(1)} all-to-all(f32[32,1,1152]{2,1,0:T(1,128)S(1)} %get-tuple-element.24), channel_id=1, replica_groups=mesh['gx'=16,'gy'=32] {'gy'}, dimensions={0} | all-to-all | bytes 294912 | tf_op jit(solution)/shard_map/all_to_all | solution.py:363
  42.3 1.0 shard_map.84
  43.3 11.4 %collective-permute-start = (f32[5,32,128]{2,1,0:T(8,128)S(1)}, f32[5,32,128]{2,1,0:T(8,128)S(1)}, u32[]{:S(2)}, u32[]{:S(2)}) collective-permute-start(f32[5,32,128]{2,1,0:T(8,128)S(1)} %get-tuple-element.26), channel_id=1, source_target_pairs={{32,64},{96,128},{160,192},{224,256},{288,320},{352,384},{416,448}... | collective-permute-start | bytes 245768 | tf_op jit(solution)/shard_map/ppermute | solution.py:371
  54.8 2.7 %collective-permute-start.1 = (f32[5,32,128]{2,1,0:T(8,128)S(1)}, f32[5,32,128]{2,1,0:T(8,128)S(1)}, u32[]{:S(2)}, u32[]{:S(2)}) collective-permute-start(f32[5,32,128]{2,1,0:T(8,128)S(1)} %get-tuple-element.27), channel_id=1, source_target_pairs={{1,2},{3,4},{5,6},{7,8},{9,10},{11,12},{13,14},{15,16},{17,18},{19... | collective-permute-start | bytes 245768 | tf_op jit(solution)/shard_map/ppermute | solution.py:371
  57.5 1.9 %collective-permute-start.2 = (f32[5,32,128]{2,1,0:T(8,128)S(1)}, f32[5,32,128]{2,1,0:T(8,128)S(1)}, u32[]{:S(2)}, u32[]{:S(2)}) collective-permute-start(f32[5,32,128]{2,1,0:T(8,128)S(1)} %get-tuple-element.28), channel_id=1, source_target_pairs={{0,32},{64,96},{128,160},{192,224},{256,288},{320,352},{384,416},{... | collective-permute-start | bytes 245768 | tf_op jit(solution)/shard_map/ppermute | solution.py:371
  59.4 1.9 %collective-permute-start.3 = (f32[5,32,128]{2,1,0:T(8,128)S(1)}, f32[5,32,128]{2,1,0:T(8,128)S(1)}, u32[]{:S(2)}, u32[]{:S(2)}) collective-permute-start(f32[5,32,128]{2,1,0:T(8,128)S(1)} %get-tuple-element.29), channel_id=1, source_target_pairs={{0,1},{2,3},{4,5},{6,7},{8,9},{10,11},{12,13},{14,15},{16,17},{18,... | collective-permute-start | bytes 245768 | tf_op jit(solution)/shard_map/ppermute | solution.py:371
  61.4 1.2 %shard_map.85.inner = f32[4,2,512,128]{3,2,1,0:T(8,128)S(1)} custom-call(f32[4,2,512,128]{3,2,1,0:T(8,128)S(1)} %get-tuple-element.25.field, f32[4,16,32]{2,1,0:T(8,128)S(1)} %bitcast.20, bf16[4,512,137]{2,1,0:T(8,128)(2,1)S(1)} %bitcast.19), custom_call_target="tpu_custom_call" | custom-call | flops 1000 | bytes 6000000 | tf_op jit(solution)/shard_map/pallas_call | solution.py:442
  62.6 0.6 collective-permute-done.2.lon_even
  63.2 1.0 shard_map.86
  64.2 16.4 %all_to_all.22.received = bf16[32,2,640]{2,1,0:T(2,128)(2,1)S(1)} all-to-all(bf16[32,2,640]{2,1,0:T(2,128)(2,1)S(1)} %get-tuple-element.30), channel_id=1, replica_groups=mesh['gx'=16,'gy'=32] {'gy'}, dimensions={0} | all-to-all | bytes 163840 | tf_op jit(solution)/shard_map/all_to_all | solution.py:363
  80.7 1.4 %shard_map.87 = f32[32,1,1152]{2,1,0:T(1,128)S(1)} custom-call(bf16[32,2,640]{2,1,0:T(2,128)(2,1)S(1)} %all_to_all.22.received, bf16[16,137,4,137]{3,2,1,0:T(4,128)(2,1)S(1)} %bitcast.16, f32[64,64]{1,0:T(8,128)S(1)} %get-tuple-element.31.chosen), custom_call_target="tpu_custom_call" | custom-call | flops 1000 | bytes 1000000 | tf_op jit(solution)/shard_map/pallas_call | solution.py:451
  82.1 14.4 %all_to_all.23.returned = f32[32,1,1152]{2,1,0:T(1,128)S(1)} all-to-all(f32[32,1,1152]{2,1,0:T(1,128)S(1)} %shard_map.87), channel_id=1, replica_groups=mesh['gx'=16,'gy'=32] {'gy'}, dimensions={0} | all-to-all | bytes 294912 | tf_op jit(solution)/shard_map/all_to_all | solution.py:363
  96.5 1.0 shard_map.88
  97.5 2.7 %collective-permute-start.4 = (bf16[5,32,128]{2,1,0:T(8,128)(2,1)S(1)}, bf16[5,32,128]{2,1,0:T(8,128)(2,1)S(1)}, u32[]{:S(2)}, u32[]{:S(2)}) collective-permute-start(bf16[5,32,128]{2,1,0:T(8,128)(2,1)S(1)} %get-tuple-element.34), channel_id=1, source_target_pairs={{32,64},{96,128},{160,192},{224,256},{288,320},{352,384},{416,448}... | collective-permute-start | bytes 122888 | tf_op jit(solution)/shard_map/ppermute | solution.py:371
  100.2 2.8 %collective-permute-start.5 = (bf16[5,32,128]{2,1,0:T(8,128)(2,1)S(1)}, bf16[5,32,128]{2,1,0:T(8,128)(2,1)S(1)}, u32[]{:S(2)}, u32[]{:S(2)}) collective-permute-start(bf16[5,32,128]{2,1,0:T(8,128)(2,1)S(1)} %get-tuple-element.35), channel_id=1, source_target_pairs={{1,2},{3,4},{5,6},{7,8},{9,10},{11,12},{13,14},{15,16},{17,18},{19... | collective-permute-start | bytes 122888 | tf_op jit(solution)/shard_map/ppermute | solution.py:371
  102.9 1.9 %collective-permute-start.6 = (bf16[5,32,128]{2,1,0:T(8,128)(2,1)S(1)}, bf16[5,32,128]{2,1,0:T(8,128)(2,1)S(1)}, u32[]{:S(2)}, u32[]{:S(2)}) collective-permute-start(bf16[5,32,128]{2,1,0:T(8,128)(2,1)S(1)} %get-tuple-element.36), channel_id=1, source_target_pairs={{0,32},{64,96},{128,160},{192,224},{256,288},{320,352},{384,416},{... | collective-permute-start | bytes 122888 | tf_op jit(solution)/shard_map/ppermute | solution.py:371
  104.9 1.9 %collective-permute-start.7 = (bf16[5,32,128]{2,1,0:T(8,128)(2,1)S(1)}, bf16[5,32,128]{2,1,0:T(8,128)(2,1)S(1)}, u32[]{:S(2)}, u32[]{:S(2)}) collective-permute-start(bf16[5,32,128]{2,1,0:T(8,128)(2,1)S(1)} %get-tuple-element.37), channel_id=1, source_target_pairs={{0,1},{2,3},{4,5},{6,7},{8,9},{10,11},{12,13},{14,15},{16,17},{18,... | collective-permute-start | bytes 122888 | tf_op jit(solution)/shard_map/ppermute | solution.py:371
  106.8 1.0 shard_map.89.inner
  107.9 0.1 collective-permute-done.7.lat_even
  108.0 1.6 %shard_map.90 = (f32[4,512,137]{2,1,0:T(8,128)}, f32[4,2,512,128]{3,2,1,0:T(8,128)S(1)}) custom-call(f32[4,2,512,128]{3,2,1,0:T(8,128)S(1)} %shard_map.89.inner, f32[4,16,32]{2,1,0:T(8,128)S(1)} %bitcast.23, bf16[5,32,128]{2,1,0:T(8,128)(2,1)S(1)} %collective-permute-done.4.lon_odd, ...), custom_call_target="tpu_custom_call", output_to_operand_aliasing={{1}: (0, {})} | custom-call | flops 1000 | bytes 1000000 | tf_op jit(solution)/shard_map/pallas_call | solution.py:457
  (20 shorter events, 0.0 us)
Async XLA Ops:
  24.1 2.3 %copy-start = (bf16[1,16,4,137,137]{4,2,3,1,0:T(4,128)(2,1)S(1)}, bf16[1,16,4,137,137]{4,2,3,1,0:T(4,128)(2,1)}, u32[]{:S(2)}) copy-start(bf16[1,16,4,137,137]{4,2,3,1,0:T(4,128)(2,1)} %param.11) | copy-start | bytes 7207300
  26.4 15.9 %copy-start.1 = (bf16[4,137,32,16]{1,3,2,0:T(8,128)(2,1)S(1)}, bf16[4,137,32,16]{1,3,2,0:T(8,128)(2,1)}, u32[]{:S(2)}) copy-start(bf16[4,137,32,16]{1,3,2,0:T(8,128)(2,1)} %param.8) | copy-start | bytes 1683460
  26.4 15.9 %copy-start.4 = (s32[97]{0:T(128)S(1)}, s32[97]{0:T(128)}, u32[]{:S(2)}) copy-start(s32[97]{0:T(128)} %get-tuple-element.22.plan) | copy-start | bytes 1168
  26.4 35.0 %copy-start.2 = (bf16[4,137,32,16]{1,3,2,0:T(8,128)(2,1)S(1)}, bf16[4,137,32,16]{1,3,2,0:T(8,128)(2,1)}, u32[]{:S(2)}) copy-start(bf16[4,137,32,16]{1,3,2,0:T(8,128)(2,1)} %param.9) | copy-start | bytes 1683460
  26.4 35.0 %copy-start.3 = (f32[4,32,16]{1,2,0:T(8,128)S(1)}, f32[4,32,16]{1,2,0:T(8,128)}, u32[]{:S(2)}) copy-start(f32[4,32,16]{1,2,0:T(8,128)} %param.10) | copy-start | bytes 24580
  42.3 38.4 %slice-start = ((s8[4489216]{0:T(1024)(128)(4,1)}), s8[4194304]{0:T(1024)(128)(4,1)S(1)}, s32[]{:S(2)}) async-start(s8[4489216]{0:T(1024)(128)(4,1)} %bitcast.14), calls=%async_computation.4 | async-start | bytes 8388608
  43.3 19.3 %collective-permute-start = (f32[5,32,128]{2,1,0:T(8,128)S(1)}, f32[5,32,128]{2,1,0:T(8,128)S(1)}, u32[]{:S(2)}, u32[]{:S(2)}) collective-permute-start(f32[5,32,128]{2,1,0:T(8,128)S(1)} %get-tuple-element.26), channel_id=1, source_target_pairs={{32,64},{96,128},{160,192},{224,256},{288,320},{352,384},{416,448}... | collective-permute-start | bytes 245768 | tf_op jit(solution)/shard_map/ppermute | solution.py:371
  54.8 7.8 %collective-permute-start.1 = (f32[5,32,128]{2,1,0:T(8,128)S(1)}, f32[5,32,128]{2,1,0:T(8,128)S(1)}, u32[]{:S(2)}, u32[]{:S(2)}) collective-permute-start(f32[5,32,128]{2,1,0:T(8,128)S(1)} %get-tuple-element.27), channel_id=1, source_target_pairs={{1,2},{3,4},{5,6},{7,8},{9,10},{11,12},{13,14},{15,16},{17,18},{19... | collective-permute-start | bytes 245768 | tf_op jit(solution)/shard_map/ppermute | solution.py:371
  57.5 5.7 %collective-permute-start.2 = (f32[5,32,128]{2,1,0:T(8,128)S(1)}, f32[5,32,128]{2,1,0:T(8,128)S(1)}, u32[]{:S(2)}, u32[]{:S(2)}) collective-permute-start(f32[5,32,128]{2,1,0:T(8,128)S(1)} %get-tuple-element.28), channel_id=1, source_target_pairs={{0,32},{64,96},{128,160},{192,224},{256,288},{320,352},{384,416},{... | collective-permute-start | bytes 245768 | tf_op jit(solution)/shard_map/ppermute | solution.py:371
  59.4 3.8 %collective-permute-start.3 = (f32[5,32,128]{2,1,0:T(8,128)S(1)}, f32[5,32,128]{2,1,0:T(8,128)S(1)}, u32[]{:S(2)}, u32[]{:S(2)}) collective-permute-start(f32[5,32,128]{2,1,0:T(8,128)S(1)} %get-tuple-element.29), channel_id=1, source_target_pairs={{0,1},{2,3},{4,5},{6,7},{8,9},{10,11},{12,13},{14,15},{16,17},{18,... | collective-permute-start | bytes 245768 | tf_op jit(solution)/shard_map/ppermute | solution.py:371
  61.4 19.3 %slice-start.1 = ((s8[4489216]{0:T(1024)(128)(4,1)}), s8[294912]{0:T(1024)(128)(4,1)S(1)}, s32[]{:S(2)}) async-start(s8[4489216]{0:T(1024)(128)(4,1)} %bitcast.14), calls=%async_computation.5 | async-start | bytes 589824
  97.5 10.3 %collective-permute-start.4 = (bf16[5,32,128]{2,1,0:T(8,128)(2,1)S(1)}, bf16[5,32,128]{2,1,0:T(8,128)(2,1)S(1)}, u32[]{:S(2)}, u32[]{:S(2)}) collective-permute-start(bf16[5,32,128]{2,1,0:T(8,128)(2,1)S(1)} %get-tuple-element.34), channel_id=1, source_target_pairs={{32,64},{96,128},{160,192},{224,256},{288,320},{352,384},{416,448}... | collective-permute-start | bytes 122888 | tf_op jit(solution)/shard_map/ppermute | solution.py:371
  100.2 7.7 %collective-permute-start.5 = (bf16[5,32,128]{2,1,0:T(8,128)(2,1)S(1)}, bf16[5,32,128]{2,1,0:T(8,128)(2,1)S(1)}, u32[]{:S(2)}, u32[]{:S(2)}) collective-permute-start(bf16[5,32,128]{2,1,0:T(8,128)(2,1)S(1)} %get-tuple-element.35), channel_id=1, source_target_pairs={{1,2},{3,4},{5,6},{7,8},{9,10},{11,12},{13,14},{15,16},{17,18},{19... | collective-permute-start | bytes 122888 | tf_op jit(solution)/shard_map/ppermute | solution.py:371
  102.9 4.9 %collective-permute-start.6 = (bf16[5,32,128]{2,1,0:T(8,128)(2,1)S(1)}, bf16[5,32,128]{2,1,0:T(8,128)(2,1)S(1)}, u32[]{:S(2)}, u32[]{:S(2)}) collective-permute-start(bf16[5,32,128]{2,1,0:T(8,128)(2,1)S(1)} %get-tuple-element.36), channel_id=1, source_target_pairs={{0,32},{64,96},{128,160},{192,224},{256,288},{320,352},{384,416},{... | collective-permute-start | bytes 122888 | tf_op jit(solution)/shard_map/ppermute | solution.py:371
  104.9 3.1 %collective-permute-start.7 = (bf16[5,32,128]{2,1,0:T(8,128)(2,1)S(1)}, bf16[5,32,128]{2,1,0:T(8,128)(2,1)S(1)}, u32[]{:S(2)}, u32[]{:S(2)}) collective-permute-start(bf16[5,32,128]{2,1,0:T(8,128)(2,1)S(1)} %get-tuple-element.37), channel_id=1, source_target_pairs={{0,1},{2,3},{4,5},{6,7},{8,9},{10,11},{12,13},{14,15},{16,17},{18,... | collective-permute-start | bytes 122888 | tf_op jit(solution)/shard_map/ppermute | solution.py:371

commit v10 on v9

--- a/solution.py
+++ b/solution.py
@@ -41,9 +41,17 @@
     lax.fori_loop(0, (plan[0] + (GROUP - 1)) // GROUP, step, 0)
 
 
-def unpack_field(packed, field, f):
-    field[f, 0] = packed[f, :, :LANES].astype(F32)
-    field[f, 1, :, : packed.shape[2] - LANES] = packed[f, :, LANES:].astype(F32)
+def shifted_tail(packed, f, at):
+    end = packed[f, at, LANES:].astype(F32)
+    end = jnp.concatenate([end, jnp.zeros((end.shape[0], LANES - end.shape[1]), F32)], axis=1)
+    return pltpu.roll(end, (packed.shape[2] - LANES) * f, 1) if f else end
+
+
+def unpack_field(packed, planes, f):
+    fields = packed.shape[0]
+    planes[f] = packed[f, :, :LANES].astype(F32)
+    end = shifted_tail(packed, f, slice(None))
+    planes[fields] = planes[fields] + end if f else end
 
 
 def tail_lanes(block, start):
@@ -77,7 +85,7 @@
         rank = used[o]
         used[o] = rank + 1
         plan[1 + e] = cols[0, 0, e]
-        plan[1 + capacity + e] = rank * (fields * owners) + o
+        plan[1 + capacity + e] = o * PAIR + rank
         codes[pl.ds(o * PAIR + rank, 1), :] = jnp.full((1, LANES), slot[0, 0, e] + 1, jnp.int32).astype(F32)
         return carry
 
@@ -93,47 +101,27 @@
     for f in range(fields):
         copies[len(small) + f].wait()
         unpack_field(late, field, f)
-    gather_columns(plan, field, rows, owners)
-    lane = lax.broadcasted_iota(jnp.int32, codes.shape, 1)
-    pack_rows(rows, jnp.where(lane == tail * fields, codes[...], 0.0), tail, outbox)
-
-
-def gather_columns(plan, field, rows, owners):
-    fields, halves = field.shape[:2]
-
+    gather_columns(plan, field, rows)
+    pack_rows(rows, codes[...], tail * fields, outbox)
+
+
+def gather_columns(plan, planes, rows):
     def body(entries):
-        found = []
-        for column, row in entries:
-            at = outbox_row(row, owners, fields)
-            for f in range(fields):
-                for h in range(halves):
-                    found.append((h, f * (PAIR * owners) + at, field[f, h, pl.ds(column, 1), :]))
-        for h, row, value in found:
-            rows[h, pl.ds(row, 1), :] = value
+        found = [(h, at, planes[h, pl.ds(column, 1), :]) for column, at in entries for h in range(planes.shape[0])]
+        for h, at, value in found:
+            rows[h, pl.ds(at, 1), :] = value
 
     entry_groups(plan, body)
 
 
-def pack_rows(rows, tails, tail, outbox):
-    count = outbox.shape[0] * outbox.shape[1]
-    blocks = [slice(f * count, (f + 1) * count) for f in range(rows.shape[1] // count)]
-    tails = tails + side_by_side([rows[1, block] for block in blocks], tail)
-    packed = jnp.concatenate([rows[0, block] for block in blocks] + [tails], axis=1)
+def pack_rows(rows, codes, code_lane, outbox):
+    fields = rows.shape[0] - 1
+    lane = lax.broadcasted_iota(jnp.int32, rows.shape[1:], 1)
+    tails = jnp.where(lane < code_lane, rows[fields], 0.0)
+    if codes is not None:
+        tails = jnp.where(lane == code_lane, codes, tails)
+    packed = jnp.concatenate([rows[f] for f in range(fields)] + [tails], axis=1)
     outbox[...] = packed.astype(BF16).reshape(outbox.shape)
-
-
-def side_by_side(ends, tail):
-    lane = lax.broadcasted_iota(jnp.int32, ends[0].shape, 1)
-    total = jnp.zeros(ends[0].shape, F32)
-    for f, end in enumerate(ends):
-        end = jnp.where(lane < tail, end, 0.0)
-        total = total + (pltpu.roll(end, tail * f, 1) if f else end)
-    return total
-
-
-def outbox_row(row, owners, fields):
-    rank = row // (fields * owners)
-    return (row - rank * (fields * owners)) * PAIR + rank
 
 
 def split_dot(chosen, value):
@@ -199,46 +187,46 @@
     products(chosen, received, matrices, answer, spread, result)
 
 
-def add_first(plan, returned, late, field, *rest, levels):
-    for f in range(field.shape[0]):
+def add_first(plan, returned, late, field, *rest, tail):
+    for f in range(late.shape[0]):
         unpack_field(late, field, f)
-    add_increments(plan, returned, field, field, *rest, levels=levels)
-
-
-def add_increments(plan, returned, base, field, lon_even, lon_odd, lat_even, lat_odd, inbox, *, levels):
-    fields, halves, columns_all, lanes = field.shape
+    add_increments(plan, returned, field, field, *rest, tail=tail)
+
+
+def add_increments(plan, returned, base, field, lon_even, lon_odd, lat_even, lat_odd, inbox, *, tail):
+    planes, columns_all, lanes = field.shape
+    fields = planes - 1
     owners = returned.shape[0]
-    per_owner = inbox.shape[1] // owners
-    tail = levels - LANES
     lines = returned[...].reshape(owners, returned.shape[2])
-    tails = lines[:, per_owner * LANES :]
-    for r in range(per_owner):
-        inbox[0, r * owners : (r + 1) * owners] = lines[:, r * LANES : (r + 1) * LANES]
-        inbox[1, r * owners : (r + 1) * owners] = pltpu.roll(tails, LANES - tail * r, 1) if r else tails
+    tails = lines[:, PAIR * fields * lanes :]
+    for k in range(PAIR):
+        at = pl.ds(k, owners, stride=PAIR)
+        for f in range(fields):
+            r = k * fields + f
+            inbox[f, at, :] = lines[:, r * lanes : (r + 1) * lanes]
+        inbox[fields, at, :] = pltpu.roll(tails, lanes - tail * fields * k, 1) if k else tails
 
     def body(entries):
         found = []
-        for column, row in entries:
-            for f in range(fields):
-                for h in range(halves):
-                    here = (f, h, pl.ds(column, 1), slice(None))
-                    found.append((here, base[here] + inbox[h, pl.ds(row + f * owners, 1), :]))
+        for column, at in entries:
+            for h in range(planes):
+                here = (h, pl.ds(column, 1), slice(None))
+                found.append((here, base[here] + inbox[h, pl.ds(at, 1), :]))
         for here, value in found:
             field[here] = value
 
     entry_groups(plan, body)
     span_lon = lat_even.shape[1]
-    span_lat = columns_all // span_lon
     lon_up, lat_up = upward()
-    places = edge_places(columns_all, span_lon)
-    lon_low, lon_high, lat_low, lat_high = [edge_blocks(field, place, tail) for place in places]
-    for up, even, odd, lows, highs in (
+    lon_low, lon_high, lat_low, lat_high = edge_places(columns_all, span_lon)
+    for up, even, odd, low_place, high_place in (
         (lon_up, lon_even, lon_odd, lon_low, lon_high),
         (lat_up, lat_even, lat_odd, lat_low, lat_high),
     ):
-        for block, (low, high) in enumerate(zip(lows, highs)):
-            even[block, : low.shape[0]] = jnp.where(up, high, low).astype(even.dtype)
-            odd[block, : low.shape[0]] = jnp.where(up, low, high).astype(odd.dtype)
+        for h in range(planes):
+            low, high = field[h, low_place, :], field[h, high_place, :]
+            even[h, : low.shape[0]] = jnp.where(up, high, low).astype(even.dtype)
+            odd[h, : low.shape[0]] = jnp.where(up, low, high).astype(odd.dtype)
 
 
 def edge_places(columns_all, span_lon):
@@ -251,19 +239,13 @@
     )
 
 
-def edge_blocks(field, place, tail):
-    fields = field.shape[0]
-    return [field[f, 0, place, :] for f in range(fields)] + [
-        side_by_side([field[f, 1, place, :] for f in range(fields)], tail)
-    ]
-
-
 def upward():
     return lax.axis_index("gx") % 2 == 0, lax.axis_index("gy") % 2 == 0
 
 
 def inner_stencil(field, coef, extra, out):
-    fields, halves, columns_all, lanes = field.shape
+    planes, columns_all, lanes = field.shape
+    fields = planes - 1
     span_lat, span_lon = coef.shape[1:]
     row = lax.broadcasted_iota(jnp.int32, (span_lat, 1), 0)
     for p in range(span_lon):
@@ -272,21 +254,19 @@
         weight[3] = jnp.where(row == span_lat - 1, 0.0, weight[3])
         weight = [jnp.broadcast_to(w, (span_lat, lanes)) for w in weight]
         at = slice(p * span_lat, (p + 1) * span_lat)
-        for f in range(fields):
-            for h in range(halves):
-                here = field[f, h, at]
-                total = here + weight[2] * pltpu.roll(here, 1, 0) + weight[3] * pltpu.roll(here, span_lat - 1, 0)
-                if p > 0:
-                    total = total + weight[0] * field[f, h, (p - 1) * span_lat : p * span_lat]
-                if p < span_lon - 1:
-                    total = total + weight[1] * field[f, h, (p + 1) * span_lat : (p + 2) * span_lat]
-                if extra is None:
-                    out[f, h, at] = total
-                elif h == 0:
-                    out[f, h, at] = total + extra[f, at, :lanes].astype(F32)
-                else:
-                    tail = extra.shape[2] - lanes
-                    out[f, h, at, :tail] = total[:, :tail] + extra[f, at, lanes:].astype(F32)
+        for h in range(planes):
+            here = field[h, at]
+            total = here + weight[2] * pltpu.roll(here, 1, 0) + weight[3] * pltpu.roll(here, span_lat - 1, 0)
+            if p > 0:
+                total = total + weight[0] * field[h, (p - 1) * span_lat : p * span_lat]
+            if p < span_lon - 1:
+                total = total + weight[1] * field[h, (p + 1) * span_lat : (p + 2) * span_lat]
+            if extra is not None and h < fields:
+                total = total + extra[h, at, :lanes].astype(F32)
+            elif extra is not None:
+                for f in range(fields):
+                    total = total + shifted_tail(extra, f, at)
+            out[h, at] = total
 
 
 def inner_first(field, coef, early, out):
@@ -314,45 +294,40 @@
     )
 
 
-def add_edges(f, weights, lon_even, lon_odd, lat_even, lat_odd, out, tail):
-    fields, _, columns_all, lanes = out.shape
+def add_edges(h, weights, lon_even, lon_odd, lat_even, lat_odd, out):
+    columns_all = out.shape[1]
     span_lon = lat_even.shape[1]
     span_lat = columns_all // span_lon
     lon_up, lat_up = upward()
-    for h, block in ((0, f), (1, fields)):
-        edges = []
-        for up, even, odd, count in ((lon_up, lon_even, lon_odd, span_lat), (lat_up, lat_even, lat_odd, span_lon)):
-            first, second = even[block, :count].astype(F32), odd[block, :count].astype(F32)
-            if h and f:
-                first, second = [pltpu.roll(edge, lanes - tail * f, 1) for edge in (first, second)]
-            edges += [jnp.where(up, second, first), jnp.where(up, first, second)]
-        for place, weight, edge in zip(edge_places(columns_all, span_lon), weights, edges):
-            at = (f, h, place, slice(None))
-            out[at] = out[at] + weight * edge
-
-
-def edges_first(plan, inner, coef, lon_odd, lat_odd, lon_even, lat_even, out, outbox, rows, *, levels):
-    fields, halves, columns_all, lanes = out.shape
-    owners = outbox.shape[0]
-    tail = levels - lanes
+    edges = []
+    for up, even, odd, count in ((lon_up, lon_even, lon_odd, span_lat), (lat_up, lat_even, lat_odd, span_lon)):
+        first, second = even[h, :count].astype(F32), odd[h, :count].astype(F32)
+        edges += [jnp.where(up, second, first), jnp.where(up, first, second)]
+    for place, weight, edge in zip(edge_places(columns_all, span_lon), weights, edges):
+        at = (h, place, slice(None))
+        out[at] = out[at] + weight * edge
+
+
+def edges_first(plan, inner, coef, lon_odd, lat_odd, lon_even, lat_even, out, outbox, rows, *, tail):
     weights = edge_weights(coef)
     rows[...] = jnp.zeros(rows.shape, F32)
-    for f in range(fields):
-        add_edges(f, weights, lon_even, lon_odd, lat_even, lat_odd, out, tail)
-
-    gather_columns(plan, out, rows, owners)
-    pack_rows(rows, 0.0, tail, outbox)
-
-
-def edges_last(inner, coef, lon_odd, lat_odd, lon_even, lat_even, out_hbm, both, out, sems):
-    fields, halves, columns_all, lanes = inner.shape
-    tail = out.shape[2] - lanes
+    for h in range(out.shape[0]):
+        add_edges(h, weights, lon_even, lon_odd, lat_even, lat_odd, out)
+    gather_columns(plan, out, rows)
+    pack_rows(rows, None, tail * (out.shape[0] - 1), outbox)
+
+
+def edges_last(inner, coef, lon_odd, lat_odd, lon_even, lat_even, out_hbm, planes, out, sems):
+    fields, _, levels = out.shape
+    tail = levels - LANES
     weights = edge_weights(coef)
+    add_edges(fields, weights, lon_even, lon_odd, lat_even, lat_odd, planes)
     copies = []
     for f in range(fields):
-        add_edges(f, weights, lon_even, lon_odd, lat_even, lat_odd, both, tail)
-        out[f, :, :lanes] = both[f, 0]
-        out[f, :, lanes:] = both[f, 1, :, :tail]
+        add_edges(f, weights, lon_even, lon_odd, lat_even, lat_odd, planes)
+        out[f, :, :LANES] = planes[f]
+        ends = planes[fields]
+        out[f, :, LANES:] = (pltpu.roll(ends, LANES - tail * f, 1) if f else ends)[:, :tail]
         copies.append(pltpu.make_async_copy(out.at[f], out_hbm.at[f], sems.at[f]))
         copies[f].start()
     for copy in copies:
@@ -391,9 +366,10 @@
     matrices = jacobian[0].transpose(0, 2, 1, 3)
     shape = jax.ShapeDtypeStruct
     per_owner = PAIR * fields
-    inbox_rows = groups * per_owner
     grid = (fields, columns_all, levels)
-    halves = (fields, 2, columns_all, LANES)
+    tail = levels - LANES
+    planes = (fields + 1, columns_all, LANES)
+    rows_shape = (fields + 1, groups * PAIR, LANES)
     plan_shape = shape((2 * capacity + 1,), jnp.int32)
 
     outbox_shape = shape((groups, PAIR, (fields + 1) * LANES), BF16)
@@ -408,8 +384,8 @@
             SMEM(owner_rank.shape, jnp.int32),
             SMEM(owner_slot.shape, jnp.int32),
             VMEM(grid, BF16),
-            VMEM(halves, F32),
-            VMEM((2, inbox_rows, LANES), F32),
+            VMEM(planes, F32),
+            VMEM(rows_shape, F32),
             VMEM((groups * PAIR, LANES), F32),
             SMEM((groups,), jnp.int32),
             pltpu.SemaphoreType.DMA((4 + fields,)),
@@ -429,23 +405,23 @@
 
     def add(kernel, returned, base, aliases, edge_type):
         return call(
-            functools.partial(kernel, levels=levels),
-            [shape(halves, F32)] + [shape((fields + 1, span_lon, LANES), edge_type)] * 4,
+            functools.partial(kernel, tail=tail),
+            [shape(planes, F32)] + [shape((fields + 1, span_lon, LANES), edge_type)] * 4,
             [SMEM] + [VMEM] * 2,
             [VMEM] * 5,
-            [VMEM((2, inbox_rows, LANES), F32)],
+            [VMEM(rows_shape, F32)],
             aliases,
         )(plan, returned, base)
 
     field, *edges = add(add_first, returned, late, {}, F32)
     neighbours = halos(*edges)
-    (inner,) = call(inner_first, [shape(halves, F32)], [VMEM] * 3, [VMEM], touched=6000000)(field, coef, early)
+    (inner,) = call(inner_first, [shape(planes, F32)], [VMEM] * 3, [VMEM], touched=6000000)(field, coef, early)
     adjoint, outbox = call(
-        functools.partial(edges_first, levels=levels),
-        [shape(halves, F32), outbox_shape],
+        functools.partial(edges_first, tail=tail),
+        [shape(planes, F32), outbox_shape],
         [SMEM] + [VMEM] * 6,
         [VMEM] * 2,
-        [VMEM((2, inbox_rows, LANES), F32)],
+        [VMEM(rows_shape, F32)],
         {1: 0},
     )(plan, inner, coef, *neighbours)
     (answer,) = call(physics_second, [answer_shape], [VMEM] * 3, [VMEM], spaces)(
@@ -453,10 +429,10 @@
     )
     field, *edges = add(add_increments, exchange(answer), adjoint, {2: 0}, BF16)
     neighbours = halos(*edges)
-    (inner,) = call(inner_last, [shape(halves, F32)], [VMEM] * 2, [VMEM], touched=6000000)(field, coef)
+    (inner,) = call(inner_last, [shape(planes, F32)], [VMEM] * 2, [VMEM], touched=6000000)(field, coef)
     final, _ = call(
         edges_last,
-        [shape(grid, F32), shape(halves, F32)],
+        [shape(grid, F32), shape(planes, F32)],
         [VMEM] * 6,
         [HBM, VMEM],
         [VMEM(grid, F32), pltpu.SemaphoreType.DMA((fields,))],

time: 110 us -> 109 us (level)
  Pallas kernels: 12 us -> 10.8 us
    pallas_call x6, Pallas kernels: 6.9 us -> 5.71 us  [the longest x2 1.85 us: add(): call(functools.partial(kernel, tail=tail), [shape(planes, F32)] + [shape(...]
    unnamed x14 -> x12, local copies, waits for them, and re-layouts: 2.3 us -> 2.3 us
  transfers between devices with their start and end apart: 8 -> 8, of which waited for: 2 -> 3; matrix products, arithmetic and copies ran while one was open for 0% -> 0% of each run, Pallas kernels for 2% -> 1%
where the time goes in v10:
time: 109 us
  blocking collectives  66.3 us (61%)
  starting transfers between devices  27.1 us (25%)
  Pallas kernels  10.8 us (10%)
  local copies, waits for them, and re-layouts  2.3 us (2%)
  waiting for transfers between devices  1.51 us (1%)
    all_to_all x4, blocking collectives, exchange(): return lax.all_to_all(lines, 'gy', split_axis=0, concat_axis=0, tiled=True)  66.3 us
    ppermute x8, starting transfers between devices, swap(): lax.ppermute(edge, axis, pairs + [(high, low) for low, high in pairs])  27.1 us
    unnamed x12, local copies, waits for them, and re-layouts  2.3 us
    pallas_call x1, Pallas kernels, on_device(): call(pack_first, [outbox_shape, plan_shape], [HBM] * 5, [VMEM, SMEM], [SM...  2.18 us
  transfers between devices with their start and end apart: 8, of which 3 were waited for; matrix products, arithmetic and copies ran while one was open for 0% of the time, Pallas kernels for 1%

profile of v10, /device:TPU:1, one launch (start us, length us, event | category | flops | bytes accessed | tf_op | source)
XLA Modules:
  0.0 108.9 jit_solution(1646250913940500033)
XLA Ops:
  0.7 2.2 %shard_map.82 = (bf16[32,2,640]{2,1,0:T(2,128)(2,1)}, s32[97]{0:T(128)}) custom-call(s32[1,1,48]{2,1,0:T(1,128)} %cols_hbm.1, s32[1,1]{1,0:T(1,128)S(6)} %copy.15.count_hbm, s32[1,1,48]{2,1,0:T(1,128)} %owner_hbm.1, s32[1,1,48]{2,1,0:T(1,128)} %slot_hbm.1, bf16[4,512,137]{2,1,0:T(8,128)(2,1)} %bitcast.15), custom_call_target="tpu_custom_call" | custom-call | flops 1000 | bytes 1000000 | tf_op jit(solution)/shard_map/pallas_call | solution.py:376
  2.8 21.2 %all_to_all.20.received = bf16[32,2,640]{2,1,0:T(2,128)(2,1)S(1)} all-to-all(bf16[32,2,640]{2,1,0:T(2,128)(2,1)} %get-tuple-element.23), channel_id=1, replica_groups=mesh['gx'=16,'gy'=32] {'gy'}, dimensions={0} | all-to-all | bytes 163840 | tf_op jit(solution)/shard_map/all_to_all | solution.py:338
  24.0 2.3 %copy-done = bf16[1,16,4,137,137]{4,2,3,1,0:T(4,128)(2,1)S(1)} copy-done((bf16[1,16,4,137,137]{4,2,3,1,0:T(4,128)(2,1)S(1)}, bf16[1,16,4,137,137]{4,2,3,1,0:T(4,128)(2,1)}, u32[]{:S(2)}) %copy-start) | copy-done | bytes 2402456
  26.3 1.5 %shard_map.83 = (f32[32,1,1152]{2,1,0:T(1,128)S(1)}, f32[64,64]{1,0:T(8,128)S(1)}) custom-call(bf16[32,2,640]{2,1,0:T(2,128)(2,1)S(1)} %all_to_all.20.received, bf16[16,137,4,137]{3,2,1,0:T(4,128)(2,1)S(1)} %bitcast.13), custom_call_target="tpu_custom_call" | custom-call | flops 1000 | bytes 1000000 | tf_op jit(solution)/shard_map/pallas_call | solution.py:401
  27.8 14.5 %all_to_all.21.returned = f32[32,1,1152]{2,1,0:T(1,128)S(1)} all-to-all(f32[32,1,1152]{2,1,0:T(1,128)S(1)} %get-tuple-element.24), channel_id=1, replica_groups=mesh['gx'=16,'gy'=32] {'gy'}, dimensions={0} | all-to-all | bytes 294912 | tf_op jit(solution)/shard_map/all_to_all | solution.py:338
  42.3 1.0 shard_map.84
  43.3 11.3 %collective-permute-start = (f32[5,32,128]{2,1,0:T(8,128)S(1)}, f32[5,32,128]{2,1,0:T(8,128)S(1)}, u32[]{:S(2)}, u32[]{:S(2)}) collective-permute-start(f32[5,32,128]{2,1,0:T(8,128)S(1)} %get-tuple-element.26), channel_id=1, source_target_pairs={{32,64},{96,128},{160,192},{224,256},{288,320},{352,384},{416,448}... | collective-permute-start | bytes 245768 | tf_op jit(solution)/shard_map/ppermute | solution.py:346
  54.6 2.7 %collective-permute-start.1 = (f32[5,32,128]{2,1,0:T(8,128)S(1)}, f32[5,32,128]{2,1,0:T(8,128)S(1)}, u32[]{:S(2)}, u32[]{:S(2)}) collective-permute-start(f32[5,32,128]{2,1,0:T(8,128)S(1)} %get-tuple-element.27), channel_id=1, source_target_pairs={{1,2},{3,4},{5,6},{7,8},{9,10},{11,12},{13,14},{15,16},{17,18},{19... | collective-permute-start | bytes 245768 | tf_op jit(solution)/shard_map/ppermute | solution.py:346
  57.3 1.9 %collective-permute-start.2 = (f32[5,32,128]{2,1,0:T(8,128)S(1)}, f32[5,32,128]{2,1,0:T(8,128)S(1)}, u32[]{:S(2)}, u32[]{:S(2)}) collective-permute-start(f32[5,32,128]{2,1,0:T(8,128)S(1)} %get-tuple-element.28), channel_id=1, source_target_pairs={{0,32},{64,96},{128,160},{192,224},{256,288},{320,352},{384,416},{... | collective-permute-start | bytes 245768 | tf_op jit(solution)/shard_map/ppermute | solution.py:346
  59.2 1.9 %collective-permute-start.3 = (f32[5,32,128]{2,1,0:T(8,128)S(1)}, f32[5,32,128]{2,1,0:T(8,128)S(1)}, u32[]{:S(2)}, u32[]{:S(2)}) collective-permute-start(f32[5,32,128]{2,1,0:T(8,128)S(1)} %get-tuple-element.29), channel_id=1, source_target_pairs={{0,1},{2,3},{4,5},{6,7},{8,9},{10,11},{12,13},{14,15},{16,17},{18,... | collective-permute-start | bytes 245768 | tf_op jit(solution)/shard_map/ppermute | solution.py:346
  61.2 0.8 shard_map.85.inner
  62.0 0.9 collective-permute-done.2.lon_even
  63.0 0.8 shard_map.86
  63.8 16.2 %all_to_all.22.received = bf16[32,2,640]{2,1,0:T(2,128)(2,1)S(1)} all-to-all(bf16[32,2,640]{2,1,0:T(2,128)(2,1)S(1)} %get-tuple-element.30), channel_id=1, replica_groups=mesh['gx'=16,'gy'=32] {'gy'}, dimensions={0} | all-to-all | bytes 163840 | tf_op jit(solution)/shard_map/all_to_all | solution.py:338
  80.1 1.4 %shard_map.87 = f32[32,1,1152]{2,1,0:T(1,128)S(1)} custom-call(bf16[32,2,640]{2,1,0:T(2,128)(2,1)S(1)} %all_to_all.22.received, bf16[16,137,4,137]{3,2,1,0:T(4,128)(2,1)S(1)} %bitcast.14, f32[64,64]{1,0:T(8,128)S(1)} %get-tuple-element.31.chosen), custom_call_target="tpu_custom_call" | custom-call | flops 1000 | bytes 1000000 | tf_op jit(solution)/shard_map/pallas_call | solution.py:427
  81.5 14.4 %all_to_all.23.returned = f32[32,1,1152]{2,1,0:T(1,128)S(1)} all-to-all(f32[32,1,1152]{2,1,0:T(1,128)S(1)} %shard_map.87), channel_id=1, replica_groups=mesh['gx'=16,'gy'=32] {'gy'}, dimensions={0} | all-to-all | bytes 294912 | tf_op jit(solution)/shard_map/all_to_all | solution.py:338
  95.9 0.8 shard_map.88
  96.8 2.7 %collective-permute-start.4 = (bf16[5,32,128]{2,1,0:T(8,128)(2,1)S(1)}, bf16[5,32,128]{2,1,0:T(8,128)(2,1)S(1)}, u32[]{:S(2)}, u32[]{:S(2)}) collective-permute-start(bf16[5,32,128]{2,1,0:T(8,128)(2,1)S(1)} %get-tuple-element.34), channel_id=1, source_target_pairs={{32,64},{96,128},{160,192},{224,256},{288,320},{352,384},{416,448}... | collective-permute-start | bytes 122888 | tf_op jit(solution)/shard_map/ppermute | solution.py:346
  99.5 2.7 %collective-permute-start.5 = (bf16[5,32,128]{2,1,0:T(8,128)(2,1)S(1)}, bf16[5,32,128]{2,1,0:T(8,128)(2,1)S(1)}, u32[]{:S(2)}, u32[]{:S(2)}) collective-permute-start(bf16[5,32,128]{2,1,0:T(8,128)(2,1)S(1)} %get-tuple-element.35), channel_id=1, source_target_pairs={{1,2},{3,4},{5,6},{7,8},{9,10},{11,12},{13,14},{15,16},{17,18},{19... | collective-permute-start | bytes 122888 | tf_op jit(solution)/shard_map/ppermute | solution.py:346
  102.2 1.9 %collective-permute-start.6 = (bf16[5,32,128]{2,1,0:T(8,128)(2,1)S(1)}, bf16[5,32,128]{2,1,0:T(8,128)(2,1)S(1)}, u32[]{:S(2)}, u32[]{:S(2)}) collective-permute-start(bf16[5,32,128]{2,1,0:T(8,128)(2,1)S(1)} %get-tuple-element.36), channel_id=1, source_target_pairs={{0,32},{64,96},{128,160},{192,224},{256,288},{320,352},{384,416},{... | collective-permute-start | bytes 122888 | tf_op jit(solution)/shard_map/ppermute | solution.py:346
  104.2 1.9 %collective-permute-start.7 = (bf16[5,32,128]{2,1,0:T(8,128)(2,1)S(1)}, bf16[5,32,128]{2,1,0:T(8,128)(2,1)S(1)}, u32[]{:S(2)}, u32[]{:S(2)}) collective-permute-start(bf16[5,32,128]{2,1,0:T(8,128)(2,1)S(1)} %get-tuple-element.37), channel_id=1, source_target_pairs={{0,1},{2,3},{4,5},{6,7},{8,9},{10,11},{12,13},{14,15},{16,17},{18,... | collective-permute-start | bytes 122888 | tf_op jit(solution)/shard_map/ppermute | solution.py:346
  106.1 0.6 shard_map.89.inner
  107.0 0.3 collective-permute-done.7.lat_even
  107.3 1.6 %shard_map.90 = (f32[4,512,137]{2,1,0:T(8,128)}, f32[5,512,128]{2,1,0:T(8,128)S(1)}) custom-call(f32[5,512,128]{2,1,0:T(8,128)S(1)} %shard_map.89.inner, f32[4,16,32]{2,1,0:T(8,128)S(1)} %bitcast.21, bf16[5,32,128]{2,1,0:T(8,128)(2,1)S(1)} %collective-permute-done.4.lon_odd, ...), custom_call_target="tpu_custom_call", output_to_operand_aliasing={{1}: (0, {})} | custom-call | flops 1000 | bytes 1000000 | tf_op jit(solution)/shard_map/pallas_call | solution.py:433
  (17 shorter events, 0.3 us)
Async XLA Ops:
  24.0 2.3 %copy-start = (bf16[1,16,4,137,137]{4,2,3,1,0:T(4,128)(2,1)S(1)}, bf16[1,16,4,137,137]{4,2,3,1,0:T(4,128)(2,1)}, u32[]{:S(2)}) copy-start(bf16[1,16,4,137,137]{4,2,3,1,0:T(4,128)(2,1)} %param.11) | copy-start | bytes 7207300
  26.3 16.0 %copy-start.2 = (bf16[4,137,32,16]{1,3,2,0:T(8,128)(2,1)S(1)}, bf16[4,137,32,16]{1,3,2,0:T(8,128)(2,1)}, u32[]{:S(2)}) copy-start(bf16[4,137,32,16]{1,3,2,0:T(8,128)(2,1)} %param.8) | copy-start | bytes 1683460
  26.3 16.0 %copy-start.5 = (s32[97]{0:T(128)S(1)}, s32[97]{0:T(128)}, u32[]{:S(2)}) copy-start(s32[97]{0:T(128)} %get-tuple-element.22.plan) | copy-start | bytes 1168
  27.8 33.4 %copy-start.3 = (bf16[4,137,32,16]{1,3,2,0:T(8,128)(2,1)S(1)}, bf16[4,137,32,16]{1,3,2,0:T(8,128)(2,1)}, u32[]{:S(2)}) copy-start(bf16[4,137,32,16]{1,3,2,0:T(8,128)(2,1)} %param.9) | copy-start | bytes 1683460
  27.8 33.4 %copy-start.4 = (f32[4,32,16]{1,2,0:T(8,128)S(1)}, f32[4,32,16]{1,2,0:T(8,128)}, u32[]{:S(2)}) copy-start(f32[4,32,16]{1,2,0:T(8,128)} %param.10) | copy-start | bytes 24580
  43.3 18.7 %collective-permute-start = (f32[5,32,128]{2,1,0:T(8,128)S(1)}, f32[5,32,128]{2,1,0:T(8,128)S(1)}, u32[]{:S(2)}, u32[]{:S(2)}) collective-permute-start(f32[5,32,128]{2,1,0:T(8,128)S(1)} %get-tuple-element.26), channel_id=1, source_target_pairs={{32,64},{96,128},{160,192},{224,256},{288,320},{352,384},{416,448}... | collective-permute-start | bytes 245768 | tf_op jit(solution)/shard_map/ppermute | solution.py:346
  54.6 7.4 %collective-permute-start.1 = (f32[5,32,128]{2,1,0:T(8,128)S(1)}, f32[5,32,128]{2,1,0:T(8,128)S(1)}, u32[]{:S(2)}, u32[]{:S(2)}) collective-permute-start(f32[5,32,128]{2,1,0:T(8,128)S(1)} %get-tuple-element.27), channel_id=1, source_target_pairs={{1,2},{3,4},{5,6},{7,8},{9,10},{11,12},{13,14},{15,16},{17,18},{19... | collective-permute-start | bytes 245768 | tf_op jit(solution)/shard_map/ppermute | solution.py:346
  57.3 5.7 %collective-permute-start.2 = (f32[5,32,128]{2,1,0:T(8,128)S(1)}, f32[5,32,128]{2,1,0:T(8,128)S(1)}, u32[]{:S(2)}, u32[]{:S(2)}) collective-permute-start(f32[5,32,128]{2,1,0:T(8,128)S(1)} %get-tuple-element.28), channel_id=1, source_target_pairs={{0,32},{64,96},{128,160},{192,224},{256,288},{320,352},{384,416},{... | collective-permute-start | bytes 245768 | tf_op jit(solution)/shard_map/ppermute | solution.py:346
  59.2 3.7 %collective-permute-start.3 = (f32[5,32,128]{2,1,0:T(8,128)S(1)}, f32[5,32,128]{2,1,0:T(8,128)S(1)}, u32[]{:S(2)}, u32[]{:S(2)}) collective-permute-start(f32[5,32,128]{2,1,0:T(8,128)S(1)} %get-tuple-element.29), channel_id=1, source_target_pairs={{0,1},{2,3},{4,5},{6,7},{8,9},{10,11},{12,13},{14,15},{16,17},{18,... | collective-permute-start | bytes 245768 | tf_op jit(solution)/shard_map/ppermute | solution.py:346
  61.2 18.9 %copy-start.1 = (bf16[1,16,4,137,137]{4,2,3,1,0:T(4,128)(2,1)S(1)}, bf16[1,16,4,137,137]{4,2,3,1,0:T(4,128)(2,1)}, u32[]{:S(2)}) copy-start(bf16[1,16,4,137,137]{4,2,3,1,0:T(4,128)(2,1)} %param.11) | copy-start | bytes 7207300
  96.8 9.9 %collective-permute-start.4 = (bf16[5,32,128]{2,1,0:T(8,128)(2,1)S(1)}, bf16[5,32,128]{2,1,0:T(8,128)(2,1)S(1)}, u32[]{:S(2)}, u32[]{:S(2)}) collective-permute-start(bf16[5,32,128]{2,1,0:T(8,128)(2,1)S(1)} %get-tuple-element.34), channel_id=1, source_target_pairs={{32,64},{96,128},{160,192},{224,256},{288,320},{352,384},{416,448}... | collective-permute-start | bytes 122888 | tf_op jit(solution)/shard_map/ppermute | solution.py:346
  99.5 7.2 %collective-permute-start.5 = (bf16[5,32,128]{2,1,0:T(8,128)(2,1)S(1)}, bf16[5,32,128]{2,1,0:T(8,128)(2,1)S(1)}, u32[]{:S(2)}, u32[]{:S(2)}) collective-permute-start(bf16[5,32,128]{2,1,0:T(8,128)(2,1)S(1)} %get-tuple-element.35), channel_id=1, source_target_pairs={{1,2},{3,4},{5,6},{7,8},{9,10},{11,12},{13,14},{15,16},{17,18},{19... | collective-permute-start | bytes 122888 | tf_op jit(solution)/shard_map/ppermute | solution.py:346
  102.2 4.7 %collective-permute-start.6 = (bf16[5,32,128]{2,1,0:T(8,128)(2,1)S(1)}, bf16[5,32,128]{2,1,0:T(8,128)(2,1)S(1)}, u32[]{:S(2)}, u32[]{:S(2)}) collective-permute-start(bf16[5,32,128]{2,1,0:T(8,128)(2,1)S(1)} %get-tuple-element.36), channel_id=1, source_target_pairs={{0,32},{64,96},{128,160},{192,224},{256,288},{320,352},{384,416},{... | collective-permute-start | bytes 122888 | tf_op jit(solution)/shard_map/ppermute | solution.py:346
  104.2 3.1 %collective-permute-start.7 = (bf16[5,32,128]{2,1,0:T(8,128)(2,1)S(1)}, bf16[5,32,128]{2,1,0:T(8,128)(2,1)S(1)}, u32[]{:S(2)}, u32[]{:S(2)}) collective-permute-start(bf16[5,32,128]{2,1,0:T(8,128)(2,1)S(1)} %get-tuple-element.37), channel_id=1, source_target_pairs={{0,1},{2,3},{4,5},{6,7},{8,9},{10,11},{12,13},{14,15},{16,17},{18,... | collective-permute-start | bytes 122888 | tf_op jit(solution)/shard_map/ppermute | solution.py:346

commit v11 on v10

--- a/solution.py
+++ b/solution.py
@@ -15,6 +15,8 @@
 PAIR = 2
 LANES = 128
 GROUP = 4
+KEEP = 11
+CHUNK = 5
 
 
 def call(kernel, out_shape, in_spaces, out_spaces, scratch=(), aliases=None, flops=1000, touched=1000000, vmem=40):
@@ -133,8 +135,15 @@
     return dot(chosen, high) + dot(chosen, middle) + dot(chosen, low)
 
 
-def products(chosen, received, matrices, answer, spread, result):
-    own_slots, levels, fields, _ = matrices.shape
+def bring(matrices_hbm, kept, sem):
+    copy = pltpu.make_async_copy(matrices_hbm.at[: kept.shape[0]], kept, sem)
+    copy.start()
+    copy.wait()
+
+
+def products(chosen, received, matrices, arrivals, answer, spread, result):
+    own_slots = len(matrices)
+    levels, fields, _ = matrices[0].shape
     owners = received.shape[0]
     depth = levels * fields
     tail = levels - LANES
@@ -157,8 +166,10 @@
     result[...] = jnp.zeros(result.shape, F32)
     for s in range(own_slots):
         at = slice(s * fields, (s + 1) * fields)
+        if s in arrivals:
+            arrivals[s].wait()
         result[at, :levels] = jnp.dot(
-            spread[at].astype(BF16), matrices[s].reshape(depth, levels), preferred_element_type=F32
+            spread[at].astype(BF16), matrices[s][...].reshape(depth, levels), preferred_element_type=F32
         )
     backward = []
     for k in range(PAIR):
@@ -173,18 +184,28 @@
     answer[...] = jnp.concatenate([block[:, :LANES] for block in blocks] + [tails], axis=1).reshape(answer.shape)
 
 
-def physics_first(received, matrices, answer, chosen_out, spread, result):
-    own_slots, levels, fields, _ = matrices.shape
+def physics_first(received, kept, matrices_hbm, answer, chosen_out, spread, result, rest, sems):
+    own_slots, levels, fields, _ = matrices_hbm.shape
+    keep = kept.shape[0]
+    arrivals = {}
+    for i, s in enumerate(range(keep, own_slots, CHUNK)):
+        count = min(CHUNK, own_slots - s)
+        arrivals[s] = pltpu.make_async_copy(
+            matrices_hbm.at[s : s + count], rest.at[s - keep : s - keep + count], sems.at[i]
+        )
+        arrivals[s].start()
     owners = received.shape[0]
     code_lane = fields * levels
     codes = received[...].reshape(owners * PAIR, received.shape[2]).astype(F32)[:, code_lane : code_lane + 1]
     wanted = (lax.broadcasted_iota(jnp.int32, chosen_out.shape, 1) // fields + 1).astype(F32)
     chosen_out[...] = (codes == wanted).astype(F32)
-    products(chosen_out, received, matrices, answer, spread, result)
+    matrices = [kept.at[s] for s in range(keep)] + [rest.at[s] for s in range(own_slots - keep)]
+    products(chosen_out, received, matrices, arrivals, answer, spread, result)
 
 
 def physics_second(received, matrices, chosen, answer, spread, result):
-    products(chosen, received, matrices, answer, spread, result)
+    each = [matrices.at[s] for s in range(matrices.shape[0])]
+    products(chosen, received, each, {}, answer, spread, result)
 
 
 def add_first(plan, returned, late, field, *rest, tail):
@@ -398,9 +419,24 @@
         VMEM((own_slots * fields, levels * fields), F32),
         VMEM((own_slots * fields, 2 * LANES), F32),
     ]
-    answer, chosen = call(physics_first, [answer_shape, chosen_shape], [VMEM] * 2, [VMEM] * 2, spaces)(
-        exchange(outbox), matrices
-    )
+    (kept,) = call(
+        bring,
+        [shape((KEEP,) + matrices.shape[1:], BF16)],
+        [HBM],
+        [VMEM],
+        [pltpu.SemaphoreType.DMA(())],
+        touched=4000000,
+        vmem=50,
+    )(matrices)
+    left = own_slots - KEEP
+    answer, chosen = call(
+        physics_first,
+        [answer_shape, chosen_shape],
+        [VMEM, VMEM, HBM],
+        [VMEM] * 2,
+        spaces + [VMEM((left,) + matrices.shape[1:], BF16), pltpu.SemaphoreType.DMA((-(-left // CHUNK),))],
+        vmem=50,
+    )(exchange(outbox), kept, matrices)
     returned = exchange(answer)
 
     def add(kernel, returned, base, aliases, edge_type):

time: 109 us -> 110 us (level)
  blocking collectives: 66.3 us -> 45 us
  starting transfers between devices: 27.1 us -> 38.8 us
  waiting for transfers between devices: 1.51 us -> 9.52 us
  Pallas kernels: 10.8 us -> 13.2 us
    all_to_all x4 -> x3, blocking collectives: 66.3 us -> 45 us  [exchange(): return lax.all_to_all(lines, 'gy', split_axis=0, concat_axis=0, tiled=True)]
    all_to_all x0 -> x1, starting transfers between devices: none -> 11.2 us  [exchange(): return lax.all_to_all(lines, 'gy', split_axis=0, concat_axis=0, tiled=True)]
    all_to_all x0 -> x1, waiting for transfers between devices: none -> 8.02 us  [exchange(): return lax.all_to_all(lines, 'gy', split_axis=0, concat_axis=0, tiled=True)]
    pallas_call x1 -> x2, Pallas kernels: 1.48 us -> 4 us  [the longest x1 2.12 us: on_device(): call(physics_first, [answer_shape, chosen_shape], [VMEM, VMEM, HBM], [VME...]
    unnamed x12 -> x10, local copies, waits for them, and re-layouts: 2.3 us -> 2.29 us
  transfers between devices with their start and end apart: 8 -> 9, of which waited for: 3 -> 4; matrix products, arithmetic and copies ran while one was open for 0% -> 0% of each run, Pallas kernels for 1% -> 3%
where the time goes in v11:
time: 110 us
  blocking collectives  45 us (41%)
  starting transfers between devices  38.8 us (35%)
  Pallas kernels  13.2 us (12%)
  waiting for transfers between devices  9.52 us (9%)
  local copies, waits for them, and re-layouts  2.29 us (2%)
    all_to_all x3, blocking collectives, exchange(): return lax.all_to_all(lines, 'gy', split_axis=0, concat_axis=0, tiled=True)  45 us
    ppermute x8, starting transfers between devices, swap(): lax.ppermute(edge, axis, pairs + [(high, low) for low, high in pairs])  27.6 us
    all_to_all x1, starting transfers between devices, exchange(): return lax.all_to_all(lines, 'gy', split_axis=0, concat_axis=0, tiled=True)  11.2 us
    all_to_all x1, waiting for transfers between devices, exchange(): return lax.all_to_all(lines, 'gy', split_axis=0, concat_axis=0, tiled=True)  8.02 us
    unnamed x10, local copies, waits for them, and re-layouts  2.29 us
  transfers between devices with their start and end apart: 9, of which 4 were waited for; matrix products, arithmetic and copies ran while one was open for 0% of the time, Pallas kernels for 3%

profile of v11, /device:TPU:1, one launch (start us, length us, event | category | flops | bytes accessed | tf_op | source)
XLA Modules:
  0.0 109.7 jit_solution(16343728310528610459)
XLA Ops:
  0.7 2.2 %shard_map.82 = (bf16[32,2,640]{2,1,0:T(2,128)(2,1)}, s32[97]{0:T(128)}) custom-call(s32[1,1,48]{2,1,0:T(1,128)} %cols_hbm.1, s32[1,1]{1,0:T(1,128)S(6)} %copy.15.count_hbm, s32[1,1,48]{2,1,0:T(1,128)} %owner_hbm.1, s32[1,1,48]{2,1,0:T(1,128)} %slot_hbm.1, bf16[4,512,137]{2,1,0:T(8,128)(2,1)} %bitcast.16), custom_call_target="tpu_custom_call" | custom-call | flops 1000 | bytes 1000000 | tf_op jit(solution)/shard_map/pallas_call | solution.py:397
  2.8 11.2 %all-to-all-start = ((bf16[32,2,640]{2,1,0:T(2,128)(2,1)}), bf16[32,2,640]{2,1,0:T(2,128)(2,1)S(1)}, u32[]{:S(2)}, u32[]{:S(2)}) async-start(bf16[32,2,640]{2,1,0:T(2,128)(2,1)} %get-tuple-element.23), calls=%async_computation | async-start | bytes 163840 | tf_op jit(solution)/shard_map/all_to_all | solution.py:359
  14.1 1.9 %shard_map.83.kept = bf16[11,137,4,137]{3,2,1,0:T(4,128)(2,1)S(1)} custom-call(bf16[16,137,4,137]{3,2,1,0:T(4,128)(2,1)} %bitcast.13), custom_call_target="tpu_custom_call" | custom-call | flops 1000 | bytes 4000000 | tf_op jit(solution)/shard_map/pallas_call | solution.py:422
  16.0 8.0 %all-to-all-done.received = bf16[32,2,640]{2,1,0:T(2,128)(2,1)S(1)} async-done(((bf16[32,2,640]{2,1,0:T(2,128)(2,1)}), bf16[32,2,640]{2,1,0:T(2,128)(2,1)S(1)}, u32[]{:S(2)}, u32[]{:S(2)}) %all-to-all-start) | async-done | bytes 81952 | tf_op jit(solution)/shard_map/all_to_all | solution.py:359
  24.0 2.1 %shard_map.84 = (f32[32,1,1152]{2,1,0:T(1,128)S(1)}, f32[64,64]{1,0:T(8,128)S(1)}) custom-call(bf16[32,2,640]{2,1,0:T(2,128)(2,1)S(1)} %all-to-all-done.received, bf16[11,137,4,137]{3,2,1,0:T(4,128)(2,1)S(1)} %shard_map.83.kept, bf16[16,137,4,137]{3,2,1,0:T(4,128)(2,1)} %bitcast.14), custom_call_target="tpu_custom_call" | custom-call | flops 1000 | bytes 1000000 | tf_op jit(solution)/shard_map/pallas_call | solution.py:432
  26.2 14.5 %all_to_all.20.returned = f32[32,1,1152]{2,1,0:T(1,128)S(1)} all-to-all(f32[32,1,1152]{2,1,0:T(1,128)S(1)} %get-tuple-element.24), channel_id=1, replica_groups=mesh['gx'=16,'gy'=32] {'gy'}, dimensions={0} | all-to-all | bytes 294912 | tf_op jit(solution)/shard_map/all_to_all | solution.py:359
  40.7 1.0 shard_map.85
  41.7 11.3 %collective-permute-start = (f32[5,32,128]{2,1,0:T(8,128)S(1)}, f32[5,32,128]{2,1,0:T(8,128)S(1)}, u32[]{:S(2)}, u32[]{:S(2)}) collective-permute-start(f32[5,32,128]{2,1,0:T(8,128)S(1)} %get-tuple-element.26), channel_id=1, source_target_pairs={{32,64},{96,128},{160,192},{224,256},{288,320},{352,384},{416,448}... | collective-permute-start | bytes 245768 | tf_op jit(solution)/shard_map/ppermute | solution.py:367
  53.0 2.8 %collective-permute-start.1 = (f32[5,32,128]{2,1,0:T(8,128)S(1)}, f32[5,32,128]{2,1,0:T(8,128)S(1)}, u32[]{:S(2)}, u32[]{:S(2)}) collective-permute-start(f32[5,32,128]{2,1,0:T(8,128)S(1)} %get-tuple-element.27), channel_id=1, source_target_pairs={{1,2},{3,4},{5,6},{7,8},{9,10},{11,12},{13,14},{15,16},{17,18},{19... | collective-permute-start | bytes 245768 | tf_op jit(solution)/shard_map/ppermute | solution.py:367
  55.7 1.9 %collective-permute-start.2 = (f32[5,32,128]{2,1,0:T(8,128)S(1)}, f32[5,32,128]{2,1,0:T(8,128)S(1)}, u32[]{:S(2)}, u32[]{:S(2)}) collective-permute-start(f32[5,32,128]{2,1,0:T(8,128)S(1)} %get-tuple-element.28), channel_id=1, source_target_pairs={{0,32},{64,96},{128,160},{192,224},{256,288},{320,352},{384,416},{... | collective-permute-start | bytes 245768 | tf_op jit(solution)/shard_map/ppermute | solution.py:367
  57.7 1.9 %collective-permute-start.3 = (f32[5,32,128]{2,1,0:T(8,128)S(1)}, f32[5,32,128]{2,1,0:T(8,128)S(1)}, u32[]{:S(2)}, u32[]{:S(2)}) collective-permute-start(f32[5,32,128]{2,1,0:T(8,128)S(1)} %get-tuple-element.29), channel_id=1, source_target_pairs={{0,1},{2,3},{4,5},{6,7},{8,9},{10,11},{12,13},{14,15},{16,17},{18,... | collective-permute-start | bytes 245768 | tf_op jit(solution)/shard_map/ppermute | solution.py:367
  59.6 0.8 shard_map.86.inner
  60.4 0.9 collective-permute-done.2.lon_even
  61.4 0.8 shard_map.87
  62.2 16.2 %all_to_all.21.received = bf16[32,2,640]{2,1,0:T(2,128)(2,1)S(1)} all-to-all(bf16[32,2,640]{2,1,0:T(2,128)(2,1)S(1)} %get-tuple-element.30), channel_id=1, replica_groups=mesh['gx'=16,'gy'=32] {'gy'}, dimensions={0} | all-to-all | bytes 163840 | tf_op jit(solution)/shard_map/all_to_all | solution.py:359
  78.4 2.3 %copy-done = bf16[1,16,4,137,137]{4,2,3,1,0:T(4,128)(2,1)S(1)} copy-done((bf16[1,16,4,137,137]{4,2,3,1,0:T(4,128)(2,1)S(1)}, bf16[1,16,4,137,137]{4,2,3,1,0:T(4,128)(2,1)}, u32[]{:S(2)}) %copy-start) | copy-done | bytes 2402456
  80.7 1.4 %shard_map.88 = f32[32,1,1152]{2,1,0:T(1,128)S(1)} custom-call(bf16[32,2,640]{2,1,0:T(2,128)(2,1)S(1)} %all_to_all.21.received, bf16[16,137,4,137]{3,2,1,0:T(4,128)(2,1)S(1)} %bitcast.15, f32[64,64]{1,0:T(8,128)S(1)} %get-tuple-element.31.chosen), custom_call_target="tpu_custom_call" | custom-call | flops 1000 | bytes 1000000 | tf_op jit(solution)/shard_map/pallas_call | solution.py:463
  82.1 14.3 %all_to_all.22.returned = f32[32,1,1152]{2,1,0:T(1,128)S(1)} all-to-all(f32[32,1,1152]{2,1,0:T(1,128)S(1)} %shard_map.88), channel_id=1, replica_groups=mesh['gx'=16,'gy'=32] {'gy'}, dimensions={0} | all-to-all | bytes 294912 | tf_op jit(solution)/shard_map/all_to_all | solution.py:359
  96.4 0.8 shard_map.89
  97.2 3.0 %collective-permute-start.4 = (bf16[5,32,128]{2,1,0:T(8,128)(2,1)S(1)}, bf16[5,32,128]{2,1,0:T(8,128)(2,1)S(1)}, u32[]{:S(2)}, u32[]{:S(2)}) collective-permute-start(bf16[5,32,128]{2,1,0:T(8,128)(2,1)S(1)} %get-tuple-element.34), channel_id=1, source_target_pairs={{32,64},{96,128},{160,192},{224,256},{288,320},{352,384},{416,448}... | collective-permute-start | bytes 122888 | tf_op jit(solution)/shard_map/ppermute | solution.py:367
  100.2 2.8 %collective-permute-start.5 = (bf16[5,32,128]{2,1,0:T(8,128)(2,1)S(1)}, bf16[5,32,128]{2,1,0:T(8,128)(2,1)S(1)}, u32[]{:S(2)}, u32[]{:S(2)}) collective-permute-start(bf16[5,32,128]{2,1,0:T(8,128)(2,1)S(1)} %get-tuple-element.35), channel_id=1, source_target_pairs={{1,2},{3,4},{5,6},{7,8},{9,10},{11,12},{13,14},{15,16},{17,18},{19... | collective-permute-start | bytes 122888 | tf_op jit(solution)/shard_map/ppermute | solution.py:367
  103.1 1.9 %collective-permute-start.6 = (bf16[5,32,128]{2,1,0:T(8,128)(2,1)S(1)}, bf16[5,32,128]{2,1,0:T(8,128)(2,1)S(1)}, u32[]{:S(2)}, u32[]{:S(2)}) collective-permute-start(bf16[5,32,128]{2,1,0:T(8,128)(2,1)S(1)} %get-tuple-element.36), channel_id=1, source_target_pairs={{0,32},{64,96},{128,160},{192,224},{256,288},{320,352},{384,416},{... | collective-permute-start | bytes 122888 | tf_op jit(solution)/shard_map/ppermute | solution.py:367
  105.0 1.9 %collective-permute-start.7 = (bf16[5,32,128]{2,1,0:T(8,128)(2,1)S(1)}, bf16[5,32,128]{2,1,0:T(8,128)(2,1)S(1)}, u32[]{:S(2)}, u32[]{:S(2)}) collective-permute-start(bf16[5,32,128]{2,1,0:T(8,128)(2,1)S(1)} %get-tuple-element.37), channel_id=1, source_target_pairs={{0,1},{2,3},{4,5},{6,7},{8,9},{10,11},{12,13},{14,15},{16,17},{18,... | collective-permute-start | bytes 122888 | tf_op jit(solution)/shard_map/ppermute | solution.py:367
  108.1 1.6 %shard_map.91 = (f32[4,512,137]{2,1,0:T(8,128)}, f32[5,512,128]{2,1,0:T(8,128)S(1)}) custom-call(f32[5,512,128]{2,1,0:T(8,128)S(1)} %shard_map.90.inner, f32[4,16,32]{2,1,0:T(8,128)S(1)} %bitcast.22, bf16[5,32,128]{2,1,0:T(8,128)(2,1)S(1)} %collective-permute-done.4.lon_odd, ...), custom_call_target="tpu_custom_call", output_to_operand_aliasing={{1}: (0, {})} | custom-call | flops 1000 | bytes 1000000 | tf_op jit(solution)/shard_map/pallas_call | solution.py:469
  (17 shorter events, 1.2 us)
Async XLA Ops:
  2.8 21.2 %all-to-all-start = ((bf16[32,2,640]{2,1,0:T(2,128)(2,1)}), bf16[32,2,640]{2,1,0:T(2,128)(2,1)S(1)}, u32[]{:S(2)}, u32[]{:S(2)}) async-start(bf16[32,2,640]{2,1,0:T(2,128)(2,1)} %get-tuple-element.23), calls=%async_computation | async-start | bytes 163840 | tf_op jit(solution)/shard_map/all_to_all | solution.py:359
  16.0 24.7 %copy-start.4 = (s32[97]{0:T(128)S(1)}, s32[97]{0:T(128)}, u32[]{:S(2)}) copy-start(s32[97]{0:T(128)} %get-tuple-element.22.plan) | copy-start | bytes 1168
  24.0 16.7 %copy-start.1 = (bf16[4,137,32,16]{1,3,2,0:T(8,128)(2,1)S(1)}, bf16[4,137,32,16]{1,3,2,0:T(8,128)(2,1)}, u32[]{:S(2)}) copy-start(bf16[4,137,32,16]{1,3,2,0:T(8,128)(2,1)} %param.8) | copy-start | bytes 1683460
  26.1 33.5 %copy-start.2 = (bf16[4,137,32,16]{1,3,2,0:T(8,128)(2,1)S(1)}, bf16[4,137,32,16]{1,3,2,0:T(8,128)(2,1)}, u32[]{:S(2)}) copy-start(bf16[4,137,32,16]{1,3,2,0:T(8,128)(2,1)} %param.9) | copy-start | bytes 1683460
  26.1 33.5 %copy-start.3 = (f32[4,32,16]{1,2,0:T(8,128)S(1)}, f32[4,32,16]{1,2,0:T(8,128)}, u32[]{:S(2)}) copy-start(f32[4,32,16]{1,2,0:T(8,128)} %param.10) | copy-start | bytes 24580
  41.7 18.7 %collective-permute-start = (f32[5,32,128]{2,1,0:T(8,128)S(1)}, f32[5,32,128]{2,1,0:T(8,128)S(1)}, u32[]{:S(2)}, u32[]{:S(2)}) collective-permute-start(f32[5,32,128]{2,1,0:T(8,128)S(1)} %get-tuple-element.26), channel_id=1, source_target_pairs={{32,64},{96,128},{160,192},{224,256},{288,320},{352,384},{416,448}... | collective-permute-start | bytes 245768 | tf_op jit(solution)/shard_map/ppermute | solution.py:367
  53.0 7.4 %collective-permute-start.1 = (f32[5,32,128]{2,1,0:T(8,128)S(1)}, f32[5,32,128]{2,1,0:T(8,128)S(1)}, u32[]{:S(2)}, u32[]{:S(2)}) collective-permute-start(f32[5,32,128]{2,1,0:T(8,128)S(1)} %get-tuple-element.27), channel_id=1, source_target_pairs={{1,2},{3,4},{5,6},{7,8},{9,10},{11,12},{13,14},{15,16},{17,18},{19... | collective-permute-start | bytes 245768 | tf_op jit(solution)/shard_map/ppermute | solution.py:367
  55.7 5.6 %collective-permute-start.2 = (f32[5,32,128]{2,1,0:T(8,128)S(1)}, f32[5,32,128]{2,1,0:T(8,128)S(1)}, u32[]{:S(2)}, u32[]{:S(2)}) collective-permute-start(f32[5,32,128]{2,1,0:T(8,128)S(1)} %get-tuple-element.28), channel_id=1, source_target_pairs={{0,32},{64,96},{128,160},{192,224},{256,288},{320,352},{384,416},{... | collective-permute-start | bytes 245768 | tf_op jit(solution)/shard_map/ppermute | solution.py:367
  57.7 3.7 %collective-permute-start.3 = (f32[5,32,128]{2,1,0:T(8,128)S(1)}, f32[5,32,128]{2,1,0:T(8,128)S(1)}, u32[]{:S(2)}, u32[]{:S(2)}) collective-permute-start(f32[5,32,128]{2,1,0:T(8,128)S(1)} %get-tuple-element.29), channel_id=1, source_target_pairs={{0,1},{2,3},{4,5},{6,7},{8,9},{10,11},{12,13},{14,15},{16,17},{18,... | collective-permute-start | bytes 245768 | tf_op jit(solution)/shard_map/ppermute | solution.py:367
  78.4 2.3 %copy-start = (bf16[1,16,4,137,137]{4,2,3,1,0:T(4,128)(2,1)S(1)}, bf16[1,16,4,137,137]{4,2,3,1,0:T(4,128)(2,1)}, u32[]{:S(2)}) copy-start(bf16[1,16,4,137,137]{4,2,3,1,0:T(4,128)(2,1)} %param.11) | copy-start | bytes 7207300
  97.2 10.3 %collective-permute-start.4 = (bf16[5,32,128]{2,1,0:T(8,128)(2,1)S(1)}, bf16[5,32,128]{2,1,0:T(8,128)(2,1)S(1)}, u32[]{:S(2)}, u32[]{:S(2)}) collective-permute-start(bf16[5,32,128]{2,1,0:T(8,128)(2,1)S(1)} %get-tuple-element.34), channel_id=1, source_target_pairs={{32,64},{96,128},{160,192},{224,256},{288,320},{352,384},{416,448}... | collective-permute-start | bytes 122888 | tf_op jit(solution)/shard_map/ppermute | solution.py:367
  100.2 7.3 %collective-permute-start.5 = (bf16[5,32,128]{2,1,0:T(8,128)(2,1)S(1)}, bf16[5,32,128]{2,1,0:T(8,128)(2,1)S(1)}, u32[]{:S(2)}, u32[]{:S(2)}) collective-permute-start(bf16[5,32,128]{2,1,0:T(8,128)(2,1)S(1)} %get-tuple-element.35), channel_id=1, source_target_pairs={{1,2},{3,4},{5,6},{7,8},{9,10},{11,12},{13,14},{15,16},{17,18},{19... | collective-permute-start | bytes 122888 | tf_op jit(solution)/shard_map/ppermute | solution.py:367
  103.1 4.7 %collective-permute-start.6 = (bf16[5,32,128]{2,1,0:T(8,128)(2,1)S(1)}, bf16[5,32,128]{2,1,0:T(8,128)(2,1)S(1)}, u32[]{:S(2)}, u32[]{:S(2)}) collective-permute-start(bf16[5,32,128]{2,1,0:T(8,128)(2,1)S(1)} %get-tuple-element.36), channel_id=1, source_target_pairs={{0,32},{64,96},{128,160},{192,224},{256,288},{320,352},{384,416},{... | collective-permute-start | bytes 122888 | tf_op jit(solution)/shard_map/ppermute | solution.py:367
  105.0 3.1 %collective-permute-start.7 = (bf16[5,32,128]{2,1,0:T(8,128)(2,1)S(1)}, bf16[5,32,128]{2,1,0:T(8,128)(2,1)S(1)}, u32[]{:S(2)}, u32[]{:S(2)}) collective-permute-start(bf16[5,32,128]{2,1,0:T(8,128)(2,1)S(1)} %get-tuple-element.37), channel_id=1, source_target_pairs={{0,1},{2,3},{4,5},{6,7},{8,9},{10,11},{12,13},{14,15},{16,17},{18,... | collective-permute-start | bytes 122888 | tf_op jit(solution)/shard_map/ppermute | solution.py:367

commit v12 on v11

--- a/solution.py
+++ b/solution.py
@@ -184,9 +184,8 @@
     answer[...] = jnp.concatenate([block[:, :LANES] for block in blocks] + [tails], axis=1).reshape(answer.shape)
 
 
-def physics_first(received, kept, matrices_hbm, answer, chosen_out, spread, result, rest, sems):
-    own_slots, levels, fields, _ = matrices_hbm.shape
-    keep = kept.shape[0]
+def fetch_rest(kept, matrices_hbm, rest, sems):
+    own_slots, keep = matrices_hbm.shape[0], kept.shape[0]
     arrivals = {}
     for i, s in enumerate(range(keep, own_slots, CHUNK)):
         count = min(CHUNK, own_slots - s)
@@ -194,18 +193,23 @@
             matrices_hbm.at[s : s + count], rest.at[s - keep : s - keep + count], sems.at[i]
         )
         arrivals[s].start()
+    return [kept.at[s] for s in range(keep)] + [rest.at[s] for s in range(own_slots - keep)], arrivals
+
+
+def physics_first(received, kept, matrices_hbm, answer, chosen_out, spread, result, rest, sems):
+    matrices, arrivals = fetch_rest(kept, matrices_hbm, rest, sems)
+    levels, fields = matrices_hbm.shape[1:3]
     owners = received.shape[0]
     code_lane = fields * levels
     codes = received[...].reshape(owners * PAIR, received.shape[2]).astype(F32)[:, code_lane : code_lane + 1]
     wanted = (lax.broadcasted_iota(jnp.int32, chosen_out.shape, 1) // fields + 1).astype(F32)
     chosen_out[...] = (codes == wanted).astype(F32)
-    matrices = [kept.at[s] for s in range(keep)] + [rest.at[s] for s in range(own_slots - keep)]
     products(chosen_out, received, matrices, arrivals, answer, spread, result)
 
 
-def physics_second(received, matrices, chosen, answer, spread, result):
-    each = [matrices.at[s] for s in range(matrices.shape[0])]
-    products(chosen, received, each, {}, answer, spread, result)
+def physics_second(received, kept, matrices_hbm, chosen, answer, spread, result, rest, sems):
+    matrices, arrivals = fetch_rest(kept, matrices_hbm, rest, sems)
+    products(chosen, received, matrices, arrivals, answer, spread, result)
 
 
 def add_first(plan, returned, late, field, *rest, tail):
@@ -415,9 +419,12 @@
     )(cloudy_cols, cloudy_count, owner_rank, owner_slot, late)
     chosen_shape = shape((groups * PAIR, own_slots * fields), F32)
     answer_shape = shape((groups, 1, (per_owner + 1) * LANES), F32)
+    left = own_slots - KEEP
     spaces = [
         VMEM((own_slots * fields, levels * fields), F32),
         VMEM((own_slots * fields, 2 * LANES), F32),
+        VMEM((left,) + matrices.shape[1:], BF16),
+        pltpu.SemaphoreType.DMA((-(-left // CHUNK),)),
     ]
     (kept,) = call(
         bring,
@@ -428,13 +435,12 @@
         touched=4000000,
         vmem=50,
     )(matrices)
-    left = own_slots - KEEP
     answer, chosen = call(
         physics_first,
         [answer_shape, chosen_shape],
         [VMEM, VMEM, HBM],
         [VMEM] * 2,
-        spaces + [VMEM((left,) + matrices.shape[1:], BF16), pltpu.SemaphoreType.DMA((-(-left // CHUNK),))],
+        spaces,
         vmem=50,
     )(exchange(outbox), kept, matrices)
     returned = exchange(answer)
@@ -460,8 +466,8 @@
         [VMEM(rows_shape, F32)],
         {1: 0},
     )(plan, inner, coef, *neighbours)
-    (answer,) = call(physics_second, [answer_shape], [VMEM] * 3, [VMEM], spaces)(
-        exchange(outbox), matrices, chosen
+    (answer,) = call(physics_second, [answer_shape], [VMEM, VMEM, HBM, VMEM], [VMEM], spaces, vmem=50)(
+        exchange(outbox), kept, matrices, chosen
     )
     field, *edges = add(add_increments, exchange(answer), adjoint, {2: 0}, BF16)
     neighbours = halos(*edges)

time: 110 us -> 108 us (0.982)
  local copies, waits for them, and re-layouts: 2.29 us -> 0.02 us
    unnamed x10 -> x8, local copies, waits for them, and re-layouts: 2.29 us -> 0.02 us
where the time goes in v12:
time: 108 us
  blocking collectives  45 us (42%)
  starting transfers between devices  38.4 us (36%)
  Pallas kernels  13.9 us (13%)
  waiting for transfers between devices  9.6 us (9%)
    all_to_all x3, blocking collectives, exchange(): return lax.all_to_all(lines, 'gy', split_axis=0, concat_axis=0, tiled=True)  45 us
    ppermute x8, starting transfers between devices, swap(): lax.ppermute(edge, axis, pairs + [(high, low) for low, high in pairs])  27.1 us
    all_to_all x1, starting transfers between devices, exchange(): return lax.all_to_all(lines, 'gy', split_axis=0, concat_axis=0, tiled=True)  11.3 us
    all_to_all x1, waiting for transfers between devices, exchange(): return lax.all_to_all(lines, 'gy', split_axis=0, concat_axis=0, tiled=True)  8.04 us
    pallas_call x1, Pallas kernels, on_device(): call(pack_first, [outbox_shape, plan_shape], [HBM] * 5, [VMEM, SMEM], [SM...  2.18 us
  transfers between devices with their start and end apart: 9, of which 4 were waited for; matrix products, arithmetic and copies ran while one was open for 0% of the time, Pallas kernels for 3%

profile of v12, /device:TPU:1, one launch (start us, length us, event | category | flops | bytes accessed | tf_op | source)
XLA Modules:
  0.0 107.8 jit_solution(2403806468831792166)
XLA Ops:
  0.7 2.2 %shard_map.82 = (bf16[32,2,640]{2,1,0:T(2,128)(2,1)}, s32[97]{0:T(128)}) custom-call(s32[1,1,48]{2,1,0:T(1,128)} %cols_hbm.1, s32[1,1]{1,0:T(1,128)S(6)} %copy.15.count_hbm, s32[1,1,48]{2,1,0:T(1,128)} %owner_hbm.1, s32[1,1,48]{2,1,0:T(1,128)} %slot_hbm.1, bf16[4,512,137]{2,1,0:T(8,128)(2,1)} %bitcast.13), custom_call_target="tpu_custom_call" | custom-call | flops 1000 | bytes 1000000 | tf_op jit(solution)/shard_map/pallas_call | solution.py:401
  2.8 11.3 %all-to-all-start = ((bf16[32,2,640]{2,1,0:T(2,128)(2,1)}), bf16[32,2,640]{2,1,0:T(2,128)(2,1)S(1)}, u32[]{:S(2)}, u32[]{:S(2)}) async-start(bf16[32,2,640]{2,1,0:T(2,128)(2,1)} %get-tuple-element.23), calls=%async_computation | async-start | bytes 163840 | tf_op jit(solution)/shard_map/all_to_all | solution.py:363
  14.1 1.9 %shard_map.83.kept = bf16[11,137,4,137]{3,2,1,0:T(4,128)(2,1)S(1)} custom-call(bf16[16,137,4,137]{3,2,1,0:T(4,128)(2,1)} %bitcast.20), custom_call_target="tpu_custom_call" | custom-call | flops 1000 | bytes 4000000 | tf_op jit(solution)/shard_map/pallas_call | solution.py:429
  16.0 8.0 %all-to-all-done.received = bf16[32,2,640]{2,1,0:T(2,128)(2,1)S(1)} async-done(((bf16[32,2,640]{2,1,0:T(2,128)(2,1)}), bf16[32,2,640]{2,1,0:T(2,128)(2,1)S(1)}, u32[]{:S(2)}, u32[]{:S(2)}) %all-to-all-start) | async-done | bytes 81952 | tf_op jit(solution)/shard_map/all_to_all | solution.py:363
  24.1 2.1 %shard_map.84 = (f32[32,1,1152]{2,1,0:T(1,128)S(1)}, f32[64,64]{1,0:T(8,128)S(1)}) custom-call(bf16[32,2,640]{2,1,0:T(2,128)(2,1)S(1)} %all-to-all-done.received, bf16[11,137,4,137]{3,2,1,0:T(4,128)(2,1)S(1)} %shard_map.83.kept, bf16[16,137,4,137]{3,2,1,0:T(4,128)(2,1)} %bitcast.21), custom_call_target="tpu_custom_call" | custom-call | flops 1000 | bytes 1000000 | tf_op jit(solution)/shard_map/pallas_call | solution.py:438
  26.2 14.5 %all_to_all.20.returned = f32[32,1,1152]{2,1,0:T(1,128)S(1)} all-to-all(f32[32,1,1152]{2,1,0:T(1,128)S(1)} %get-tuple-element.24), channel_id=1, replica_groups=mesh['gx'=16,'gy'=32] {'gy'}, dimensions={0} | all-to-all | bytes 294912 | tf_op jit(solution)/shard_map/all_to_all | solution.py:363
  40.7 1.0 shard_map.85
  41.8 11.2 %collective-permute-start = (f32[5,32,128]{2,1,0:T(8,128)S(1)}, f32[5,32,128]{2,1,0:T(8,128)S(1)}, u32[]{:S(2)}, u32[]{:S(2)}) collective-permute-start(f32[5,32,128]{2,1,0:T(8,128)S(1)} %get-tuple-element.26), channel_id=1, source_target_pairs={{32,64},{96,128},{160,192},{224,256},{288,320},{352,384},{416,448}... | collective-permute-start | bytes 245768 | tf_op jit(solution)/shard_map/ppermute | solution.py:371
  53.0 2.7 %collective-permute-start.1 = (f32[5,32,128]{2,1,0:T(8,128)S(1)}, f32[5,32,128]{2,1,0:T(8,128)S(1)}, u32[]{:S(2)}, u32[]{:S(2)}) collective-permute-start(f32[5,32,128]{2,1,0:T(8,128)S(1)} %get-tuple-element.27), channel_id=1, source_target_pairs={{1,2},{3,4},{5,6},{7,8},{9,10},{11,12},{13,14},{15,16},{17,18},{19... | collective-permute-start | bytes 245768 | tf_op jit(solution)/shard_map/ppermute | solution.py:371
  55.7 1.9 %collective-permute-start.2 = (f32[5,32,128]{2,1,0:T(8,128)S(1)}, f32[5,32,128]{2,1,0:T(8,128)S(1)}, u32[]{:S(2)}, u32[]{:S(2)}) collective-permute-start(f32[5,32,128]{2,1,0:T(8,128)S(1)} %get-tuple-element.28), channel_id=1, source_target_pairs={{0,32},{64,96},{128,160},{192,224},{256,288},{320,352},{384,416},{... | collective-permute-start | bytes 245768 | tf_op jit(solution)/shard_map/ppermute | solution.py:371
  57.6 1.9 %collective-permute-start.3 = (f32[5,32,128]{2,1,0:T(8,128)S(1)}, f32[5,32,128]{2,1,0:T(8,128)S(1)}, u32[]{:S(2)}, u32[]{:S(2)}) collective-permute-start(f32[5,32,128]{2,1,0:T(8,128)S(1)} %get-tuple-element.29), channel_id=1, source_target_pairs={{0,1},{2,3},{4,5},{6,7},{8,9},{10,11},{12,13},{14,15},{16,17},{18,... | collective-permute-start | bytes 245768 | tf_op jit(solution)/shard_map/ppermute | solution.py:371
  59.5 0.8 shard_map.86.inner
  60.3 1.0 collective-permute-done.2.lon_even
  61.3 0.8 shard_map.87
  62.2 16.2 %all_to_all.21.received = bf16[32,2,640]{2,1,0:T(2,128)(2,1)S(1)} all-to-all(bf16[32,2,640]{2,1,0:T(2,128)(2,1)S(1)} %get-tuple-element.30), channel_id=1, replica_groups=mesh['gx'=16,'gy'=32] {'gy'}, dimensions={0} | all-to-all | bytes 163840 | tf_op jit(solution)/shard_map/all_to_all | solution.py:363
  78.3 2.1 %shard_map.88 = f32[32,1,1152]{2,1,0:T(1,128)S(1)} custom-call(bf16[32,2,640]{2,1,0:T(2,128)(2,1)S(1)} %all_to_all.21.received, bf16[11,137,4,137]{3,2,1,0:T(4,128)(2,1)S(1)} %shard_map.83.kept, bf16[16,137,4,137]{3,2,1,0:T(4,128)(2,1)} %bitcast.22, f32[64,64]{1,0:T(8,128)S(1)} %get-tuple-element.31.chosen), custom_call_target="tpu_custom_call" | custom-call | flops 1000 | bytes 1000000 | tf_op jit(solution)/shard_map/pallas_call | solution.py:469
  80.4 14.3 %all_to_all.22.returned = f32[32,1,1152]{2,1,0:T(1,128)S(1)} all-to-all(f32[32,1,1152]{2,1,0:T(1,128)S(1)} %shard_map.88), channel_id=1, replica_groups=mesh['gx'=16,'gy'=32] {'gy'}, dimensions={0} | all-to-all | bytes 294912 | tf_op jit(solution)/shard_map/all_to_all | solution.py:363
  94.7 0.8 shard_map.89
  95.6 2.9 %collective-permute-start.4 = (bf16[5,32,128]{2,1,0:T(8,128)(2,1)S(1)}, bf16[5,32,128]{2,1,0:T(8,128)(2,1)S(1)}, u32[]{:S(2)}, u32[]{:S(2)}) collective-permute-start(bf16[5,32,128]{2,1,0:T(8,128)(2,1)S(1)} %get-tuple-element.34), channel_id=1, source_target_pairs={{32,64},{96,128},{160,192},{224,256},{288,320},{352,384},{416,448}... | collective-permute-start | bytes 122888 | tf_op jit(solution)/shard_map/ppermute | solution.py:371
  98.4 2.7 %collective-permute-start.5 = (bf16[5,32,128]{2,1,0:T(8,128)(2,1)S(1)}, bf16[5,32,128]{2,1,0:T(8,128)(2,1)S(1)}, u32[]{:S(2)}, u32[]{:S(2)}) collective-permute-start(bf16[5,32,128]{2,1,0:T(8,128)(2,1)S(1)} %get-tuple-element.35), channel_id=1, source_target_pairs={{1,2},{3,4},{5,6},{7,8},{9,10},{11,12},{13,14},{15,16},{17,18},{19... | collective-permute-start | bytes 122888 | tf_op jit(solution)/shard_map/ppermute | solution.py:371
  101.2 1.9 %collective-permute-start.6 = (bf16[5,32,128]{2,1,0:T(8,128)(2,1)S(1)}, bf16[5,32,128]{2,1,0:T(8,128)(2,1)S(1)}, u32[]{:S(2)}, u32[]{:S(2)}) collective-permute-start(bf16[5,32,128]{2,1,0:T(8,128)(2,1)S(1)} %get-tuple-element.36), channel_id=1, source_target_pairs={{0,32},{64,96},{128,160},{192,224},{256,288},{320,352},{384,416},{... | collective-permute-start | bytes 122888 | tf_op jit(solution)/shard_map/ppermute | solution.py:371
  103.1 1.9 %collective-permute-start.7 = (bf16[5,32,128]{2,1,0:T(8,128)(2,1)S(1)}, bf16[5,32,128]{2,1,0:T(8,128)(2,1)S(1)}, u32[]{:S(2)}, u32[]{:S(2)}) collective-permute-start(bf16[5,32,128]{2,1,0:T(8,128)(2,1)S(1)} %get-tuple-element.37), channel_id=1, source_target_pairs={{0,1},{2,3},{4,5},{6,7},{8,9},{10,11},{12,13},{14,15},{16,17},{18,... | collective-permute-start | bytes 122888 | tf_op jit(solution)/shard_map/ppermute | solution.py:371
  105.0 0.6 shard_map.90.inner
  106.2 1.6 %shard_map.91 = (f32[4,512,137]{2,1,0:T(8,128)}, f32[5,512,128]{2,1,0:T(8,128)S(1)}) custom-call(f32[5,512,128]{2,1,0:T(8,128)S(1)} %shard_map.90.inner, f32[4,16,32]{2,1,0:T(8,128)S(1)} %bitcast.19, bf16[5,32,128]{2,1,0:T(8,128)(2,1)S(1)} %collective-permute-done.4.lon_odd, ...), custom_call_target="tpu_custom_call", output_to_operand_aliasing={{1}: (0, {})} | custom-call | flops 1000 | bytes 1000000 | tf_op jit(solution)/shard_map/pallas_call | solution.py:475
  (15 shorter events, 0.6 us)
Async XLA Ops:
  2.8 21.2 %all-to-all-start = ((bf16[32,2,640]{2,1,0:T(2,128)(2,1)}), bf16[32,2,640]{2,1,0:T(2,128)(2,1)S(1)}, u32[]{:S(2)}, u32[]{:S(2)}) async-start(bf16[32,2,640]{2,1,0:T(2,128)(2,1)} %get-tuple-element.23), calls=%async_computation | async-start | bytes 163840 | tf_op jit(solution)/shard_map/all_to_all | solution.py:363
  16.0 24.7 %copy-start.3 = (s32[97]{0:T(128)S(1)}, s32[97]{0:T(128)}, u32[]{:S(2)}) copy-start(s32[97]{0:T(128)} %get-tuple-element.22.plan) | copy-start | bytes 1168
  24.1 16.7 %copy-start = (bf16[4,137,32,16]{1,3,2,0:T(8,128)(2,1)S(1)}, bf16[4,137,32,16]{1,3,2,0:T(8,128)(2,1)}, u32[]{:S(2)}) copy-start(bf16[4,137,32,16]{1,3,2,0:T(8,128)(2,1)} %param.8) | copy-start | bytes 1683460
  26.2 33.3 %copy-start.1 = (bf16[4,137,32,16]{1,3,2,0:T(8,128)(2,1)S(1)}, bf16[4,137,32,16]{1,3,2,0:T(8,128)(2,1)}, u32[]{:S(2)}) copy-start(bf16[4,137,32,16]{1,3,2,0:T(8,128)(2,1)} %param.9) | copy-start | bytes 1683460
  26.2 33.3 %copy-start.2 = (f32[4,32,16]{1,2,0:T(8,128)S(1)}, f32[4,32,16]{1,2,0:T(8,128)}, u32[]{:S(2)}) copy-start(f32[4,32,16]{1,2,0:T(8,128)} %param.10) | copy-start | bytes 24580
  41.8 18.6 %collective-permute-start = (f32[5,32,128]{2,1,0:T(8,128)S(1)}, f32[5,32,128]{2,1,0:T(8,128)S(1)}, u32[]{:S(2)}, u32[]{:S(2)}) collective-permute-start(f32[5,32,128]{2,1,0:T(8,128)S(1)} %get-tuple-element.26), channel_id=1, source_target_pairs={{32,64},{96,128},{160,192},{224,256},{288,320},{352,384},{416,448}... | collective-permute-start | bytes 245768 | tf_op jit(solution)/shard_map/ppermute | solution.py:371
  53.0 7.4 %collective-permute-start.1 = (f32[5,32,128]{2,1,0:T(8,128)S(1)}, f32[5,32,128]{2,1,0:T(8,128)S(1)}, u32[]{:S(2)}, u32[]{:S(2)}) collective-permute-start(f32[5,32,128]{2,1,0:T(8,128)S(1)} %get-tuple-element.27), channel_id=1, source_target_pairs={{1,2},{3,4},{5,6},{7,8},{9,10},{11,12},{13,14},{15,16},{17,18},{19... | collective-permute-start | bytes 245768 | tf_op jit(solution)/shard_map/ppermute | solution.py:371
  55.7 5.7 %collective-permute-start.2 = (f32[5,32,128]{2,1,0:T(8,128)S(1)}, f32[5,32,128]{2,1,0:T(8,128)S(1)}, u32[]{:S(2)}, u32[]{:S(2)}) collective-permute-start(f32[5,32,128]{2,1,0:T(8,128)S(1)} %get-tuple-element.28), channel_id=1, source_target_pairs={{0,32},{64,96},{128,160},{192,224},{256,288},{320,352},{384,416},{... | collective-permute-start | bytes 245768 | tf_op jit(solution)/shard_map/ppermute | solution.py:371
  57.6 3.7 %collective-permute-start.3 = (f32[5,32,128]{2,1,0:T(8,128)S(1)}, f32[5,32,128]{2,1,0:T(8,128)S(1)}, u32[]{:S(2)}, u32[]{:S(2)}) collective-permute-start(f32[5,32,128]{2,1,0:T(8,128)S(1)} %get-tuple-element.29), channel_id=1, source_target_pairs={{0,1},{2,3},{4,5},{6,7},{8,9},{10,11},{12,13},{14,15},{16,17},{18,... | collective-permute-start | bytes 245768 | tf_op jit(solution)/shard_map/ppermute | solution.py:371
  95.6 10.1 %collective-permute-start.4 = (bf16[5,32,128]{2,1,0:T(8,128)(2,1)S(1)}, bf16[5,32,128]{2,1,0:T(8,128)(2,1)S(1)}, u32[]{:S(2)}, u32[]{:S(2)}) collective-permute-start(bf16[5,32,128]{2,1,0:T(8,128)(2,1)S(1)} %get-tuple-element.34), channel_id=1, source_target_pairs={{32,64},{96,128},{160,192},{224,256},{288,320},{352,384},{416,448}... | collective-permute-start | bytes 122888 | tf_op jit(solution)/shard_map/ppermute | solution.py:371
  98.4 7.2 %collective-permute-start.5 = (bf16[5,32,128]{2,1,0:T(8,128)(2,1)S(1)}, bf16[5,32,128]{2,1,0:T(8,128)(2,1)S(1)}, u32[]{:S(2)}, u32[]{:S(2)}) collective-permute-start(bf16[5,32,128]{2,1,0:T(8,128)(2,1)S(1)} %get-tuple-element.35), channel_id=1, source_target_pairs={{1,2},{3,4},{5,6},{7,8},{9,10},{11,12},{13,14},{15,16},{17,18},{19... | collective-permute-start | bytes 122888 | tf_op jit(solution)/shard_map/ppermute | solution.py:371
  101.2 4.7 %collective-permute-start.6 = (bf16[5,32,128]{2,1,0:T(8,128)(2,1)S(1)}, bf16[5,32,128]{2,1,0:T(8,128)(2,1)S(1)}, u32[]{:S(2)}, u32[]{:S(2)}) collective-permute-start(bf16[5,32,128]{2,1,0:T(8,128)(2,1)S(1)} %get-tuple-element.36), channel_id=1, source_target_pairs={{0,32},{64,96},{128,160},{192,224},{256,288},{320,352},{384,416},{... | collective-permute-start | bytes 122888 | tf_op jit(solution)/shard_map/ppermute | solution.py:371
  103.1 3.1 %collective-permute-start.7 = (bf16[5,32,128]{2,1,0:T(8,128)(2,1)S(1)}, bf16[5,32,128]{2,1,0:T(8,128)(2,1)S(1)}, u32[]{:S(2)}, u32[]{:S(2)}) collective-permute-start(bf16[5,32,128]{2,1,0:T(8,128)(2,1)S(1)} %get-tuple-element.37), channel_id=1, source_target_pairs={{0,1},{2,3},{4,5},{6,7},{8,9},{10,11},{12,13},{14,15},{16,17},{18,... | collective-permute-start | bytes 122888 | tf_op jit(solution)/shard_map/ppermute | solution.py:371

commit v13 on v12

--- a/solution.py
+++ b/solution.py
@@ -15,8 +15,8 @@
 PAIR = 2
 LANES = 128
 GROUP = 4
-KEEP = 11
-CHUNK = 5
+KEEP = 12
+CHUNK = 1
 
 
 def call(kernel, out_shape, in_spaces, out_spaces, scratch=(), aliases=None, flops=1000, touched=1000000, vmem=40):

time: 108 us -> 109 us (level)
  no operation moved by 1% of the time
where the time goes in v13:
time: 109 us; the launch traced here: 108 us
  blocking collectives  45 us (41%)
  starting transfers between devices  38.5 us (35%)
  Pallas kernels  14.1 us (13%)
  waiting for transfers between devices  9.54 us (9%)
    all_to_all x3, blocking collectives, exchange(): return lax.all_to_all(lines, 'gy', split_axis=0, concat_axis=0, tiled=True)  45 us
    ppermute x8, starting transfers between devices, swap(): lax.ppermute(edge, axis, pairs + [(high, low) for low, high in pairs])  27.2 us
    all_to_all x1, starting transfers between devices, exchange(): return lax.all_to_all(lines, 'gy', split_axis=0, concat_axis=0, tiled=True)  11.2 us
    all_to_all x1, waiting for transfers between devices, exchange(): return lax.all_to_all(lines, 'gy', split_axis=0, concat_axis=0, tiled=True)  7.96 us
    pallas_call x1, Pallas kernels, on_device(): call(pack_first, [outbox_shape, plan_shape], [HBM] * 5, [VMEM, SMEM], [SM...  2.18 us
  transfers between devices with their start and end apart: 9, of which 4 were waited for; matrix products, arithmetic and copies ran while one was open for 0% of the time, Pallas kernels for 3%

profile of v13, /device:TPU:1, one launch (start us, length us, event | category | flops | bytes accessed | tf_op | source)
XLA Modules:
  0.0 108.0 jit_solution(7504649933892144857)
XLA Ops:
  0.7 2.2 %shard_map.82 = (bf16[32,2,640]{2,1,0:T(2,128)(2,1)}, s32[97]{0:T(128)}) custom-call(s32[1,1,48]{2,1,0:T(1,128)} %cols_hbm.1, s32[1,1]{1,0:T(1,128)S(6)} %copy.15.count_hbm, s32[1,1,48]{2,1,0:T(1,128)} %owner_hbm.1, s32[1,1,48]{2,1,0:T(1,128)} %slot_hbm.1, bf16[4,512,137]{2,1,0:T(8,128)(2,1)} %bitcast.13), custom_call_target="tpu_custom_call" | custom-call | flops 1000 | bytes 1000000 | tf_op jit(solution)/shard_map/pallas_call | solution.py:401
  2.8 11.2 %all-to-all-start = ((bf16[32,2,640]{2,1,0:T(2,128)(2,1)}), bf16[32,2,640]{2,1,0:T(2,128)(2,1)S(1)}, u32[]{:S(2)}, u32[]{:S(2)}) async-start(bf16[32,2,640]{2,1,0:T(2,128)(2,1)} %get-tuple-element.23), calls=%async_computation | async-start | bytes 163840 | tf_op jit(solution)/shard_map/all_to_all | solution.py:363
  14.1 2.0 %shard_map.83.kept = bf16[12,137,4,137]{3,2,1,0:T(4,128)(2,1)S(1)} custom-call(bf16[16,137,4,137]{3,2,1,0:T(4,128)(2,1)} %bitcast.20), custom_call_target="tpu_custom_call" | custom-call | flops 1000 | bytes 4000000 | tf_op jit(solution)/shard_map/pallas_call | solution.py:429
  16.0 8.0 %all-to-all-done.received = bf16[32,2,640]{2,1,0:T(2,128)(2,1)S(1)} async-done(((bf16[32,2,640]{2,1,0:T(2,128)(2,1)}), bf16[32,2,640]{2,1,0:T(2,128)(2,1)S(1)}, u32[]{:S(2)}, u32[]{:S(2)}) %all-to-all-start) | async-done | bytes 81952 | tf_op jit(solution)/shard_map/all_to_all | solution.py:363
  24.0 2.2 %shard_map.84 = (f32[32,1,1152]{2,1,0:T(1,128)S(1)}, f32[64,64]{1,0:T(8,128)S(1)}) custom-call(bf16[32,2,640]{2,1,0:T(2,128)(2,1)S(1)} %all-to-all-done.received, bf16[12,137,4,137]{3,2,1,0:T(4,128)(2,1)S(1)} %shard_map.83.kept, bf16[16,137,4,137]{3,2,1,0:T(4,128)(2,1)} %bitcast.21), custom_call_target="tpu_custom_call" | custom-call | flops 1000 | bytes 1000000 | tf_op jit(solution)/shard_map/pallas_call | solution.py:438
  26.2 14.5 %all_to_all.20.returned = f32[32,1,1152]{2,1,0:T(1,128)S(1)} all-to-all(f32[32,1,1152]{2,1,0:T(1,128)S(1)} %get-tuple-element.24), channel_id=1, replica_groups=mesh['gx'=16,'gy'=32] {'gy'}, dimensions={0} | all-to-all | bytes 294912 | tf_op jit(solution)/shard_map/all_to_all | solution.py:363
  40.7 1.0 shard_map.85
  41.8 11.5 %collective-permute-start = (f32[5,32,128]{2,1,0:T(8,128)S(1)}, f32[5,32,128]{2,1,0:T(8,128)S(1)}, u32[]{:S(2)}, u32[]{:S(2)}) collective-permute-start(f32[5,32,128]{2,1,0:T(8,128)S(1)} %get-tuple-element.26), channel_id=1, source_target_pairs={{32,64},{96,128},{160,192},{224,256},{288,320},{352,384},{416,448}... | collective-permute-start | bytes 245768 | tf_op jit(solution)/shard_map/ppermute | solution.py:371
  53.3 2.5 %collective-permute-start.1 = (f32[5,32,128]{2,1,0:T(8,128)S(1)}, f32[5,32,128]{2,1,0:T(8,128)S(1)}, u32[]{:S(2)}, u32[]{:S(2)}) collective-permute-start(f32[5,32,128]{2,1,0:T(8,128)S(1)} %get-tuple-element.27), channel_id=1, source_target_pairs={{1,2},{3,4},{5,6},{7,8},{9,10},{11,12},{13,14},{15,16},{17,18},{19... | collective-permute-start | bytes 245768 | tf_op jit(solution)/shard_map/ppermute | solution.py:371
  55.8 1.9 %collective-permute-start.2 = (f32[5,32,128]{2,1,0:T(8,128)S(1)}, f32[5,32,128]{2,1,0:T(8,128)S(1)}, u32[]{:S(2)}, u32[]{:S(2)}) collective-permute-start(f32[5,32,128]{2,1,0:T(8,128)S(1)} %get-tuple-element.28), channel_id=1, source_target_pairs={{0,32},{64,96},{128,160},{192,224},{256,288},{320,352},{384,416},{... | collective-permute-start | bytes 245768 | tf_op jit(solution)/shard_map/ppermute | solution.py:371
  57.7 1.9 %collective-permute-start.3 = (f32[5,32,128]{2,1,0:T(8,128)S(1)}, f32[5,32,128]{2,1,0:T(8,128)S(1)}, u32[]{:S(2)}, u32[]{:S(2)}) collective-permute-start(f32[5,32,128]{2,1,0:T(8,128)S(1)} %get-tuple-element.29), channel_id=1, source_target_pairs={{0,1},{2,3},{4,5},{6,7},{8,9},{10,11},{12,13},{14,15},{16,17},{18,... | collective-permute-start | bytes 245768 | tf_op jit(solution)/shard_map/ppermute | solution.py:371
  59.6 0.8 shard_map.86.inner
  60.4 1.0 collective-permute-done.2.lon_even
  61.5 0.8 shard_map.87
  62.3 16.2 %all_to_all.21.received = bf16[32,2,640]{2,1,0:T(2,128)(2,1)S(1)} all-to-all(bf16[32,2,640]{2,1,0:T(2,128)(2,1)S(1)} %get-tuple-element.30), channel_id=1, replica_groups=mesh['gx'=16,'gy'=32] {'gy'}, dimensions={0} | all-to-all | bytes 163840 | tf_op jit(solution)/shard_map/all_to_all | solution.py:363
  78.5 2.1 %shard_map.88 = f32[32,1,1152]{2,1,0:T(1,128)S(1)} custom-call(bf16[32,2,640]{2,1,0:T(2,128)(2,1)S(1)} %all_to_all.21.received, bf16[12,137,4,137]{3,2,1,0:T(4,128)(2,1)S(1)} %shard_map.83.kept, bf16[16,137,4,137]{3,2,1,0:T(4,128)(2,1)} %bitcast.22, f32[64,64]{1,0:T(8,128)S(1)} %get-tuple-element.31.chosen), custom_call_target="tpu_custom_call" | custom-call | flops 1000 | bytes 1000000 | tf_op jit(solution)/shard_map/pallas_call | solution.py:469
  80.6 14.3 %all_to_all.22.returned = f32[32,1,1152]{2,1,0:T(1,128)S(1)} all-to-all(f32[32,1,1152]{2,1,0:T(1,128)S(1)} %shard_map.88), channel_id=1, replica_groups=mesh['gx'=16,'gy'=32] {'gy'}, dimensions={0} | all-to-all | bytes 294912 | tf_op jit(solution)/shard_map/all_to_all | solution.py:363
  94.9 0.8 shard_map.89
  95.7 3.1 %collective-permute-start.4 = (bf16[5,32,128]{2,1,0:T(8,128)(2,1)S(1)}, bf16[5,32,128]{2,1,0:T(8,128)(2,1)S(1)}, u32[]{:S(2)}, u32[]{:S(2)}) collective-permute-start(bf16[5,32,128]{2,1,0:T(8,128)(2,1)S(1)} %get-tuple-element.34), channel_id=1, source_target_pairs={{32,64},{96,128},{160,192},{224,256},{288,320},{352,384},{416,448}... | collective-permute-start | bytes 122888 | tf_op jit(solution)/shard_map/ppermute | solution.py:371
  98.8 2.5 %collective-permute-start.5 = (bf16[5,32,128]{2,1,0:T(8,128)(2,1)S(1)}, bf16[5,32,128]{2,1,0:T(8,128)(2,1)S(1)}, u32[]{:S(2)}, u32[]{:S(2)}) collective-permute-start(bf16[5,32,128]{2,1,0:T(8,128)(2,1)S(1)} %get-tuple-element.35), channel_id=1, source_target_pairs={{1,2},{3,4},{5,6},{7,8},{9,10},{11,12},{13,14},{15,16},{17,18},{19... | collective-permute-start | bytes 122888 | tf_op jit(solution)/shard_map/ppermute | solution.py:371
  101.3 1.9 %collective-permute-start.6 = (bf16[5,32,128]{2,1,0:T(8,128)(2,1)S(1)}, bf16[5,32,128]{2,1,0:T(8,128)(2,1)S(1)}, u32[]{:S(2)}, u32[]{:S(2)}) collective-permute-start(bf16[5,32,128]{2,1,0:T(8,128)(2,1)S(1)} %get-tuple-element.36), channel_id=1, source_target_pairs={{0,32},{64,96},{128,160},{192,224},{256,288},{320,352},{384,416},{... | collective-permute-start | bytes 122888 | tf_op jit(solution)/shard_map/ppermute | solution.py:371
  103.3 1.9 %collective-permute-start.7 = (bf16[5,32,128]{2,1,0:T(8,128)(2,1)S(1)}, bf16[5,32,128]{2,1,0:T(8,128)(2,1)S(1)}, u32[]{:S(2)}, u32[]{:S(2)}) collective-permute-start(bf16[5,32,128]{2,1,0:T(8,128)(2,1)S(1)} %get-tuple-element.37), channel_id=1, source_target_pairs={{0,1},{2,3},{4,5},{6,7},{8,9},{10,11},{12,13},{14,15},{16,17},{18,... | collective-permute-start | bytes 122888 | tf_op jit(solution)/shard_map/ppermute | solution.py:371
  105.2 0.6 shard_map.90.inner
  106.4 1.6 %shard_map.91 = (f32[4,512,137]{2,1,0:T(8,128)}, f32[5,512,128]{2,1,0:T(8,128)S(1)}) custom-call(f32[5,512,128]{2,1,0:T(8,128)S(1)} %shard_map.90.inner, f32[4,16,32]{2,1,0:T(8,128)S(1)} %bitcast.19, bf16[5,32,128]{2,1,0:T(8,128)(2,1)S(1)} %collective-permute-done.4.lon_odd, ...), custom_call_target="tpu_custom_call", output_to_operand_aliasing={{1}: (0, {})} | custom-call | flops 1000 | bytes 1000000 | tf_op jit(solution)/shard_map/pallas_call | solution.py:475
  (15 shorter events, 0.6 us)
Async XLA Ops:
  2.8 21.2 %all-to-all-start = ((bf16[32,2,640]{2,1,0:T(2,128)(2,1)}), bf16[32,2,640]{2,1,0:T(2,128)(2,1)S(1)}, u32[]{:S(2)}, u32[]{:S(2)}) async-start(bf16[32,2,640]{2,1,0:T(2,128)(2,1)} %get-tuple-element.23), calls=%async_computation | async-start | bytes 163840 | tf_op jit(solution)/shard_map/all_to_all | solution.py:363
  16.0 24.7 %copy-start.3 = (s32[97]{0:T(128)S(1)}, s32[97]{0:T(128)}, u32[]{:S(2)}) copy-start(s32[97]{0:T(128)} %get-tuple-element.22.plan) | copy-start | bytes 1168
  24.0 16.7 %copy-start = (bf16[4,137,32,16]{1,3,2,0:T(8,128)(2,1)S(1)}, bf16[4,137,32,16]{1,3,2,0:T(8,128)(2,1)}, u32[]{:S(2)}) copy-start(bf16[4,137,32,16]{1,3,2,0:T(8,128)(2,1)} %param.8) | copy-start | bytes 1683460
  26.2 33.4 %copy-start.1 = (bf16[4,137,32,16]{1,3,2,0:T(8,128)(2,1)S(1)}, bf16[4,137,32,16]{1,3,2,0:T(8,128)(2,1)}, u32[]{:S(2)}) copy-start(bf16[4,137,32,16]{1,3,2,0:T(8,128)(2,1)} %param.9) | copy-start | bytes 1683460
  26.2 33.4 %copy-start.2 = (f32[4,32,16]{1,2,0:T(8,128)S(1)}, f32[4,32,16]{1,2,0:T(8,128)}, u32[]{:S(2)}) copy-start(f32[4,32,16]{1,2,0:T(8,128)} %param.10) | copy-start | bytes 24580
  41.8 18.7 %collective-permute-start = (f32[5,32,128]{2,1,0:T(8,128)S(1)}, f32[5,32,128]{2,1,0:T(8,128)S(1)}, u32[]{:S(2)}, u32[]{:S(2)}) collective-permute-start(f32[5,32,128]{2,1,0:T(8,128)S(1)} %get-tuple-element.26), channel_id=1, source_target_pairs={{32,64},{96,128},{160,192},{224,256},{288,320},{352,384},{416,448}... | collective-permute-start | bytes 245768 | tf_op jit(solution)/shard_map/ppermute | solution.py:371
  53.3 7.2 %collective-permute-start.1 = (f32[5,32,128]{2,1,0:T(8,128)S(1)}, f32[5,32,128]{2,1,0:T(8,128)S(1)}, u32[]{:S(2)}, u32[]{:S(2)}) collective-permute-start(f32[5,32,128]{2,1,0:T(8,128)S(1)} %get-tuple-element.27), channel_id=1, source_target_pairs={{1,2},{3,4},{5,6},{7,8},{9,10},{11,12},{13,14},{15,16},{17,18},{19... | collective-permute-start | bytes 245768 | tf_op jit(solution)/shard_map/ppermute | solution.py:371
  55.8 5.7 %collective-permute-start.2 = (f32[5,32,128]{2,1,0:T(8,128)S(1)}, f32[5,32,128]{2,1,0:T(8,128)S(1)}, u32[]{:S(2)}, u32[]{:S(2)}) collective-permute-start(f32[5,32,128]{2,1,0:T(8,128)S(1)} %get-tuple-element.28), channel_id=1, source_target_pairs={{0,32},{64,96},{128,160},{192,224},{256,288},{320,352},{384,416},{... | collective-permute-start | bytes 245768 | tf_op jit(solution)/shard_map/ppermute | solution.py:371
  57.7 3.8 %collective-permute-start.3 = (f32[5,32,128]{2,1,0:T(8,128)S(1)}, f32[5,32,128]{2,1,0:T(8,128)S(1)}, u32[]{:S(2)}, u32[]{:S(2)}) collective-permute-start(f32[5,32,128]{2,1,0:T(8,128)S(1)} %get-tuple-element.29), channel_id=1, source_target_pairs={{0,1},{2,3},{4,5},{6,7},{8,9},{10,11},{12,13},{14,15},{16,17},{18,... | collective-permute-start | bytes 245768 | tf_op jit(solution)/shard_map/ppermute | solution.py:371
  95.7 10.1 %collective-permute-start.4 = (bf16[5,32,128]{2,1,0:T(8,128)(2,1)S(1)}, bf16[5,32,128]{2,1,0:T(8,128)(2,1)S(1)}, u32[]{:S(2)}, u32[]{:S(2)}) collective-permute-start(bf16[5,32,128]{2,1,0:T(8,128)(2,1)S(1)} %get-tuple-element.34), channel_id=1, source_target_pairs={{32,64},{96,128},{160,192},{224,256},{288,320},{352,384},{416,448}... | collective-permute-start | bytes 122888 | tf_op jit(solution)/shard_map/ppermute | solution.py:371
  98.8 7.0 %collective-permute-start.5 = (bf16[5,32,128]{2,1,0:T(8,128)(2,1)S(1)}, bf16[5,32,128]{2,1,0:T(8,128)(2,1)S(1)}, u32[]{:S(2)}, u32[]{:S(2)}) collective-permute-start(bf16[5,32,128]{2,1,0:T(8,128)(2,1)S(1)} %get-tuple-element.35), channel_id=1, source_target_pairs={{1,2},{3,4},{5,6},{7,8},{9,10},{11,12},{13,14},{15,16},{17,18},{19... | collective-permute-start | bytes 122888 | tf_op jit(solution)/shard_map/ppermute | solution.py:371
  101.3 4.7 %collective-permute-start.6 = (bf16[5,32,128]{2,1,0:T(8,128)(2,1)S(1)}, bf16[5,32,128]{2,1,0:T(8,128)(2,1)S(1)}, u32[]{:S(2)}, u32[]{:S(2)}) collective-permute-start(bf16[5,32,128]{2,1,0:T(8,128)(2,1)S(1)} %get-tuple-element.36), channel_id=1, source_target_pairs={{0,32},{64,96},{128,160},{192,224},{256,288},{320,352},{384,416},{... | collective-permute-start | bytes 122888 | tf_op jit(solution)/shard_map/ppermute | solution.py:371
  103.3 3.1 %collective-permute-start.7 = (bf16[5,32,128]{2,1,0:T(8,128)(2,1)S(1)}, bf16[5,32,128]{2,1,0:T(8,128)(2,1)S(1)}, u32[]{:S(2)}, u32[]{:S(2)}) collective-permute-start(bf16[5,32,128]{2,1,0:T(8,128)(2,1)S(1)} %get-tuple-element.37), channel_id=1, source_target_pairs={{0,1},{2,3},{4,5},{6,7},{8,9},{10,11},{12,13},{14,15},{16,17},{18,... | collective-permute-start | bytes 122888 | tf_op jit(solution)/shard_map/ppermute | solution.py:371

commit v14 on v12

--- a/solution.py
+++ b/solution.py
@@ -14,7 +14,7 @@
 HBM = pltpu.HBM
 PAIR = 2
 LANES = 128
-GROUP = 4
+GROUP = 8
 KEEP = 11
 CHUNK = 5
 

time: 108 us -> 108 us (level)
  no operation moved by 1% of the time
where the time goes in v14:
time: 108 us
  blocking collectives  45 us (42%)
  starting transfers between devices  38.5 us (36%)
  Pallas kernels  13.9 us (13%)
  waiting for transfers between devices  9.58 us (9%)
    all_to_all x3, blocking collectives, exchange(): return lax.all_to_all(lines, 'gy', split_axis=0, concat_axis=0, tiled=True)  45 us
    ppermute x8, starting transfers between devices, swap(): lax.ppermute(edge, axis, pairs + [(high, low) for low, high in pairs])  27.3 us
    all_to_all x1, starting transfers between devices, exchange(): return lax.all_to_all(lines, 'gy', split_axis=0, concat_axis=0, tiled=True)  11.2 us
    all_to_all x1, waiting for transfers between devices, exchange(): return lax.all_to_all(lines, 'gy', split_axis=0, concat_axis=0, tiled=True)  8.04 us
    pallas_call x1, Pallas kernels, on_device(): call(pack_first, [outbox_shape, plan_shape], [HBM] * 5, [VMEM, SMEM], [SM...  2.18 us
  transfers between devices with their start and end apart: 9, of which 4 were waited for; matrix products, arithmetic and copies ran while one was open for 0% of the time, Pallas kernels for 3%

profile of v14, /device:TPU:1, one launch (start us, length us, event | category | flops | bytes accessed | tf_op | source)
XLA Modules:
  0.0 107.9 jit_solution(16417182547454299980)
XLA Ops:
  0.7 2.2 %shard_map.82 = (bf16[32,2,640]{2,1,0:T(2,128)(2,1)}, s32[97]{0:T(128)}) custom-call(s32[1,1,48]{2,1,0:T(1,128)} %cols_hbm.1, s32[1,1]{1,0:T(1,128)S(6)} %copy.15.count_hbm, s32[1,1,48]{2,1,0:T(1,128)} %owner_hbm.1, s32[1,1,48]{2,1,0:T(1,128)} %slot_hbm.1, bf16[4,512,137]{2,1,0:T(8,128)(2,1)} %bitcast.13), custom_call_target="tpu_custom_call" | custom-call | flops 1000 | bytes 1000000 | tf_op jit(solution)/shard_map/pallas_call | solution.py:401
  2.8 11.2 %all-to-all-start = ((bf16[32,2,640]{2,1,0:T(2,128)(2,1)}), bf16[32,2,640]{2,1,0:T(2,128)(2,1)S(1)}, u32[]{:S(2)}, u32[]{:S(2)}) async-start(bf16[32,2,640]{2,1,0:T(2,128)(2,1)} %get-tuple-element.23), calls=%async_computation | async-start | bytes 163840 | tf_op jit(solution)/shard_map/all_to_all | solution.py:363
  14.1 1.9 %shard_map.83.kept = bf16[11,137,4,137]{3,2,1,0:T(4,128)(2,1)S(1)} custom-call(bf16[16,137,4,137]{3,2,1,0:T(4,128)(2,1)} %bitcast.20), custom_call_target="tpu_custom_call" | custom-call | flops 1000 | bytes 4000000 | tf_op jit(solution)/shard_map/pallas_call | solution.py:429
  16.0 8.0 %all-to-all-done.received = bf16[32,2,640]{2,1,0:T(2,128)(2,1)S(1)} async-done(((bf16[32,2,640]{2,1,0:T(2,128)(2,1)}), bf16[32,2,640]{2,1,0:T(2,128)(2,1)S(1)}, u32[]{:S(2)}, u32[]{:S(2)}) %all-to-all-start) | async-done | bytes 81952 | tf_op jit(solution)/shard_map/all_to_all | solution.py:363
  24.0 2.1 %shard_map.84 = (f32[32,1,1152]{2,1,0:T(1,128)S(1)}, f32[64,64]{1,0:T(8,128)S(1)}) custom-call(bf16[32,2,640]{2,1,0:T(2,128)(2,1)S(1)} %all-to-all-done.received, bf16[11,137,4,137]{3,2,1,0:T(4,128)(2,1)S(1)} %shard_map.83.kept, bf16[16,137,4,137]{3,2,1,0:T(4,128)(2,1)} %bitcast.21), custom_call_target="tpu_custom_call" | custom-call | flops 1000 | bytes 1000000 | tf_op jit(solution)/shard_map/pallas_call | solution.py:438
  26.2 14.5 %all_to_all.20.returned = f32[32,1,1152]{2,1,0:T(1,128)S(1)} all-to-all(f32[32,1,1152]{2,1,0:T(1,128)S(1)} %get-tuple-element.24), channel_id=1, replica_groups=mesh['gx'=16,'gy'=32] {'gy'}, dimensions={0} | all-to-all | bytes 294912 | tf_op jit(solution)/shard_map/all_to_all | solution.py:363
  40.7 1.0 shard_map.85
  41.7 11.2 %collective-permute-start = (f32[5,32,128]{2,1,0:T(8,128)S(1)}, f32[5,32,128]{2,1,0:T(8,128)S(1)}, u32[]{:S(2)}, u32[]{:S(2)}) collective-permute-start(f32[5,32,128]{2,1,0:T(8,128)S(1)} %get-tuple-element.26), channel_id=1, source_target_pairs={{32,64},{96,128},{160,192},{224,256},{288,320},{352,384},{416,448}... | collective-permute-start | bytes 245768 | tf_op jit(solution)/shard_map/ppermute | solution.py:371
  52.9 2.8 %collective-permute-start.1 = (f32[5,32,128]{2,1,0:T(8,128)S(1)}, f32[5,32,128]{2,1,0:T(8,128)S(1)}, u32[]{:S(2)}, u32[]{:S(2)}) collective-permute-start(f32[5,32,128]{2,1,0:T(8,128)S(1)} %get-tuple-element.27), channel_id=1, source_target_pairs={{1,2},{3,4},{5,6},{7,8},{9,10},{11,12},{13,14},{15,16},{17,18},{19... | collective-permute-start | bytes 245768 | tf_op jit(solution)/shard_map/ppermute | solution.py:371
  55.7 1.9 %collective-permute-start.2 = (f32[5,32,128]{2,1,0:T(8,128)S(1)}, f32[5,32,128]{2,1,0:T(8,128)S(1)}, u32[]{:S(2)}, u32[]{:S(2)}) collective-permute-start(f32[5,32,128]{2,1,0:T(8,128)S(1)} %get-tuple-element.28), channel_id=1, source_target_pairs={{0,32},{64,96},{128,160},{192,224},{256,288},{320,352},{384,416},{... | collective-permute-start | bytes 245768 | tf_op jit(solution)/shard_map/ppermute | solution.py:371
  57.6 1.9 %collective-permute-start.3 = (f32[5,32,128]{2,1,0:T(8,128)S(1)}, f32[5,32,128]{2,1,0:T(8,128)S(1)}, u32[]{:S(2)}, u32[]{:S(2)}) collective-permute-start(f32[5,32,128]{2,1,0:T(8,128)S(1)} %get-tuple-element.29), channel_id=1, source_target_pairs={{0,1},{2,3},{4,5},{6,7},{8,9},{10,11},{12,13},{14,15},{16,17},{18,... | collective-permute-start | bytes 245768 | tf_op jit(solution)/shard_map/ppermute | solution.py:371
  59.6 0.8 shard_map.86.inner
  60.4 1.0 collective-permute-done.2.lon_even
  61.3 0.8 shard_map.87
  62.2 16.2 %all_to_all.21.received = bf16[32,2,640]{2,1,0:T(2,128)(2,1)S(1)} all-to-all(bf16[32,2,640]{2,1,0:T(2,128)(2,1)S(1)} %get-tuple-element.30), channel_id=1, replica_groups=mesh['gx'=16,'gy'=32] {'gy'}, dimensions={0} | all-to-all | bytes 163840 | tf_op jit(solution)/shard_map/all_to_all | solution.py:363
  78.4 2.1 %shard_map.88 = f32[32,1,1152]{2,1,0:T(1,128)S(1)} custom-call(bf16[32,2,640]{2,1,0:T(2,128)(2,1)S(1)} %all_to_all.21.received, bf16[11,137,4,137]{3,2,1,0:T(4,128)(2,1)S(1)} %shard_map.83.kept, bf16[16,137,4,137]{3,2,1,0:T(4,128)(2,1)} %bitcast.22, f32[64,64]{1,0:T(8,128)S(1)} %get-tuple-element.31.chosen), custom_call_target="tpu_custom_call" | custom-call | flops 1000 | bytes 1000000 | tf_op jit(solution)/shard_map/pallas_call | solution.py:469
  80.4 14.3 %all_to_all.22.returned = f32[32,1,1152]{2,1,0:T(1,128)S(1)} all-to-all(f32[32,1,1152]{2,1,0:T(1,128)S(1)} %shard_map.88), channel_id=1, replica_groups=mesh['gx'=16,'gy'=32] {'gy'}, dimensions={0} | all-to-all | bytes 294912 | tf_op jit(solution)/shard_map/all_to_all | solution.py:363
  94.7 0.8 shard_map.89
  95.6 2.9 %collective-permute-start.4 = (bf16[5,32,128]{2,1,0:T(8,128)(2,1)S(1)}, bf16[5,32,128]{2,1,0:T(8,128)(2,1)S(1)}, u32[]{:S(2)}, u32[]{:S(2)}) collective-permute-start(bf16[5,32,128]{2,1,0:T(8,128)(2,1)S(1)} %get-tuple-element.34), channel_id=1, source_target_pairs={{32,64},{96,128},{160,192},{224,256},{288,320},{352,384},{416,448}... | collective-permute-start | bytes 122888 | tf_op jit(solution)/shard_map/ppermute | solution.py:371
  98.4 2.8 %collective-permute-start.5 = (bf16[5,32,128]{2,1,0:T(8,128)(2,1)S(1)}, bf16[5,32,128]{2,1,0:T(8,128)(2,1)S(1)}, u32[]{:S(2)}, u32[]{:S(2)}) collective-permute-start(bf16[5,32,128]{2,1,0:T(8,128)(2,1)S(1)} %get-tuple-element.35), channel_id=1, source_target_pairs={{1,2},{3,4},{5,6},{7,8},{9,10},{11,12},{13,14},{15,16},{17,18},{19... | collective-permute-start | bytes 122888 | tf_op jit(solution)/shard_map/ppermute | solution.py:371
  101.2 1.9 %collective-permute-start.6 = (bf16[5,32,128]{2,1,0:T(8,128)(2,1)S(1)}, bf16[5,32,128]{2,1,0:T(8,128)(2,1)S(1)}, u32[]{:S(2)}, u32[]{:S(2)}) collective-permute-start(bf16[5,32,128]{2,1,0:T(8,128)(2,1)S(1)} %get-tuple-element.36), channel_id=1, source_target_pairs={{0,32},{64,96},{128,160},{192,224},{256,288},{320,352},{384,416},{... | collective-permute-start | bytes 122888 | tf_op jit(solution)/shard_map/ppermute | solution.py:371
  103.2 1.9 %collective-permute-start.7 = (bf16[5,32,128]{2,1,0:T(8,128)(2,1)S(1)}, bf16[5,32,128]{2,1,0:T(8,128)(2,1)S(1)}, u32[]{:S(2)}, u32[]{:S(2)}) collective-permute-start(bf16[5,32,128]{2,1,0:T(8,128)(2,1)S(1)} %get-tuple-element.37), channel_id=1, source_target_pairs={{0,1},{2,3},{4,5},{6,7},{8,9},{10,11},{12,13},{14,15},{16,17},{18,... | collective-permute-start | bytes 122888 | tf_op jit(solution)/shard_map/ppermute | solution.py:371
  105.1 0.6 shard_map.90.inner
  106.3 1.6 %shard_map.91 = (f32[4,512,137]{2,1,0:T(8,128)}, f32[5,512,128]{2,1,0:T(8,128)S(1)}) custom-call(f32[5,512,128]{2,1,0:T(8,128)S(1)} %shard_map.90.inner, f32[4,16,32]{2,1,0:T(8,128)S(1)} %bitcast.19, bf16[5,32,128]{2,1,0:T(8,128)(2,1)S(1)} %collective-permute-done.4.lon_odd, ...), custom_call_target="tpu_custom_call", output_to_operand_aliasing={{1}: (0, {})} | custom-call | flops 1000 | bytes 1000000 | tf_op jit(solution)/shard_map/pallas_call | solution.py:475
  (15 shorter events, 0.6 us)
Async XLA Ops:
  2.8 21.2 %all-to-all-start = ((bf16[32,2,640]{2,1,0:T(2,128)(2,1)}), bf16[32,2,640]{2,1,0:T(2,128)(2,1)S(1)}, u32[]{:S(2)}, u32[]{:S(2)}) async-start(bf16[32,2,640]{2,1,0:T(2,128)(2,1)} %get-tuple-element.23), calls=%async_computation | async-start | bytes 163840 | tf_op jit(solution)/shard_map/all_to_all | solution.py:363
  16.0 24.7 %copy-start.3 = (s32[97]{0:T(128)S(1)}, s32[97]{0:T(128)}, u32[]{:S(2)}) copy-start(s32[97]{0:T(128)} %get-tuple-element.22.plan) | copy-start | bytes 1168
  24.0 16.7 %copy-start = (bf16[4,137,32,16]{1,3,2,0:T(8,128)(2,1)S(1)}, bf16[4,137,32,16]{1,3,2,0:T(8,128)(2,1)}, u32[]{:S(2)}) copy-start(bf16[4,137,32,16]{1,3,2,0:T(8,128)(2,1)} %param.8) | copy-start | bytes 1683460
  26.1 33.4 %copy-start.1 = (bf16[4,137,32,16]{1,3,2,0:T(8,128)(2,1)S(1)}, bf16[4,137,32,16]{1,3,2,0:T(8,128)(2,1)}, u32[]{:S(2)}) copy-start(bf16[4,137,32,16]{1,3,2,0:T(8,128)(2,1)} %param.9) | copy-start | bytes 1683460
  26.2 33.4 %copy-start.2 = (f32[4,32,16]{1,2,0:T(8,128)S(1)}, f32[4,32,16]{1,2,0:T(8,128)}, u32[]{:S(2)}) copy-start(f32[4,32,16]{1,2,0:T(8,128)} %param.10) | copy-start | bytes 24580
  41.7 18.6 %collective-permute-start = (f32[5,32,128]{2,1,0:T(8,128)S(1)}, f32[5,32,128]{2,1,0:T(8,128)S(1)}, u32[]{:S(2)}, u32[]{:S(2)}) collective-permute-start(f32[5,32,128]{2,1,0:T(8,128)S(1)} %get-tuple-element.26), channel_id=1, source_target_pairs={{32,64},{96,128},{160,192},{224,256},{288,320},{352,384},{416,448}... | collective-permute-start | bytes 245768 | tf_op jit(solution)/shard_map/ppermute | solution.py:371
  52.9 7.4 %collective-permute-start.1 = (f32[5,32,128]{2,1,0:T(8,128)S(1)}, f32[5,32,128]{2,1,0:T(8,128)S(1)}, u32[]{:S(2)}, u32[]{:S(2)}) collective-permute-start(f32[5,32,128]{2,1,0:T(8,128)S(1)} %get-tuple-element.27), channel_id=1, source_target_pairs={{1,2},{3,4},{5,6},{7,8},{9,10},{11,12},{13,14},{15,16},{17,18},{19... | collective-permute-start | bytes 245768 | tf_op jit(solution)/shard_map/ppermute | solution.py:371
  55.7 5.7 %collective-permute-start.2 = (f32[5,32,128]{2,1,0:T(8,128)S(1)}, f32[5,32,128]{2,1,0:T(8,128)S(1)}, u32[]{:S(2)}, u32[]{:S(2)}) collective-permute-start(f32[5,32,128]{2,1,0:T(8,128)S(1)} %get-tuple-element.28), channel_id=1, source_target_pairs={{0,32},{64,96},{128,160},{192,224},{256,288},{320,352},{384,416},{... | collective-permute-start | bytes 245768 | tf_op jit(solution)/shard_map/ppermute | solution.py:371
  57.6 3.7 %collective-permute-start.3 = (f32[5,32,128]{2,1,0:T(8,128)S(1)}, f32[5,32,128]{2,1,0:T(8,128)S(1)}, u32[]{:S(2)}, u32[]{:S(2)}) collective-permute-start(f32[5,32,128]{2,1,0:T(8,128)S(1)} %get-tuple-element.29), channel_id=1, source_target_pairs={{0,1},{2,3},{4,5},{6,7},{8,9},{10,11},{12,13},{14,15},{16,17},{18,... | collective-permute-start | bytes 245768 | tf_op jit(solution)/shard_map/ppermute | solution.py:371
  95.6 10.1 %collective-permute-start.4 = (bf16[5,32,128]{2,1,0:T(8,128)(2,1)S(1)}, bf16[5,32,128]{2,1,0:T(8,128)(2,1)S(1)}, u32[]{:S(2)}, u32[]{:S(2)}) collective-permute-start(bf16[5,32,128]{2,1,0:T(8,128)(2,1)S(1)} %get-tuple-element.34), channel_id=1, source_target_pairs={{32,64},{96,128},{160,192},{224,256},{288,320},{352,384},{416,448}... | collective-permute-start | bytes 122888 | tf_op jit(solution)/shard_map/ppermute | solution.py:371
  98.4 7.3 %collective-permute-start.5 = (bf16[5,32,128]{2,1,0:T(8,128)(2,1)S(1)}, bf16[5,32,128]{2,1,0:T(8,128)(2,1)S(1)}, u32[]{:S(2)}, u32[]{:S(2)}) collective-permute-start(bf16[5,32,128]{2,1,0:T(8,128)(2,1)S(1)} %get-tuple-element.35), channel_id=1, source_target_pairs={{1,2},{3,4},{5,6},{7,8},{9,10},{11,12},{13,14},{15,16},{17,18},{19... | collective-permute-start | bytes 122888 | tf_op jit(solution)/shard_map/ppermute | solution.py:371
  101.2 4.7 %collective-permute-start.6 = (bf16[5,32,128]{2,1,0:T(8,128)(2,1)S(1)}, bf16[5,32,128]{2,1,0:T(8,128)(2,1)S(1)}, u32[]{:S(2)}, u32[]{:S(2)}) collective-permute-start(bf16[5,32,128]{2,1,0:T(8,128)(2,1)S(1)} %get-tuple-element.36), channel_id=1, source_target_pairs={{0,32},{64,96},{128,160},{192,224},{256,288},{320,352},{384,416},{... | collective-permute-start | bytes 122888 | tf_op jit(solution)/shard_map/ppermute | solution.py:371
  103.2 3.1 %collective-permute-start.7 = (bf16[5,32,128]{2,1,0:T(8,128)(2,1)S(1)}, bf16[5,32,128]{2,1,0:T(8,128)(2,1)S(1)}, u32[]{:S(2)}, u32[]{:S(2)}) collective-permute-start(bf16[5,32,128]{2,1,0:T(8,128)(2,1)S(1)} %get-tuple-element.37), channel_id=1, source_target_pairs={{0,1},{2,3},{4,5},{6,7},{8,9},{10,11},{12,13},{14,15},{16,17},{18,... | collective-permute-start | bytes 122888 | tf_op jit(solution)/shard_map/ppermute | solution.py:371
